TPU v7x, 32 devices: a whole 2x2x4 slice. The times are simulated.
32 devices in a mesh: rep: 4 (over y, x), own: 8 (over z, core).
Axes of the slice: x: 2, y: 2, z: 4, core: 2. Of those that a mesh axis runs over, the one named last changes fastest.
Arguments:
- owners: int32 [16, 1], replicated, may hold values from 0 to 7; in each aligned block of 16 rows (0 to 15, 16 to 31, ...) at most 4 rows name the same one
- inner_dense: float32 [4, 16, 65536], P('rep', None, 'own'), may hold values from -6 to 6
- anchor_dense: float32 [16, 65536], P(None, 'own'), may hold values from -6 to 6
- momentum_dense: float32 [32, 65536], P('own'), may hold values from -6 to 6
- inner_emb: float32 [4, 1600, 1024], P('rep', 'own'), may hold values from -6 to 6
- anchor_emb: float32 [1600, 1024], P('own'), may hold values from -6 to 6
- momentum_emb: float32 [1600, 64], P('own'), may hold values from -6 to 6
- basis: float32 [1024, 64], replicated, may hold values from -0.1875 to 0.1875
Outputs:
- new_dense: float32 [16, 65536], P(None, 'own')
- new_momentum_dense: float32 [32, 65536], P('own')
- new_emb: float32 [1600, 1024], P('own')
- new_momentum_emb: float32 [1600, 64], P('own')
Inputs may be any that keep to these rules, and one draw needn't show every extreme that they name: `owners`: each owner position owns at most 4 blocks, and some position owns exactly 4.
All inputs are finite; a program needn't handle non-finite values.
Results may differ from a plain program's by a relative error of at most 0.00011.
Values sent between devices are 32-bit elements; how exact they have to be, the bound alone decides.
No kernel may reach another device: no remote copies, remote signals or barrier semaphores. Data moves between devices by JAX's collectives and lax.ppermute only.
A program may use at most 64 MiB of HBM per device.

v0:
```python
import jax
import jax.numpy as jnp
from jax import lax
from jax.sharding import PartitionSpec as P

outer_rate = 0.7
momentum_decay = 0.9


def slot_positions(owner_column, owner_count):
    owner_flat = owner_column[:, 0]
    onehot = (owner_flat[:, None] == jnp.arange(owner_count, dtype=jnp.int32)[None, :]).astype(
        jnp.int32
    )
    running = jnp.cumsum(onehot, axis=0) - onehot
    slot_of = jnp.sum(running * onehot, axis=1)
    return (owner_flat, slot_of)


def per_device(
    owners, inner_dense, anchor_dense, momentum_dense, inner_emb, anchor_emb, momentum_emb, basis
):
    owner_count = lax.axis_size("own")
    groups = lax.axis_size("rep")
    my_index = lax.axis_index("own")
    slot_count = momentum_dense.shape[0]
    flat_len = momentum_dense.shape[1]
    piece_len = anchor_dense.shape[1]
    owner_flat, slot_of = slot_positions(owners, owner_count)
    position = slot_of * owner_count + owner_flat
    owned_count = jnp.sum((owner_flat == my_index).astype(jnp.int32))
    live_mask = (jnp.arange(slot_count, dtype=jnp.int32) < owned_count)[:, None]
    difference = anchor_dense - inner_dense[0]
    factor = jnp.dot(
        anchor_emb - inner_emb[0],
        basis,
        precision=lax.Precision.HIGHEST,
        preferred_element_type=jnp.float32,
    )
    summed, factor_sum = lax.psum((difference, factor), "rep")
    mean_grad = summed / groups
    filled = (
        jnp.zeros((slot_count * owner_count, piece_len), jnp.float32).at[position].set(mean_grad)
    )
    received = lax.all_to_all(
        filled.reshape(slot_count, owner_count, piece_len),
        "own",
        split_axis=1,
        concat_axis=1,
        tiled=True,
    ).reshape(slot_count, flat_len)
    new_momentum_dense = jnp.where(live_mask, momentum_decay * momentum_dense + received, 0.0)
    slot_update = received + momentum_decay * new_momentum_dense
    returned = lax.all_to_all(
        slot_update.reshape(slot_count, owner_count, piece_len),
        "own",
        split_axis=1,
        concat_axis=1,
        tiled=True,
    )
    update = returned.reshape(slot_count * owner_count, piece_len)[position]
    new_dense = anchor_dense - outer_rate * update
    mean_factor = factor_sum / groups
    new_momentum_emb = momentum_decay * momentum_emb + mean_factor
    emb_update = mean_factor + momentum_decay * new_momentum_emb
    new_emb = anchor_emb - outer_rate * jnp.dot(
        emb_update, basis.T, precision=lax.Precision.HIGHEST, preferred_element_type=jnp.float32
    )
    return (new_dense, new_momentum_dense, new_emb, new_momentum_emb)


def solution(mesh):
    placed = (
        P(),
        P("rep", None, "own"),
        P(None, "own"),
        P("own", None),
        P("rep", "own", None),
        P("own", None),
        P("own", None),
        P(),
    )
    return jax.shard_map(
        per_device,
        mesh=mesh,
        in_specs=placed,
        out_specs=(P(None, "own"), P("own", None), P("own", None), P("own", None)),
        check_vma=False,
    )
```

profile of v0, /device:TPU:0, one launch (start us, length us, event | category | flops | bytes accessed | tf_op | source)
XLA Modules:
  0.0 135.9 jit_solution(17245028798882744797)
XLA Ops:
  7.2 0.0 copy-start
  7.2 0.0 all-reduce.2.cloned.1.call-start
  7.2 2.1 %bitcast_subtract_fusion.2 = f32[16,8192]{1,0:T(8,128)} fusion(f32[16,8192]{1,0:T(8,128)} %param.10, f32[1,16,8192]{2,1,0:T(8,128)} %param.9), kind=kLoop, calls=%fused_computation.9 | loop fusion | flops 131072 | bytes 1572864 | tf_op jit(solution)/shard_map/sub | solution.py:33
  9.3 0.0 all-reduce.2.cloned.1.call-update
  9.3 0.0 copy-start.7
  9.3 0.6 copy-done.7
  10.0 0.1 fusion.11
  10.1 0.2 select_reduce_fusion
  10.3 49.4 %all-reduce.2.cloned.1.call-done = f32[16,8192]{1,0:T(8,128)} async-done(((f32[16,8192]{1,0:T(8,128)}), f32[16,8192]{1,0:T(8,128)}) %all-reduce.2.cloned.1.call-update) | async-done | bytes 524304 | tf_op jit(solution)/shard_map/psum | solution.py:40
  59.7 1.7 %scatter_custom_fusion = f32[32,8192]{1,0:T(8,128)S(1)} fusion(s32[16]{0:T(128)S(1)} %fusion.13, f32[16,8192]{1,0:T(8,128)} %all-reduce.2.cloned.1.call-done, f32[]{:T(128)} %constant.8.clone.1, f32[]{:T(128)} %constant.12.clone.1), kind=kCustom, calls=%fused_computation.11 | custom fusion | flops 131072 | bytes 1572872 | tf_op jit(solution)/shard_map/scatter | solution.py:43
  61.3 1.6 %copy.12 = f32[4,8,8192]{2,0,1:T(4,128)} copy(f32[4,8,8192]{2,1,0:T(8,128)S(1)} %bitcast.23) | data formatting | bytes 2097152 | tf_op jit(solution)/shard_map/reshape | solution.py:46
  63.0 4.7 %all-to-all-start = ((f32[4,8,8192]{2,0,1:T(4,128)}), f32[4,8,8192]{2,0,1:T(4,128)S(1)}, u32[]{:S(2)}, u32[]{:S(2)}) async-start(f32[4,8,8192]{2,0,1:T(4,128)} %copy.12), calls=%async_computation | async-start | bytes 2097152 | tf_op jit(solution)/shard_map/all_to_all | solution.py:45
  67.7 0.6 fusion.12
  68.4 0.6 iota_compare_fusion.1
  69.0 25.3 %all-to-all-done = f32[4,8,8192]{2,0,1:T(4,128)S(1)} async-done(((f32[4,8,8192]{2,0,1:T(4,128)}), f32[4,8,8192]{2,0,1:T(4,128)S(1)}, u32[]{:S(2)}, u32[]{:S(2)}) %all-to-all-start) | async-done | bytes 1048608 | tf_op jit(solution)/shard_map/all_to_all | solution.py:45
  94.3 0.0 copy-done.3
  94.3 2.0 %multiply_add_fusion = (f32[4,65536]{1,0:T(4,128)}, f32[4,65536]{1,0:T(4,128)}) fusion(f32[4,65536]{1,0:T(4,128)S(1)} %bitcast.22, f32[4,65536]{1,0:T(4,128)S(1)} %copy-done.3, pred[4]{0:T(512)(128)(4,1)S(1)} %iota_compare_fusion.1), kind=kLoop, calls=%fused_computation.5 | loop fusion | flops 1310720 | bytes 4194308 | tf_op jit(solution)/shard_map/add | solution.py:53
  96.3 3.7 %all-to-all-start.1 = ((f32[4,8,8192]{2,0,1:T(4,128)}), f32[4,8,8192]{2,0,1:T(4,128)S(1)}, u32[]{:S(2)}, u32[]{:S(2)}) async-start(f32[4,8,8192]{2,0,1:T(4,128)} %bitcast.6), calls=%async_computation.1 | async-start | bytes 2097152 | tf_op jit(solution)/shard_map/all_to_all | solution.py:54
  100.0 0.0 copy-done
  100.0 0.0 copy-done.1
  100.0 0.0 copy-done.4
  100.0 0.9 fusion.1
  100.9 16.2 %psum.15 = f32[200,64]{0,1:T(8,128)S(1)} all-reduce(f32[200,64]{0,1:T(8,128)S(1)} %fusion.1), channel_id=1, replica_groups=mesh['rep'=4,'own'=8] {'rep'}, use_global_device_ids=true, to_apply=%region_5.6 | all-reduce | flops 12800 | bytes 102400 | tf_op jit(solution)/shard_map/psum | solution.py:40
  117.2 0.0 copy-done.6
  117.2 0.0 copy-start.5
  117.2 1.8 %fusion = f32[200,1024]{1,0:T(8,128)} fusion(f32[200,1024]{1,0:T(8,128)S(1)} %copy-done.1, f32[1024,64]{0,1:T(8,128)S(1)} %copy-done, f32[200,64]{0,1:T(8,128)S(1)} %multiply_add_fusion.1, f32[200,64]{0,1:T(8,128)S(1)} %psum.15), kind=kOutput, calls=%fused_computation.3 | convolution fusion | flops 157734400 | bytes 2002944 | tf_op jit(solution)/shard_map/dot_general | solution.py:66
  119.0 7.5 %all-to-all-done.1 = f32[4,8,8192]{2,0,1:T(4,128)S(1)} async-done(((f32[4,8,8192]{2,0,1:T(4,128)}), f32[4,8,8192]{2,0,1:T(4,128)S(1)}, u32[]{:S(2)}, u32[]{:S(2)}) %all-to-all-start.1) | async-done | bytes 1048608 | tf_op jit(solution)/shard_map/all_to_all | solution.py:54
  126.5 0.6 copy.15
  127.1 0.0 copy-start.2
  127.1 0.7 gather_fusion
  127.9 0.3 copy-done.2
  128.2 0.9 multiply_subtract_fusion
  (9 shorter events, 0.1 us)
Async XLA Ops:
  7.2 92.8 %copy-start = (f32[1024,64]{0,1:T(8,128)S(1)}, f32[1024,64]{0,1:T(8,128)}, u32[]{:S(2)}) copy-start(f32[1024,64]{0,1:T(8,128)} %param.15) | copy-start | bytes 786436
  7.2 52.5 %all-reduce.2.cloned.1.call-start = ((), (), s32[]{:S(2)}) async-start(), calls=%async_computation.2 | async-start | bytes 1048576 | tf_op jit(solution)/shard_map/psum | solution.py:40
  9.3 0.7 copy-start.7
  63.0 31.3 %copy-start.3 = (f32[4,65536]{1,0:T(4,128)S(1)}, f32[4,65536]{1,0:T(4,128)}, u32[]{:S(2)}) copy-start(f32[4,65536]{1,0:T(4,128)} %param.11) | copy-start | bytes 3145732
  63.0 31.3 %all-to-all-start = ((f32[4,8,8192]{2,0,1:T(4,128)}), f32[4,8,8192]{2,0,1:T(4,128)S(1)}, u32[]{:S(2)}, u32[]{:S(2)}) async-start(f32[4,8,8192]{2,0,1:T(4,128)} %copy.12), calls=%async_computation | async-start | bytes 2097152 | tf_op jit(solution)/shard_map/all_to_all | solution.py:45
  96.3 3.7 %copy-start.1 = (f32[200,1024]{1,0:T(8,128)S(1)}, f32[200,1024]{1,0:T(8,128)}, u32[]{:S(2)}) copy-start(f32[200,1024]{1,0:T(8,128)} %param.13) | copy-start | bytes 2457604
  96.3 3.7 %copy-start.4 = (f32[1,200,1024]{2,1,0:T(8,128)S(1)}, f32[1,200,1024]{2,1,0:T(8,128)}, u32[]{:S(2)}) copy-start(f32[1,200,1024]{2,1,0:T(8,128)} %param.12) | copy-start | bytes 2457604
  96.3 30.2 %all-to-all-start.1 = ((f32[4,8,8192]{2,0,1:T(4,128)}), f32[4,8,8192]{2,0,1:T(4,128)S(1)}, u32[]{:S(2)}, u32[]{:S(2)}) async-start(f32[4,8,8192]{2,0,1:T(4,128)} %bitcast.6), calls=%async_computation.1 | async-start | bytes 2097152 | tf_op jit(solution)/shard_map/all_to_all | solution.py:54
  100.9 16.2 %copy-start.6 = (f32[200,64]{0,1:T(8,128)S(1)}, f32[200,64]{0,1:T(8,128)}, u32[]{:S(2)}) copy-start(f32[200,64]{0,1:T(8,128)} %param.14) | copy-start | bytes 153604
  117.2 1.8 %copy-start.5 = (f32[200,64]{0,1:T(8,128)}, f32[200,64]{0,1:T(8,128)S(1)}, u32[]{:S(2)}) copy-start(f32[200,64]{0,1:T(8,128)S(1)} %multiply_add_fusion.1) | copy-start | bytes 153604
  127.1 1.0 copy-start.2
Sparse Core Ops, SparseCore 0:
  11.6 48.0 all-reduce.1
where the time goes:
time: 136 us
  waiting for transfers between devices  82.2 us (60%)
  blocking collectives  16.2 us (12%)
  between operations  14.2 us (10%)
  starting transfers between devices  8.46 us (6%)
  other arithmetic  8.19 us (6%)
  local copies, waits for them, and re-layouts  3.97 us (3%)
  matrix products  2.67 us (2%)
    psum x1, waiting for transfers between devices, per_device(): summed, factor_sum = lax.psum((difference, factor), 'rep')  49.4 us
    all_to_all x1, waiting for transfers between devices, per_device(): lax.all_to_all(filled.reshape(slot_count, owner_count, piece_len), 'own',...  25.3 us
    psum x1, blocking collectives, per_device(): summed, factor_sum = lax.psum((difference, factor), 'rep')  16.2 us
    all_to_all x1, waiting for transfers between devices, per_device(): lax.all_to_all(slot_update.reshape(slot_count, owner_count, piece_len), '...  7.53 us
    all_to_all x1, starting transfers between devices, per_device(): lax.all_to_all(filled.reshape(slot_count, owner_count, piece_len), 'own',...  4.74 us
    all_to_all x1, starting transfers between devices, per_device(): lax.all_to_all(slot_update.reshape(slot_count, owner_count, piece_len), '...  3.69 us
  transfers between devices with their start and end apart: 3, of which 3 were waited for; matrix products, arithmetic and copies ran while one was open for 3% of the time, Pallas kernels for 0%

commit v1 on v0

v1 whole, which is shorter than its diff:
```python
import functools

import jax
import jax.numpy as jnp
from jax import lax
from jax.experimental import pallas as pl
from jax.experimental.pallas import tpu as pltpu
from jax.sharding import PartitionSpec as P

outer_rate = 0.7
momentum_decay = 0.9
most_direct_chips = 8
f32 = jnp.float32
vmem_limit = 48 * 1024 * 1024


def on_chip(x):
    return pltpu.with_memory_space_constraint(x, pltpu.VMEM)


def kept(shape):
    return pltpu.VMEM(shape, f32)


def stored(shape):
    return jax.ShapeDtypeStruct(shape, f32)


def run(body, outs, operands, scalars=(), scratch=(), name=None):
    vmem = pl.BlockSpec(memory_space=pltpu.VMEM)
    smem = pl.BlockSpec(memory_space=pltpu.SMEM)
    return pl.pallas_call(
        body,
        out_shape=list(outs),
        in_specs=[smem] * len(scalars) + [vmem] * len(operands),
        out_specs=[vmem] * len(outs),
        scratch_shapes=list(scratch),
        compiler_params=pltpu.CompilerParams(vmem_limit_bytes=vmem_limit),
        name=name,
    )(*scalars, *operands)


def swap(x, axis, count, mask):
    return lax.ppermute(x, axis, [(i, i ^ mask) for i in range(count)])


def places(owners, owner_count, slot_count):
    owner_flat = owners[:, 0]
    onehot = (owner_flat[:, None] == jnp.arange(owner_count, dtype=jnp.int32)[None, :]).astype(
        jnp.int32
    )
    running = jnp.cumsum(onehot, axis=0) - onehot
    slot_of = jnp.sum(running * onehot, axis=1)
    row_of = owner_flat * slot_count + slot_of
    rows = jnp.arange(owner_count * slot_count, dtype=jnp.int32)
    named = (row_of[:, None] == rows[None, :]).astype(jnp.int32)
    block_of = jnp.sum(named * jnp.arange(owner_flat.shape[0], dtype=jnp.int32)[:, None], axis=0)
    return row_of, block_of, jnp.sum(onehot, axis=0)


def difference_body(part, groups, me, anchor, inner, *outs):
    for k in range(groups):
        at = pl.ds(pl.multiple_of((me[0] ^ k) * part, 128), part)
        outs[k][...] = anchor[:, at] - inner[0, :, at]


def momentum_body(part, groups, me, momentum, same, other):
    chips = same.shape[0]
    for chip in range(chips):
        for o, out in enumerate((same, other)):
            piece = 2 * chip + (me[2] ^ o)
            at = pl.multiple_of((piece * groups + me[0]) * part, 128)
            out[chip] = momentum[:, pl.ds(at, part)]


def mean_body(groups, me, block_of, *refs):
    parts, (mean, same, other) = refs[:groups], refs[groups:]
    total = parts[0][...]
    for ref in parts[1:]:
        total = total + ref[...]
    mean[...] = total / groups
    chips, slots, _ = same.shape

    def fill(chip, carry):
        for o, out in enumerate((same, other)):
            for s in range(slots):
                block = block_of[(2 * chip + (me[2] ^ o)) * slots + s]
                out[chip, pl.ds(s, 1), :] = mean[pl.ds(block, 1), :]
        return carry

    lax.fori_loop(0, chips, fill, 0, unroll=chips <= 8)


def pack_body(direct, me, same, other, *outs):
    if direct:
        for k, out in enumerate(outs):
            out[0] = same[me[1] ^ k]
            out[1] = other[me[1] ^ k]
    else:
        outs[0][:, 0] = same[...]
        outs[0][:, 1] = other[...]


def join_body(*refs):
    out = refs[-1]
    for k, ref in enumerate(refs[:-1]):
        out[k] = ref[...]


def dense_body(part, direct, me, row_of, anchor, mean, *refs):
    *received, out, rows = refs
    slots = received[0].shape[-2]
    blocks = mean.shape[0]
    if direct:
        for k, ref in enumerate(received):
            rows[k] = ref[...]
        table = rows
    else:
        table = received[0]

    def update(block, carry):
        row = row_of[block]
        owner = row // slots
        chip = (owner // 2) ^ me[1] if direct else owner // 2
        momentum = table[chip, (owner % 2) ^ me[2], pl.ds(row % slots, 1), :]
        mean_row = mean[pl.ds(block, 1), :]
        new_momentum = momentum_decay * momentum + mean_row
        out[pl.ds(block, 1), :] = out[pl.ds(block, 1), :] - outer_rate * (
            mean_row + momentum_decay * new_momentum
        )
        return carry

    out[...] = anchor[:, pl.ds(pl.multiple_of(me[0] * part, 128), part)]

    lax.fori_loop(0, blocks, update, 0, unroll=blocks <= 16)


def dense_out_body(part, me, *refs):
    out = refs[-1]
    for k, ref in enumerate(refs[:-1]):
        out[:, pl.ds(pl.multiple_of((me[0] ^ k) * part, 128), part)] = ref[...]


def momentum_out_body(part, direct, me, owned, momentum, *refs):
    out = refs[-1]
    groups = len(refs) - 1
    chips = refs[0].shape[0]
    slots = momentum.shape[0]
    live = lax.broadcasted_iota(jnp.int32, (slots, part), 0) < owned[me[1] * 2 + me[2]]

    def fill(k, carry):
        chip = me[1] ^ k if direct else k
        for o in range(2):
            piece = 2 * chip + (me[2] ^ o)
            for g in range(groups):
                at = pl.ds(pl.multiple_of((piece * groups + (me[0] ^ g)) * part, 128), part)
                out[:, at] = jnp.where(
                    live, momentum_decay * momentum[:, at] + refs[g][k, o], 0.0
                )
        return carry

    lax.fori_loop(0, chips, fill, 0, unroll=chips <= 8)


def dot(a, b, contract):
    return lax.dot_general(
        a,
        b,
        ((contract), ((), ())),
        precision=lax.Precision.HIGHEST,
        preferred_element_type=f32,
    )


def factor_body(anchor, inner, basis_t, out):
    out[...] = dot(basis_t[...], anchor[...] - inner[0], ((1,), (1,)))


def embedding_body(groups, anchor, momentum_t, basis_t, *refs):
    parts, (new_emb, new_momentum_t) = refs[:groups], refs[groups:]
    total = parts[0][...]
    for ref in parts[1:]:
        total = total + ref[...]
    mean = total / groups
    moved = momentum_decay * momentum_t[...] + mean
    new_momentum_t[...] = moved
    update = mean + momentum_decay * moved
    new_emb[...] = anchor[...] - outer_rate * dot(update, basis_t[...], ((0,), (0,)))


def over_chips(same, other, me, chips, owner_count):
    other = swap(other, "own", owner_count, 1)
    shape = (2,) + same.shape[1:]
    if chips <= most_direct_chips:
        outs = run(
            functools.partial(pack_body, True),
            [kept(shape)] * chips,
            [on_chip(same), on_chip(other)],
            [me],
            name="pack",
        )
        return [outs[0]] + [swap(outs[k], "own", owner_count, 2 * k) for k in range(1, chips)]
    (packed,) = run(
        functools.partial(pack_body, False),
        [stored((chips,) + shape)],
        [same, other],
        [me],
        name="pack",
    )
    groups = [list(range(core, owner_count, 2)) for core in range(2)]
    return [
        lax.all_to_all(
            packed, "own", split_axis=0, concat_axis=0, axis_index_groups=groups, tiled=True
        )
    ]


def per_device(
    owners, inner_dense, anchor_dense, momentum_dense, inner_emb, anchor_emb, momentum_emb, basis
):
    owner_count = lax.axis_size("own")
    groups = lax.axis_size("rep")
    chips = owner_count // 2
    direct = chips <= most_direct_chips
    slot_count = momentum_dense.shape[0]
    blocks, piece_len = anchor_dense.shape
    part = piece_len // groups
    position = lax.axis_index("own")
    me = jnp.stack([lax.axis_index("rep"), position // 2, position % 2]).astype(jnp.int32)
    row_of, block_of, owned = places(owners, owner_count, slot_count)

    parts = run(
        functools.partial(difference_body, part, groups),
        [kept((blocks, part))] * groups,
        [anchor_dense, inner_dense],
        [me],
        name="difference",
    )
    parts = [parts[0]] + [swap(parts[k], "rep", groups, k) for k in range(1, groups)]

    chunk = (chips, slot_count, part)
    same, other = run(
        functools.partial(momentum_body, part, groups),
        [kept(chunk)] * 2,
        [momentum_dense],
        [me],
        name="momentum_pieces",
    )
    momentum_rows = over_chips(same, other, me, chips, owner_count)

    rows = anchor_emb.shape[0]
    rank = basis.shape[1]
    basis_t = basis.T
    (factor,) = run(
        factor_body, [kept((rank, rows))], [anchor_emb, inner_emb, basis_t], name="factor"
    )
    factors = [factor] + [swap(factor, "rep", groups, k) for k in range(1, groups)]

    mean, same, other = run(
        functools.partial(mean_body, groups),
        [kept((blocks, part)), kept(chunk), kept(chunk)],
        [on_chip(x) for x in parts],
        [me, block_of],
        name="mean",
    )
    table = (chips, 2, slot_count, part)
    gradient_rows = over_chips(same, other, me, chips, owner_count)

    (dense,) = run(
        functools.partial(dense_body, part, direct),
        [kept((blocks, part))],
        [anchor_dense, on_chip(mean)] + [on_chip(x) for x in momentum_rows],
        [me, row_of],
        [pltpu.VMEM(table if direct else (8, 128), f32)],
        name="dense",
    )
    dense = [dense] + [swap(dense, "rep", groups, k) for k in range(1, groups)]

    if direct:
        (gradient,) = run(
            join_body, [kept(table)], [on_chip(x) for x in gradient_rows], name="join"
        )
    else:
        (gradient,) = gradient_rows
    gradient = [gradient] + [swap(gradient, "rep", groups, k) for k in range(1, groups)]

    (new_dense,) = run(
        functools.partial(dense_out_body, part),
        [stored((blocks, piece_len))],
        [on_chip(x) for x in dense],
        [me],
        name="dense_out",
    )
    new_emb, new_momentum_t = run(
        functools.partial(embedding_body, groups),
        [stored(anchor_emb.shape), stored((rank, rows))],
        [anchor_emb, momentum_emb.T, basis_t] + [on_chip(x) for x in factors],
        name="embedding",
    )
    (new_momentum_dense,) = run(
        functools.partial(momentum_out_body, part, direct),
        [stored(momentum_dense.shape)],
        [momentum_dense] + [on_chip(x) for x in gradient],
        [me, owned],
        name="momentum_out",
    )
    return (new_dense, new_momentum_dense, new_emb, new_momentum_t.T)


def solution(mesh):
    placed = (
        P(),
        P("rep", None, "own"),
        P(None, "own"),
        P("own", None),
        P("rep", "own", None),
        P("own", None),
        P("own", None),
        P(),
    )
    return jax.shard_map(
        per_device,
        mesh=mesh,
        in_specs=placed,
        out_specs=(P(None, "own"), P("own", None), P("own", None), P("own", None)),
        check_vma=False,
    )
```

time: 136 us -> 64.3 us (0.47)
  waiting for transfers between devices: 82.2 us -> 25.7 us
  blocking collectives: 16.2 us -> 0 us
  starting transfers between devices: 8.46 us -> 24.1 us
  between operations: 14.2 us -> 0.76 us
  Pallas kernels: 0 us -> 10.9 us
  other arithmetic: 8.19 us -> 0.47 us
  matrix products: 2.67 us -> 0 us
  local copies, waits for them, and re-layouts: 3.97 us -> 2.18 us
    psum x1 -> x0, waiting for transfers between devices: 49.4 us -> none  [per_device(): summed, factor_sum = lax.psum((difference, factor), 'rep')]
    all_to_all x2 -> x0, waiting for transfers between devices: 32.8 us -> none  [the longest x1 25.3 us: per_device(): lax.all_to_all(filled.reshape(slot_count, owner_count, piece_len), 'own',...]
    ppermute x0 -> x20, waiting for transfers between devices: none -> 25.7 us  [swap(): return lax.ppermute(x, axis, [(i, i ^ mask) for i in range(count)])]
    ppermute x0 -> x20, starting transfers between devices: none -> 24.1 us  [swap(): return lax.ppermute(x, axis, [(i, i ^ mask) for i in range(count)])]
    psum x1 -> x0, blocking collectives: 16.2 us -> none  [per_device(): summed, factor_sum = lax.psum((difference, factor), 'rep')]
    pallas_call x0 -> x11, Pallas kernels: none -> 10.9 us  [run(): pl.pallas_call(body, out_shape=list(outs), in_specs=[smem] * len(scalars)...]
    all_to_all x2 -> x0, starting transfers between devices: 8.42 us -> none  [the longest x1 4.74 us: per_device(): lax.all_to_all(filled.reshape(slot_count, owner_count, piece_len), 'own',...]
    sub x2 -> x0, other arithmetic: 2.93 us -> none  [the longest x1 2.08 us: per_device(): difference = anchor_dense - inner_dense[0]]
  transfers between devices with their start and end apart: 3 -> 20, of which waited for: 3 -> 9; matrix products, arithmetic and copies ran while one was open for 3% -> 1% of each run, Pallas kernels for 0% -> 12%
where the time goes in v1:
time: 64.3 us; the launch traced here: 64.1 us
  waiting for transfers between devices  25.7 us (40%)
  starting transfers between devices  24.1 us (37%)
  Pallas kernels  10.9 us (17%)
  local copies, waits for them, and re-layouts  2.18 us (3%)
  between operations  0.76 us (1%)
    ppermute x20, waiting for transfers between devices, swap(): return lax.ppermute(x, axis, [(i, i ^ mask) for i in range(count)])  25.7 us
    ppermute x20, starting transfers between devices, swap(): return lax.ppermute(x, axis, [(i, i ^ mask) for i in range(count)])  24.1 us
    pallas_call x11, Pallas kernels, run(): pl.pallas_call(body, out_shape=list(outs), in_specs=[smem] * len(scalars)...  10.9 us
    unnamed x18, local copies, waits for them, and re-layouts  2.18 us
  transfers between devices with their start and end apart: 20, of which 9 were waited for; matrix products, arithmetic and copies ran while one was open for 1% of the time, Pallas kernels for 12%

profile of v1, /device:TPU:0, one launch (start us, length us, event | category | flops | bytes accessed | tf_op | source)
XLA Modules:
  0.0 64.1 jit_solution(166172716908483196)
XLA Ops:
  0.7 1.1 %copy-done.2 = f32[16,8192]{1,0:T(8,128)S(1)} copy-done((f32[16,8192]{1,0:T(8,128)S(1)}, f32[16,8192]{1,0:T(8,128)}, u32[]{:S(2)}) %copy-start.2) | copy-done | bytes 524312
  1.9 1.0 %copy-done.6 = f32[1,16,8192]{2,1,0:T(8,128)S(1)} copy-done((f32[1,16,8192]{2,1,0:T(8,128)S(1)}, f32[1,16,8192]{2,1,0:T(8,128)}, u32[]{:S(2)}) %copy-start.6) | copy-done | bytes 524312
  2.9 1.3 %difference.1 = (f32[16,2048]{1,0:T(8,128)S(1)}, f32[16,2048]{1,0:T(8,128)}, f32[16,2048]{1,0:T(8,128)}, f32[16,2048]{1,0:T(8,128)}) custom-call(s32[3]{0:T(128)S(1)} %pad_add_fusion.me, f32[16,8192]{1,0:T(8,128)S(1)} %copy-done.2, f32[1,16,8192]{2,1,0:T(8,128)S(1)} %copy-done.6), custom_call_target="tpu_custom_call" | custom-call | tf_op jit(solution)/shard_map/difference/pallas_call | solution.py:32
  4.2 2.9 %collective-permute-start = (f32[16,2048]{1,0:T(8,128)}, f32[16,2048]{1,0:T(8,128)S(1)}, u32[]{:S(2)}, u32[]{:S(2)}) collective-permute-start(f32[16,2048]{1,0:T(8,128)} %get-tuple-element.24), channel_id=1, source_target_pairs={{0,8},{8,0},{16,24},{24,16},{1,9},{9,1},{17,25},{25,17},{2,10},{10... | collective-permute-start | bytes 393224 | tf_op jit(solution)/shard_map/ppermute | solution.py:44
  7.2 1.5 %collective-permute-start.1 = (f32[16,2048]{1,0:T(8,128)}, f32[16,2048]{1,0:T(8,128)S(1)}, u32[]{:S(2)}, u32[]{:S(2)}) collective-permute-start(f32[16,2048]{1,0:T(8,128)} %get-tuple-element.25), channel_id=1, source_target_pairs={{0,16},{8,24},{16,0},{24,8},{1,17},{9,25},{17,1},{25,9},{2,18},{10... | collective-permute-start | bytes 393224 | tf_op jit(solution)/shard_map/ppermute | solution.py:44
  8.7 1.2 %momentum_pieces.1 = (f32[4,4,2048]{2,1,0:T(4,128)S(1)}, f32[4,4,2048]{2,1,0:T(4,128)}) custom-call(s32[3]{0:T(128)S(1)} %pad_add_fusion.me, f32[4,65536]{1,0:T(4,128)S(1)} %copy-done), custom_call_target="tpu_custom_call" | custom-call | tf_op jit(solution)/shard_map/momentum_pieces/pallas_call | solution.py:32
  10.3 1.1 %collective-permute-done.refs_1_ = f32[16,2048]{1,0:T(8,128)S(1)} collective-permute-done((f32[16,2048]{1,0:T(8,128)}, f32[16,2048]{1,0:T(8,128)S(1)}, u32[]{:S(2)}, u32[]{:S(2)}) %collective-permute-start) | collective-permute-done | bytes 131104 | tf_op jit(solution)/shard_map/ppermute | solution.py:44
  11.4 3.8 %collective-permute-done.1.refs_2_ = f32[16,2048]{1,0:T(8,128)S(1)} collective-permute-done((f32[16,2048]{1,0:T(8,128)}, f32[16,2048]{1,0:T(8,128)S(1)}, u32[]{:S(2)}, u32[]{:S(2)}) %collective-permute-start.1) | collective-permute-done | bytes 131104 | tf_op jit(solution)/shard_map/ppermute | solution.py:44
  16.5 1.6 %collective-permute-start.4 = (f32[2,4,2048]{2,1,0:T(4,128)S(1)}, f32[2,4,2048]{2,1,0:T(4,128)S(1)}, u32[]{:S(2)}, u32[]{:S(2)}) collective-permute-start(f32[2,4,2048]{2,1,0:T(4,128)S(1)} %get-tuple-element.31), channel_id=1, source_target_pairs={{0,2},{1,3},{2,0},{3,1},{4,6},{5,7},{6,4},{7,5},{8,10},{9,11},{10,... | collective-permute-start | bytes 196616 | tf_op jit(solution)/shard_map/ppermute | solution.py:44
  18.1 2.6 %collective-permute-start.5 = (f32[2,4,2048]{2,1,0:T(4,128)S(1)}, f32[2,4,2048]{2,1,0:T(4,128)S(1)}, u32[]{:S(2)}, u32[]{:S(2)}) collective-permute-start(f32[2,4,2048]{2,1,0:T(4,128)S(1)} %get-tuple-element.32), channel_id=1, source_target_pairs={{0,4},{1,5},{2,6},{3,7},{4,0},{5,1},{6,2},{7,3},{8,12},{9,13},{10,... | collective-permute-start | bytes 196616 | tf_op jit(solution)/shard_map/ppermute | solution.py:44
  20.7 0.9 %factor.1.refs_0_ = f32[64,200]{1,0:T(8,128)S(1)} custom-call(f32[200,1024]{1,0:T(8,128)S(1)} %copy-done.1, f32[1,200,1024]{2,1,0:T(8,128)S(1)} %copy-done.5, f32[64,1024]{1,0:T(8,128)S(1)} %bitcast.14), custom_call_target="tpu_custom_call" | custom-call | tf_op jit(solution)/shard_map/factor/pallas_call | solution.py:32
  21.6 1.3 %collective-permute-start.17 = (f32[64,200]{1,0:T(8,128)S(1)}, f32[64,200]{1,0:T(8,128)S(1)}, u32[]{:S(2)}, u32[]{:S(2)}) collective-permute-start(f32[64,200]{1,0:T(8,128)S(1)} %factor.1.refs_0_), channel_id=1, source_target_pairs={{0,8},{8,0},{16,24},{24,16},{1,9},{9,1},{17,25},{25,17},{2,10},{10... | collective-permute-start | bytes 153608 | tf_op jit(solution)/shard_map/ppermute | solution.py:44
  23.7 0.7 %collective-permute-start.11 = (f32[2,4,2048]{2,1,0:T(4,128)S(1)}, f32[2,4,2048]{2,1,0:T(4,128)S(1)}, u32[]{:S(2)}, u32[]{:S(2)}) collective-permute-start(f32[2,4,2048]{2,1,0:T(4,128)S(1)} %get-tuple-element.37), channel_id=1, source_target_pairs={{0,2},{1,3},{2,0},{3,1},{4,6},{5,7},{6,4},{7,5},{8,10},{9,11},{10,... | collective-permute-start | bytes 196616 | tf_op jit(solution)/shard_map/ppermute | solution.py:44
  24.5 3.5 %collective-permute-start.12 = (f32[2,4,2048]{2,1,0:T(4,128)S(1)}, f32[2,4,2048]{2,1,0:T(4,128)S(1)}, u32[]{:S(2)}, u32[]{:S(2)}) collective-permute-start(f32[2,4,2048]{2,1,0:T(4,128)S(1)} %get-tuple-element.38), channel_id=1, source_target_pairs={{0,4},{1,5},{2,6},{3,7},{4,0},{5,1},{6,2},{7,3},{8,12},{9,13},{10,... | collective-permute-start | bytes 196616 | tf_op jit(solution)/shard_map/ppermute | solution.py:44
  28.2 1.7 %collective-permute-done.6.refs_3_ = f32[2,4,2048]{2,1,0:T(4,128)S(1)} collective-permute-done((f32[2,4,2048]{2,1,0:T(4,128)S(1)}, f32[2,4,2048]{2,1,0:T(4,128)S(1)}, u32[]{:S(2)}, u32[]{:S(2)}) %collective-permute-start.6) | collective-permute-done | bytes 65568 | tf_op jit(solution)/shard_map/ppermute | solution.py:44
  29.8 0.8 %dense.1.refs_0_ = f32[16,2048]{1,0:T(8,128)S(1)} custom-call(s32[3]{0:T(128)S(1)} %pad_add_fusion.me, s32[16]{0:T(128)S(1)} %multiply_add_fusion.row_of, f32[16,8192]{1,0:T(8,128)S(1)} %copy-done.3, f32[16,2048]{1,0:T(8,128)S(1)} %get-tuple-element.27.mean, f32[2,4,2048]{2,1,0:T(4,128)S(1)} %get-tuple-element.30.refs_0_, ...), custom_call_target="tpu_custom_call" | custom-call | tf_op jit(solution)/shard_map/dense/pallas_call | solution.py:32
  30.6 0.9 %collective-permute-start.7 = (f32[16,2048]{1,0:T(8,128)S(1)}, f32[16,2048]{1,0:T(8,128)S(1)}, u32[]{:S(2)}, u32[]{:S(2)}) collective-permute-start(f32[16,2048]{1,0:T(8,128)S(1)} %dense.1.refs_0_), channel_id=1, source_target_pairs={{0,8},{8,0},{16,24},{24,16},{1,9},{9,1},{17,25},{25,17},{2,10},{10... | collective-permute-start | bytes 393224 | tf_op jit(solution)/shard_map/ppermute | solution.py:44
  31.5 1.2 %collective-permute-done.12.refs_2_ = f32[2,4,2048]{2,1,0:T(4,128)S(1)} collective-permute-done((f32[2,4,2048]{2,1,0:T(4,128)S(1)}, f32[2,4,2048]{2,1,0:T(4,128)S(1)}, u32[]{:S(2)}, u32[]{:S(2)}) %collective-permute-start.12) | collective-permute-done | bytes 65568 | tf_op jit(solution)/shard_map/ppermute | solution.py:44
  32.7 1.4 %collective-permute-done.13.refs_3_ = f32[2,4,2048]{2,1,0:T(4,128)S(1)} collective-permute-done((f32[2,4,2048]{2,1,0:T(4,128)S(1)}, f32[2,4,2048]{2,1,0:T(4,128)S(1)}, u32[]{:S(2)}, u32[]{:S(2)}) %collective-permute-start.13) | collective-permute-done | bytes 65568 | tf_op jit(solution)/shard_map/ppermute | solution.py:44
  34.2 0.9 %collective-permute-start.14 = (f32[4,2,4,2048]{3,2,1,0:T(4,128)S(1)}, f32[4,2,4,2048]{3,2,1,0:T(4,128)S(1)}, u32[]{:S(2)}, u32[]{:S(2)}) collective-permute-start(f32[4,2,4,2048]{3,2,1,0:T(4,128)S(1)} %join.1.refs_0_), channel_id=1, source_target_pairs={{0,8},{8,0},{16,24},{24,16},{1,9},{9,1},{17,25},{25,17},{2,10},{10... | collective-permute-start | bytes 786440 | tf_op jit(solution)/shard_map/ppermute | solution.py:44
  35.0 1.5 %collective-permute-start.15 = (f32[4,2,4,2048]{3,2,1,0:T(4,128)S(1)}, f32[4,2,4,2048]{3,2,1,0:T(4,128)S(1)}, u32[]{:S(2)}, u32[]{:S(2)}) collective-permute-start(f32[4,2,4,2048]{3,2,1,0:T(4,128)S(1)} %join.1.refs_0_), channel_id=1, source_target_pairs={{0,16},{8,24},{16,0},{24,8},{1,17},{9,25},{17,1},{25,9},{2,18},{10... | collective-permute-start | bytes 786440 | tf_op jit(solution)/shard_map/ppermute | solution.py:44
  36.5 1.2 %collective-permute-start.16 = (f32[4,2,4,2048]{3,2,1,0:T(4,128)S(1)}, f32[4,2,4,2048]{3,2,1,0:T(4,128)S(1)}, u32[]{:S(2)}, u32[]{:S(2)}) collective-permute-start(f32[4,2,4,2048]{3,2,1,0:T(4,128)S(1)} %join.1.refs_0_), channel_id=1, source_target_pairs={{0,24},{8,16},{16,8},{24,0},{1,25},{9,17},{17,9},{25,1},{2,26},{10... | collective-permute-start | bytes 786440 | tf_op jit(solution)/shard_map/ppermute | solution.py:44
  37.7 0.8 %collective-permute-start.18 = (f32[64,200]{1,0:T(8,128)S(1)}, f32[64,200]{1,0:T(8,128)S(1)}, u32[]{:S(2)}, u32[]{:S(2)}) collective-permute-start(f32[64,200]{1,0:T(8,128)S(1)} %factor.1.refs_0_), channel_id=1, source_target_pairs={{0,16},{8,24},{16,0},{24,8},{1,17},{9,25},{17,1},{25,9},{2,18},{10... | collective-permute-start | bytes 153608 | tf_op jit(solution)/shard_map/ppermute | solution.py:44
  38.5 9.9 %collective-permute-done.18.refs_2_ = f32[64,200]{1,0:T(8,128)S(1)} collective-permute-done((f32[64,200]{1,0:T(8,128)S(1)}, f32[64,200]{1,0:T(8,128)S(1)}, u32[]{:S(2)}, u32[]{:S(2)}) %collective-permute-start.18) | collective-permute-done | bytes 51232 | tf_op jit(solution)/shard_map/ppermute | solution.py:44
  48.4 1.5 %collective-permute-start.19 = (f32[64,200]{1,0:T(8,128)S(1)}, f32[64,200]{1,0:T(8,128)S(1)}, u32[]{:S(2)}, u32[]{:S(2)}) collective-permute-start(f32[64,200]{1,0:T(8,128)S(1)} %factor.1.refs_0_), channel_id=1, source_target_pairs={{0,24},{8,16},{16,8},{24,0},{1,25},{9,17},{17,9},{25,1},{2,26},{10... | collective-permute-start | bytes 153608 | tf_op jit(solution)/shard_map/ppermute | solution.py:44
  49.9 3.7 %collective-permute-done.19.refs_3_ = f32[64,200]{1,0:T(8,128)S(1)} collective-permute-done((f32[64,200]{1,0:T(8,128)S(1)}, f32[64,200]{1,0:T(8,128)S(1)}, u32[]{:S(2)}, u32[]{:S(2)}) %collective-permute-start.19) | collective-permute-done | bytes 51232 | tf_op jit(solution)/shard_map/ppermute | solution.py:44
  53.6 1.5 %collective-permute-start.8 = (f32[16,2048]{1,0:T(8,128)S(1)}, f32[16,2048]{1,0:T(8,128)S(1)}, u32[]{:S(2)}, u32[]{:S(2)}) collective-permute-start(f32[16,2048]{1,0:T(8,128)S(1)} %dense.1.refs_0_), channel_id=1, source_target_pairs={{0,16},{8,24},{16,0},{24,8},{1,17},{9,25},{17,1},{25,9},{2,18},{10... | collective-permute-start | bytes 393224 | tf_op jit(solution)/shard_map/ppermute | solution.py:44
  55.1 1.2 %collective-permute-start.9 = (f32[16,2048]{1,0:T(8,128)S(1)}, f32[16,2048]{1,0:T(8,128)S(1)}, u32[]{:S(2)}, u32[]{:S(2)}) collective-permute-start(f32[16,2048]{1,0:T(8,128)S(1)} %dense.1.refs_0_), channel_id=1, source_target_pairs={{0,24},{8,16},{16,8},{24,0},{1,25},{9,17},{17,9},{25,1},{2,26},{10... | collective-permute-start | bytes 393224 | tf_op jit(solution)/shard_map/ppermute | solution.py:44
  56.3 1.8 %embedding.1 = (f32[200,1024]{1,0:T(8,128)}, f32[64,200]{1,0:T(8,128)}) custom-call(f32[200,1024]{1,0:T(8,128)S(1)} %copy-done.1, f32[64,200]{1,0:T(8,128)S(1)} %bitcast.16, f32[64,1024]{1,0:T(8,128)S(1)} %bitcast.15, f32[64,200]{1,0:T(8,128)S(1)} %factor.1.refs_0_, f32[64,200]{1,0:T(8,128)S(1)} %collective-permute-done.17.refs_1_, ...), custom_call_target="tpu_custom_call" | custom-call | tf_op jit(solution)/shard_map/embedding/pallas_call | solution.py:32
  58.6 2.4 %collective-permute-done.9.refs_3_ = f32[16,2048]{1,0:T(8,128)S(1)} collective-permute-done((f32[16,2048]{1,0:T(8,128)S(1)}, f32[16,2048]{1,0:T(8,128)S(1)}, u32[]{:S(2)}, u32[]{:S(2)}) %collective-permute-start.9) | collective-permute-done | bytes 131104 | tf_op jit(solution)/shard_map/ppermute | solution.py:44
  61.0 1.4 %dense_out.1 = f32[16,8192]{1,0:T(8,128)} custom-call(s32[3]{0:T(128)S(1)} %pad_add_fusion.me, f32[16,2048]{1,0:T(8,128)S(1)} %dense.1.refs_0_, f32[16,2048]{1,0:T(8,128)S(1)} %collective-permute-done.7.refs_1_, f32[16,2048]{1,0:T(8,128)S(1)} %collective-permute-done.8.refs_2_, f32[16,2048]{1,0:T(8,128)S(1)} %collective-permute-done.9.refs_3_), custom_call_target="tpu_custom_call" | custom-call | tf_op jit(solution)/shard_map/dense_out/pallas_call | solution.py:32
  62.3 1.8 %momentum_out.1 = f32[4,65536]{1,0:T(4,128)} custom-call(s32[3]{0:T(128)S(1)} %pad_add_fusion.me, s32[8]{0:T(128)S(1)} %get-tuple-element.42.owned, f32[4,65536]{1,0:T(4,128)S(1)} %copy-done, f32[4,2,4,2048]{3,2,1,0:T(4,128)S(1)} %join.1.refs_0_, f32[4,2,4,2048]{3,2,1,0:T(4,128)S(1)} %collective-permute-done.14.refs_1_, ...), custom_call_target="tpu_custom_call" | custom-call | tf_op jit(solution)/shard_map/momentum_out/pallas_call | solution.py:32
  (44 shorter events, 3.4 us)
Async XLA Ops:
  0.6 8.1 %copy-start = (f32[4,65536]{1,0:T(4,128)S(1)}, f32[4,65536]{1,0:T(4,128)}, u32[]{:S(2)}) copy-start(f32[4,65536]{1,0:T(4,128)} %momentum.3) | copy-start | bytes 3145732
  0.7 1.1 %copy-start.2 = (f32[16,8192]{1,0:T(8,128)S(1)}, f32[16,8192]{1,0:T(8,128)}, u32[]{:S(2)}) copy-start(f32[16,8192]{1,0:T(8,128)} %anchor.5) | copy-start | bytes 1572868
  1.8 1.0 %copy-start.6 = (f32[1,16,8192]{2,1,0:T(8,128)S(1)}, f32[1,16,8192]{2,1,0:T(8,128)}, u32[]{:S(2)}) copy-start(f32[1,16,8192]{2,1,0:T(8,128)} %inner.2) | copy-start | bytes 1572868
  2.9 7.0 %copy-start.8 = (s32[16,1]{0,1:T(1,128)S(1)}, s32[16,1]{0,1:T(1,128)}, u32[]{:S(2)}) copy-start(s32[16,1]{0,1:T(1,128)} %param.8) | copy-start | bytes 196
  2.9 17.8 %copy-start.5 = (f32[1,200,1024]{2,1,0:T(8,128)S(1)}, f32[1,200,1024]{2,1,0:T(8,128)}, u32[]{:S(2)}) copy-start(f32[1,200,1024]{2,1,0:T(8,128)} %inner.3) | copy-start | bytes 2457604
  4.2 7.2 %collective-permute-start = (f32[16,2048]{1,0:T(8,128)}, f32[16,2048]{1,0:T(8,128)S(1)}, u32[]{:S(2)}, u32[]{:S(2)}) collective-permute-start(f32[16,2048]{1,0:T(8,128)} %get-tuple-element.24), channel_id=1, source_target_pairs={{0,8},{8,0},{16,24},{24,16},{1,9},{9,1},{17,25},{25,17},{2,10},{10... | collective-permute-start | bytes 393224 | tf_op jit(solution)/shard_map/ppermute | solution.py:44
  7.2 8.0 %collective-permute-start.1 = (f32[16,2048]{1,0:T(8,128)}, f32[16,2048]{1,0:T(8,128)S(1)}, u32[]{:S(2)}, u32[]{:S(2)}) collective-permute-start(f32[16,2048]{1,0:T(8,128)} %get-tuple-element.25), channel_id=1, source_target_pairs={{0,16},{8,24},{16,0},{24,8},{1,17},{9,25},{17,1},{25,9},{2,18},{10... | collective-permute-start | bytes 393224 | tf_op jit(solution)/shard_map/ppermute | solution.py:44
  8.7 12.0 %copy-start.1 = (f32[200,1024]{1,0:T(8,128)S(1)}, f32[200,1024]{1,0:T(8,128)}, u32[]{:S(2)}) copy-start(f32[200,1024]{1,0:T(8,128)} %anchor.7) | copy-start | bytes 2457604
  8.7 6.5 %collective-permute-start.2 = (f32[16,2048]{1,0:T(8,128)}, f32[16,2048]{1,0:T(8,128)S(1)}, u32[]{:S(2)}, u32[]{:S(2)}) collective-permute-start(f32[16,2048]{1,0:T(8,128)} %get-tuple-element.26), channel_id=1, source_target_pairs={{0,24},{8,16},{16,8},{24,0},{1,25},{9,17},{17,9},{25,1},{2,26},{10... | collective-permute-start | bytes 393224 | tf_op jit(solution)/shard_map/ppermute | solution.py:44
  9.9 6.0 %collective-permute-start.3 = (f32[4,4,2048]{2,1,0:T(4,128)}, f32[4,4,2048]{2,1,0:T(4,128)S(1)}, u32[]{:S(2)}, u32[]{:S(2)}) collective-permute-start(f32[4,4,2048]{2,1,0:T(4,128)} %get-tuple-element.29), channel_id=1, source_target_pairs={{0,1},{1,0},{2,3},{3,2},{4,5},{5,4},{6,7},{7,6},{8,9},{9,8},{10,11... | collective-permute-start | bytes 393224 | tf_op jit(solution)/shard_map/ppermute | solution.py:44
  15.8 4.9 %copy-start.4 = (f32[1024,64]{0,1:T(8,128)S(1)}, f32[1024,64]{0,1:T(8,128)}, u32[]{:S(2)}) copy-start(f32[1024,64]{0,1:T(8,128)} %param.15) | copy-start | bytes 786436
  15.8 7.3 %collective-permute-start.10 = (f32[4,4,2048]{2,1,0:T(4,128)S(1)}, f32[4,4,2048]{2,1,0:T(4,128)S(1)}, u32[]{:S(2)}, u32[]{:S(2)}) collective-permute-start(f32[4,4,2048]{2,1,0:T(4,128)S(1)} %get-tuple-element.35), channel_id=1, source_target_pairs={{0,1},{1,0},{2,3},{3,2},{4,5},{5,4},{6,7},{7,6},{8,9},{9,8},{10,11... | collective-permute-start | bytes 393224 | tf_op jit(solution)/shard_map/ppermute | solution.py:44
  16.5 8.0 %collective-permute-start.4 = (f32[2,4,2048]{2,1,0:T(4,128)S(1)}, f32[2,4,2048]{2,1,0:T(4,128)S(1)}, u32[]{:S(2)}, u32[]{:S(2)}) collective-permute-start(f32[2,4,2048]{2,1,0:T(4,128)S(1)} %get-tuple-element.31), channel_id=1, source_target_pairs={{0,2},{1,3},{2,0},{3,1},{4,6},{5,7},{6,4},{7,5},{8,10},{9,11},{10,... | collective-permute-start | bytes 196616 | tf_op jit(solution)/shard_map/ppermute | solution.py:44
  18.1 9.8 %collective-permute-start.5 = (f32[2,4,2048]{2,1,0:T(4,128)S(1)}, f32[2,4,2048]{2,1,0:T(4,128)S(1)}, u32[]{:S(2)}, u32[]{:S(2)}) collective-permute-start(f32[2,4,2048]{2,1,0:T(4,128)S(1)} %get-tuple-element.32), channel_id=1, source_target_pairs={{0,4},{1,5},{2,6},{3,7},{4,0},{5,1},{6,2},{7,3},{8,12},{9,13},{10,... | collective-permute-start | bytes 196616 | tf_op jit(solution)/shard_map/ppermute | solution.py:44
  20.7 9.1 %copy-start.3 = (f32[16,8192]{1,0:T(8,128)S(1)}, f32[16,8192]{1,0:T(8,128)}, u32[]{:S(2)}) copy-start(f32[16,8192]{1,0:T(8,128)} %anchor.5) | copy-start | bytes 1572868
  21.6 16.1 %collective-permute-start.17 = (f32[64,200]{1,0:T(8,128)S(1)}, f32[64,200]{1,0:T(8,128)S(1)}, u32[]{:S(2)}, u32[]{:S(2)}) collective-permute-start(f32[64,200]{1,0:T(8,128)S(1)} %factor.1.refs_0_), channel_id=1, source_target_pairs={{0,8},{8,0},{16,24},{24,16},{1,9},{9,1},{17,25},{25,17},{2,10},{10... | collective-permute-start | bytes 153608 | tf_op jit(solution)/shard_map/ppermute | solution.py:44
  22.9 6.9 %collective-permute-start.6 = (f32[2,4,2048]{2,1,0:T(4,128)S(1)}, f32[2,4,2048]{2,1,0:T(4,128)S(1)}, u32[]{:S(2)}, u32[]{:S(2)}) collective-permute-start(f32[2,4,2048]{2,1,0:T(4,128)S(1)} %get-tuple-element.33), channel_id=1, source_target_pairs={{0,6},{1,7},{2,4},{3,5},{4,2},{5,3},{6,0},{7,1},{8,14},{9,15},{10,... | collective-permute-start | bytes 196616 | tf_op jit(solution)/shard_map/ppermute | solution.py:44
  23.7 7.8 %collective-permute-start.11 = (f32[2,4,2048]{2,1,0:T(4,128)S(1)}, f32[2,4,2048]{2,1,0:T(4,128)S(1)}, u32[]{:S(2)}, u32[]{:S(2)}) collective-permute-start(f32[2,4,2048]{2,1,0:T(4,128)S(1)} %get-tuple-element.37), channel_id=1, source_target_pairs={{0,2},{1,3},{2,0},{3,1},{4,6},{5,7},{6,4},{7,5},{8,10},{9,11},{10,... | collective-permute-start | bytes 196616 | tf_op jit(solution)/shard_map/ppermute | solution.py:44
  24.5 8.3 %collective-permute-start.12 = (f32[2,4,2048]{2,1,0:T(4,128)S(1)}, f32[2,4,2048]{2,1,0:T(4,128)S(1)}, u32[]{:S(2)}, u32[]{:S(2)}) collective-permute-start(f32[2,4,2048]{2,1,0:T(4,128)S(1)} %get-tuple-element.38), channel_id=1, source_target_pairs={{0,4},{1,5},{2,6},{3,7},{4,0},{5,1},{6,2},{7,3},{8,12},{9,13},{10,... | collective-permute-start | bytes 196616 | tf_op jit(solution)/shard_map/ppermute | solution.py:44
  28.0 6.2 %collective-permute-start.13 = (f32[2,4,2048]{2,1,0:T(4,128)S(1)}, f32[2,4,2048]{2,1,0:T(4,128)S(1)}, u32[]{:S(2)}, u32[]{:S(2)}) collective-permute-start(f32[2,4,2048]{2,1,0:T(4,128)S(1)} %get-tuple-element.39), channel_id=1, source_target_pairs={{0,6},{1,7},{2,4},{3,5},{4,2},{5,3},{6,0},{7,1},{8,14},{9,15},{10,... | collective-permute-start | bytes 196616 | tf_op jit(solution)/shard_map/ppermute | solution.py:44
  30.6 24.5 %collective-permute-start.7 = (f32[16,2048]{1,0:T(8,128)S(1)}, f32[16,2048]{1,0:T(8,128)S(1)}, u32[]{:S(2)}, u32[]{:S(2)}) collective-permute-start(f32[16,2048]{1,0:T(8,128)S(1)} %dense.1.refs_0_), channel_id=1, source_target_pairs={{0,8},{8,0},{16,24},{24,16},{1,9},{9,1},{17,25},{25,17},{2,10},{10... | collective-permute-start | bytes 393224 | tf_op jit(solution)/shard_map/ppermute | solution.py:44
  34.1 22.1 %copy-start.7 = (f32[200,64]{0,1:T(8,128)S(1)}, f32[200,64]{0,1:T(8,128)}, u32[]{:S(2)}) copy-start(f32[200,64]{0,1:T(8,128)} %param.14) | copy-start | bytes 153604
  34.2 28.2 %collective-permute-start.14 = (f32[4,2,4,2048]{3,2,1,0:T(4,128)S(1)}, f32[4,2,4,2048]{3,2,1,0:T(4,128)S(1)}, u32[]{:S(2)}, u32[]{:S(2)}) collective-permute-start(f32[4,2,4,2048]{3,2,1,0:T(4,128)S(1)} %join.1.refs_0_), channel_id=1, source_target_pairs={{0,8},{8,0},{16,24},{24,16},{1,9},{9,1},{17,25},{25,17},{2,10},{10... | collective-permute-start | bytes 786440 | tf_op jit(solution)/shard_map/ppermute | solution.py:44
  35.0 27.3 %collective-permute-start.15 = (f32[4,2,4,2048]{3,2,1,0:T(4,128)S(1)}, f32[4,2,4,2048]{3,2,1,0:T(4,128)S(1)}, u32[]{:S(2)}, u32[]{:S(2)}) collective-permute-start(f32[4,2,4,2048]{3,2,1,0:T(4,128)S(1)} %join.1.refs_0_), channel_id=1, source_target_pairs={{0,16},{8,24},{16,0},{24,8},{1,17},{9,25},{17,1},{25,9},{2,18},{10... | collective-permute-start | bytes 786440 | tf_op jit(solution)/shard_map/ppermute | solution.py:44
  36.5 25.8 %collective-permute-start.16 = (f32[4,2,4,2048]{3,2,1,0:T(4,128)S(1)}, f32[4,2,4,2048]{3,2,1,0:T(4,128)S(1)}, u32[]{:S(2)}, u32[]{:S(2)}) collective-permute-start(f32[4,2,4,2048]{3,2,1,0:T(4,128)S(1)} %join.1.refs_0_), channel_id=1, source_target_pairs={{0,24},{8,16},{16,8},{24,0},{1,25},{9,17},{17,9},{25,1},{2,26},{10... | collective-permute-start | bytes 786440 | tf_op jit(solution)/shard_map/ppermute | solution.py:44
  37.7 10.7 %collective-permute-start.18 = (f32[64,200]{1,0:T(8,128)S(1)}, f32[64,200]{1,0:T(8,128)S(1)}, u32[]{:S(2)}, u32[]{:S(2)}) collective-permute-start(f32[64,200]{1,0:T(8,128)S(1)} %factor.1.refs_0_), channel_id=1, source_target_pairs={{0,16},{8,24},{16,0},{24,8},{1,17},{9,25},{17,1},{25,9},{2,18},{10... | collective-permute-start | bytes 153608 | tf_op jit(solution)/shard_map/ppermute | solution.py:44
  48.4 5.2 %collective-permute-start.19 = (f32[64,200]{1,0:T(8,128)S(1)}, f32[64,200]{1,0:T(8,128)S(1)}, u32[]{:S(2)}, u32[]{:S(2)}) collective-permute-start(f32[64,200]{1,0:T(8,128)S(1)} %factor.1.refs_0_), channel_id=1, source_target_pairs={{0,24},{8,16},{16,8},{24,0},{1,25},{9,17},{17,9},{25,1},{2,26},{10... | collective-permute-start | bytes 153608 | tf_op jit(solution)/shard_map/ppermute | solution.py:44
  53.6 5.0 %collective-permute-start.8 = (f32[16,2048]{1,0:T(8,128)S(1)}, f32[16,2048]{1,0:T(8,128)S(1)}, u32[]{:S(2)}, u32[]{:S(2)}) collective-permute-start(f32[16,2048]{1,0:T(8,128)S(1)} %dense.1.refs_0_), channel_id=1, source_target_pairs={{0,16},{8,24},{16,0},{24,8},{1,17},{9,25},{17,1},{25,9},{2,18},{10... | collective-permute-start | bytes 393224 | tf_op jit(solution)/shard_map/ppermute | solution.py:44
  55.1 5.9 %collective-permute-start.9 = (f32[16,2048]{1,0:T(8,128)S(1)}, f32[16,2048]{1,0:T(8,128)S(1)}, u32[]{:S(2)}, u32[]{:S(2)}) collective-permute-start(f32[16,2048]{1,0:T(8,128)S(1)} %dense.1.refs_0_), channel_id=1, source_target_pairs={{0,24},{8,16},{16,8},{24,0},{1,25},{9,17},{17,9},{25,1},{2,26},{10... | collective-permute-start | bytes 393224 | tf_op jit(solution)/shard_map/ppermute | solution.py:44

commit v2 on v1

v2 whole, which is shorter than its diff:
```python
import functools

import jax
import jax.numpy as jnp
from jax import lax
from jax.experimental import pallas as pl
from jax.experimental.pallas import tpu as pltpu
from jax.sharding import PartitionSpec as P

outer_rate = 0.7
momentum_decay = 0.9
most_direct_chips = 8
f32 = jnp.float32
vmem_limit = 48 * 1024 * 1024


def on_chip(x):
    return pltpu.with_memory_space_constraint(x, pltpu.VMEM)


def kept(shape):
    return pltpu.VMEM(shape, f32)


def stored(shape):
    return jax.ShapeDtypeStruct(shape, f32)


def in_scalars(x):
    return pltpu.with_memory_space_constraint(x, pltpu.SMEM)


def in_hbm(x):
    return pltpu.with_memory_space_constraint(x, pltpu.HBM)


vmem = pl.BlockSpec(memory_space=pltpu.VMEM)
smem = pl.BlockSpec(memory_space=pltpu.SMEM)
anywhere = pl.BlockSpec(memory_space=pl.ANY)


def run(body, outs, operands, scalars=(), scratch=(), far=(), out_specs=None, name=None):
    return pl.pallas_call(
        body,
        out_shape=list(outs),
        in_specs=[smem] * len(scalars) + [anywhere] * len(far) + [vmem] * len(operands),
        out_specs=out_specs or [vmem] * len(outs),
        scratch_shapes=list(scratch),
        compiler_params=pltpu.CompilerParams(vmem_limit_bytes=vmem_limit),
        name=name,
    )(*[in_scalars(x) for x in scalars], *[in_hbm(x) for x in far], *operands)


def swap(x, axis, count, mask):
    return lax.ppermute(x, axis, [(i, i ^ mask) for i in range(count)])


def place():
    position = lax.axis_index("own")
    return lax.axis_index("rep"), lax.shift_right_logical(position, 1), position & 1


def column(index, part):
    return pl.ds(pl.multiple_of(index * part, 128), part)


def places_body(slots, owners, row_of, block_of, owned):
    blocks, owner_count = row_of.shape[0], owned.shape[0]

    def clear(i, carry):
        block_of[i] = 0
        return carry

    def clear_count(i, carry):
        owned[i] = 0
        return carry

    def name(u, carry):
        owner = owners[u]
        slot = owned[owner]
        row = owner * slots + slot
        row_of[u] = row
        block_of[row] = u
        owned[owner] = slot + 1
        return carry

    lax.fori_loop(0, block_of.shape[0], clear, 0)
    lax.fori_loop(0, owner_count, clear_count, 0)
    lax.fori_loop(0, blocks, name, 0)


def start_body(groups, part, anchor, inner, momentum, *refs):
    outs, (quarter, same, other, held), (far, near, sem) = (
        refs[:groups],
        refs[groups : groups + 4],
        refs[groups + 4 :],
    )
    rep, chip, core = place()
    copies = []
    for k in (*range(1, groups), 0):
        at = column(rep ^ k, part)
        pair = (
            pltpu.make_async_copy(anchor.at[:, at], far.at[k], sem.at[k]),
            pltpu.make_async_copy(inner.at[0, :, at], near.at[k], sem.at[groups + k]),
        )
        for copy in pair:
            copy.start()
        copies.append((k, pair))
    whole = pltpu.make_async_copy(momentum, held, sem.at[2 * groups])
    whole.start()
    for k, pair in copies:
        for copy in pair:
            copy.wait()
        outs[k][...] = far[k] - near[k]
        if k == 0:
            quarter[...] = far[0]
    whole.wait()

    def take(to, carry):
        for o, out in enumerate((same, other)):
            piece = 2 * to + (core ^ o)
            out[to] = held[:, column(piece * groups + rep, part)]
        return carry

    lax.fori_loop(0, same.shape[0], take, 0, unroll=same.shape[0] <= 8)


def mean_body(groups, block_of, *refs):
    parts, (mean, same, other) = refs[:groups], refs[groups:]
    _, _, core = place()
    total = parts[0][...]
    for ref in parts[1:]:
        total = total + ref[...]
    mean[...] = total / groups
    chips, slots, _ = same.shape

    def fill(chip, carry):
        for o, out in enumerate((same, other)):
            for s in range(slots):
                block = block_of[(2 * chip + (core ^ o)) * slots + s]
                out[chip, pl.ds(s, 1), :] = mean[pl.ds(block, 1), :]
        return carry

    lax.fori_loop(0, chips, fill, 0, unroll=chips <= 8)


def pack_body(direct, same, other, *outs):
    _, chip, _ = place()
    if direct:
        for k, out in enumerate(outs):
            out[0] = same[chip ^ k]
            out[1] = other[chip ^ k]
    else:
        outs[0][:, 0] = same[...]
        outs[0][:, 1] = other[...]


def join_body(*refs):
    out = refs[-1]
    for k, ref in enumerate(refs[:-1]):
        out[k] = ref[...]


def tiles(rows, columns):
    return [
        (i, min(8, rows - i), j, min(128, columns - j))
        for i in range(0, rows, 8)
        for j in range(0, columns, 128)
    ]


def dense_body(direct, row_of, quarter, mean, factor, *refs):
    *received, out, rows, work = refs
    _, here, core = place()
    slots = received[0].shape[-2]
    blocks, part = mean.shape
    if direct:
        for k, ref in enumerate(received):
            rows[k] = ref[...]
        table = rows
    else:
        table = received[0]

    def update(block, carry):
        row = row_of[block]
        owner = row // slots
        chip = (owner // 2) ^ here if direct else owner // 2
        momentum = table[chip, (owner % 2) ^ core, pl.ds(row % slots, 1), :]
        mean_row = mean[pl.ds(block, 1), :]
        new_momentum = momentum_decay * momentum + mean_row
        work[pl.ds(block, 1), :] = quarter[pl.ds(block, 1), :] - outer_rate * (
            mean_row + momentum_decay * new_momentum
        )
        return carry

    lax.fori_loop(0, blocks, update, 0, unroll=blocks <= 16)
    at = 0
    for ref in (work, factor):
        for i, height, j, width in tiles(*ref.shape):
            out[at : at + height, :width] = ref[i : i + height, j : j + width]
            at += 8


def dense_out_body(part, *refs):
    out = refs[-1]
    rep, _, _ = place()
    blocks = out.shape[0]
    for k, ref in enumerate(refs[:-1]):
        for t, (i, height, j, width) in enumerate(tiles(blocks, part)):
            at = pl.multiple_of((rep ^ k) * part, 128) + j
            out[i : i + height, pl.ds(pl.multiple_of(at, 128), width)] = ref[
                8 * t : 8 * t + height, :width
            ]


def momentum_out_body(part, direct, owned, momentum, *refs):
    out = refs[-1]
    rep, here, core = place()
    groups = len(refs) - 1
    chips = refs[0].shape[0]
    slots = momentum.shape[0]
    live = lax.broadcasted_iota(jnp.int32, (slots, part), 0) < owned[here * 2 + core]

    def fill(k, carry):
        chip = here ^ k if direct else k
        for o in range(2):
            piece = 2 * chip + (core ^ o)
            for g in range(groups):
                at = column(piece * groups + (rep ^ g), part)
                out[:, at] = jnp.where(
                    live, momentum_decay * momentum[:, at] + refs[g][k, o], 0.0
                )
        return carry

    lax.fori_loop(0, chips, fill, 0, unroll=chips <= 8)


def dot(a, b, contract):
    return lax.dot_general(
        a,
        b,
        ((contract), ((), ())),
        precision=lax.Precision.HIGHEST,
        preferred_element_type=f32,
    )


def factor_body(anchor, inner, basis_t, out):
    out[...] = dot(basis_t[...], anchor[...] - inner[0], ((1,), (1,)))


def embedding_body(groups, skip, anchor, momentum_t, basis_t, *refs):
    parts, (new_emb, new_momentum_t, mean) = refs[:groups], refs[groups:]
    for t, (i, height, j, width) in enumerate(tiles(*mean.shape)):
        at = slice(skip + 8 * t, skip + 8 * t + height)
        total = parts[0][at, :width]
        for ref in parts[1:]:
            total = total + ref[at, :width]
        mean[i : i + height, j : j + width] = total / groups
    moved = momentum_decay * momentum_t[...] + mean[...]
    new_momentum_t[...] = moved
    update = mean[...] + momentum_decay * moved
    new_emb[...] = anchor[...] - outer_rate * dot(update, basis_t[...], ((0,), (0,)))


def over_chips(same, other, chips, owner_count, name):
    other = swap(other, "own", owner_count, 1)
    shape = (2,) + same.shape[1:]
    if chips <= most_direct_chips:
        outs = run(
            functools.partial(pack_body, True),
            [kept(shape)] * chips,
            [on_chip(same), on_chip(other)],
            name=name,
        )
        return [outs[0]] + [swap(outs[k], "own", owner_count, 2 * k) for k in range(1, chips)]
    (packed,) = run(
        functools.partial(pack_body, False),
        [stored((chips,) + shape)],
        [same, other],
        name=name,
    )
    groups = [list(range(core, owner_count, 2)) for core in range(2)]
    return [
        lax.all_to_all(
            packed, "own", split_axis=0, concat_axis=0, axis_index_groups=groups, tiled=True
        )
    ]


def per_device(
    owners, inner_dense, anchor_dense, momentum_dense, inner_emb, anchor_emb, momentum_emb, basis
):
    owner_count = lax.axis_size("own")
    groups = lax.axis_size("rep")
    chips = owner_count // 2
    direct = chips <= most_direct_chips
    slot_count = momentum_dense.shape[0]
    blocks, piece_len = anchor_dense.shape
    part = piece_len // groups
    rows, rank = momentum_emb.shape
    chunk = (chips, slot_count, part)
    table = (chips, 2, slot_count, part)

    *parts, quarter, same, other, momentum = run(
        functools.partial(start_body, groups, part),
        [kept((blocks, part))] * (groups + 1) + [kept(chunk)] * 2 + [kept(momentum_dense.shape)],
        [],
        far=[anchor_dense, inner_dense, momentum_dense],
        scratch=[
            pltpu.VMEM((groups, blocks, part), f32),
            pltpu.VMEM((groups, blocks, part), f32),
            pltpu.SemaphoreType.DMA((2 * groups + 1,)),
        ],
        name="start",
    )
    parts = [parts[0]] + [swap(parts[k], "rep", groups, k) for k in range(1, groups)]
    momentum_rows = over_chips(same, other, chips, owner_count, "pack_momentum")

    row_of, block_of, owned = run(
        functools.partial(places_body, slot_count),
        [
            pltpu.SMEM((blocks,), jnp.int32),
            pltpu.SMEM((owner_count * slot_count,), jnp.int32),
            pltpu.SMEM((owner_count,), jnp.int32),
        ],
        [],
        scalars=[owners[:, 0]],
        out_specs=[smem] * 3,
        name="places",
    )
    basis_t = basis.T
    (factor,) = run(
        factor_body, [kept((rank, rows))], [anchor_emb, inner_emb, basis_t], name="factor"
    )

    mean, same, other = run(
        functools.partial(mean_body, groups),
        [kept((blocks, part)), kept(chunk), kept(chunk)],
        [on_chip(x) for x in parts],
        [block_of],
        name="mean",
    )
    gradient_rows = over_chips(same, other, chips, owner_count, "pack_mean")

    skip = 8 * len(tiles(blocks, part))
    (dense,) = run(
        functools.partial(dense_body, direct),
        [kept((skip + 8 * len(tiles(rank, rows)), 128))],
        [on_chip(x) for x in (quarter, mean, factor, *momentum_rows)],
        [row_of],
        [
            pltpu.VMEM(table if direct else (8, 128), f32),
            pltpu.VMEM((blocks, part), f32),
        ],
        name="dense",
    )
    dense = [dense] + [swap(dense, "rep", groups, k) for k in range(1, groups)]

    if direct:
        (gradient,) = run(
            join_body, [kept(table)], [on_chip(x) for x in gradient_rows], name="join"
        )
    else:
        (gradient,) = gradient_rows
    gradient = [gradient] + [swap(gradient, "rep", groups, k) for k in range(1, groups)]

    (new_dense,) = run(
        functools.partial(dense_out_body, part),
        [stored((blocks, piece_len))],
        [on_chip(x) for x in dense],
        name="dense_out",
    )
    new_emb, new_momentum_t = run(
        functools.partial(embedding_body, groups, skip),
        [stored(anchor_emb.shape), stored((rank, rows))],
        [anchor_emb, momentum_emb.T, basis_t] + [on_chip(x) for x in dense],
        scratch=[pltpu.VMEM((rank, rows), f32)],
        name="embedding",
    )
    (new_momentum_dense,) = run(
        functools.partial(momentum_out_body, part, direct),
        [stored(momentum_dense.shape)],
        [on_chip(momentum)] + [on_chip(x) for x in gradient],
        [owned],
        name="momentum_out",
    )
    return (new_dense, new_momentum_dense, new_emb, new_momentum_t.T)


def solution(mesh):
    placed = (
        P(),
        P("rep", None, "own"),
        P(None, "own"),
        P("own", None),
        P("rep", "own", None),
        P("own", None),
        P("own", None),
        P(),
    )
    return jax.shard_map(
        per_device,
        mesh=mesh,
        in_specs=placed,
        out_specs=(P(None, "own"), P("own", None), P("own", None), P("own", None)),
        check_vma=False,
    )
```

time: 64.3 us -> 49.2 us (0.77)
  waiting for transfers between devices: 25.7 us -> 17.3 us
  Pallas kernels: 10.9 us -> 8.05 us
  starting transfers between devices: 24.1 us -> 21.5 us
  local copies, waits for them, and re-layouts: 2.18 us -> 1.39 us
    ppermute x20 -> x17, waiting for transfers between devices: 25.7 us -> 17.3 us  [swap(): return lax.ppermute(x, axis, [(i, i ^ mask) for i in range(count)])]
    pallas_call x11, Pallas kernels: 10.9 us -> 8.05 us  [run(): pl.pallas_call(body, out_shape=list(outs), in_specs=[smem] * len(scalars)...]
    ppermute x20 -> x17, starting transfers between devices: 24.1 us -> 21.5 us  [swap(): return lax.ppermute(x, axis, [(i, i ^ mask) for i in range(count)])]
    unnamed x18 -> x10, local copies, waits for them, and re-layouts: 2.18 us -> 1.39 us
  transfers between devices with their start and end apart: 20 -> 17, of which waited for: 9 -> 7; matrix products, arithmetic and copies ran while one was open for 1% -> 0% of each run, Pallas kernels for 12% -> 10%
where the time goes in v2:
time: 49.2 us; the launch traced here: 49 us
  starting transfers between devices  21.5 us (44%)
  waiting for transfers between devices  17.3 us (35%)
  Pallas kernels  8.05 us (16%)
  local copies, waits for them, and re-layouts  1.39 us (3%)
  between operations  0.77 us (2%)
    ppermute x17, starting transfers between devices, swap(): return lax.ppermute(x, axis, [(i, i ^ mask) for i in range(count)])  21.5 us
    ppermute x17, waiting for transfers between devices, swap(): return lax.ppermute(x, axis, [(i, i ^ mask) for i in range(count)])  17.3 us
    pallas_call x11, Pallas kernels, run(): pl.pallas_call(body, out_shape=list(outs), in_specs=[smem] * len(scalars)...  8.05 us
    unnamed x10, local copies, waits for them, and re-layouts  1.39 us
  transfers between devices with their start and end apart: 17, of which 7 were waited for; matrix products, arithmetic and copies ran while one was open for 0% of the time, Pallas kernels for 10%

profile of v2, /device:TPU:0, one launch (start us, length us, event | category | flops | bytes accessed | tf_op | source)
XLA Modules:
  0.0 49.0 jit_solution(17757262566358934220)
XLA Ops:
  0.7 1.9 %start.1 = (f32[16,2048]{1,0:T(8,128)S(1)}, f32[16,2048]{1,0:T(8,128)S(1)}, f32[16,2048]{1,0:T(8,128)S(1)}, f32[16,2048]{1,0:T(8,128)S(1)}, f32[16,2048]{1,0:T(8...) custom-call(f32[16,8192]{1,0:T(8,128)} %anchor.3, f32[1,16,8192]{2,1,0:T(8,128)} %inner.2, ...), custom_call_target="tpu_custom_call" | custom-call | tf_op jit(solution)/shard_map/start/pallas_call | solution.py:43
  2.5 0.5 %collective-permute-start.3 = (f32[4,4,2048]{2,1,0:T(4,128)S(1)}, f32[4,4,2048]{2,1,0:T(4,128)S(1)}, u32[]{:S(2)}, u32[]{:S(2)}) collective-permute-start(f32[4,4,2048]{2,1,0:T(4,128)S(1)} %get-tuple-element.37), channel_id=1, source_target_pairs={{0,1},{1,0},{2,3},{3,2},{4,5},{5,4},{6,7},{7,6},{8,9},{9,8},{10,11... | collective-permute-start | bytes 393224 | tf_op jit(solution)/shard_map/ppermute | solution.py:55
  3.0 2.6 %collective-permute-start = (f32[16,2048]{1,0:T(8,128)S(1)}, f32[16,2048]{1,0:T(8,128)S(1)}, u32[]{:S(2)}, u32[]{:S(2)}) collective-permute-start(f32[16,2048]{1,0:T(8,128)S(1)} %get-tuple-element.32), channel_id=1, source_target_pairs={{0,8},{8,0},{16,24},{24,16},{1,9},{9,1},{17,25},{25,17},{2,10},{10... | collective-permute-start | bytes 393224 | tf_op jit(solution)/shard_map/ppermute | solution.py:55
  5.6 1.5 %collective-permute-start.1 = (f32[16,2048]{1,0:T(8,128)S(1)}, f32[16,2048]{1,0:T(8,128)S(1)}, u32[]{:S(2)}, u32[]{:S(2)}) collective-permute-start(f32[16,2048]{1,0:T(8,128)S(1)} %get-tuple-element.33), channel_id=1, source_target_pairs={{0,16},{8,24},{16,0},{24,8},{1,17},{9,25},{17,1},{25,9},{2,18},{10... | collective-permute-start | bytes 393224 | tf_op jit(solution)/shard_map/ppermute | solution.py:55
  7.1 0.6 %copy-done.4 = s32[16,1]{0,1:T(1,128)S(1)} copy-done((s32[16,1]{0,1:T(1,128)S(1)}, s32[16,1]{0,1:T(1,128)}, u32[]{:S(2)}) %copy-start.4) | copy-done | bytes 88
  7.8 1.0 %places.1 = (s32[16]{0:T(128)S(4)}, s32[32]{0:T(128)S(4)}, s32[8]{0:T(128)S(4)}) custom-call(s32[16]{0:T(128)S(1)} %bitcast.7), custom_call_target="tpu_custom_call" | custom-call | tf_op jit(solution)/shard_map/places/pallas_call | solution.py:43
  8.8 1.6 %collective-permute-start.4 = (f32[2,4,2048]{2,1,0:T(4,128)S(1)}, f32[2,4,2048]{2,1,0:T(4,128)S(1)}, u32[]{:S(2)}, u32[]{:S(2)}) collective-permute-start(f32[2,4,2048]{2,1,0:T(4,128)S(1)} %get-tuple-element.39), channel_id=1, source_target_pairs={{0,2},{1,3},{2,0},{3,1},{4,6},{5,7},{6,4},{7,5},{8,10},{9,11},{10,... | collective-permute-start | bytes 196616 | tf_op jit(solution)/shard_map/ppermute | solution.py:55
  10.5 2.6 %collective-permute-start.5 = (f32[2,4,2048]{2,1,0:T(4,128)S(1)}, f32[2,4,2048]{2,1,0:T(4,128)S(1)}, u32[]{:S(2)}, u32[]{:S(2)}) collective-permute-start(f32[2,4,2048]{2,1,0:T(4,128)S(1)} %get-tuple-element.40), channel_id=1, source_target_pairs={{0,4},{1,5},{2,6},{3,7},{4,0},{5,1},{6,2},{7,3},{8,12},{9,13},{10,... | collective-permute-start | bytes 196616 | tf_op jit(solution)/shard_map/ppermute | solution.py:55
  13.1 0.8 %collective-permute-start.6 = (f32[2,4,2048]{2,1,0:T(4,128)S(1)}, f32[2,4,2048]{2,1,0:T(4,128)S(1)}, u32[]{:S(2)}, u32[]{:S(2)}) collective-permute-start(f32[2,4,2048]{2,1,0:T(4,128)S(1)} %get-tuple-element.41), channel_id=1, source_target_pairs={{0,6},{1,7},{2,4},{3,5},{4,2},{5,3},{6,0},{7,1},{8,14},{9,15},{10,... | collective-permute-start | bytes 196616 | tf_op jit(solution)/shard_map/ppermute | solution.py:55
  13.9 0.1 collective-permute-done.1.refs_2_
  14.0 0.1 mean.1
  14.1 0.1 collective-permute-start.10
  14.2 0.7 %copy-done.1 = f32[1024,64]{0,1:T(8,128)S(1)} copy-done((f32[1024,64]{0,1:T(8,128)S(1)}, f32[1024,64]{0,1:T(8,128)}, u32[]{:S(2)}) %copy-start.1) | copy-done | bytes 262168
  14.9 0.9 %factor.1 = f32[64,200]{1,0:T(8,128)S(1)} custom-call(f32[200,1024]{1,0:T(8,128)S(1)} %copy-done, f32[1,200,1024]{2,1,0:T(8,128)S(1)} %copy-done.2, f32[64,1024]{1,0:T(8,128)S(1)} %bitcast.4), custom_call_target="tpu_custom_call" | custom-call | tf_op jit(solution)/shard_map/factor/pallas_call | solution.py:43
  15.9 1.9 %collective-permute-done.5.refs_2_ = f32[2,4,2048]{2,1,0:T(4,128)S(1)} collective-permute-done((f32[2,4,2048]{2,1,0:T(4,128)S(1)}, f32[2,4,2048]{2,1,0:T(4,128)S(1)}, u32[]{:S(2)}, u32[]{:S(2)}) %collective-permute-start.5) | collective-permute-done | bytes 65568 | tf_op jit(solution)/shard_map/ppermute | solution.py:55
  17.8 1.4 %collective-permute-done.6.refs_3_ = f32[2,4,2048]{2,1,0:T(4,128)S(1)} collective-permute-done((f32[2,4,2048]{2,1,0:T(4,128)S(1)}, f32[2,4,2048]{2,1,0:T(4,128)S(1)}, u32[]{:S(2)}, u32[]{:S(2)}) %collective-permute-start.6) | collective-permute-done | bytes 65568 | tf_op jit(solution)/shard_map/ppermute | solution.py:55
  19.2 0.2 dense.1.refs_0_
  19.4 2.3 %collective-permute-start.9 = (f32[384,128]{1,0:T(8,128)S(1)}, f32[384,128]{1,0:T(8,128)S(1)}, u32[]{:S(2)}, u32[]{:S(2)}) collective-permute-start(f32[384,128]{1,0:T(8,128)S(1)} %dense.1.refs_0_), channel_id=1, source_target_pairs={{0,24},{8,16},{16,8},{24,0},{1,25},{9,17},{17,9},{25,1},{2,26},{10... | collective-permute-start | bytes 589832 | tf_op jit(solution)/shard_map/ppermute | solution.py:55
  21.8 2.1 %collective-permute-start.12 = (f32[2,4,2048]{2,1,0:T(4,128)S(1)}, f32[2,4,2048]{2,1,0:T(4,128)S(1)}, u32[]{:S(2)}, u32[]{:S(2)}) collective-permute-start(f32[2,4,2048]{2,1,0:T(4,128)S(1)} %get-tuple-element.48), channel_id=1, source_target_pairs={{0,4},{1,5},{2,6},{3,7},{4,0},{5,1},{6,2},{7,3},{8,12},{9,13},{10,... | collective-permute-start | bytes 196616 | tf_op jit(solution)/shard_map/ppermute | solution.py:55
  23.9 2.3 %collective-permute-start.13 = (f32[2,4,2048]{2,1,0:T(4,128)S(1)}, f32[2,4,2048]{2,1,0:T(4,128)S(1)}, u32[]{:S(2)}, u32[]{:S(2)}) collective-permute-start(f32[2,4,2048]{2,1,0:T(4,128)S(1)} %get-tuple-element.49), channel_id=1, source_target_pairs={{0,6},{1,7},{2,4},{3,5},{4,2},{5,3},{6,0},{7,1},{8,14},{9,15},{10,... | collective-permute-start | bytes 196616 | tf_op jit(solution)/shard_map/ppermute | solution.py:55
  26.2 1.3 %collective-permute-done.11.refs_1_ = f32[2,4,2048]{2,1,0:T(4,128)S(1)} collective-permute-done((f32[2,4,2048]{2,1,0:T(4,128)S(1)}, f32[2,4,2048]{2,1,0:T(4,128)S(1)}, u32[]{:S(2)}, u32[]{:S(2)}) %collective-permute-start.11) | collective-permute-done | bytes 65568 | tf_op jit(solution)/shard_map/ppermute | solution.py:55
  27.4 2.5 %collective-permute-done.13.refs_3_ = f32[2,4,2048]{2,1,0:T(4,128)S(1)} collective-permute-done((f32[2,4,2048]{2,1,0:T(4,128)S(1)}, f32[2,4,2048]{2,1,0:T(4,128)S(1)}, u32[]{:S(2)}, u32[]{:S(2)}) %collective-permute-start.13) | collective-permute-done | bytes 65568 | tf_op jit(solution)/shard_map/ppermute | solution.py:55
  30.0 1.0 %collective-permute-start.16 = (f32[4,2,4,2048]{3,2,1,0:T(4,128)S(1)}, f32[4,2,4,2048]{3,2,1,0:T(4,128)S(1)}, u32[]{:S(2)}, u32[]{:S(2)}) collective-permute-start(f32[4,2,4,2048]{3,2,1,0:T(4,128)S(1)} %join.1.refs_0_), channel_id=1, source_target_pairs={{0,24},{8,16},{16,8},{24,0},{1,25},{9,17},{17,9},{25,1},{2,26},{10... | collective-permute-start | bytes 786440 | tf_op jit(solution)/shard_map/ppermute | solution.py:55
  31.0 1.1 %collective-permute-start.15 = (f32[4,2,4,2048]{3,2,1,0:T(4,128)S(1)}, f32[4,2,4,2048]{3,2,1,0:T(4,128)S(1)}, u32[]{:S(2)}, u32[]{:S(2)}) collective-permute-start(f32[4,2,4,2048]{3,2,1,0:T(4,128)S(1)} %join.1.refs_0_), channel_id=1, source_target_pairs={{0,16},{8,24},{16,0},{24,8},{1,17},{9,25},{17,1},{25,9},{2,18},{10... | collective-permute-start | bytes 786440 | tf_op jit(solution)/shard_map/ppermute | solution.py:55
  32.1 1.5 %collective-permute-start.14 = (f32[4,2,4,2048]{3,2,1,0:T(4,128)S(1)}, f32[4,2,4,2048]{3,2,1,0:T(4,128)S(1)}, u32[]{:S(2)}, u32[]{:S(2)}) collective-permute-start(f32[4,2,4,2048]{3,2,1,0:T(4,128)S(1)} %join.1.refs_0_), channel_id=1, source_target_pairs={{0,8},{8,0},{16,24},{24,16},{1,9},{9,1},{17,25},{25,17},{2,10},{10... | collective-permute-start | bytes 786440 | tf_op jit(solution)/shard_map/ppermute | solution.py:55
  33.6 0.5 %collective-permute-start.8 = (f32[384,128]{1,0:T(8,128)S(1)}, f32[384,128]{1,0:T(8,128)S(1)}, u32[]{:S(2)}, u32[]{:S(2)}) collective-permute-start(f32[384,128]{1,0:T(8,128)S(1)} %dense.1.refs_0_), channel_id=1, source_target_pairs={{0,16},{8,24},{16,0},{24,8},{1,17},{9,25},{17,1},{25,9},{2,18},{10... | collective-permute-start | bytes 589832 | tf_op jit(solution)/shard_map/ppermute | solution.py:55
  34.1 1.0 %collective-permute-start.7 = (f32[384,128]{1,0:T(8,128)S(1)}, f32[384,128]{1,0:T(8,128)S(1)}, u32[]{:S(2)}, u32[]{:S(2)}) collective-permute-start(f32[384,128]{1,0:T(8,128)S(1)} %dense.1.refs_0_), channel_id=1, source_target_pairs={{0,8},{8,0},{16,24},{24,16},{1,9},{9,1},{17,25},{25,17},{2,10},{10... | collective-permute-start | bytes 589832 | tf_op jit(solution)/shard_map/ppermute | solution.py:55
  35.1 9.9 %collective-permute-done.8.refs_2_ = f32[384,128]{1,0:T(8,128)S(1)} collective-permute-done((f32[384,128]{1,0:T(8,128)S(1)}, f32[384,128]{1,0:T(8,128)S(1)}, u32[]{:S(2)}, u32[]{:S(2)}) %collective-permute-start.8) | collective-permute-done | bytes 196640 | tf_op jit(solution)/shard_map/ppermute | solution.py:55
  45.0 0.1 collective-permute-done.7.refs_1_
  45.1 0.9 %dense_out.1 = f32[16,8192]{1,0:T(8,128)} custom-call(f32[384,128]{1,0:T(8,128)S(1)} %dense.1.refs_0_, f32[384,128]{1,0:T(8,128)S(1)} %collective-permute-done.7.refs_1_, f32[384,128]{1,0:T(8,128)S(1)} %collective-permute-done.8.refs_2_, f32[384,128]{1,0:T(8,128)S(1)} %collective-permute-done.9.refs_3_), custom_call_target="tpu_custom_call" | custom-call | tf_op jit(solution)/shard_map/dense_out/pallas_call | solution.py:43
  46.0 1.8 %embedding.1 = (f32[200,1024]{1,0:T(8,128)}, f32[64,200]{1,0:T(8,128)}) custom-call(f32[200,1024]{1,0:T(8,128)S(1)} %copy-done, f32[64,200]{1,0:T(8,128)S(1)} %bitcast.6, f32[64,1024]{1,0:T(8,128)S(1)} %bitcast.5, f32[384,128]{1,0:T(8,128)S(1)} %dense.1.refs_0_, f32[384,128]{1,0:T(8,128)S(1)} %collective-permute-done.7.refs_1_, ...), custom_call_target="tpu_custom_call" | custom-call | tf_op jit(solution)/shard_map/embedding/pallas_call | solution.py:43
  47.8 1.2 %momentum_out.1 = f32[4,65536]{1,0:T(4,128)} custom-call(s32[8]{0:T(128)S(4)} %get-tuple-element.42.owned, f32[4,65536]{1,0:T(4,128)S(1)} %get-tuple-element.43.momentum, f32[4,2,4,2048]{3,2,1,0:T(4,128)S(1)} %join.1.refs_0_, f32[4,2,4,2048]{3,2,1,0:T(4,128)S(1)} %collective-permute-done.14.refs_1_, f32[4,2,4,2048]{3,2,1,0:T(4,128)S(1)} %collective-permute-done.15.refs_2_, ...), custom_call_target="tpu_custom_call" | custom-call | tf_op jit(solution)/shard_map/momentum_out/pallas_call | solution.py:43
  (23 shorter events, 0.2 us)
Async XLA Ops:
  0.6 13.5 %copy-start = (f32[200,1024]{1,0:T(8,128)S(1)}, f32[200,1024]{1,0:T(8,128)}, u32[]{:S(2)}) copy-start(f32[200,1024]{1,0:T(8,128)} %anchor.5) | copy-start | bytes 2457604
  0.6 13.5 %copy-start.2 = (f32[1,200,1024]{2,1,0:T(8,128)S(1)}, f32[1,200,1024]{2,1,0:T(8,128)}, u32[]{:S(2)}) copy-start(f32[1,200,1024]{2,1,0:T(8,128)} %inner.3) | copy-start | bytes 2457604
  2.5 6.3 %collective-permute-start.3 = (f32[4,4,2048]{2,1,0:T(4,128)S(1)}, f32[4,4,2048]{2,1,0:T(4,128)S(1)}, u32[]{:S(2)}, u32[]{:S(2)}) collective-permute-start(f32[4,4,2048]{2,1,0:T(4,128)S(1)} %get-tuple-element.37), channel_id=1, source_target_pairs={{0,1},{1,0},{2,3},{3,2},{4,5},{5,4},{6,7},{7,6},{8,9},{9,8},{10,11... | collective-permute-start | bytes 393224 | tf_op jit(solution)/shard_map/ppermute | solution.py:55
  3.0 10.0 %collective-permute-start = (f32[16,2048]{1,0:T(8,128)S(1)}, f32[16,2048]{1,0:T(8,128)S(1)}, u32[]{:S(2)}, u32[]{:S(2)}) collective-permute-start(f32[16,2048]{1,0:T(8,128)S(1)} %get-tuple-element.32), channel_id=1, source_target_pairs={{0,8},{8,0},{16,24},{24,16},{1,9},{9,1},{17,25},{25,17},{2,10},{10... | collective-permute-start | bytes 393224 | tf_op jit(solution)/shard_map/ppermute | solution.py:55
  5.6 8.4 %collective-permute-start.1 = (f32[16,2048]{1,0:T(8,128)S(1)}, f32[16,2048]{1,0:T(8,128)S(1)}, u32[]{:S(2)}, u32[]{:S(2)}) collective-permute-start(f32[16,2048]{1,0:T(8,128)S(1)} %get-tuple-element.33), channel_id=1, source_target_pairs={{0,16},{8,24},{16,0},{24,8},{1,17},{9,25},{17,1},{25,9},{2,18},{10... | collective-permute-start | bytes 393224 | tf_op jit(solution)/shard_map/ppermute | solution.py:55
  7.1 0.7 %copy-start.4 = (s32[16,1]{0,1:T(1,128)S(1)}, s32[16,1]{0,1:T(1,128)}, u32[]{:S(2)}) copy-start(s32[16,1]{0,1:T(1,128)} %param.8) | copy-start | bytes 196
  7.1 6.9 %collective-permute-start.2 = (f32[16,2048]{1,0:T(8,128)S(1)}, f32[16,2048]{1,0:T(8,128)S(1)}, u32[]{:S(2)}, u32[]{:S(2)}) collective-permute-start(f32[16,2048]{1,0:T(8,128)S(1)} %get-tuple-element.34), channel_id=1, source_target_pairs={{0,24},{8,16},{16,8},{24,0},{1,25},{9,17},{17,9},{25,1},{2,26},{10... | collective-permute-start | bytes 393224 | tf_op jit(solution)/shard_map/ppermute | solution.py:55
  8.8 7.0 %collective-permute-start.4 = (f32[2,4,2048]{2,1,0:T(4,128)S(1)}, f32[2,4,2048]{2,1,0:T(4,128)S(1)}, u32[]{:S(2)}, u32[]{:S(2)}) collective-permute-start(f32[2,4,2048]{2,1,0:T(4,128)S(1)} %get-tuple-element.39), channel_id=1, source_target_pairs={{0,2},{1,3},{2,0},{3,1},{4,6},{5,7},{6,4},{7,5},{8,10},{9,11},{10,... | collective-permute-start | bytes 196616 | tf_op jit(solution)/shard_map/ppermute | solution.py:55
  10.5 7.3 %collective-permute-start.5 = (f32[2,4,2048]{2,1,0:T(4,128)S(1)}, f32[2,4,2048]{2,1,0:T(4,128)S(1)}, u32[]{:S(2)}, u32[]{:S(2)}) collective-permute-start(f32[2,4,2048]{2,1,0:T(4,128)S(1)} %get-tuple-element.40), channel_id=1, source_target_pairs={{0,4},{1,5},{2,6},{3,7},{4,0},{5,1},{6,2},{7,3},{8,12},{9,13},{10,... | collective-permute-start | bytes 196616 | tf_op jit(solution)/shard_map/ppermute | solution.py:55
  13.1 6.1 %collective-permute-start.6 = (f32[2,4,2048]{2,1,0:T(4,128)S(1)}, f32[2,4,2048]{2,1,0:T(4,128)S(1)}, u32[]{:S(2)}, u32[]{:S(2)}) collective-permute-start(f32[2,4,2048]{2,1,0:T(4,128)S(1)} %get-tuple-element.41), channel_id=1, source_target_pairs={{0,6},{1,7},{2,4},{3,5},{4,2},{5,3},{6,0},{7,1},{8,14},{9,15},{10,... | collective-permute-start | bytes 196616 | tf_op jit(solution)/shard_map/ppermute | solution.py:55
  14.0 1.0 %copy-start.1 = (f32[1024,64]{0,1:T(8,128)S(1)}, f32[1024,64]{0,1:T(8,128)}, u32[]{:S(2)}) copy-start(f32[1024,64]{0,1:T(8,128)} %param.15) | copy-start | bytes 786436
  14.1 7.6 %collective-permute-start.10 = (f32[4,4,2048]{2,1,0:T(4,128)S(1)}, f32[4,4,2048]{2,1,0:T(4,128)S(1)}, u32[]{:S(2)}, u32[]{:S(2)}) collective-permute-start(f32[4,4,2048]{2,1,0:T(4,128)S(1)} %get-tuple-element.45), channel_id=1, source_target_pairs={{0,1},{1,0},{2,3},{3,2},{4,5},{5,4},{6,7},{7,6},{8,9},{9,8},{10,11... | collective-permute-start | bytes 393224 | tf_op jit(solution)/shard_map/ppermute | solution.py:55
  19.4 14.6 %collective-permute-start.9 = (f32[384,128]{1,0:T(8,128)S(1)}, f32[384,128]{1,0:T(8,128)S(1)}, u32[]{:S(2)}, u32[]{:S(2)}) collective-permute-start(f32[384,128]{1,0:T(8,128)S(1)} %dense.1.refs_0_), channel_id=1, source_target_pairs={{0,24},{8,16},{16,8},{24,0},{1,25},{9,17},{17,9},{25,1},{2,26},{10... | collective-permute-start | bytes 589832 | tf_op jit(solution)/shard_map/ppermute | solution.py:55
  21.7 5.7 %collective-permute-start.11 = (f32[2,4,2048]{2,1,0:T(4,128)S(1)}, f32[2,4,2048]{2,1,0:T(4,128)S(1)}, u32[]{:S(2)}, u32[]{:S(2)}) collective-permute-start(f32[2,4,2048]{2,1,0:T(4,128)S(1)} %get-tuple-element.47), channel_id=1, source_target_pairs={{0,2},{1,3},{2,0},{3,1},{4,6},{5,7},{6,4},{7,5},{8,10},{9,11},{10,... | collective-permute-start | bytes 196616 | tf_op jit(solution)/shard_map/ppermute | solution.py:55
  21.8 5.6 %collective-permute-start.12 = (f32[2,4,2048]{2,1,0:T(4,128)S(1)}, f32[2,4,2048]{2,1,0:T(4,128)S(1)}, u32[]{:S(2)}, u32[]{:S(2)}) collective-permute-start(f32[2,4,2048]{2,1,0:T(4,128)S(1)} %get-tuple-element.48), channel_id=1, source_target_pairs={{0,4},{1,5},{2,6},{3,7},{4,0},{5,1},{6,2},{7,3},{8,12},{9,13},{10,... | collective-permute-start | bytes 196616 | tf_op jit(solution)/shard_map/ppermute | solution.py:55
  23.9 6.1 %collective-permute-start.13 = (f32[2,4,2048]{2,1,0:T(4,128)S(1)}, f32[2,4,2048]{2,1,0:T(4,128)S(1)}, u32[]{:S(2)}, u32[]{:S(2)}) collective-permute-start(f32[2,4,2048]{2,1,0:T(4,128)S(1)} %get-tuple-element.49), channel_id=1, source_target_pairs={{0,6},{1,7},{2,4},{3,5},{4,2},{5,3},{6,0},{7,1},{8,14},{9,15},{10,... | collective-permute-start | bytes 196616 | tf_op jit(solution)/shard_map/ppermute | solution.py:55
  30.0 16.0 %copy-start.3 = (f32[200,64]{0,1:T(8,128)S(1)}, f32[200,64]{0,1:T(8,128)}, u32[]{:S(2)}) copy-start(f32[200,64]{0,1:T(8,128)} %param.14) | copy-start | bytes 153604
  30.0 17.7 %collective-permute-start.16 = (f32[4,2,4,2048]{3,2,1,0:T(4,128)S(1)}, f32[4,2,4,2048]{3,2,1,0:T(4,128)S(1)}, u32[]{:S(2)}, u32[]{:S(2)}) collective-permute-start(f32[4,2,4,2048]{3,2,1,0:T(4,128)S(1)} %join.1.refs_0_), channel_id=1, source_target_pairs={{0,24},{8,16},{16,8},{24,0},{1,25},{9,17},{17,9},{25,1},{2,26},{10... | collective-permute-start | bytes 786440 | tf_op jit(solution)/shard_map/ppermute | solution.py:55
  31.0 16.7 %collective-permute-start.15 = (f32[4,2,4,2048]{3,2,1,0:T(4,128)S(1)}, f32[4,2,4,2048]{3,2,1,0:T(4,128)S(1)}, u32[]{:S(2)}, u32[]{:S(2)}) collective-permute-start(f32[4,2,4,2048]{3,2,1,0:T(4,128)S(1)} %join.1.refs_0_), channel_id=1, source_target_pairs={{0,16},{8,24},{16,0},{24,8},{1,17},{9,25},{17,1},{25,9},{2,18},{10... | collective-permute-start | bytes 786440 | tf_op jit(solution)/shard_map/ppermute | solution.py:55
  32.1 15.7 %collective-permute-start.14 = (f32[4,2,4,2048]{3,2,1,0:T(4,128)S(1)}, f32[4,2,4,2048]{3,2,1,0:T(4,128)S(1)}, u32[]{:S(2)}, u32[]{:S(2)}) collective-permute-start(f32[4,2,4,2048]{3,2,1,0:T(4,128)S(1)} %join.1.refs_0_), channel_id=1, source_target_pairs={{0,8},{8,0},{16,24},{24,16},{1,9},{9,1},{17,25},{25,17},{2,10},{10... | collective-permute-start | bytes 786440 | tf_op jit(solution)/shard_map/ppermute | solution.py:55
  33.6 11.4 %collective-permute-start.8 = (f32[384,128]{1,0:T(8,128)S(1)}, f32[384,128]{1,0:T(8,128)S(1)}, u32[]{:S(2)}, u32[]{:S(2)}) collective-permute-start(f32[384,128]{1,0:T(8,128)S(1)} %dense.1.refs_0_), channel_id=1, source_target_pairs={{0,16},{8,24},{16,0},{24,8},{1,17},{9,25},{17,1},{25,9},{2,18},{10... | collective-permute-start | bytes 589832 | tf_op jit(solution)/shard_map/ppermute | solution.py:55
  34.1 11.0 %collective-permute-start.7 = (f32[384,128]{1,0:T(8,128)S(1)}, f32[384,128]{1,0:T(8,128)S(1)}, u32[]{:S(2)}, u32[]{:S(2)}) collective-permute-start(f32[384,128]{1,0:T(8,128)S(1)} %dense.1.refs_0_), channel_id=1, source_target_pairs={{0,8},{8,0},{16,24},{24,16},{1,9},{9,1},{17,25},{25,17},{2,10},{10... | collective-permute-start | bytes 589832 | tf_op jit(solution)/shard_map/ppermute | solution.py:55

commit v3 on v2

--- a/solution.py
+++ b/solution.py
@@ -39,16 +39,31 @@
 anywhere = pl.BlockSpec(memory_space=pl.ANY)
 
 
-def run(body, outs, operands, scalars=(), scratch=(), far=(), out_specs=None, name=None):
+def run(
+    body, outs, operands, scalars=(), scratch=(), far=(), after=(), out_specs=None, name=None
+):
+    skip = len(after)
+
+    def whole(*refs):
+        body(*refs[skip:])
+
     return pl.pallas_call(
-        body,
+        whole,
         out_shape=list(outs),
-        in_specs=[smem] * len(scalars) + [anywhere] * len(far) + [vmem] * len(operands),
+        in_specs=[anywhere] * skip
+        + [smem] * len(scalars)
+        + [anywhere] * len(far)
+        + [vmem] * len(operands),
         out_specs=out_specs or [vmem] * len(outs),
         scratch_shapes=list(scratch),
         compiler_params=pltpu.CompilerParams(vmem_limit_bytes=vmem_limit),
         name=name,
-    )(*[in_scalars(x) for x in scalars], *[in_hbm(x) for x in far], *operands)
+    )(
+        *[on_chip(x) for x in after],
+        *[in_scalars(x) for x in scalars],
+        *[in_hbm(x) for x in far],
+        *operands,
+    )
 
 
 def swap(x, axis, count, mask):
@@ -64,7 +79,7 @@
     return pl.ds(pl.multiple_of(index * part, 128), part)
 
 
-def places_body(slots, owners, row_of, block_of, owned):
+def name_places(slots, owners, row_of, block_of, owned):
     blocks, owner_count = row_of.shape[0], owned.shape[0]
 
     def clear(i, carry):
@@ -84,18 +99,22 @@
         owned[owner] = slot + 1
         return carry
 
-    lax.fori_loop(0, block_of.shape[0], clear, 0)
-    lax.fori_loop(0, owner_count, clear_count, 0)
-    lax.fori_loop(0, blocks, name, 0)
-
-
-def start_body(groups, part, anchor, inner, momentum, *refs):
-    outs, (quarter, same, other, held), (far, near, sem) = (
+    short = blocks <= 16
+    lax.fori_loop(0, block_of.shape[0], clear, 0, unroll=short)
+    lax.fori_loop(0, owner_count, clear_count, 0, unroll=short)
+    lax.fori_loop(0, blocks, name, 0, unroll=short)
+
+
+def start_body(groups, part, owners, anchor, inner, momentum, *refs):
+    outs, (quarter, same, other, held), named, (own, far, near, sem) = (
         refs[:groups],
         refs[groups : groups + 4],
-        refs[groups + 4 :],
+        refs[groups + 4 : groups + 7],
+        refs[groups + 7 :],
     )
     rep, chip, core = place()
+    listed = pltpu.make_async_copy(owners, own, sem.at[2 * groups + 1])
+    listed.start()
     copies = []
     for k in (*range(1, groups), 0):
         at = column(rep ^ k, part)
@@ -108,6 +127,8 @@
         copies.append((k, pair))
     whole = pltpu.make_async_copy(momentum, held, sem.at[2 * groups])
     whole.start()
+    listed.wait()
+    name_places(same.shape[1], own, *named)
     for k, pair in copies:
         for copy in pair:
             copy.wait()
@@ -155,10 +176,37 @@
         outs[0][:, 1] = other[...]
 
 
-def join_body(*refs):
-    out = refs[-1]
-    for k, ref in enumerate(refs[:-1]):
-        out[k] = ref[...]
+def join_body(direct, half, *refs):
+    *received, first, second, out1, out2, out3 = refs
+    chips = received[0].shape[0] if not direct else len(received)
+    part = received[0].shape[-1]
+
+    def fill(k, carry):
+        for o in range(2):
+            rows = received[k][o] if direct else received[0][k, o]
+            for out in (out1, out2, out3):
+                out[:, column(2 * k + o, part)] = rows
+        return carry
+
+    if direct:
+        for k in range(chips):
+            fill(k, 0)
+    else:
+        lax.fori_loop(0, chips, fill, 0)
+    skip = 2 * chips * part
+    for out, ref, start in ((out2, first, 0), (out1, second, half)):
+        for t in range((out.shape[1] - skip) // 128):
+            out[:, skip + 128 * t : skip + 128 * (t + 1)] = ref[start + 4 * t : start + 4 * t + 4, :]
+
+
+def unfold(half, extra, messages):
+    first, second = messages[1], messages[0]
+    skip = first.shape[1] - 32 * half
+    for t in range(extra.shape[0] // 8):
+        ref, at = (first, 8 * t) if 8 * t < half else (second, 8 * t - half)
+        for h in range(2):
+            lane = skip + 32 * (at + 4 * h)
+            extra[8 * t + 4 * h : 8 * t + 4 * h + 4, :] = ref[:, lane : lane + 128]
 
 
 def tiles(rows, columns):
@@ -201,66 +249,84 @@
             at += 8
 
 
-def dense_out_body(part, *refs):
-    out = refs[-1]
-    rep, _, _ = place()
-    blocks = out.shape[0]
-    for k, ref in enumerate(refs[:-1]):
-        for t, (i, height, j, width) in enumerate(tiles(blocks, part)):
-            at = pl.multiple_of((rep ^ k) * part, 128) + j
-            out[i : i + height, pl.ds(pl.multiple_of(at, 128), width)] = ref[
-                8 * t : 8 * t + height, :width
-            ]
-
-
-def momentum_out_body(part, direct, owned, momentum, *refs):
-    out = refs[-1]
+def two_parts(x):
+    high = x.astype(jnp.bfloat16)
+    return high, (x - high.astype(f32)).astype(jnp.bfloat16)
+
+
+def dot(a, b, contract):
+    return lax.dot_general(a, b, (contract, ((), ())), preferred_element_type=f32)
+
+
+def factor_body(anchor, inner, basis_t, out):
+    rank = out.shape[0]
+    high, low = two_parts(anchor[...] - inner[0])
+    basis_high, basis_low = two_parts(basis_t[...])
+    both = dot(jnp.concatenate([basis_high, basis_low], axis=0), high, ((1,), (1,)))
+    out[...] = both[:rank] + (both[rank:] + dot(basis_high, low, ((1,), (1,))))
+
+
+def finish_body(
+    part, half, direct, owned, anchor, momentum_t, basis_t, momentum, *refs
+):
+    dense, gradient, results, (extra, mean, sem, *made) = (
+        refs[:3],
+        refs[3:7],
+        refs[7:11],
+        refs[11:],
+    )
+    new_dense, new_momentum, new_emb, new_momentum_t = made
+    copies = [
+        pltpu.make_async_copy(ref, result, sem.at[i])
+        for i, (ref, result) in enumerate(zip(made, results))
+    ]
     rep, here, core = place()
-    groups = len(refs) - 1
-    chips = refs[0].shape[0]
-    slots = momentum.shape[0]
+    slots, groups = momentum.shape[0], 4
+    pieces = momentum.shape[1] // part // groups
     live = lax.broadcasted_iota(jnp.int32, (slots, part), 0) < owned[here * 2 + core]
 
-    def fill(k, carry):
-        chip = here ^ k if direct else k
-        for o in range(2):
-            piece = 2 * chip + (core ^ o)
-            for g in range(groups):
-                at = column(piece * groups + (rep ^ g), part)
-                out[:, at] = jnp.where(
-                    live, momentum_decay * momentum[:, at] + refs[g][k, o], 0.0
-                )
-        return carry
-
-    lax.fori_loop(0, chips, fill, 0, unroll=chips <= 8)
-
-
-def dot(a, b, contract):
-    return lax.dot_general(
-        a,
-        b,
-        ((contract), ((), ())),
-        precision=lax.Precision.HIGHEST,
-        preferred_element_type=f32,
-    )
-
-
-def factor_body(anchor, inner, basis_t, out):
-    out[...] = dot(basis_t[...], anchor[...] - inner[0], ((1,), (1,)))
-
-
-def embedding_body(groups, skip, anchor, momentum_t, basis_t, *refs):
-    parts, (new_emb, new_momentum_t, mean) = refs[:groups], refs[groups:]
+    def fill(i, carry):
+        k, o = (i >> 1, i & 1)
+        piece = 2 * (here ^ k if direct else k) + (core ^ o)
+        for g, ref in enumerate(gradient):
+            at = column(piece * groups + (rep ^ g), part)
+            rows = momentum_decay * momentum[:, at] + ref[:, column(i, part)]
+            new_momentum[:, at] = jnp.where(live, rows, 0.0)
+        return carry
+
+    lax.fori_loop(0, pieces, fill, 0, unroll=pieces <= 16)
+    copies[1].start()
+
+    unfold(half, extra, (gradient[1], gradient[2]))
+    parts = (*dense, extra)
+    blocks = new_dense.shape[0]
+    dense_tiles = tiles(blocks, part)
+    for k, ref in enumerate(parts):
+        for t, (i, height, j, width) in enumerate(dense_tiles):
+            at = pl.multiple_of((rep ^ k) * part + j, 128)
+            new_dense[i : i + height, pl.ds(at, width)] = ref[8 * t : 8 * t + height, :width]
+    copies[0].start()
+
     for t, (i, height, j, width) in enumerate(tiles(*mean.shape)):
-        at = slice(skip + 8 * t, skip + 8 * t + height)
-        total = parts[0][at, :width]
-        for ref in parts[1:]:
-            total = total + ref[at, :width]
-        mean[i : i + height, j : j + width] = total / groups
+        at = slice(8 * (len(dense_tiles) + t), 8 * (len(dense_tiles) + t) + height)
+        sums = [ref[at, :width] for ref in parts]
+        while len(sums) > 1:
+            sums = [a + b for a, b in zip(sums[::2], sums[1::2])]
+        mean[i : i + height, j : j + width] = sums[0] / groups
     moved = momentum_decay * momentum_t[...] + mean[...]
     new_momentum_t[...] = moved
-    update = mean[...] + momentum_decay * moved
-    new_emb[...] = anchor[...] - outer_rate * dot(update, basis_t[...], ((0,), (0,)))
+    copies[3].start()
+    high, low = two_parts(mean[...] + momentum_decay * moved)
+    basis_high, basis_low = two_parts(basis_t[...])
+    back = dot(
+        jnp.concatenate([high, low, high], axis=0),
+        jnp.concatenate([basis_high, basis_high, basis_low], axis=0),
+        ((0,), (0,)),
+    )
+    new_emb[...] = anchor[...] - outer_rate * back
+    copies[2].start()
+    for copy in copies:
+        copy.wait()
 
 
 def over_chips(same, other, chips, owner_count, name):
@@ -273,7 +339,8 @@
             [on_chip(same), on_chip(other)],
             name=name,
         )
-        return [outs[0]] + [swap(outs[k], "own", owner_count, 2 * k) for k in range(1, chips)]
+        moved = [outs[0]] + [swap(outs[k], "own", owner_count, 2 * k) for k in range(1, chips)]
+        return moved, outs
     (packed,) = run(
         functools.partial(pack_body, False),
         [stored((chips,) + shape)],
@@ -281,11 +348,10 @@
         name=name,
     )
     groups = [list(range(core, owner_count, 2)) for core in range(2)]
-    return [
-        lax.all_to_all(
-            packed, "own", split_axis=0, concat_axis=0, axis_index_groups=groups, tiled=True
-        )
-    ]
+    moved = lax.all_to_all(
+        packed, "own", split_axis=0, concat_axis=0, axis_index_groups=groups, tiled=True
+    )
+    return [moved], []
 
 
 def per_device(
@@ -302,33 +368,26 @@
     chunk = (chips, slot_count, part)
     table = (chips, 2, slot_count, part)
 
-    *parts, quarter, same, other, momentum = run(
+    *parts, quarter, same, other, momentum, row_of, block_of, owned = run(
         functools.partial(start_body, groups, part),
-        [kept((blocks, part))] * (groups + 1) + [kept(chunk)] * 2 + [kept(momentum_dense.shape)],
+        [kept((blocks, part))] * (groups + 1)
+        + [kept(chunk)] * 2
+        + [kept(momentum_dense.shape)]
+        + [pltpu.SMEM((n,), jnp.int32) for n in (blocks, owner_count * slot_count, owner_count)],
         [],
-        far=[anchor_dense, inner_dense, momentum_dense],
+        far=[owners[:, 0], anchor_dense, inner_dense, momentum_dense],
+        out_specs=[vmem] * (groups + 4) + [smem] * 3,
         scratch=[
+            pltpu.SMEM((blocks,), jnp.int32),
             pltpu.VMEM((groups, blocks, part), f32),
             pltpu.VMEM((groups, blocks, part), f32),
-            pltpu.SemaphoreType.DMA((2 * groups + 1,)),
+            pltpu.SemaphoreType.DMA((2 * groups + 2,)),
         ],
         name="start",
     )
     parts = [parts[0]] + [swap(parts[k], "rep", groups, k) for k in range(1, groups)]
-    momentum_rows = over_chips(same, other, chips, owner_count, "pack_momentum")
-
-    row_of, block_of, owned = run(
-        functools.partial(places_body, slot_count),
-        [
-            pltpu.SMEM((blocks,), jnp.int32),
-            pltpu.SMEM((owner_count * slot_count,), jnp.int32),
-            pltpu.SMEM((owner_count,), jnp.int32),
-        ],
-        [],
-        scalars=[owners[:, 0]],
-        out_specs=[smem] * 3,
-        name="places",
-    )
+    momentum_rows, packed_momentum = over_chips(same, other, chips, owner_count, "pack_momentum")
+
     basis_t = basis.T
     (factor,) = run(
         factor_body, [kept((rank, rows))], [anchor_emb, inner_emb, basis_t], name="factor"
@@ -341,7 +400,7 @@
         [block_of],
         name="mean",
     )
-    gradient_rows = over_chips(same, other, chips, owner_count, "pack_mean")
+    gradient_rows, packed_mean = over_chips(same, other, chips, owner_count, "pack_mean")
 
     skip = 8 * len(tiles(blocks, part))
     (dense,) = run(
@@ -355,35 +414,35 @@
         ],
         name="dense",
     )
-    dense = [dense] + [swap(dense, "rep", groups, k) for k in range(1, groups)]
-
-    if direct:
-        (gradient,) = run(
-            join_body, [kept(table)], [on_chip(x) for x in gradient_rows], name="join"
-        )
-    else:
-        (gradient,) = gradient_rows
-    gradient = [gradient] + [swap(gradient, "rep", groups, k) for k in range(1, groups)]
-
-    (new_dense,) = run(
-        functools.partial(dense_out_body, part),
-        [stored((blocks, piece_len))],
-        [on_chip(x) for x in dense],
-        name="dense_out",
-    )
-    new_emb, new_momentum_t = run(
-        functools.partial(embedding_body, groups, skip),
-        [stored(anchor_emb.shape), stored((rank, rows))],
-        [anchor_emb, momentum_emb.T, basis_t] + [on_chip(x) for x in dense],
-        scratch=[pltpu.VMEM((rank, rows), f32)],
-        name="embedding",
-    )
-    (new_momentum_dense,) = run(
-        functools.partial(momentum_out_body, part, direct),
-        [stored(momentum_dense.shape)],
-        [on_chip(momentum)] + [on_chip(x) for x in gradient],
+    half = dense.shape[0] // 2
+    dense = [dense] + [swap(dense, "rep", groups, k) for k in (1, 2)]
+
+    length = 2 * chips * part
+    messages = run(
+        functools.partial(join_body, direct, half),
+        [kept((slot_count, length + 32 * half))] * 2 + [kept((slot_count, length))],
+        [on_chip(x) for x in (*gradient_rows, dense[1], dense[2])],
+        name="join",
+    )
+    gradient = [messages[2]] + [swap(m, "rep", groups, k + 1) for k, m in enumerate(messages)]
+
+    shapes = [anchor_dense.shape, momentum_dense.shape, anchor_emb.shape, (rank, rows)]
+    new_dense, new_momentum_dense, new_emb, new_momentum_t = run(
+        functools.partial(finish_body, part, half, direct),
+        [stored(shape) for shape in shapes],
+        [
+            on_chip(x)
+            for x in (anchor_emb, momentum_emb.T, basis_t, momentum, *dense, *gradient)
+        ],
         [owned],
-        name="momentum_out",
+        out_specs=[anywhere] * 4,
+        scratch=[
+            pltpu.VMEM(dense[0].shape, f32),
+            pltpu.VMEM((rank, rows), f32),
+            pltpu.SemaphoreType.DMA((4,)),
+        ]
+        + [pltpu.VMEM(shape, f32) for shape in shapes],
+        name="finish",
     )
     return (new_dense, new_momentum_dense, new_emb, new_momentum_t.T)
 

time: 49.2 us -> 45.3 us (0.921)
  Pallas kernels: 8.05 us -> 4.71 us
  local copies, waits for them, and re-layouts: 1.39 us -> 0.02 us
  starting transfers between devices: 21.5 us -> 22.5 us
    pallas_call x11 -> x8, Pallas kernels: 8.05 us -> 4.71 us  [run(): pl.pallas_call(whole, out_shape=list(outs), in_specs=[anywhere] * skip +...]
    unnamed x10 -> x8, local copies, waits for them, and re-layouts: 1.39 us -> 0.02 us
    ppermute x17 -> x16, starting transfers between devices: 21.5 us -> 22.5 us  [swap(): return lax.ppermute(x, axis, [(i, i ^ mask) for i in range(count)])]
    ppermute x17 -> x16, waiting for transfers between devices: 17.3 us -> 17.2 us  [swap(): return lax.ppermute(x, axis, [(i, i ^ mask) for i in range(count)])]
  transfers between devices with their start and end apart: 17 -> 16, of which waited for: 7 -> 6; matrix products, arithmetic and copies ran while one was open for 0% -> 0% of each run, Pallas kernels for 10% -> 2%
where the time goes in v3:
time: 45.3 us; the launch traced here: 45.2 us
  starting transfers between devices  22.5 us (50%)
  waiting for transfers between devices  17.2 us (38%)
  Pallas kernels  4.71 us (10%)
  between operations  0.75 us (2%)
    ppermute x16, starting transfers between devices, swap(): return lax.ppermute(x, axis, [(i, i ^ mask) for i in range(count)])  22.5 us
    ppermute x16, waiting for transfers between devices, swap(): return lax.ppermute(x, axis, [(i, i ^ mask) for i in range(count)])  17.2 us
    pallas_call x8, Pallas kernels, run(): pl.pallas_call(whole, out_shape=list(outs), in_specs=[anywhere] * skip +...  4.71 us
  transfers between devices with their start and end apart: 16, of which 6 were waited for; matrix products, arithmetic and copies ran while one was open for 0% of the time, Pallas kernels for 2%

profile of v3, /device:TPU:0, one launch (start us, length us, event | category | flops | bytes accessed | tf_op | source)
XLA Modules:
  0.0 45.2 jit_solution(17473832036659337438)
XLA Ops:
  0.7 1.9 %start.1 = (f32[16,2048]{1,0:T(8,128)S(1)}, f32[16,2048]{1,0:T(8,128)S(1)}, f32[16,2048]{1,0:T(8,128)S(1)}, f32[16,2048]{1,0:T(8,128)S(1)}, f32[16,2048]{1,0:T(8...) custom-call(s32[16]{0:T(128)} %bitcast.7, ...), custom_call_target="tpu_custom_call" | custom-call | tf_op jit(solution)/shard_map/start/pallas_call | solution.py:50
  2.5 0.0 copy-start.1
  2.5 0.5 %collective-permute-start.3 = (f32[4,4,2048]{2,1,0:T(4,128)S(1)}, f32[4,4,2048]{2,1,0:T(4,128)S(1)}, u32[]{:S(2)}, u32[]{:S(2)}) collective-permute-start(f32[4,4,2048]{2,1,0:T(4,128)S(1)} %get-tuple-element.44), channel_id=1, source_target_pairs={{0,1},{1,0},{2,3},{3,2},{4,5},{5,4},{6,7},{7,6},{8,9},{9,8},{10,11... | collective-permute-start | bytes 393224 | tf_op jit(solution)/shard_map/ppermute | solution.py:70
  3.1 2.6 %collective-permute-start = (f32[16,2048]{1,0:T(8,128)S(1)}, f32[16,2048]{1,0:T(8,128)S(1)}, u32[]{:S(2)}, u32[]{:S(2)}) collective-permute-start(f32[16,2048]{1,0:T(8,128)S(1)} %get-tuple-element.39), channel_id=1, source_target_pairs={{0,8},{8,0},{16,24},{24,16},{1,9},{9,1},{17,25},{25,17},{2,10},{10... | collective-permute-start | bytes 393224 | tf_op jit(solution)/shard_map/ppermute | solution.py:70
  5.6 1.5 %collective-permute-start.1 = (f32[16,2048]{1,0:T(8,128)S(1)}, f32[16,2048]{1,0:T(8,128)S(1)}, u32[]{:S(2)}, u32[]{:S(2)}) collective-permute-start(f32[16,2048]{1,0:T(8,128)S(1)} %get-tuple-element.40), channel_id=1, source_target_pairs={{0,16},{8,24},{16,0},{24,8},{1,17},{9,25},{17,1},{25,9},{2,18},{10... | collective-permute-start | bytes 393224 | tf_op jit(solution)/shard_map/ppermute | solution.py:70
  7.1 0.0 collective-permute-start.2
  7.2 0.0 collective-permute-done.3.refs_1_
  7.2 2.1 %collective-permute-start.4 = (f32[2,4,2048]{2,1,0:T(4,128)S(1)}, f32[2,4,2048]{2,1,0:T(4,128)S(1)}, u32[]{:S(2)}, u32[]{:S(2)}) collective-permute-start(f32[2,4,2048]{2,1,0:T(4,128)S(1)} %get-tuple-element.46), channel_id=1, source_target_pairs={{0,2},{1,3},{2,0},{3,1},{4,6},{5,7},{6,4},{7,5},{8,10},{9,11},{10,... | collective-permute-start | bytes 196616 | tf_op jit(solution)/shard_map/ppermute | solution.py:70
  9.3 2.6 %collective-permute-start.5 = (f32[2,4,2048]{2,1,0:T(4,128)S(1)}, f32[2,4,2048]{2,1,0:T(4,128)S(1)}, u32[]{:S(2)}, u32[]{:S(2)}) collective-permute-start(f32[2,4,2048]{2,1,0:T(4,128)S(1)} %get-tuple-element.47), channel_id=1, source_target_pairs={{0,4},{1,5},{2,6},{3,7},{4,0},{5,1},{6,2},{7,3},{8,12},{9,13},{10,... | collective-permute-start | bytes 196616 | tf_op jit(solution)/shard_map/ppermute | solution.py:70
  11.9 0.0 collective-permute-done.refs_2_
  11.9 2.0 %collective-permute-start.6 = (f32[2,4,2048]{2,1,0:T(4,128)S(1)}, f32[2,4,2048]{2,1,0:T(4,128)S(1)}, u32[]{:S(2)}, u32[]{:S(2)}) collective-permute-start(f32[2,4,2048]{2,1,0:T(4,128)S(1)} %get-tuple-element.48), channel_id=1, source_target_pairs={{0,6},{1,7},{2,4},{3,5},{4,2},{5,3},{6,0},{7,1},{8,14},{9,15},{10,... | collective-permute-start | bytes 196616 | tf_op jit(solution)/shard_map/ppermute | solution.py:70
  13.9 0.4 factor.1.refs_3_
  14.4 0.1 mean.1
  14.5 0.1 collective-permute-start.9
  14.6 0.0 collective-permute-done.4.refs_5_
  14.6 1.8 %collective-permute-done.5.refs_6_ = f32[2,4,2048]{2,1,0:T(4,128)S(1)} collective-permute-done((f32[2,4,2048]{2,1,0:T(4,128)S(1)}, f32[2,4,2048]{2,1,0:T(4,128)S(1)}, u32[]{:S(2)}, u32[]{:S(2)}) %collective-permute-start.5) | collective-permute-done | bytes 65568 | tf_op jit(solution)/shard_map/ppermute | solution.py:70
  16.3 1.6 %collective-permute-done.6.refs_7_ = f32[2,4,2048]{2,1,0:T(4,128)S(1)} collective-permute-done((f32[2,4,2048]{2,1,0:T(4,128)S(1)}, f32[2,4,2048]{2,1,0:T(4,128)S(1)}, u32[]{:S(2)}, u32[]{:S(2)}) %collective-permute-start.6) | collective-permute-done | bytes 65568 | tf_op jit(solution)/shard_map/ppermute | solution.py:70
  17.9 0.2 dense.1.refs_5_
  18.2 1.6 %collective-permute-start.8 = (f32[384,128]{1,0:T(8,128)S(1)}, f32[384,128]{1,0:T(8,128)S(1)}, u32[]{:S(2)}, u32[]{:S(2)}) collective-permute-start(f32[384,128]{1,0:T(8,128)S(1)} %dense.1.refs_5_), channel_id=1, source_target_pairs={{0,16},{8,24},{16,0},{24,8},{1,17},{9,25},{17,1},{25,9},{2,18},{10... | collective-permute-start | bytes 589832 | tf_op jit(solution)/shard_map/ppermute | solution.py:70
  19.8 1.5 %collective-permute-start.7 = (f32[384,128]{1,0:T(8,128)S(1)}, f32[384,128]{1,0:T(8,128)S(1)}, u32[]{:S(2)}, u32[]{:S(2)}) collective-permute-start(f32[384,128]{1,0:T(8,128)S(1)} %dense.1.refs_5_), channel_id=1, source_target_pairs={{0,8},{8,0},{16,24},{24,16},{1,9},{9,1},{17,25},{25,17},{2,10},{10... | collective-permute-start | bytes 589832 | tf_op jit(solution)/shard_map/ppermute | solution.py:70
  21.3 0.1 collective-permute-start.10
  21.4 2.8 %collective-permute-start.11 = (f32[2,4,2048]{2,1,0:T(4,128)S(1)}, f32[2,4,2048]{2,1,0:T(4,128)S(1)}, u32[]{:S(2)}, u32[]{:S(2)}) collective-permute-start(f32[2,4,2048]{2,1,0:T(4,128)S(1)} %get-tuple-element.53), channel_id=1, source_target_pairs={{0,4},{1,5},{2,6},{3,7},{4,0},{5,1},{6,2},{7,3},{8,12},{9,13},{10,... | collective-permute-start | bytes 196616 | tf_op jit(solution)/shard_map/ppermute | solution.py:70
  24.2 1.6 %collective-permute-start.12 = (f32[2,4,2048]{2,1,0:T(4,128)S(1)}, f32[2,4,2048]{2,1,0:T(4,128)S(1)}, u32[]{:S(2)}, u32[]{:S(2)}) collective-permute-start(f32[2,4,2048]{2,1,0:T(4,128)S(1)} %get-tuple-element.54), channel_id=1, source_target_pairs={{0,6},{1,7},{2,4},{3,5},{4,2},{5,3},{6,0},{7,1},{8,14},{9,15},{10,... | collective-permute-start | bytes 196616 | tf_op jit(solution)/shard_map/ppermute | solution.py:70
  25.8 1.5 %collective-permute-done.11.refs_2_ = f32[2,4,2048]{2,1,0:T(4,128)S(1)} collective-permute-done((f32[2,4,2048]{2,1,0:T(4,128)S(1)}, f32[2,4,2048]{2,1,0:T(4,128)S(1)}, u32[]{:S(2)}, u32[]{:S(2)}) %collective-permute-start.11) | collective-permute-done | bytes 65568 | tf_op jit(solution)/shard_map/ppermute | solution.py:70
  27.2 3.0 %collective-permute-done.12.refs_3_ = f32[2,4,2048]{2,1,0:T(4,128)S(1)} collective-permute-done((f32[2,4,2048]{2,1,0:T(4,128)S(1)}, f32[2,4,2048]{2,1,0:T(4,128)S(1)}, u32[]{:S(2)}, u32[]{:S(2)}) %collective-permute-start.12) | collective-permute-done | bytes 65568 | tf_op jit(solution)/shard_map/ppermute | solution.py:70
  30.3 0.1 join.1
  30.3 0.5 %collective-permute-start.13 = (f32[4,22528]{1,0:T(4,128)S(1)}, f32[4,22528]{1,0:T(4,128)S(1)}, u32[]{:S(2)}, u32[]{:S(2)}) collective-permute-start(f32[4,22528]{1,0:T(4,128)S(1)} %get-tuple-element.56), channel_id=1, source_target_pairs={{0,8},{8,0},{16,24},{24,16},{1,9},{9,1},{17,25},{25,17},{2,10},{10... | collective-permute-start | bytes 1081352 | tf_op jit(solution)/shard_map/ppermute | solution.py:70
  30.8 0.5 %collective-permute-start.14 = (f32[4,22528]{1,0:T(4,128)S(1)}, f32[4,22528]{1,0:T(4,128)S(1)}, u32[]{:S(2)}, u32[]{:S(2)}) collective-permute-start(f32[4,22528]{1,0:T(4,128)S(1)} %get-tuple-element.57), channel_id=1, source_target_pairs={{0,16},{8,24},{16,0},{24,8},{1,17},{9,25},{17,1},{25,9},{2,18},{10... | collective-permute-start | bytes 1081352 | tf_op jit(solution)/shard_map/ppermute | solution.py:70
  31.3 2.6 %collective-permute-start.15 = (f32[4,16384]{1,0:T(4,128)S(1)}, f32[4,16384]{1,0:T(4,128)S(1)}, u32[]{:S(2)}, u32[]{:S(2)}) collective-permute-start(f32[4,16384]{1,0:T(4,128)S(1)} %get-tuple-element.55.refs_8_), channel_id=1, source_target_pairs={{0,24},{8,16},{16,8},{24,0},{1,25},{9,17},{17,9},{25,1},{2,26},{10... | collective-permute-start | bytes 786440 | tf_op jit(solution)/shard_map/ppermute | solution.py:70
  33.9 9.1 %collective-permute-done.15.refs_11_ = f32[4,16384]{1,0:T(4,128)S(1)} collective-permute-done((f32[4,16384]{1,0:T(4,128)S(1)}, f32[4,16384]{1,0:T(4,128)S(1)}, u32[]{:S(2)}, u32[]{:S(2)}) %collective-permute-start.15) | collective-permute-done | bytes 262176 | tf_op jit(solution)/shard_map/ppermute | solution.py:70
  43.0 0.2 collective-permute-done.14.refs_10_
  43.2 2.0 %finish.1 = (f32[16,8192]{1,0:T(8,128)}, f32[4,65536]{1,0:T(4,128)}, f32[200,1024]{1,0:T(8,128)}, f32[64,200]{1,0:T(8,128)}) custom-call(s32[8]{0:T(128)S(4)} %get-tuple-element.33.refs_0_, f32[200,1024]{1,0:T(8,128)S(1)} %copy-done, f32[64,200]{1,0:T(8,128)S(1)} %bitcast.6, f32[64,1024]{1,0:T(8,128)S(1)} %bitcast.5, ...), custom_call_target="tpu_custom_call" | custom-call | tf_op jit(solution)/shard_map/finish/pallas_call | solution.py:50
  (16 shorter events, 0.1 us)
Async XLA Ops:
  0.6 13.3 %copy-start = (f32[200,1024]{1,0:T(8,128)S(1)}, f32[200,1024]{1,0:T(8,128)}, u32[]{:S(2)}) copy-start(f32[200,1024]{1,0:T(8,128)} %refs_1_.5) | copy-start | bytes 2457604
  0.6 13.3 %copy-start.2 = (f32[1,200,1024]{2,1,0:T(8,128)S(1)}, f32[1,200,1024]{2,1,0:T(8,128)}, u32[]{:S(2)}) copy-start(f32[1,200,1024]{2,1,0:T(8,128)} %refs_1_.4) | copy-start | bytes 2457604
  2.5 11.4 %copy-start.1 = (f32[1024,64]{0,1:T(8,128)S(1)}, f32[1024,64]{0,1:T(8,128)}, u32[]{:S(2)}) copy-start(f32[1024,64]{0,1:T(8,128)} %param.15) | copy-start | bytes 786436
  2.5 4.6 %collective-permute-start.3 = (f32[4,4,2048]{2,1,0:T(4,128)S(1)}, f32[4,4,2048]{2,1,0:T(4,128)S(1)}, u32[]{:S(2)}, u32[]{:S(2)}) collective-permute-start(f32[4,4,2048]{2,1,0:T(4,128)S(1)} %get-tuple-element.44), channel_id=1, source_target_pairs={{0,1},{1,0},{2,3},{3,2},{4,5},{5,4},{6,7},{7,6},{8,9},{9,8},{10,11... | collective-permute-start | bytes 393224 | tf_op jit(solution)/shard_map/ppermute | solution.py:70
  3.1 8.8 %collective-permute-start = (f32[16,2048]{1,0:T(8,128)S(1)}, f32[16,2048]{1,0:T(8,128)S(1)}, u32[]{:S(2)}, u32[]{:S(2)}) collective-permute-start(f32[16,2048]{1,0:T(8,128)S(1)} %get-tuple-element.39), channel_id=1, source_target_pairs={{0,8},{8,0},{16,24},{24,16},{1,9},{9,1},{17,25},{25,17},{2,10},{10... | collective-permute-start | bytes 393224 | tf_op jit(solution)/shard_map/ppermute | solution.py:70
  5.6 8.7 %collective-permute-start.1 = (f32[16,2048]{1,0:T(8,128)S(1)}, f32[16,2048]{1,0:T(8,128)S(1)}, u32[]{:S(2)}, u32[]{:S(2)}) collective-permute-start(f32[16,2048]{1,0:T(8,128)S(1)} %get-tuple-element.40), channel_id=1, source_target_pairs={{0,16},{8,24},{16,0},{24,8},{1,17},{9,25},{17,1},{25,9},{2,18},{10... | collective-permute-start | bytes 393224 | tf_op jit(solution)/shard_map/ppermute | solution.py:70
  7.1 7.2 %collective-permute-start.2 = (f32[16,2048]{1,0:T(8,128)S(1)}, f32[16,2048]{1,0:T(8,128)S(1)}, u32[]{:S(2)}, u32[]{:S(2)}) collective-permute-start(f32[16,2048]{1,0:T(8,128)S(1)} %get-tuple-element.41), channel_id=1, source_target_pairs={{0,24},{8,16},{16,8},{24,0},{1,25},{9,17},{17,9},{25,1},{2,26},{10... | collective-permute-start | bytes 393224 | tf_op jit(solution)/shard_map/ppermute | solution.py:70
  7.2 7.4 %collective-permute-start.4 = (f32[2,4,2048]{2,1,0:T(4,128)S(1)}, f32[2,4,2048]{2,1,0:T(4,128)S(1)}, u32[]{:S(2)}, u32[]{:S(2)}) collective-permute-start(f32[2,4,2048]{2,1,0:T(4,128)S(1)} %get-tuple-element.46), channel_id=1, source_target_pairs={{0,2},{1,3},{2,0},{3,1},{4,6},{5,7},{6,4},{7,5},{8,10},{9,11},{10,... | collective-permute-start | bytes 196616 | tf_op jit(solution)/shard_map/ppermute | solution.py:70
  9.3 7.0 %collective-permute-start.5 = (f32[2,4,2048]{2,1,0:T(4,128)S(1)}, f32[2,4,2048]{2,1,0:T(4,128)S(1)}, u32[]{:S(2)}, u32[]{:S(2)}) collective-permute-start(f32[2,4,2048]{2,1,0:T(4,128)S(1)} %get-tuple-element.47), channel_id=1, source_target_pairs={{0,4},{1,5},{2,6},{3,7},{4,0},{5,1},{6,2},{7,3},{8,12},{9,13},{10,... | collective-permute-start | bytes 196616 | tf_op jit(solution)/shard_map/ppermute | solution.py:70
  11.9 6.1 %collective-permute-start.6 = (f32[2,4,2048]{2,1,0:T(4,128)S(1)}, f32[2,4,2048]{2,1,0:T(4,128)S(1)}, u32[]{:S(2)}, u32[]{:S(2)}) collective-permute-start(f32[2,4,2048]{2,1,0:T(4,128)S(1)} %get-tuple-element.48), channel_id=1, source_target_pairs={{0,6},{1,7},{2,4},{3,5},{4,2},{5,3},{6,0},{7,1},{8,14},{9,15},{10,... | collective-permute-start | bytes 196616 | tf_op jit(solution)/shard_map/ppermute | solution.py:70
  14.5 6.8 %collective-permute-start.9 = (f32[4,4,2048]{2,1,0:T(4,128)S(1)}, f32[4,4,2048]{2,1,0:T(4,128)S(1)}, u32[]{:S(2)}, u32[]{:S(2)}) collective-permute-start(f32[4,4,2048]{2,1,0:T(4,128)S(1)} %get-tuple-element.50), channel_id=1, source_target_pairs={{0,1},{1,0},{2,3},{3,2},{4,5},{5,4},{6,7},{7,6},{8,9},{9,8},{10,11... | collective-permute-start | bytes 393224 | tf_op jit(solution)/shard_map/ppermute | solution.py:70
  18.2 12.1 %collective-permute-start.8 = (f32[384,128]{1,0:T(8,128)S(1)}, f32[384,128]{1,0:T(8,128)S(1)}, u32[]{:S(2)}, u32[]{:S(2)}) collective-permute-start(f32[384,128]{1,0:T(8,128)S(1)} %dense.1.refs_5_), channel_id=1, source_target_pairs={{0,16},{8,24},{16,0},{24,8},{1,17},{9,25},{17,1},{25,9},{2,18},{10... | collective-permute-start | bytes 589832 | tf_op jit(solution)/shard_map/ppermute | solution.py:70
  19.8 10.5 %collective-permute-start.7 = (f32[384,128]{1,0:T(8,128)S(1)}, f32[384,128]{1,0:T(8,128)S(1)}, u32[]{:S(2)}, u32[]{:S(2)}) collective-permute-start(f32[384,128]{1,0:T(8,128)S(1)} %dense.1.refs_5_), channel_id=1, source_target_pairs={{0,8},{8,0},{16,24},{24,16},{1,9},{9,1},{17,25},{25,17},{2,10},{10... | collective-permute-start | bytes 589832 | tf_op jit(solution)/shard_map/ppermute | solution.py:70
  21.3 4.5 %collective-permute-start.10 = (f32[2,4,2048]{2,1,0:T(4,128)S(1)}, f32[2,4,2048]{2,1,0:T(4,128)S(1)}, u32[]{:S(2)}, u32[]{:S(2)}) collective-permute-start(f32[2,4,2048]{2,1,0:T(4,128)S(1)} %get-tuple-element.52), channel_id=1, source_target_pairs={{0,2},{1,3},{2,0},{3,1},{4,6},{5,7},{6,4},{7,5},{8,10},{9,11},{10,... | collective-permute-start | bytes 196616 | tf_op jit(solution)/shard_map/ppermute | solution.py:70
  21.4 5.8 %collective-permute-start.11 = (f32[2,4,2048]{2,1,0:T(4,128)S(1)}, f32[2,4,2048]{2,1,0:T(4,128)S(1)}, u32[]{:S(2)}, u32[]{:S(2)}) collective-permute-start(f32[2,4,2048]{2,1,0:T(4,128)S(1)} %get-tuple-element.53), channel_id=1, source_target_pairs={{0,4},{1,5},{2,6},{3,7},{4,0},{5,1},{6,2},{7,3},{8,12},{9,13},{10,... | collective-permute-start | bytes 196616 | tf_op jit(solution)/shard_map/ppermute | solution.py:70
  24.2 6.1 %collective-permute-start.12 = (f32[2,4,2048]{2,1,0:T(4,128)S(1)}, f32[2,4,2048]{2,1,0:T(4,128)S(1)}, u32[]{:S(2)}, u32[]{:S(2)}) collective-permute-start(f32[2,4,2048]{2,1,0:T(4,128)S(1)} %get-tuple-element.54), channel_id=1, source_target_pairs={{0,6},{1,7},{2,4},{3,5},{4,2},{5,3},{6,0},{7,1},{8,14},{9,15},{10,... | collective-permute-start | bytes 196616 | tf_op jit(solution)/shard_map/ppermute | solution.py:70
  30.3 12.9 %copy-start.3 = (f32[200,64]{0,1:T(8,128)S(1)}, f32[200,64]{0,1:T(8,128)}, u32[]{:S(2)}) copy-start(f32[200,64]{0,1:T(8,128)} %param.14) | copy-start | bytes 153604
  30.3 12.6 %collective-permute-start.13 = (f32[4,22528]{1,0:T(4,128)S(1)}, f32[4,22528]{1,0:T(4,128)S(1)}, u32[]{:S(2)}, u32[]{:S(2)}) collective-permute-start(f32[4,22528]{1,0:T(4,128)S(1)} %get-tuple-element.56), channel_id=1, source_target_pairs={{0,8},{8,0},{16,24},{24,16},{1,9},{9,1},{17,25},{25,17},{2,10},{10... | collective-permute-start | bytes 1081352 | tf_op jit(solution)/shard_map/ppermute | solution.py:70
  30.8 12.3 %collective-permute-start.14 = (f32[4,22528]{1,0:T(4,128)S(1)}, f32[4,22528]{1,0:T(4,128)S(1)}, u32[]{:S(2)}, u32[]{:S(2)}) collective-permute-start(f32[4,22528]{1,0:T(4,128)S(1)} %get-tuple-element.57), channel_id=1, source_target_pairs={{0,16},{8,24},{16,0},{24,8},{1,17},{9,25},{17,1},{25,9},{2,18},{10... | collective-permute-start | bytes 1081352 | tf_op jit(solution)/shard_map/ppermute | solution.py:70
  31.3 11.6 %collective-permute-start.15 = (f32[4,16384]{1,0:T(4,128)S(1)}, f32[4,16384]{1,0:T(4,128)S(1)}, u32[]{:S(2)}, u32[]{:S(2)}) collective-permute-start(f32[4,16384]{1,0:T(4,128)S(1)} %get-tuple-element.55.refs_8_), channel_id=1, source_target_pairs={{0,24},{8,16},{16,8},{24,0},{1,25},{9,17},{17,9},{25,1},{2,26},{10... | collective-permute-start | bytes 786440 | tf_op jit(solution)/shard_map/ppermute | solution.py:70

commit v4 on v3

v4 whole, which is shorter than its diff:
```python
import functools

import jax
import jax.numpy as jnp
from jax import lax
from jax.experimental import pallas as pl
from jax.experimental.pallas import tpu as pltpu
from jax.sharding import PartitionSpec as P

outer_rate = 0.7
momentum_decay = 0.9
most_direct_chips = 8
f32 = jnp.float32
vmem_limit = 48 * 1024 * 1024

vmem = pl.BlockSpec(memory_space=pltpu.VMEM)
smem = pl.BlockSpec(memory_space=pltpu.SMEM)
anywhere = pl.BlockSpec(memory_space=pl.ANY)


def on_chip(x):
    return pltpu.with_memory_space_constraint(x, pltpu.VMEM)


def in_scalars(x):
    return pltpu.with_memory_space_constraint(x, pltpu.SMEM)


def in_hbm(x):
    return pltpu.with_memory_space_constraint(x, pltpu.HBM)


def kept(shape):
    return pltpu.VMEM(shape, f32)


def stored(shape):
    return jax.ShapeDtypeStruct(shape, f32)


def run(
    body, outs, operands, scalars=(), scratch=(), far=(), after=(), out_specs=None, name=None
):
    skip = len(after)

    def whole(*refs):
        body(*refs[skip:])

    return pl.pallas_call(
        whole,
        out_shape=list(outs),
        in_specs=[anywhere] * skip
        + [smem] * len(scalars)
        + [anywhere] * len(far)
        + [vmem] * len(operands),
        out_specs=out_specs or [vmem] * len(outs),
        scratch_shapes=list(scratch),
        compiler_params=pltpu.CompilerParams(vmem_limit_bytes=vmem_limit),
        name=name,
    )(
        *[on_chip(x) for x in after],
        *[in_scalars(x) for x in scalars],
        *[in_hbm(x) for x in far],
        *[on_chip(x) for x in operands],
    )


def swap(x, axis, count, mask):
    return lax.ppermute(x, axis, [(i, i ^ mask) for i in range(count)])


def place():
    position = lax.axis_index("own")
    return lax.axis_index("rep"), lax.shift_right_logical(position, 1), position & 1


def column(index, part):
    return pl.ds(pl.multiple_of(index * part, 128), part)


def tiles(rows, columns):
    return [
        (i, min(8, rows - i), j, min(128, columns - j))
        for i in range(0, rows, 8)
        for j in range(0, columns, 128)
    ]


def two_parts(x):
    high = x.astype(jnp.bfloat16)
    return high, (x - high.astype(f32)).astype(jnp.bfloat16)


def dot(a, b, contract):
    return lax.dot_general(a, b, (contract, ((), ())), preferred_element_type=f32)


def name_places(slots, owners, row_of, block_of, owned):
    blocks, owner_count = row_of.shape[0], owned.shape[0]

    def clear(i, carry):
        block_of[i] = 0
        return carry

    def clear_count(i, carry):
        owned[i] = 0
        return carry

    def name(u, carry):
        owner = owners[u]
        slot = owned[owner]
        row = owner * slots + slot
        row_of[u] = row
        block_of[row] = u
        owned[owner] = slot + 1
        return carry

    short = blocks <= 16
    lax.fori_loop(0, block_of.shape[0], clear, 0, unroll=short)
    lax.fori_loop(0, owner_count, clear_count, 0, unroll=short)
    lax.fori_loop(0, blocks, name, 0, unroll=short)


def start_body(groups, part, owners, anchor, inner, momentum, emb, inner_emb, basis_t, *refs):
    outs, (quarter, same, other, held), named, scratch = (
        refs[:groups],
        refs[groups : groups + 4],
        refs[groups + 4 : groups + 7],
        refs[groups + 7 :],
    )
    own, far, near, emb_far, emb_near, basis, factor, sem = scratch
    rep, chip, core = place()
    blocks, rank = quarter.shape[0], basis.shape[0]
    share = rank // groups
    moves = [pltpu.make_async_copy(owners, own, sem.at[2 * groups])]
    for k in range(groups):
        at = column(rep ^ k, part)
        moves.append(pltpu.make_async_copy(anchor.at[:, at], far.at[k], sem.at[k]))
        moves.append(pltpu.make_async_copy(inner.at[0, :, at], near.at[k], sem.at[groups + k]))
    for i, (a, b) in enumerate(
        ((emb, emb_far), (inner_emb.at[0], emb_near), (basis_t, basis), (momentum, held))
    ):
        moves.append(pltpu.make_async_copy(a, b, sem.at[2 * groups + 1 + i]))
    for move in moves:
        move.start()
    moves[0].wait()
    name_places(same.shape[1], own, *named)

    for k in range(groups):
        moves[2 * k + 1].wait()
        moves[2 * k + 2].wait()
        for t, (i, height, j, width) in enumerate(tiles(blocks, part)):
            rows, columns = slice(i, i + height), slice(j, j + width)
            outs[k][8 * t : 8 * t + height, :width] = far[k, rows, columns] - near[k, rows, columns]
        if k == 0:
            quarter[...] = far[0]
    for move in moves[2 * groups + 1 : 2 * groups + 4]:
        move.wait()
    high, low = two_parts(emb_far[...] - emb_near[...])
    basis_high, basis_low = two_parts(basis[...])
    both = dot(jnp.concatenate([basis_high, basis_low], axis=0), high, ((1,), (1,)))
    factor[...] = both[:rank] + (both[rank:] + dot(basis_high, low, ((1,), (1,))))
    skip = 8 * len(tiles(blocks, part))
    for k in range(groups):
        for t, (i, height, j, width) in enumerate(tiles(share, factor.shape[1])):
            rows = pl.ds(pl.multiple_of((rep ^ k) * share + i, 8), height)
            outs[k][skip + 8 * t : skip + 8 * t + height, :width] = factor[rows, j : j + width]

    moves[2 * groups + 4].wait()

    def take(to, carry):
        for o, out in enumerate((same, other)):
            piece = 2 * to + (core ^ o)
            out[to] = held[:, column(piece * groups + rep, part)]
        return carry

    lax.fori_loop(0, same.shape[0], take, 0, unroll=same.shape[0] <= 8)


def mean_body(groups, direct, block_of, *refs):
    parts, (mean, shared, *outs) = refs[:groups], refs[groups:]
    _, here, core = place()
    dense_tiles = tiles(*mean.shape)
    for t, (i, height, j, width) in enumerate(dense_tiles):
        at = slice(8 * t, 8 * t + height)
        total = parts[0][at, :width]
        for ref in parts[1:]:
            total = total + ref[at, :width]
        mean[i : i + height, j : j + width] = total / groups
    at = slice(8 * len(dense_tiles), parts[0].shape[0])
    total = parts[0][at, :]
    for ref in parts[1:]:
        total = total + ref[at, :]
    shared[...] = total / groups
    slots = outs[0].shape[-2]

    def fill(k, carry):
        for o in range(2):
            owner = 2 * (here ^ k if direct else k) + (core ^ o)
            for s in range(slots):
                row = mean[pl.ds(block_of[owner * slots + s], 1), :]
                if direct:
                    outs[k][o, pl.ds(s, 1), :] = row
                else:
                    outs[0][k, o, pl.ds(s, 1), :] = row
        return carry

    if direct:
        for k in range(len(outs)):
            fill(k, 0)
    else:
        lax.fori_loop(0, outs[0].shape[0], fill, 0)


def pack_body(direct, same, other, *outs):
    _, chip, _ = place()
    if direct:
        for k, out in enumerate(outs):
            out[0] = same[chip ^ k]
            out[1] = other[chip ^ k]
    else:
        outs[0][:, 0] = same[...]
        outs[0][:, 1] = other[...]


def other_body(direct, *refs):
    *received, out = refs
    if direct:
        for k, ref in enumerate(received):
            out[k] = ref[1]
    else:
        out[...] = received[0][:, 1]


def join_body(direct, *refs):
    *received, crossed, out = refs
    chips, _, part = crossed.shape

    def fill(k, carry):
        out[:, column(2 * k, part)] = received[k][0] if direct else received[0][k, 0]
        out[:, column(2 * k + 1, part)] = crossed[k]
        return carry

    if direct:
        for k in range(chips):
            fill(k, 0)
    else:
        lax.fori_loop(0, chips, fill, 0)


def dense_body(direct, row_of, quarter, mean, shared, *refs):
    *received, out, rows, work = refs
    _, here, core = place()
    slots = received[0].shape[-2]
    blocks = mean.shape[0]
    if direct:
        for k, ref in enumerate(received):
            rows[k] = ref[...]
        table = rows
    else:
        table = received[0]

    def update(block, carry):
        row = row_of[block]
        owner = row // slots
        chip = (owner // 2) ^ here if direct else owner // 2
        momentum = table[chip, (owner % 2) ^ core, pl.ds(row % slots, 1), :]
        mean_row = mean[pl.ds(block, 1), :]
        new_momentum = momentum_decay * momentum + mean_row
        work[pl.ds(block, 1), :] = quarter[pl.ds(block, 1), :] - outer_rate * (
            mean_row + momentum_decay * new_momentum
        )
        return carry

    lax.fori_loop(0, blocks, update, 0, unroll=blocks <= 16)
    dense_tiles = tiles(*work.shape)
    for t, (i, height, j, width) in enumerate(dense_tiles):
        out[8 * t : 8 * t + height, :width] = work[i : i + height, j : j + width]
    out[8 * len(dense_tiles) :, :] = shared[...]


def finish_body(part, anchor, momentum_t, basis_t, *refs):
    *parts, result0, result1, result2, mean, sem, new_dense, new_emb, new_momentum_t = refs
    copies = [
        pltpu.make_async_copy(ref, result, sem.at[i])
        for i, (ref, result) in enumerate(
            ((new_dense, result0), (new_emb, result1), (new_momentum_t, result2))
        )
    ]
    rep, _, _ = place()
    blocks, (rank, rows) = new_dense.shape[0], mean.shape
    share = rank // len(parts)
    dense_tiles = tiles(blocks, part)
    for k, ref in enumerate(parts):
        for t, (i, height, j, width) in enumerate(dense_tiles):
            at = pl.multiple_of((rep ^ k) * part + j, 128)
            new_dense[i : i + height, pl.ds(at, width)] = ref[8 * t : 8 * t + height, :width]
        for t, (i, height, j, width) in enumerate(tiles(share, rows)):
            at = 8 * (len(dense_tiles) + t)
            mean[pl.ds(pl.multiple_of((rep ^ k) * share + i, 8), height), j : j + width] = ref[
                at : at + height, :width
            ]
    copies[0].start()

    moved = momentum_decay * momentum_t[...] + mean[...]
    new_momentum_t[...] = moved
    copies[2].start()
    high, low = two_parts(mean[...] + momentum_decay * moved)
    basis_high, basis_low = two_parts(basis_t[...])
    back = dot(
        jnp.concatenate([high, low, high], axis=0),
        jnp.concatenate([basis_high, basis_high, basis_low], axis=0),
        ((0,), (0,)),
    )
    new_emb[...] = anchor[...] - outer_rate * back
    copies[1].start()
    for copy in copies:
        copy.wait()


def finish_momentum_body(part, direct, owned, momentum, *refs):
    *gradient, result, made, sem = refs
    rep, here, core = place()
    slots, groups = momentum.shape[0], len(gradient)
    pieces = momentum.shape[1] // part // groups
    live = lax.broadcasted_iota(jnp.int32, (slots, part), 0) < owned[here * 2 + core]

    def fill(i, carry):
        k, o = (i >> 1, i & 1)
        piece = 2 * (here ^ k if direct else k) + (core ^ o)
        for g, ref in enumerate(gradient):
            at = column(piece * groups + (rep ^ g), part)
            rows = momentum_decay * momentum[:, at] + ref[:, column(i, part)]
            made[:, at] = jnp.where(live, rows, 0.0)
        return carry

    lax.fori_loop(0, pieces, fill, 0, unroll=pieces <= 16)
    copy = pltpu.make_async_copy(made, result, sem)
    copy.start()
    copy.wait()


def over_chips(outs, direct, owner_count):
    if direct:
        return [outs[0]] + [swap(outs[k], "own", owner_count, 2 * k) for k in range(1, len(outs))]
    groups = [list(range(core, owner_count, 2)) for core in range(2)]
    return [
        lax.all_to_all(
            outs[0], "own", split_axis=0, concat_axis=0, axis_index_groups=groups, tiled=True
        )
    ]


def per_device(
    owners, inner_dense, anchor_dense, momentum_dense, inner_emb, anchor_emb, momentum_emb, basis
):
    owner_count = lax.axis_size("own")
    groups = lax.axis_size("rep")
    chips = owner_count // 2
    direct = chips <= most_direct_chips
    slot_count = momentum_dense.shape[0]
    blocks, piece_len = anchor_dense.shape
    part = piece_len // groups
    rows, rank = momentum_emb.shape
    basis_t = basis.T
    chunk = (chips, slot_count, part)
    table = (chips, 2, slot_count, part)
    message = (8 * (len(tiles(blocks, part)) + len(tiles(rank // groups, rows))), 128)
    parted = [kept(table[1:])] * chips if direct else [kept(table)]

    *parts, quarter, same, other, momentum, row_of, block_of, owned = run(
        functools.partial(start_body, groups, part),
        [kept(message)] * groups
        + [kept((blocks, part))]
        + [kept(chunk)] * 2
        + [kept(momentum_dense.shape)]
        + [pltpu.SMEM((n,), jnp.int32) for n in (blocks, owner_count * slot_count, owner_count)],
        [],
        far=[
            owners[:, 0],
            anchor_dense,
            inner_dense,
            momentum_dense,
            anchor_emb,
            inner_emb,
            basis_t,
        ],
        out_specs=[vmem] * (groups + 4) + [smem] * 3,
        scratch=[
            pltpu.SMEM((blocks,), jnp.int32),
            pltpu.VMEM((groups, blocks, part), f32),
            pltpu.VMEM((groups, blocks, part), f32),
            pltpu.VMEM(anchor_emb.shape, f32),
            pltpu.VMEM(anchor_emb.shape, f32),
            pltpu.VMEM(basis_t.shape, f32),
            pltpu.VMEM((rank, rows), f32),
            pltpu.SemaphoreType.DMA((2 * groups + 5,)),
        ],
        name="start",
    )
    parts = [parts[0]] + [swap(parts[k], "rep", groups, k) for k in range(1, groups)]

    other = swap(other, "own", owner_count, 1)
    packed = run(functools.partial(pack_body, direct), parted, [same, other], name="pack")
    momentum_rows = over_chips(packed, direct, owner_count)

    mean, shared, *sent = run(
        functools.partial(mean_body, groups, direct),
        [kept((blocks, part)), kept((8 * len(tiles(rank // groups, rows)), 128))] + parted,
        parts,
        [block_of],
        name="mean",
    )
    gradient_rows = over_chips(sent, direct, owner_count)
    (other,) = run(
        functools.partial(other_body, direct),
        [kept(chunk)],
        gradient_rows,
        name="other",
    )
    crossed = swap(other, "own", owner_count, 1)

    (dense,) = run(
        functools.partial(dense_body, direct),
        [kept(message)],
        [quarter, mean, shared, *momentum_rows],
        [row_of],
        [
            pltpu.VMEM(table if direct else (8, 128), f32),
            pltpu.VMEM((blocks, part), f32),
        ],
        name="dense",
    )
    dense = [dense] + [swap(dense, "rep", groups, k) for k in range(1, groups)]

    (gradient,) = run(
        functools.partial(join_body, direct),
        [kept((slot_count, 2 * chips * part))],
        [*gradient_rows, crossed],
        after=dense[1:],
        name="join",
    )
    gradient = [gradient] + [swap(gradient, "rep", groups, k) for k in range(1, groups)]

    shapes = [anchor_dense.shape, anchor_emb.shape, (rank, rows)]
    new_dense, new_emb, new_momentum_t = run(
        functools.partial(finish_body, part),
        [stored(shape) for shape in shapes],
        [anchor_emb, momentum_emb.T, basis_t, *dense],
        out_specs=[anywhere] * 3,
        scratch=[pltpu.VMEM((rank, rows), f32), pltpu.SemaphoreType.DMA((3,))]
        + [pltpu.VMEM(shape, f32) for shape in shapes],
        name="finish",
    )
    (new_momentum_dense,) = run(
        functools.partial(finish_momentum_body, part, direct),
        [stored(momentum_dense.shape)],
        [momentum, *gradient],
        [owned],
        out_specs=[anywhere],
        scratch=[pltpu.VMEM(momentum_dense.shape, f32), pltpu.SemaphoreType.DMA],
        name="finish_momentum",
    )
    return (new_dense, new_momentum_dense, new_emb, new_momentum_t.T)


def solution(mesh):
    placed = (
        P(),
        P("rep", None, "own"),
        P(None, "own"),
        P("own", None),
        P("rep", "own", None),
        P("own", None),
        P("own", None),
        P(),
    )
    return jax.shard_map(
        per_device,
        mesh=mesh,
        in_specs=placed,
        out_specs=(P(None, "own"), P("own", None), P("own", None), P("own", None)),
        check_vma=False,
    )
```

time: 45.3 us -> 43.9 us (0.969)
  waiting for transfers between devices: 17.2 us -> 14.1 us
  starting transfers between devices: 22.5 us -> 23.4 us
  Pallas kernels: 4.71 us -> 5.46 us
    ppermute x16 -> x17, waiting for transfers between devices: 17.2 us -> 14.1 us  [swap(): return lax.ppermute(x, axis, [(i, i ^ mask) for i in range(count)])]
    ppermute x16 -> x17, starting transfers between devices: 22.5 us -> 23.4 us  [swap(): return lax.ppermute(x, axis, [(i, i ^ mask) for i in range(count)])]
    pallas_call x8, Pallas kernels: 4.71 us -> 5.46 us  [run(): pl.pallas_call(whole, out_shape=list(outs), in_specs=[anywhere] * skip +...]
  transfers between devices with their start and end apart: 16 -> 17, of which waited for: 6 -> 9; matrix products, arithmetic and copies ran while one was open for 0% -> 0% of each run, Pallas kernels for 2% -> 4%
where the time goes in v4:
time: 43.9 us; the launch traced here: 43.7 us
  starting transfers between devices  23.4 us (53%)
  waiting for transfers between devices  14.1 us (32%)
  Pallas kernels  5.46 us (12%)
  between operations  0.72 us (2%)
    ppermute x17, starting transfers between devices, swap(): return lax.ppermute(x, axis, [(i, i ^ mask) for i in range(count)])  23.4 us
    ppermute x17, waiting for transfers between devices, swap(): return lax.ppermute(x, axis, [(i, i ^ mask) for i in range(count)])  14.1 us
    pallas_call x8, Pallas kernels, run(): pl.pallas_call(whole, out_shape=list(outs), in_specs=[anywhere] * skip +...  5.46 us
  transfers between devices with their start and end apart: 17, of which 9 were waited for; matrix products, arithmetic and copies ran while one was open for 0% of the time, Pallas kernels for 4%

profile of v4, /device:TPU:0, one launch (start us, length us, event | category | flops | bytes accessed | tf_op | source)
XLA Modules:
  0.0 43.7 jit_solution(1750418217637372420)
XLA Ops:
  0.6 2.4 %start.1 = (f32[288,128]{1,0:T(8,128)S(1)}, f32[288,128]{1,0:T(8,128)S(1)}, f32[288,128]{1,0:T(8,128)S(1)}, f32[288,128]{1,0:T(8,128)S(1)}, f32[16,2048]{1,0:T(8...) custom-call(s32[16]{0:T(128)} %bitcast.7, ...), custom_call_target="tpu_custom_call" | custom-call | tf_op jit(solution)/shard_map/start/pallas_call | solution.py:49
  3.1 0.5 %collective-permute-start.3 = (f32[4,4,2048]{2,1,0:T(4,128)S(1)}, f32[4,4,2048]{2,1,0:T(4,128)S(1)}, u32[]{:S(2)}, u32[]{:S(2)}) collective-permute-start(f32[4,4,2048]{2,1,0:T(4,128)S(1)} %get-tuple-element.38), channel_id=1, source_target_pairs={{0,1},{1,0},{2,3},{3,2},{4,5},{5,4},{6,7},{7,6},{8,9},{9,8},{10,11... | collective-permute-start | bytes 393224 | tf_op jit(solution)/shard_map/ppermute | solution.py:69
  3.6 2.6 %collective-permute-start = (f32[288,128]{1,0:T(8,128)S(1)}, f32[288,128]{1,0:T(8,128)S(1)}, u32[]{:S(2)}, u32[]{:S(2)}) collective-permute-start(f32[288,128]{1,0:T(8,128)S(1)} %get-tuple-element.32), channel_id=1, source_target_pairs={{0,8},{8,0},{16,24},{24,16},{1,9},{9,1},{17,25},{25,17},{2,10},{10... | collective-permute-start | bytes 442376 | tf_op jit(solution)/shard_map/ppermute | solution.py:69
  6.1 1.5 %collective-permute-start.1 = (f32[288,128]{1,0:T(8,128)S(1)}, f32[288,128]{1,0:T(8,128)S(1)}, u32[]{:S(2)}, u32[]{:S(2)}) collective-permute-start(f32[288,128]{1,0:T(8,128)S(1)} %get-tuple-element.33), channel_id=1, source_target_pairs={{0,16},{8,24},{16,0},{24,8},{1,17},{9,25},{17,1},{25,9},{2,18},{10... | collective-permute-start | bytes 442376 | tf_op jit(solution)/shard_map/ppermute | solution.py:69
  7.7 0.0 collective-permute-start.2
  7.7 2.1 %collective-permute-start.4 = (f32[2,4,2048]{2,1,0:T(4,128)S(1)}, f32[2,4,2048]{2,1,0:T(4,128)S(1)}, u32[]{:S(2)}, u32[]{:S(2)}) collective-permute-start(f32[2,4,2048]{2,1,0:T(4,128)S(1)} %get-tuple-element.40), channel_id=1, source_target_pairs={{0,2},{1,3},{2,0},{3,1},{4,6},{5,7},{6,4},{7,5},{8,10},{9,11},{10,... | collective-permute-start | bytes 196616 | tf_op jit(solution)/shard_map/ppermute | solution.py:69
  9.8 2.6 %collective-permute-start.5 = (f32[2,4,2048]{2,1,0:T(4,128)S(1)}, f32[2,4,2048]{2,1,0:T(4,128)S(1)}, u32[]{:S(2)}, u32[]{:S(2)}) collective-permute-start(f32[2,4,2048]{2,1,0:T(4,128)S(1)} %get-tuple-element.41), channel_id=1, source_target_pairs={{0,4},{1,5},{2,6},{3,7},{4,0},{5,1},{6,2},{7,3},{8,12},{9,13},{10,... | collective-permute-start | bytes 196616 | tf_op jit(solution)/shard_map/ppermute | solution.py:69
  12.4 2.5 %collective-permute-start.6 = (f32[2,4,2048]{2,1,0:T(4,128)S(1)}, f32[2,4,2048]{2,1,0:T(4,128)S(1)}, u32[]{:S(2)}, u32[]{:S(2)}) collective-permute-start(f32[2,4,2048]{2,1,0:T(4,128)S(1)} %get-tuple-element.42), channel_id=1, source_target_pairs={{0,6},{1,7},{2,4},{3,5},{4,2},{5,3},{6,0},{7,1},{8,14},{9,15},{10,... | collective-permute-start | bytes 196616 | tf_op jit(solution)/shard_map/ppermute | solution.py:69
  14.9 0.3 collective-permute-done.1.refs_3_
  15.2 0.1 mean.1
  15.3 1.6 %collective-permute-start.10 = (f32[2,4,2048]{2,1,0:T(4,128)S(1)}, f32[2,4,2048]{2,1,0:T(4,128)S(1)}, u32[]{:S(2)}, u32[]{:S(2)}) collective-permute-start(f32[2,4,2048]{2,1,0:T(4,128)S(1)} %get-tuple-element.47), channel_id=1, source_target_pairs={{0,2},{1,3},{2,0},{3,1},{4,6},{5,7},{6,4},{7,5},{8,10},{9,11},{10,... | collective-permute-start | bytes 196616 | tf_op jit(solution)/shard_map/ppermute | solution.py:69
  17.0 2.6 %collective-permute-start.11 = (f32[2,4,2048]{2,1,0:T(4,128)S(1)}, f32[2,4,2048]{2,1,0:T(4,128)S(1)}, u32[]{:S(2)}, u32[]{:S(2)}) collective-permute-start(f32[2,4,2048]{2,1,0:T(4,128)S(1)} %get-tuple-element.48), channel_id=1, source_target_pairs={{0,4},{1,5},{2,6},{3,7},{4,0},{5,1},{6,2},{7,3},{8,12},{9,13},{10,... | collective-permute-start | bytes 196616 | tf_op jit(solution)/shard_map/ppermute | solution.py:69
  19.6 0.2 collective-permute-start.12
  19.8 0.2 dense.1.refs_3_
  20.0 0.0 copy-start
  20.0 2.2 %collective-permute-start.9 = (f32[288,128]{1,0:T(8,128)S(1)}, f32[288,128]{1,0:T(8,128)S(1)}, u32[]{:S(2)}, u32[]{:S(2)}) collective-permute-start(f32[288,128]{1,0:T(8,128)S(1)} %dense.1.refs_3_), channel_id=1, source_target_pairs={{0,24},{8,16},{16,8},{24,0},{1,25},{9,17},{17,9},{25,1},{2,26},{10... | collective-permute-start | bytes 442376 | tf_op jit(solution)/shard_map/ppermute | solution.py:69
  22.2 0.6 %collective-permute-start.8 = (f32[288,128]{1,0:T(8,128)S(1)}, f32[288,128]{1,0:T(8,128)S(1)}, u32[]{:S(2)}, u32[]{:S(2)}) collective-permute-start(f32[288,128]{1,0:T(8,128)S(1)} %dense.1.refs_3_), channel_id=1, source_target_pairs={{0,16},{8,24},{16,0},{24,8},{1,17},{9,25},{17,1},{25,9},{2,18},{10... | collective-permute-start | bytes 442376 | tf_op jit(solution)/shard_map/ppermute | solution.py:69
  22.8 0.8 %collective-permute-start.7 = (f32[288,128]{1,0:T(8,128)S(1)}, f32[288,128]{1,0:T(8,128)S(1)}, u32[]{:S(2)}, u32[]{:S(2)}) collective-permute-start(f32[288,128]{1,0:T(8,128)S(1)} %dense.1.refs_3_), channel_id=1, source_target_pairs={{0,8},{8,0},{16,24},{24,16},{1,9},{9,1},{17,25},{25,17},{2,10},{10... | collective-permute-start | bytes 442376 | tf_op jit(solution)/shard_map/ppermute | solution.py:69
  23.6 0.2 collective-permute-done.11.refs_2_.refs_5_
  23.8 1.8 %collective-permute-done.12.refs_3_.refs_6_ = f32[2,4,2048]{2,1,0:T(4,128)S(1)} collective-permute-done((f32[2,4,2048]{2,1,0:T(4,128)S(1)}, f32[2,4,2048]{2,1,0:T(4,128)S(1)}, u32[]{:S(2)}, u32[]{:S(2)}) %collective-permute-start.12) | collective-permute-done | bytes 65568 | tf_op jit(solution)/shard_map/ppermute | solution.py:69
  25.7 0.1 collective-permute-start.13
  25.7 1.3 %collective-permute-done.13.refs_7_ = f32[4,4,2048]{2,1,0:T(4,128)S(1)} collective-permute-done((f32[4,4,2048]{2,1,0:T(4,128)S(1)}, f32[4,4,2048]{2,1,0:T(4,128)S(1)}, u32[]{:S(2)}, u32[]{:S(2)}) %collective-permute-start.13) | collective-permute-done | bytes 131104 | tf_op jit(solution)/shard_map/ppermute | solution.py:69
  27.1 0.1 collective-permute-done.9.refs_6_.refs_2_
  27.1 1.5 %collective-permute-done.8.refs_5_.refs_1_ = f32[288,128]{1,0:T(8,128)S(1)} collective-permute-done((f32[288,128]{1,0:T(8,128)S(1)}, f32[288,128]{1,0:T(8,128)S(1)}, u32[]{:S(2)}, u32[]{:S(2)}) %collective-permute-start.8) | collective-permute-done | bytes 147488 | tf_op jit(solution)/shard_map/ppermute | solution.py:69
  28.6 1.6 %collective-permute-start.16 = (f32[4,16384]{1,0:T(4,128)S(1)}, f32[4,16384]{1,0:T(4,128)S(1)}, u32[]{:S(2)}, u32[]{:S(2)}) collective-permute-start(f32[4,16384]{1,0:T(4,128)S(1)} %join.1.refs_2_), channel_id=1, source_target_pairs={{0,24},{8,16},{16,8},{24,0},{1,25},{9,17},{17,9},{25,1},{2,26},{10... | collective-permute-start | bytes 786440 | tf_op jit(solution)/shard_map/ppermute | solution.py:69
  30.2 1.4 %collective-permute-start.15 = (f32[4,16384]{1,0:T(4,128)S(1)}, f32[4,16384]{1,0:T(4,128)S(1)}, u32[]{:S(2)}, u32[]{:S(2)}) collective-permute-start(f32[4,16384]{1,0:T(4,128)S(1)} %join.1.refs_2_), channel_id=1, source_target_pairs={{0,16},{8,24},{16,0},{24,8},{1,17},{9,25},{17,1},{25,9},{2,18},{10... | collective-permute-start | bytes 786440 | tf_op jit(solution)/shard_map/ppermute | solution.py:69
  31.6 0.6 %collective-permute-start.14 = (f32[4,16384]{1,0:T(4,128)S(1)}, f32[4,16384]{1,0:T(4,128)S(1)}, u32[]{:S(2)}, u32[]{:S(2)}) collective-permute-start(f32[4,16384]{1,0:T(4,128)S(1)} %join.1.refs_2_), channel_id=1, source_target_pairs={{0,8},{8,0},{16,24},{24,16},{1,9},{9,1},{17,25},{25,17},{2,10},{10... | collective-permute-start | bytes 786440 | tf_op jit(solution)/shard_map/ppermute | solution.py:69
  32.2 1.4 %finish.1 = (f32[16,8192]{1,0:T(8,128)}, f32[200,1024]{1,0:T(8,128)}, f32[64,200]{1,0:T(8,128)}) custom-call(f32[200,1024]{1,0:T(8,128)S(1)} %copy-done, f32[64,200]{1,0:T(8,128)S(1)} %bitcast.6, f32[64,1024]{1,0:T(8,128)S(1)} %bitcast.5, f32[288,128]{1,0:T(8,128)S(1)} %dense.1.refs_3_, f32[288,128]{1,0:T(8,128)S(1)} %collective-permute-done.7.refs_4_.refs_0_, ...), custom_call_target="tpu_custom_call" | custom-call | tf_op jit(solution)/shard_map/finish/pallas_call | solution.py:49
  33.6 5.2 %collective-permute-done.16.refs_5_ = f32[4,16384]{1,0:T(4,128)S(1)} collective-permute-done((f32[4,16384]{1,0:T(4,128)S(1)}, f32[4,16384]{1,0:T(4,128)S(1)}, u32[]{:S(2)}, u32[]{:S(2)}) %collective-permute-start.16) | collective-permute-done | bytes 262176 | tf_op jit(solution)/shard_map/ppermute | solution.py:69
  38.9 3.3 %collective-permute-done.15.refs_4_ = f32[4,16384]{1,0:T(4,128)S(1)} collective-permute-done((f32[4,16384]{1,0:T(4,128)S(1)}, f32[4,16384]{1,0:T(4,128)S(1)}, u32[]{:S(2)}, u32[]{:S(2)}) %collective-permute-start.15) | collective-permute-done | bytes 262176 | tf_op jit(solution)/shard_map/ppermute | solution.py:69
  42.1 0.4 collective-permute-done.14.refs_3_
  42.5 1.2 %finish_momentum.1 = f32[4,65536]{1,0:T(4,128)} custom-call(s32[8]{0:T(128)S(4)} %get-tuple-element.44.refs_0_, f32[4,65536]{1,0:T(4,128)S(1)} %get-tuple-element.45.refs_1_, f32[4,16384]{1,0:T(4,128)S(1)} %join.1.refs_2_, f32[4,16384]{1,0:T(4,128)S(1)} %collective-permute-done.14.refs_3_, f32[4,16384]{1,0:T(4,128)S(1)} %collective-permute-done.15.refs_4_, ...), custom_call_target="tpu_custom_call" | custom-call | tf_op jit(solution)/shard_map/finish_momentum/pallas_call | solution.py:49
  (16 shorter events, 0.1 us)
Async XLA Ops:
  3.1 4.6 %collective-permute-start.3 = (f32[4,4,2048]{2,1,0:T(4,128)S(1)}, f32[4,4,2048]{2,1,0:T(4,128)S(1)}, u32[]{:S(2)}, u32[]{:S(2)}) collective-permute-start(f32[4,4,2048]{2,1,0:T(4,128)S(1)} %get-tuple-element.38), channel_id=1, source_target_pairs={{0,1},{1,0},{2,3},{3,2},{4,5},{5,4},{6,7},{7,6},{8,9},{9,8},{10,11... | collective-permute-start | bytes 393224 | tf_op jit(solution)/shard_map/ppermute | solution.py:69
  3.6 8.8 %collective-permute-start = (f32[288,128]{1,0:T(8,128)S(1)}, f32[288,128]{1,0:T(8,128)S(1)}, u32[]{:S(2)}, u32[]{:S(2)}) collective-permute-start(f32[288,128]{1,0:T(8,128)S(1)} %get-tuple-element.32), channel_id=1, source_target_pairs={{0,8},{8,0},{16,24},{24,16},{1,9},{9,1},{17,25},{25,17},{2,10},{10... | collective-permute-start | bytes 442376 | tf_op jit(solution)/shard_map/ppermute | solution.py:69
  6.1 9.1 %collective-permute-start.1 = (f32[288,128]{1,0:T(8,128)S(1)}, f32[288,128]{1,0:T(8,128)S(1)}, u32[]{:S(2)}, u32[]{:S(2)}) collective-permute-start(f32[288,128]{1,0:T(8,128)S(1)} %get-tuple-element.33), channel_id=1, source_target_pairs={{0,16},{8,24},{16,0},{24,8},{1,17},{9,25},{17,1},{25,9},{2,18},{10... | collective-permute-start | bytes 442376 | tf_op jit(solution)/shard_map/ppermute | solution.py:69
  7.7 7.6 %collective-permute-start.2 = (f32[288,128]{1,0:T(8,128)S(1)}, f32[288,128]{1,0:T(8,128)S(1)}, u32[]{:S(2)}, u32[]{:S(2)}) collective-permute-start(f32[288,128]{1,0:T(8,128)S(1)} %get-tuple-element.34), channel_id=1, source_target_pairs={{0,24},{8,16},{16,8},{24,0},{1,25},{9,17},{17,9},{25,1},{2,26},{10... | collective-permute-start | bytes 442376 | tf_op jit(solution)/shard_map/ppermute | solution.py:69
  7.7 11.9 %collective-permute-start.4 = (f32[2,4,2048]{2,1,0:T(4,128)S(1)}, f32[2,4,2048]{2,1,0:T(4,128)S(1)}, u32[]{:S(2)}, u32[]{:S(2)}) collective-permute-start(f32[2,4,2048]{2,1,0:T(4,128)S(1)} %get-tuple-element.40), channel_id=1, source_target_pairs={{0,2},{1,3},{2,0},{3,1},{4,6},{5,7},{6,4},{7,5},{8,10},{9,11},{10,... | collective-permute-start | bytes 196616 | tf_op jit(solution)/shard_map/ppermute | solution.py:69
  9.8 10.0 %collective-permute-start.5 = (f32[2,4,2048]{2,1,0:T(4,128)S(1)}, f32[2,4,2048]{2,1,0:T(4,128)S(1)}, u32[]{:S(2)}, u32[]{:S(2)}) collective-permute-start(f32[2,4,2048]{2,1,0:T(4,128)S(1)} %get-tuple-element.41), channel_id=1, source_target_pairs={{0,4},{1,5},{2,6},{3,7},{4,0},{5,1},{6,2},{7,3},{8,12},{9,13},{10,... | collective-permute-start | bytes 196616 | tf_op jit(solution)/shard_map/ppermute | solution.py:69
  12.4 7.4 %collective-permute-start.6 = (f32[2,4,2048]{2,1,0:T(4,128)S(1)}, f32[2,4,2048]{2,1,0:T(4,128)S(1)}, u32[]{:S(2)}, u32[]{:S(2)}) collective-permute-start(f32[2,4,2048]{2,1,0:T(4,128)S(1)} %get-tuple-element.42), channel_id=1, source_target_pairs={{0,6},{1,7},{2,4},{3,5},{4,2},{5,3},{6,0},{7,1},{8,14},{9,15},{10,... | collective-permute-start | bytes 196616 | tf_op jit(solution)/shard_map/ppermute | solution.py:69
  15.3 7.5 %collective-permute-start.10 = (f32[2,4,2048]{2,1,0:T(4,128)S(1)}, f32[2,4,2048]{2,1,0:T(4,128)S(1)}, u32[]{:S(2)}, u32[]{:S(2)}) collective-permute-start(f32[2,4,2048]{2,1,0:T(4,128)S(1)} %get-tuple-element.47), channel_id=1, source_target_pairs={{0,2},{1,3},{2,0},{3,1},{4,6},{5,7},{6,4},{7,5},{8,10},{9,11},{10,... | collective-permute-start | bytes 196616 | tf_op jit(solution)/shard_map/ppermute | solution.py:69
  17.0 6.9 %collective-permute-start.11 = (f32[2,4,2048]{2,1,0:T(4,128)S(1)}, f32[2,4,2048]{2,1,0:T(4,128)S(1)}, u32[]{:S(2)}, u32[]{:S(2)}) collective-permute-start(f32[2,4,2048]{2,1,0:T(4,128)S(1)} %get-tuple-element.48), channel_id=1, source_target_pairs={{0,4},{1,5},{2,6},{3,7},{4,0},{5,1},{6,2},{7,3},{8,12},{9,13},{10,... | collective-permute-start | bytes 196616 | tf_op jit(solution)/shard_map/ppermute | solution.py:69
  19.6 6.1 %collective-permute-start.12 = (f32[2,4,2048]{2,1,0:T(4,128)S(1)}, f32[2,4,2048]{2,1,0:T(4,128)S(1)}, u32[]{:S(2)}, u32[]{:S(2)}) collective-permute-start(f32[2,4,2048]{2,1,0:T(4,128)S(1)} %get-tuple-element.49), channel_id=1, source_target_pairs={{0,6},{1,7},{2,4},{3,5},{4,2},{5,3},{6,0},{7,1},{8,14},{9,15},{10,... | collective-permute-start | bytes 196616 | tf_op jit(solution)/shard_map/ppermute | solution.py:69
  20.0 12.2 %copy-start = (f32[200,1024]{1,0:T(8,128)S(1)}, f32[200,1024]{1,0:T(8,128)}, u32[]{:S(2)}) copy-start(f32[200,1024]{1,0:T(8,128)} %refs_0_.1) | copy-start | bytes 2457604
  20.0 7.1 %collective-permute-start.9 = (f32[288,128]{1,0:T(8,128)S(1)}, f32[288,128]{1,0:T(8,128)S(1)}, u32[]{:S(2)}, u32[]{:S(2)}) collective-permute-start(f32[288,128]{1,0:T(8,128)S(1)} %dense.1.refs_3_), channel_id=1, source_target_pairs={{0,24},{8,16},{16,8},{24,0},{1,25},{9,17},{17,9},{25,1},{2,26},{10... | collective-permute-start | bytes 442376 | tf_op jit(solution)/shard_map/ppermute | solution.py:69
  22.2 6.4 %collective-permute-start.8 = (f32[288,128]{1,0:T(8,128)S(1)}, f32[288,128]{1,0:T(8,128)S(1)}, u32[]{:S(2)}, u32[]{:S(2)}) collective-permute-start(f32[288,128]{1,0:T(8,128)S(1)} %dense.1.refs_3_), channel_id=1, source_target_pairs={{0,16},{8,24},{16,0},{24,8},{1,17},{9,25},{17,1},{25,9},{2,18},{10... | collective-permute-start | bytes 442376 | tf_op jit(solution)/shard_map/ppermute | solution.py:69
  22.8 5.8 %collective-permute-start.7 = (f32[288,128]{1,0:T(8,128)S(1)}, f32[288,128]{1,0:T(8,128)S(1)}, u32[]{:S(2)}, u32[]{:S(2)}) collective-permute-start(f32[288,128]{1,0:T(8,128)S(1)} %dense.1.refs_3_), channel_id=1, source_target_pairs={{0,8},{8,0},{16,24},{24,16},{1,9},{9,1},{17,25},{25,17},{2,10},{10... | collective-permute-start | bytes 442376 | tf_op jit(solution)/shard_map/ppermute | solution.py:69
  25.6 6.6 %copy-start.1 = (f32[1024,64]{0,1:T(8,128)S(1)}, f32[1024,64]{0,1:T(8,128)}, u32[]{:S(2)}) copy-start(f32[1024,64]{0,1:T(8,128)} %param.15) | copy-start | bytes 786436
  25.6 6.5 %copy-start.2 = (f32[200,64]{0,1:T(8,128)S(1)}, f32[200,64]{0,1:T(8,128)}, u32[]{:S(2)}) copy-start(f32[200,64]{0,1:T(8,128)} %param.14) | copy-start | bytes 153604
  25.7 1.4 %collective-permute-start.13 = (f32[4,4,2048]{2,1,0:T(4,128)S(1)}, f32[4,4,2048]{2,1,0:T(4,128)S(1)}, u32[]{:S(2)}, u32[]{:S(2)}) collective-permute-start(f32[4,4,2048]{2,1,0:T(4,128)S(1)} %other.1), channel_id=1, source_target_pairs={{0,1},{1,0},{2,3},{3,2},{4,5},{5,4},{6,7},{7,6},{8,9},{9,8},{10,11... | collective-permute-start | bytes 393224 | tf_op jit(solution)/shard_map/ppermute | solution.py:69
  28.6 10.2 %collective-permute-start.16 = (f32[4,16384]{1,0:T(4,128)S(1)}, f32[4,16384]{1,0:T(4,128)S(1)}, u32[]{:S(2)}, u32[]{:S(2)}) collective-permute-start(f32[4,16384]{1,0:T(4,128)S(1)} %join.1.refs_2_), channel_id=1, source_target_pairs={{0,24},{8,16},{16,8},{24,0},{1,25},{9,17},{17,9},{25,1},{2,26},{10... | collective-permute-start | bytes 786440 | tf_op jit(solution)/shard_map/ppermute | solution.py:69
  30.2 11.9 %collective-permute-start.15 = (f32[4,16384]{1,0:T(4,128)S(1)}, f32[4,16384]{1,0:T(4,128)S(1)}, u32[]{:S(2)}, u32[]{:S(2)}) collective-permute-start(f32[4,16384]{1,0:T(4,128)S(1)} %join.1.refs_2_), channel_id=1, source_target_pairs={{0,16},{8,24},{16,0},{24,8},{1,17},{9,25},{17,1},{25,9},{2,18},{10... | collective-permute-start | bytes 786440 | tf_op jit(solution)/shard_map/ppermute | solution.py:69
  31.6 10.9 %collective-permute-start.14 = (f32[4,16384]{1,0:T(4,128)S(1)}, f32[4,16384]{1,0:T(4,128)S(1)}, u32[]{:S(2)}, u32[]{:S(2)}) collective-permute-start(f32[4,16384]{1,0:T(4,128)S(1)} %join.1.refs_2_), channel_id=1, source_target_pairs={{0,8},{8,0},{16,24},{24,16},{1,9},{9,1},{17,25},{25,17},{2,10},{10... | collective-permute-start | bytes 786440 | tf_op jit(solution)/shard_map/ppermute | solution.py:69

commit v5 on v4

--- a/solution.py
+++ b/solution.py
@@ -122,59 +122,71 @@
 
 
 def start_body(groups, part, owners, anchor, inner, momentum, emb, inner_emb, basis_t, *refs):
-    outs, (quarter, same, other, held), named, scratch = (
+    outs, (quarter, same, other), named, scratch = (
         refs[:groups],
-        refs[groups : groups + 4],
-        refs[groups + 4 : groups + 7],
-        refs[groups + 7 :],
-    )
-    own, far, near, emb_far, emb_near, basis, factor, sem = scratch
+        refs[groups : groups + 3],
+        refs[groups + 3 : groups + 6],
+        refs[groups + 6 :],
+    )
+    own, far, near, emb_far, emb_near, basis, factor, sem, piece_sem = scratch
     rep, chip, core = place()
     blocks, rank = quarter.shape[0], basis.shape[0]
     share = rank // groups
-    moves = [pltpu.make_async_copy(owners, own, sem.at[2 * groups])]
-    for k in range(groups):
+    chips = same.shape[0]
+    listed = pltpu.make_async_copy(owners, own, sem.at[2 * groups])
+    listed.start()
+    moves = {}
+    for k in (*range(groups - 1, 0, -1), 0):
         at = column(rep ^ k, part)
-        moves.append(pltpu.make_async_copy(anchor.at[:, at], far.at[k], sem.at[k]))
-        moves.append(pltpu.make_async_copy(inner.at[0, :, at], near.at[k], sem.at[groups + k]))
-    for i, (a, b) in enumerate(
-        ((emb, emb_far), (inner_emb.at[0], emb_near), (basis_t, basis), (momentum, held))
-    ):
-        moves.append(pltpu.make_async_copy(a, b, sem.at[2 * groups + 1 + i]))
-    for move in moves:
+        moves[k] = (
+            pltpu.make_async_copy(anchor.at[:, at], far.at[k], sem.at[k]),
+            pltpu.make_async_copy(inner.at[0, :, at], near.at[k], sem.at[groups + k]),
+        )
+        for move in moves[k]:
+            move.start()
+    emb_moves = [
+        pltpu.make_async_copy(a, b, sem.at[2 * groups + 1 + i])
+        for i, (a, b) in enumerate(
+            ((basis_t, basis), (emb, emb_far), (inner_emb.at[0], emb_near))
+        )
+    ]
+    for move in emb_moves:
         move.start()
-    moves[0].wait()
+    pieces = [
+        pltpu.make_async_copy(
+            momentum.at[:, column((2 * to + (core ^ o)) * groups + rep, part)],
+            out.at[to],
+            piece_sem.at[2 * to + o],
+        )
+        for to in range(chips)
+        for o, out in enumerate((same, other))
+    ]
+    for piece in pieces:
+        piece.start()
+    listed.wait()
     name_places(same.shape[1], own, *named)
 
-    for k in range(groups):
-        moves[2 * k + 1].wait()
-        moves[2 * k + 2].wait()
-        for t, (i, height, j, width) in enumerate(tiles(blocks, part)):
+    dense_tiles = tiles(blocks, part)
+    for k in moves:
+        for move in moves[k]:
+            move.wait()
+        for t, (i, height, j, width) in enumerate(dense_tiles):
             rows, columns = slice(i, i + height), slice(j, j + width)
             outs[k][8 * t : 8 * t + height, :width] = far[k, rows, columns] - near[k, rows, columns]
-        if k == 0:
-            quarter[...] = far[0]
-    for move in moves[2 * groups + 1 : 2 * groups + 4]:
+    quarter[...] = far[0]
+    for move in emb_moves:
         move.wait()
     high, low = two_parts(emb_far[...] - emb_near[...])
     basis_high, basis_low = two_parts(basis[...])
-    both = dot(jnp.concatenate([basis_high, basis_low], axis=0), high, ((1,), (1,)))
-    factor[...] = both[:rank] + (both[rank:] + dot(basis_high, low, ((1,), (1,))))
-    skip = 8 * len(tiles(blocks, part))
+    products = dot(jnp.concatenate([basis_high, basis_low], axis=0), high, ((1,), (1,)))
+    factor[...] = products[:rank] + (products[rank:] + dot(basis_high, low, ((1,), (1,))))
+    skip = 8 * len(dense_tiles)
     for k in range(groups):
         for t, (i, height, j, width) in enumerate(tiles(share, factor.shape[1])):
             rows = pl.ds(pl.multiple_of((rep ^ k) * share + i, 8), height)
             outs[k][skip + 8 * t : skip + 8 * t + height, :width] = factor[rows, j : j + width]
-
-    moves[2 * groups + 4].wait()
-
-    def take(to, carry):
-        for o, out in enumerate((same, other)):
-            piece = 2 * to + (core ^ o)
-            out[to] = held[:, column(piece * groups + rep, part)]
-        return carry
-
-    lax.fori_loop(0, same.shape[0], take, 0, unroll=same.shape[0] <= 8)
+    for piece in pieces:
+        piece.wait()
 
 
 def mean_body(groups, direct, block_of, *refs):
@@ -233,19 +245,34 @@
 
 
 def join_body(direct, *refs):
-    *received, crossed, out = refs
+    *received, crossed, first, second = refs
     chips, _, part = crossed.shape
+    half = chips // 2
 
     def fill(k, carry):
-        out[:, column(2 * k, part)] = received[k][0] if direct else received[0][k, 0]
-        out[:, column(2 * k + 1, part)] = crossed[k]
+        for out, chip in ((first, k), (second, k + half)):
+            mine = received[chip][0] if direct else received[0][chip, 0]
+            out[:, column(2 * k, part)] = mine
+            out[:, column(2 * k + 1, part)] = crossed[chip]
         return carry
 
     if direct:
-        for k in range(chips):
+        for k in range(half):
             fill(k, 0)
     else:
-        lax.fori_loop(0, chips, fill, 0)
+        lax.fori_loop(0, half, fill, 0)
+
+
+def cut_body(ref, out):
+    out[...] = ref[: out.shape[0], :]
+
+
+def copies_body(*refs):
+    count = len(refs) // 2
+    for ref, out in zip(refs[:count], refs[count:]):
+        out[:, : ref.shape[1]] = ref[...]
+        if out.shape[1] > ref.shape[1]:
+            out[:, ref.shape[1] :] = jnp.zeros((out.shape[0], out.shape[1] - ref.shape[1]), f32)
 
 
 def dense_body(direct, row_of, quarter, mean, shared, *refs):
@@ -318,26 +345,37 @@
         copy.wait()
 
 
-def finish_momentum_body(part, direct, owned, momentum, *refs):
+def finish_momentum_body(part, direct, members, owned, _, momentum, *refs):
     *gradient, result, made, sem = refs
     rep, here, core = place()
-    slots, groups = momentum.shape[0], len(gradient)
-    pieces = momentum.shape[1] // part // groups
+    slots, pieces = momentum.shape[0], made.shape[1]
+    groups = momentum.shape[1] // part // pieces
+    half = pieces // 2
     live = lax.broadcasted_iota(jnp.int32, (slots, part), 0) < owned[here * 2 + core]
 
-    def fill(i, carry):
+    def move(n, g, i):
         k, o = (i >> 1, i & 1)
         piece = 2 * (here ^ k if direct else k) + (core ^ o)
-        for g, ref in enumerate(gradient):
-            at = column(piece * groups + (rep ^ g), part)
-            rows = momentum_decay * momentum[:, at] + ref[:, column(i, part)]
-            made[:, at] = jnp.where(live, rows, 0.0)
-        return carry
-
-    lax.fori_loop(0, pieces, fill, 0, unroll=pieces <= 16)
-    copy = pltpu.make_async_copy(made, result, sem)
-    copy.start()
-    copy.wait()
+        at = column(piece * groups + (rep ^ g), part)
+        return at, pltpu.make_async_copy(made.at[n, i], result.at[:, at], sem.at[n, i])
+
+    def fill(h, i, carry):
+        for n, g in enumerate(members):
+            at, copy = move(n, g, i + h * half)
+            rows = momentum_decay * momentum[:, at] + gradient[2 * n + h][:, column(i, part)]
+            made[n, i + h * half] = jnp.where(live, rows, 0.0)
+            copy.start()
+        return carry
+
+    def finish(i, carry):
+        for n, g in enumerate(members):
+            move(n, g, i)[1].wait()
+        return carry
+
+    short = pieces <= 16
+    for h in range(2):
+        lax.fori_loop(0, half, functools.partial(fill, h), 0, unroll=short)
+    lax.fori_loop(0, pieces, finish, 0, unroll=short)
 
 
 def over_chips(outs, direct, owner_count):
@@ -368,12 +406,11 @@
     message = (8 * (len(tiles(blocks, part)) + len(tiles(rank // groups, rows))), 128)
     parted = [kept(table[1:])] * chips if direct else [kept(table)]
 
-    *parts, quarter, same, other, momentum, row_of, block_of, owned = run(
+    *parts, quarter, same, other, row_of, block_of, owned = run(
         functools.partial(start_body, groups, part),
         [kept(message)] * groups
         + [kept((blocks, part))]
         + [kept(chunk)] * 2
-        + [kept(momentum_dense.shape)]
         + [pltpu.SMEM((n,), jnp.int32) for n in (blocks, owner_count * slot_count, owner_count)],
         [],
         far=[
@@ -385,7 +422,7 @@
             inner_emb,
             basis_t,
         ],
-        out_specs=[vmem] * (groups + 4) + [smem] * 3,
+        out_specs=[vmem] * (groups + 3) + [smem] * 3,
         scratch=[
             pltpu.SMEM((blocks,), jnp.int32),
             pltpu.VMEM((groups, blocks, part), f32),
@@ -394,7 +431,8 @@
             pltpu.VMEM(anchor_emb.shape, f32),
             pltpu.VMEM(basis_t.shape, f32),
             pltpu.VMEM((rank, rows), f32),
-            pltpu.SemaphoreType.DMA((2 * groups + 5,)),
+            pltpu.SemaphoreType.DMA((2 * groups + 4,)),
+            pltpu.SemaphoreType.DMA((owner_count,)),
         ],
         name="start",
     )
@@ -433,14 +471,42 @@
     )
     dense = [dense] + [swap(dense, "rep", groups, k) for k in range(1, groups)]
 
-    (gradient,) = run(
+    length = chips * part
+    halves = run(
         functools.partial(join_body, direct),
-        [kept((slot_count, 2 * chips * part))],
+        [kept((slot_count, length))] * 2,
         [*gradient_rows, crossed],
-        after=dense[1:],
+        after=gradient_rows[:0:-1],
         name="join",
     )
-    gradient = [gradient] + [swap(gradient, "rep", groups, k) for k in range(1, groups)]
+    again = run(
+        copies_body,
+        [kept((slot_count, length + 128))] * 2,
+        halves,
+        name="again",
+    )
+    (sign,) = run(
+        cut_body, [kept((248, 128))], [dense[0]], after=dense[1:], name="gathered"
+    )
+    sign = swap(sign, "own", owner_count, 1)
+    near1 = swap(halves[0], "rep", groups, 1)
+    near2 = swap(halves[1], "rep", groups, 2)
+    passed = run(
+        copies_body,
+        [kept((slot_count, length))] * 2,
+        [near1, near2],
+        after=[sign],
+        name="pass_on",
+    )
+    gradient = [
+        *halves,
+        near1,
+        swap(again[1], "rep", groups, 1),
+        swap(again[0], "rep", groups, 2),
+        near2,
+        swap(passed[0], "rep", groups, 2),
+        swap(passed[1], "rep", groups, 1),
+    ]
 
     shapes = [anchor_dense.shape, anchor_emb.shape, (rank, rows)]
     new_dense, new_emb, new_momentum_t = run(
@@ -452,15 +518,26 @@
         + [pltpu.VMEM(shape, f32) for shape in shapes],
         name="finish",
     )
-    (new_momentum_dense,) = run(
-        functools.partial(finish_momentum_body, part, direct),
-        [stored(momentum_dense.shape)],
-        [momentum, *gradient],
-        [owned],
-        out_specs=[anywhere],
-        scratch=[pltpu.VMEM(momentum_dense.shape, f32), pltpu.SemaphoreType.DMA],
-        name="finish_momentum",
-    )
+    new_momentum_dense = new_momentum_t
+    for members in (tuple(range(groups - 1)), (groups - 1,)):
+        (new_momentum_dense,) = pl.pallas_call(
+            functools.partial(finish_momentum_body, part, direct, members),
+            out_shape=[stored(momentum_dense.shape)],
+            in_specs=[smem, anywhere] + [vmem] * (1 + 2 * len(members)),
+            out_specs=[anywhere],
+            scratch_shapes=[
+                pltpu.VMEM((len(members), owner_count, slot_count, part), f32),
+                pltpu.SemaphoreType.DMA((len(members), owner_count)),
+            ],
+            input_output_aliases={1: 0} if members[0] else {},
+            compiler_params=pltpu.CompilerParams(vmem_limit_bytes=vmem_limit),
+            name="finish_momentum",
+        )(
+            in_scalars(owned),
+            new_momentum_dense,
+            on_chip(momentum_dense),
+            *[on_chip(gradient[2 * g + h]) for g in members for h in range(2)],
+        )
     return (new_dense, new_momentum_dense, new_emb, new_momentum_t.T)
 
 

time: 43.9 us -> 39.9 us (0.909)
  waiting for transfers between devices: 14.1 us -> 4.87 us
  starting transfers between devices: 23.4 us -> 26.9 us
  Pallas kernels: 5.46 us -> 6.37 us
  local copies, waits for them, and re-layouts: 0.02 us -> 0.86 us
    ppermute x17 -> x21, waiting for transfers between devices: 14.1 us -> 4.87 us  [swap(): return lax.ppermute(x, axis, [(i, i ^ mask) for i in range(count)])]
    ppermute x17 -> x21, starting transfers between devices: 23.4 us -> 26.9 us  [swap(): return lax.ppermute(x, axis, [(i, i ^ mask) for i in range(count)])]
    pallas_call x0 -> x2, Pallas kernels: none -> 1.92 us  [per_device(): pl.pallas_call(functools.partial(finish_momentum_body, part, direct, memb...]
    pallas_call x8 -> x10, Pallas kernels: 5.46 us -> 4.45 us  [run(): pl.pallas_call(whole, out_shape=list(outs), in_specs=[anywhere] * skip +...]
    unnamed x6 -> x10, local copies, waits for them, and re-layouts: 0.02 us -> 0.86 us
  transfers between devices with their start and end apart: 17 -> 21, of which waited for: 9 -> 9; matrix products, arithmetic and copies ran while one was open for 0% -> 0% of each run, Pallas kernels for 4% -> 8%
where the time goes in v5:
time: 39.9 us; the launch traced here: 39.8 us
  starting transfers between devices  26.9 us (67%)
  Pallas kernels  6.37 us (16%)
  waiting for transfers between devices  4.87 us (12%)
  local copies, waits for them, and re-layouts  0.86 us (2%)
  between operations  0.76 us (2%)
    ppermute x21, starting transfers between devices, swap(): return lax.ppermute(x, axis, [(i, i ^ mask) for i in range(count)])  26.9 us
    ppermute x21, waiting for transfers between devices, swap(): return lax.ppermute(x, axis, [(i, i ^ mask) for i in range(count)])  4.87 us
    pallas_call x10, Pallas kernels, run(): pl.pallas_call(whole, out_shape=list(outs), in_specs=[anywhere] * skip +...  4.45 us
    pallas_call x2, Pallas kernels, per_device(): pl.pallas_call(functools.partial(finish_momentum_body, part, direct, memb...  1.92 us
    unnamed x10, local copies, waits for them, and re-layouts  0.86 us
  transfers between devices with their start and end apart: 21, of which 9 were waited for; matrix products, arithmetic and copies ran while one was open for 0% of the time, Pallas kernels for 8%

profile of v5, /device:TPU:0, one launch (start us, length us, event | category | flops | bytes accessed | tf_op | source)
XLA Modules:
  0.0 39.8 jit_solution(13780220568097114560)
XLA Ops:
  0.6 2.6 %start.1 = (f32[288,128]{1,0:T(8,128)S(1)}, f32[288,128]{1,0:T(8,128)S(1)}, f32[288,128]{1,0:T(8,128)S(1)}, f32[288,128]{1,0:T(8,128)S(1)}, f32[16,2048]{1,0:T(8...) custom-call(s32[16]{0:T(128)} %bitcast.8, ...), custom_call_target="tpu_custom_call" | custom-call | tf_op jit(solution)/shard_map/start/pallas_call | solution.py:49
  3.2 0.5 %collective-permute-start.3 = (f32[4,4,2048]{2,1,0:T(4,128)S(1)}, f32[4,4,2048]{2,1,0:T(4,128)S(1)}, u32[]{:S(2)}, u32[]{:S(2)}) collective-permute-start(f32[4,4,2048]{2,1,0:T(4,128)S(1)} %get-tuple-element.43), channel_id=1, source_target_pairs={{0,1},{1,0},{2,3},{3,2},{4,5},{5,4},{6,7},{7,6},{8,9},{9,8},{10,11... | collective-permute-start | bytes 393224 | tf_op jit(solution)/shard_map/ppermute | solution.py:69
  3.7 2.6 %collective-permute-start = (f32[288,128]{1,0:T(8,128)S(1)}, f32[288,128]{1,0:T(8,128)S(1)}, u32[]{:S(2)}, u32[]{:S(2)}) collective-permute-start(f32[288,128]{1,0:T(8,128)S(1)} %get-tuple-element.37), channel_id=1, source_target_pairs={{0,8},{8,0},{16,24},{24,16},{1,9},{9,1},{17,25},{25,17},{2,10},{10... | collective-permute-start | bytes 442376 | tf_op jit(solution)/shard_map/ppermute | solution.py:69
  6.3 1.5 %collective-permute-start.1 = (f32[288,128]{1,0:T(8,128)S(1)}, f32[288,128]{1,0:T(8,128)S(1)}, u32[]{:S(2)}, u32[]{:S(2)}) collective-permute-start(f32[288,128]{1,0:T(8,128)S(1)} %get-tuple-element.38), channel_id=1, source_target_pairs={{0,16},{8,24},{16,0},{24,8},{1,17},{9,25},{17,1},{25,9},{2,18},{10... | collective-permute-start | bytes 442376 | tf_op jit(solution)/shard_map/ppermute | solution.py:69
  7.9 2.1 %collective-permute-start.4 = (f32[2,4,2048]{2,1,0:T(4,128)S(1)}, f32[2,4,2048]{2,1,0:T(4,128)S(1)}, u32[]{:S(2)}, u32[]{:S(2)}) collective-permute-start(f32[2,4,2048]{2,1,0:T(4,128)S(1)} %get-tuple-element.45), channel_id=1, source_target_pairs={{0,2},{1,3},{2,0},{3,1},{4,6},{5,7},{6,4},{7,5},{8,10},{9,11},{10,... | collective-permute-start | bytes 196616 | tf_op jit(solution)/shard_map/ppermute | solution.py:69
  10.0 2.6 %collective-permute-start.5 = (f32[2,4,2048]{2,1,0:T(4,128)S(1)}, f32[2,4,2048]{2,1,0:T(4,128)S(1)}, u32[]{:S(2)}, u32[]{:S(2)}) collective-permute-start(f32[2,4,2048]{2,1,0:T(4,128)S(1)} %get-tuple-element.46), channel_id=1, source_target_pairs={{0,4},{1,5},{2,6},{3,7},{4,0},{5,1},{6,2},{7,3},{8,12},{9,13},{10,... | collective-permute-start | bytes 196616 | tf_op jit(solution)/shard_map/ppermute | solution.py:69
  12.6 2.5 %collective-permute-start.6 = (f32[2,4,2048]{2,1,0:T(4,128)S(1)}, f32[2,4,2048]{2,1,0:T(4,128)S(1)}, u32[]{:S(2)}, u32[]{:S(2)}) collective-permute-start(f32[2,4,2048]{2,1,0:T(4,128)S(1)} %get-tuple-element.47), channel_id=1, source_target_pairs={{0,6},{1,7},{2,4},{3,5},{4,2},{5,3},{6,0},{7,1},{8,14},{9,15},{10,... | collective-permute-start | bytes 196616 | tf_op jit(solution)/shard_map/ppermute | solution.py:69
  15.1 0.3 collective-permute-done.1.refs_3_
  15.4 0.1 mean.1
  15.5 3.7 %collective-permute-start.10 = (f32[2,4,2048]{2,1,0:T(4,128)S(1)}, f32[2,4,2048]{2,1,0:T(4,128)S(1)}, u32[]{:S(2)}, u32[]{:S(2)}) collective-permute-start(f32[2,4,2048]{2,1,0:T(4,128)S(1)} %get-tuple-element.51), channel_id=1, source_target_pairs={{0,6},{1,7},{2,4},{3,5},{4,2},{5,3},{6,0},{7,1},{8,14},{9,15},{10,... | collective-permute-start | bytes 196616 | tf_op jit(solution)/shard_map/ppermute | solution.py:69
  19.2 0.8 %collective-permute-start.12 = (f32[2,4,2048]{2,1,0:T(4,128)S(1)}, f32[2,4,2048]{2,1,0:T(4,128)S(1)}, u32[]{:S(2)}, u32[]{:S(2)}) collective-permute-start(f32[2,4,2048]{2,1,0:T(4,128)S(1)} %get-tuple-element.53), channel_id=1, source_target_pairs={{0,2},{1,3},{2,0},{3,1},{4,6},{5,7},{6,4},{7,5},{8,10},{9,11},{10,... | collective-permute-start | bytes 196616 | tf_op jit(solution)/shard_map/ppermute | solution.py:69
  20.0 0.2 dense.1.refs_3_
  20.2 2.2 %collective-permute-start.9 = (f32[288,128]{1,0:T(8,128)S(1)}, f32[288,128]{1,0:T(8,128)S(1)}, u32[]{:S(2)}, u32[]{:S(2)}) collective-permute-start(f32[288,128]{1,0:T(8,128)S(1)} %dense.1.refs_3_), channel_id=1, source_target_pairs={{0,24},{8,16},{16,8},{24,0},{1,25},{9,17},{17,9},{25,1},{2,26},{10... | collective-permute-start | bytes 442376 | tf_op jit(solution)/shard_map/ppermute | solution.py:69
  22.4 0.6 %collective-permute-start.8 = (f32[288,128]{1,0:T(8,128)S(1)}, f32[288,128]{1,0:T(8,128)S(1)}, u32[]{:S(2)}, u32[]{:S(2)}) collective-permute-start(f32[288,128]{1,0:T(8,128)S(1)} %dense.1.refs_3_), channel_id=1, source_target_pairs={{0,16},{8,24},{16,0},{24,8},{1,17},{9,25},{17,1},{25,9},{2,18},{10... | collective-permute-start | bytes 442376 | tf_op jit(solution)/shard_map/ppermute | solution.py:69
  23.0 0.8 %collective-permute-start.7 = (f32[288,128]{1,0:T(8,128)S(1)}, f32[288,128]{1,0:T(8,128)S(1)}, u32[]{:S(2)}, u32[]{:S(2)}) collective-permute-start(f32[288,128]{1,0:T(8,128)S(1)} %dense.1.refs_3_), channel_id=1, source_target_pairs={{0,8},{8,0},{16,24},{24,16},{1,9},{9,1},{17,25},{25,17},{2,10},{10... | collective-permute-start | bytes 442376 | tf_op jit(solution)/shard_map/ppermute | solution.py:69
  23.8 0.7 %collective-permute-done.11.refs_2_.refs_1_.refs_5_ = f32[2,4,2048]{2,1,0:T(4,128)S(1)} collective-permute-done((f32[2,4,2048]{2,1,0:T(4,128)S(1)}, f32[2,4,2048]{2,1,0:T(4,128)S(1)}, u32[]{:S(2)}, u32[]{:S(2)}) %collective-permute-start.11) | collective-permute-done | bytes 65568 | tf_op jit(solution)/shard_map/ppermute | solution.py:69
  24.6 1.3 %collective-permute-done.13.refs_7_ = f32[4,4,2048]{2,1,0:T(4,128)S(1)} collective-permute-done((f32[4,4,2048]{2,1,0:T(4,128)S(1)}, f32[4,4,2048]{2,1,0:T(4,128)S(1)}, u32[]{:S(2)}, u32[]{:S(2)}) %collective-permute-start.13) | collective-permute-done | bytes 131104 | tf_op jit(solution)/shard_map/ppermute | solution.py:69
  26.0 1.5 %collective-permute-start.14 = (f32[4,8192]{1,0:T(4,128)S(1)}, f32[4,8192]{1,0:T(4,128)S(1)}, u32[]{:S(2)}, u32[]{:S(2)}) collective-permute-start(f32[4,8192]{1,0:T(4,128)S(1)} %get-tuple-element.55.refs_0_), channel_id=1, source_target_pairs={{0,8},{8,0},{16,24},{24,16},{1,9},{9,1},{17,25},{25,17},{2,10},{10... | collective-permute-start | bytes 393224 | tf_op jit(solution)/shard_map/ppermute | solution.py:69
  27.5 1.2 %collective-permute-start.17 = (f32[4,8192]{1,0:T(4,128)S(1)}, f32[4,8192]{1,0:T(4,128)S(1)}, u32[]{:S(2)}, u32[]{:S(2)}) collective-permute-start(f32[4,8192]{1,0:T(4,128)S(1)} %get-tuple-element.56.refs_1_), channel_id=1, source_target_pairs={{0,16},{8,24},{16,0},{24,8},{1,17},{9,25},{17,1},{25,9},{2,18},{10... | collective-permute-start | bytes 393224 | tf_op jit(solution)/shard_map/ppermute | solution.py:69
  28.7 0.2 collective-permute-done.8.refs_5_.refs_1_
  29.0 1.5 %collective-permute-start.15 = (f32[4,8320]{1,0:T(4,128)S(1)}, f32[4,8320]{1,0:T(4,128)S(1)}, u32[]{:S(2)}, u32[]{:S(2)}) collective-permute-start(f32[4,8320]{1,0:T(4,128)S(1)} %get-tuple-element.57), channel_id=1, source_target_pairs={{0,8},{8,0},{16,24},{24,16},{1,9},{9,1},{17,25},{25,17},{2,10},{10... | collective-permute-start | bytes 399368 | tf_op jit(solution)/shard_map/ppermute | solution.py:69
  30.5 0.6 %collective-permute-start.16 = (f32[4,8320]{1,0:T(4,128)S(1)}, f32[4,8320]{1,0:T(4,128)S(1)}, u32[]{:S(2)}, u32[]{:S(2)}) collective-permute-start(f32[4,8320]{1,0:T(4,128)S(1)} %get-tuple-element.58), channel_id=1, source_target_pairs={{0,16},{8,24},{16,0},{24,8},{1,17},{9,25},{17,1},{25,9},{2,18},{10... | collective-permute-start | bytes 399368 | tf_op jit(solution)/shard_map/ppermute | solution.py:69
  31.1 0.5 %collective-permute-done.14.refs_2_.refs_1_ = f32[4,8192]{1,0:T(4,128)S(1)} collective-permute-done((f32[4,8192]{1,0:T(4,128)S(1)}, f32[4,8192]{1,0:T(4,128)S(1)}, u32[]{:S(2)}, u32[]{:S(2)}) %collective-permute-start.14) | collective-permute-done | bytes 131104 | tf_op jit(solution)/shard_map/ppermute | solution.py:69
  31.6 1.2 %collective-permute-done.17.refs_5_.refs_2_ = f32[4,8192]{1,0:T(4,128)S(1)} collective-permute-done((f32[4,8192]{1,0:T(4,128)S(1)}, f32[4,8192]{1,0:T(4,128)S(1)}, u32[]{:S(2)}, u32[]{:S(2)}) %collective-permute-start.17) | collective-permute-done | bytes 131104 | tf_op jit(solution)/shard_map/ppermute | solution.py:69
  32.8 1.3 %collective-permute-start.19 = (f32[4,8192]{1,0:T(4,128)S(1)}, f32[4,8192]{1,0:T(4,128)S(1)}, u32[]{:S(2)}, u32[]{:S(2)}) collective-permute-start(f32[4,8192]{1,0:T(4,128)S(1)} %get-tuple-element.59), channel_id=1, source_target_pairs={{0,16},{8,24},{16,0},{24,8},{1,17},{9,25},{17,1},{25,9},{2,18},{10... | collective-permute-start | bytes 393224 | tf_op jit(solution)/shard_map/ppermute | solution.py:69
  34.0 0.9 %collective-permute-start.20 = (f32[4,8192]{1,0:T(4,128)S(1)}, f32[4,8192]{1,0:T(4,128)S(1)}, u32[]{:S(2)}, u32[]{:S(2)}) collective-permute-start(f32[4,8192]{1,0:T(4,128)S(1)} %get-tuple-element.60), channel_id=1, source_target_pairs={{0,8},{8,0},{16,24},{24,16},{1,9},{9,1},{17,25},{25,17},{2,10},{10... | collective-permute-start | bytes 393224 | tf_op jit(solution)/shard_map/ppermute | solution.py:69
  34.9 1.4 %finish.1 = (f32[16,8192]{1,0:T(8,128)}, f32[200,1024]{1,0:T(8,128)}, f32[64,200]{1,0:T(8,128)}) custom-call(f32[200,1024]{1,0:T(8,128)S(1)} %copy-done.1, f32[64,200]{1,0:T(8,128)S(1)} %bitcast.7, f32[64,1024]{1,0:T(8,128)S(1)} %bitcast.5, f32[288,128]{1,0:T(8,128)S(1)} %dense.1.refs_3_, f32[288,128]{1,0:T(8,128)S(1)} %collective-permute-done.7.refs_4_.refs_0_, ...), custom_call_target="tpu_custom_call" | custom-call | tf_op jit(solution)/shard_map/finish/pallas_call | solution.py:49
  36.4 0.5 %collective-permute-done.16.refs_4_ = f32[4,8320]{1,0:T(4,128)S(1)} collective-permute-done((f32[4,8320]{1,0:T(4,128)S(1)}, f32[4,8320]{1,0:T(4,128)S(1)}, u32[]{:S(2)}, u32[]{:S(2)}) %collective-permute-start.16) | collective-permute-done | bytes 133152 | tf_op jit(solution)/shard_map/ppermute | solution.py:69
  36.9 0.8 %copy-done.3 = f32[64,200]{1,0:T(8,128)S(1)} copy-done((f32[64,200]{1,0:T(8,128)S(1)}, f32[64,200]{1,0:T(8,128)}, u32[]{:S(2)}) %copy-start.3) | copy-done | bytes 51224
  37.7 1.1 %finish_momentum.2._ = f32[4,65536]{1,0:T(4,128)} custom-call(s32[8]{0:T(128)S(4)} %get-tuple-element.49.owned, f32[64,200]{1,0:T(8,128)S(1)} %copy-done.3, f32[4,65536]{1,0:T(4,128)S(1)} %copy-done, f32[4,8192]{1,0:T(4,128)S(1)} %get-tuple-element.55.refs_0_, f32[4,8192]{1,0:T(4,128)S(1)} %get-tuple-element.56.refs_1_, ...), custom_call_target="tpu_custom_call" | custom-call | tf_op jit(solution)/shard_map/finish_momentum/pallas_call | solution.py:523
  38.9 0.1 collective-permute-done.19.refs_0_
  39.0 0.8 %finish_momentum.3 = f32[4,65536]{1,0:T(4,128)} custom-call(s32[8]{0:T(128)S(4)} %get-tuple-element.49.owned, f32[4,65536]{1,0:T(4,128)} %finish_momentum.2._, f32[4,65536]{1,0:T(4,128)S(1)} %copy-done, f32[4,8192]{1,0:T(4,128)S(1)} %collective-permute-done.19.refs_0_, f32[4,8192]{1,0:T(4,128)S(1)} %collective-permute-done.20.refs_1_), custom_call_target="tpu_custom_call", output_to_operand_aliasing={{}: (1, {})} | custom-call | tf_op jit(solution)/shard_map/finish_momentum/pallas_call | solution.py:523
  (32 shorter events, 0.4 us)
Async XLA Ops:
  3.2 4.6 %collective-permute-start.3 = (f32[4,4,2048]{2,1,0:T(4,128)S(1)}, f32[4,4,2048]{2,1,0:T(4,128)S(1)}, u32[]{:S(2)}, u32[]{:S(2)}) collective-permute-start(f32[4,4,2048]{2,1,0:T(4,128)S(1)} %get-tuple-element.43), channel_id=1, source_target_pairs={{0,1},{1,0},{2,3},{3,2},{4,5},{5,4},{6,7},{7,6},{8,9},{9,8},{10,11... | collective-permute-start | bytes 393224 | tf_op jit(solution)/shard_map/ppermute | solution.py:69
  3.7 8.8 %collective-permute-start = (f32[288,128]{1,0:T(8,128)S(1)}, f32[288,128]{1,0:T(8,128)S(1)}, u32[]{:S(2)}, u32[]{:S(2)}) collective-permute-start(f32[288,128]{1,0:T(8,128)S(1)} %get-tuple-element.37), channel_id=1, source_target_pairs={{0,8},{8,0},{16,24},{24,16},{1,9},{9,1},{17,25},{25,17},{2,10},{10... | collective-permute-start | bytes 442376 | tf_op jit(solution)/shard_map/ppermute | solution.py:69
  6.3 9.1 %collective-permute-start.1 = (f32[288,128]{1,0:T(8,128)S(1)}, f32[288,128]{1,0:T(8,128)S(1)}, u32[]{:S(2)}, u32[]{:S(2)}) collective-permute-start(f32[288,128]{1,0:T(8,128)S(1)} %get-tuple-element.38), channel_id=1, source_target_pairs={{0,16},{8,24},{16,0},{24,8},{1,17},{9,25},{17,1},{25,9},{2,18},{10... | collective-permute-start | bytes 442376 | tf_op jit(solution)/shard_map/ppermute | solution.py:69
  7.8 7.6 %collective-permute-start.2 = (f32[288,128]{1,0:T(8,128)S(1)}, f32[288,128]{1,0:T(8,128)S(1)}, u32[]{:S(2)}, u32[]{:S(2)}) collective-permute-start(f32[288,128]{1,0:T(8,128)S(1)} %get-tuple-element.39), channel_id=1, source_target_pairs={{0,24},{8,16},{16,8},{24,0},{1,25},{9,17},{17,9},{25,1},{2,26},{10... | collective-permute-start | bytes 442376 | tf_op jit(solution)/shard_map/ppermute | solution.py:69
  7.9 11.3 %collective-permute-start.4 = (f32[2,4,2048]{2,1,0:T(4,128)S(1)}, f32[2,4,2048]{2,1,0:T(4,128)S(1)}, u32[]{:S(2)}, u32[]{:S(2)}) collective-permute-start(f32[2,4,2048]{2,1,0:T(4,128)S(1)} %get-tuple-element.45), channel_id=1, source_target_pairs={{0,2},{1,3},{2,0},{3,1},{4,6},{5,7},{6,4},{7,5},{8,10},{9,11},{10,... | collective-permute-start | bytes 196616 | tf_op jit(solution)/shard_map/ppermute | solution.py:69
  10.0 10.0 %collective-permute-start.5 = (f32[2,4,2048]{2,1,0:T(4,128)S(1)}, f32[2,4,2048]{2,1,0:T(4,128)S(1)}, u32[]{:S(2)}, u32[]{:S(2)}) collective-permute-start(f32[2,4,2048]{2,1,0:T(4,128)S(1)} %get-tuple-element.46), channel_id=1, source_target_pairs={{0,4},{1,5},{2,6},{3,7},{4,0},{5,1},{6,2},{7,3},{8,12},{9,13},{10,... | collective-permute-start | bytes 196616 | tf_op jit(solution)/shard_map/ppermute | solution.py:69
  12.6 7.4 %collective-permute-start.6 = (f32[2,4,2048]{2,1,0:T(4,128)S(1)}, f32[2,4,2048]{2,1,0:T(4,128)S(1)}, u32[]{:S(2)}, u32[]{:S(2)}) collective-permute-start(f32[2,4,2048]{2,1,0:T(4,128)S(1)} %get-tuple-element.47), channel_id=1, source_target_pairs={{0,6},{1,7},{2,4},{3,5},{4,2},{5,3},{6,0},{7,1},{8,14},{9,15},{10,... | collective-permute-start | bytes 196616 | tf_op jit(solution)/shard_map/ppermute | solution.py:69
  15.5 7.5 %collective-permute-start.10 = (f32[2,4,2048]{2,1,0:T(4,128)S(1)}, f32[2,4,2048]{2,1,0:T(4,128)S(1)}, u32[]{:S(2)}, u32[]{:S(2)}) collective-permute-start(f32[2,4,2048]{2,1,0:T(4,128)S(1)} %get-tuple-element.51), channel_id=1, source_target_pairs={{0,6},{1,7},{2,4},{3,5},{4,2},{5,3},{6,0},{7,1},{8,14},{9,15},{10,... | collective-permute-start | bytes 196616 | tf_op jit(solution)/shard_map/ppermute | solution.py:69
  19.2 5.3 %collective-permute-start.11 = (f32[2,4,2048]{2,1,0:T(4,128)S(1)}, f32[2,4,2048]{2,1,0:T(4,128)S(1)}, u32[]{:S(2)}, u32[]{:S(2)}) collective-permute-start(f32[2,4,2048]{2,1,0:T(4,128)S(1)} %get-tuple-element.52), channel_id=1, source_target_pairs={{0,4},{1,5},{2,6},{3,7},{4,0},{5,1},{6,2},{7,3},{8,12},{9,13},{10,... | collective-permute-start | bytes 196616 | tf_op jit(solution)/shard_map/ppermute | solution.py:69
  19.2 5.3 %collective-permute-start.12 = (f32[2,4,2048]{2,1,0:T(4,128)S(1)}, f32[2,4,2048]{2,1,0:T(4,128)S(1)}, u32[]{:S(2)}, u32[]{:S(2)}) collective-permute-start(f32[2,4,2048]{2,1,0:T(4,128)S(1)} %get-tuple-element.53), channel_id=1, source_target_pairs={{0,2},{1,3},{2,0},{3,1},{4,6},{5,7},{6,4},{7,5},{8,10},{9,11},{10,... | collective-permute-start | bytes 196616 | tf_op jit(solution)/shard_map/ppermute | solution.py:69
  20.2 8.5 %collective-permute-start.9 = (f32[288,128]{1,0:T(8,128)S(1)}, f32[288,128]{1,0:T(8,128)S(1)}, u32[]{:S(2)}, u32[]{:S(2)}) collective-permute-start(f32[288,128]{1,0:T(8,128)S(1)} %dense.1.refs_3_), channel_id=1, source_target_pairs={{0,24},{8,16},{16,8},{24,0},{1,25},{9,17},{17,9},{25,1},{2,26},{10... | collective-permute-start | bytes 442376 | tf_op jit(solution)/shard_map/ppermute | solution.py:69
  22.4 6.4 %collective-permute-start.8 = (f32[288,128]{1,0:T(8,128)S(1)}, f32[288,128]{1,0:T(8,128)S(1)}, u32[]{:S(2)}, u32[]{:S(2)}) collective-permute-start(f32[288,128]{1,0:T(8,128)S(1)} %dense.1.refs_3_), channel_id=1, source_target_pairs={{0,16},{8,24},{16,0},{24,8},{1,17},{9,25},{17,1},{25,9},{2,18},{10... | collective-permute-start | bytes 442376 | tf_op jit(solution)/shard_map/ppermute | solution.py:69
  23.0 5.9 %collective-permute-start.7 = (f32[288,128]{1,0:T(8,128)S(1)}, f32[288,128]{1,0:T(8,128)S(1)}, u32[]{:S(2)}, u32[]{:S(2)}) collective-permute-start(f32[288,128]{1,0:T(8,128)S(1)} %dense.1.refs_3_), channel_id=1, source_target_pairs={{0,8},{8,0},{16,24},{24,16},{1,9},{9,1},{17,25},{25,17},{2,10},{10... | collective-permute-start | bytes 442376 | tf_op jit(solution)/shard_map/ppermute | solution.py:69
  24.5 1.4 %collective-permute-start.13 = (f32[4,4,2048]{2,1,0:T(4,128)S(1)}, f32[4,4,2048]{2,1,0:T(4,128)S(1)}, u32[]{:S(2)}, u32[]{:S(2)}) collective-permute-start(f32[4,4,2048]{2,1,0:T(4,128)S(1)} %other.1), channel_id=1, source_target_pairs={{0,1},{1,0},{2,3},{3,2},{4,5},{5,4},{6,7},{7,6},{8,9},{9,8},{10,11... | collective-permute-start | bytes 393224 | tf_op jit(solution)/shard_map/ppermute | solution.py:69
  26.0 9.0 %copy-start.1 = (f32[200,1024]{1,0:T(8,128)S(1)}, f32[200,1024]{1,0:T(8,128)}, u32[]{:S(2)}) copy-start(f32[200,1024]{1,0:T(8,128)} %refs_0_.1) | copy-start | bytes 2457604
  26.0 5.6 %collective-permute-start.14 = (f32[4,8192]{1,0:T(4,128)S(1)}, f32[4,8192]{1,0:T(4,128)S(1)}, u32[]{:S(2)}, u32[]{:S(2)}) collective-permute-start(f32[4,8192]{1,0:T(4,128)S(1)} %get-tuple-element.55.refs_0_), channel_id=1, source_target_pairs={{0,8},{8,0},{16,24},{24,16},{1,9},{9,1},{17,25},{25,17},{2,10},{10... | collective-permute-start | bytes 393224 | tf_op jit(solution)/shard_map/ppermute | solution.py:69
  27.5 5.3 %collective-permute-start.17 = (f32[4,8192]{1,0:T(4,128)S(1)}, f32[4,8192]{1,0:T(4,128)S(1)}, u32[]{:S(2)}, u32[]{:S(2)}) collective-permute-start(f32[4,8192]{1,0:T(4,128)S(1)} %get-tuple-element.56.refs_1_), channel_id=1, source_target_pairs={{0,16},{8,24},{16,0},{24,8},{1,17},{9,25},{17,1},{25,9},{2,18},{10... | collective-permute-start | bytes 393224 | tf_op jit(solution)/shard_map/ppermute | solution.py:69
  28.9 2.2 %collective-permute-start.18 = (f32[248,128]{1,0:T(8,128)S(1)}, f32[248,128]{1,0:T(8,128)S(1)}, u32[]{:S(2)}, u32[]{:S(2)}) collective-permute-start(f32[248,128]{1,0:T(8,128)S(1)} %gathered.1), channel_id=1, source_target_pairs={{0,1},{1,0},{2,3},{3,2},{4,5},{5,4},{6,7},{7,6},{8,9},{9,8},{10,11... | collective-permute-start | bytes 380936 | tf_op jit(solution)/shard_map/ppermute | solution.py:69
  29.0 5.9 %copy-start.2 = (f32[1024,64]{0,1:T(8,128)S(1)}, f32[1024,64]{0,1:T(8,128)}, u32[]{:S(2)}) copy-start(f32[1024,64]{0,1:T(8,128)} %param.15) | copy-start | bytes 786436
  29.0 7.4 %collective-permute-start.15 = (f32[4,8320]{1,0:T(4,128)S(1)}, f32[4,8320]{1,0:T(4,128)S(1)}, u32[]{:S(2)}, u32[]{:S(2)}) collective-permute-start(f32[4,8320]{1,0:T(4,128)S(1)} %get-tuple-element.57), channel_id=1, source_target_pairs={{0,8},{8,0},{16,24},{24,16},{1,9},{9,1},{17,25},{25,17},{2,10},{10... | collective-permute-start | bytes 399368 | tf_op jit(solution)/shard_map/ppermute | solution.py:69
  30.5 4.4 %copy-start.4 = (f32[200,64]{0,1:T(8,128)S(1)}, f32[200,64]{0,1:T(8,128)}, u32[]{:S(2)}) copy-start(f32[200,64]{0,1:T(8,128)} %param.14) | copy-start | bytes 153604
  30.5 6.4 %copy-start = (f32[4,65536]{1,0:T(4,128)S(1)}, f32[4,65536]{1,0:T(4,128)}, u32[]{:S(2)}) copy-start(f32[4,65536]{1,0:T(4,128)} %momentum.3) | copy-start | bytes 3145732
  30.5 6.4 %collective-permute-start.16 = (f32[4,8320]{1,0:T(4,128)S(1)}, f32[4,8320]{1,0:T(4,128)S(1)}, u32[]{:S(2)}, u32[]{:S(2)}) collective-permute-start(f32[4,8320]{1,0:T(4,128)S(1)} %get-tuple-element.58), channel_id=1, source_target_pairs={{0,16},{8,24},{16,0},{24,8},{1,17},{9,25},{17,1},{25,9},{2,18},{10... | collective-permute-start | bytes 399368 | tf_op jit(solution)/shard_map/ppermute | solution.py:69
  32.8 6.2 %collective-permute-start.19 = (f32[4,8192]{1,0:T(4,128)S(1)}, f32[4,8192]{1,0:T(4,128)S(1)}, u32[]{:S(2)}, u32[]{:S(2)}) collective-permute-start(f32[4,8192]{1,0:T(4,128)S(1)} %get-tuple-element.59), channel_id=1, source_target_pairs={{0,16},{8,24},{16,0},{24,8},{1,17},{9,25},{17,1},{25,9},{2,18},{10... | collective-permute-start | bytes 393224 | tf_op jit(solution)/shard_map/ppermute | solution.py:69
  34.0 5.0 %collective-permute-start.20 = (f32[4,8192]{1,0:T(4,128)S(1)}, f32[4,8192]{1,0:T(4,128)S(1)}, u32[]{:S(2)}, u32[]{:S(2)}) collective-permute-start(f32[4,8192]{1,0:T(4,128)S(1)} %get-tuple-element.60), channel_id=1, source_target_pairs={{0,8},{8,0},{16,24},{24,16},{1,9},{9,1},{17,25},{25,17},{2,10},{10... | collective-permute-start | bytes 393224 | tf_op jit(solution)/shard_map/ppermute | solution.py:69
  36.9 0.8 %copy-start.3 = (f32[64,200]{1,0:T(8,128)S(1)}, f32[64,200]{1,0:T(8,128)}, u32[]{:S(2)}) copy-start(f32[64,200]{1,0:T(8,128)} %get-tuple-element.50._) | copy-start | bytes 153604

commit v6 on v5

v6 whole, which is shorter than its diff:
```python
import functools

import jax
import jax.numpy as jnp
from jax import lax
from jax.experimental import pallas as pl
from jax.experimental.pallas import tpu as pltpu
from jax.sharding import PartitionSpec as P

outer_rate = 0.7
momentum_decay = 0.9
most_direct_chips = 8
f32 = jnp.float32
vmem_limit = 48 * 1024 * 1024

vmem = pl.BlockSpec(memory_space=pltpu.VMEM)
smem = pl.BlockSpec(memory_space=pltpu.SMEM)
anywhere = pl.BlockSpec(memory_space=pl.ANY)


def on_chip(x):
    return pltpu.with_memory_space_constraint(x, pltpu.VMEM)


def in_scalars(x):
    return pltpu.with_memory_space_constraint(x, pltpu.SMEM)


def in_hbm(x):
    return pltpu.with_memory_space_constraint(x, pltpu.HBM)


def kept(shape):
    return pltpu.VMEM(shape, f32)


def stored(shape):
    return jax.ShapeDtypeStruct(shape, f32)


def run(
    body, outs, operands, scalars=(), scratch=(), far=(), after=(), out_specs=None, name=None
):
    skip = len(after)

    def whole(*refs):
        body(*refs[skip:])

    return pl.pallas_call(
        whole,
        out_shape=list(outs),
        in_specs=[anywhere] * skip
        + [smem] * len(scalars)
        + [anywhere] * len(far)
        + [vmem] * len(operands),
        out_specs=out_specs or [vmem] * len(outs),
        scratch_shapes=list(scratch),
        compiler_params=pltpu.CompilerParams(vmem_limit_bytes=vmem_limit),
        name=name,
    )(
        *[on_chip(x) for x in after],
        *[in_scalars(x) for x in scalars],
        *[in_hbm(x) for x in far],
        *[on_chip(x) for x in operands],
    )


def swap(x, axis, count, mask):
    return lax.ppermute(x, axis, [(i, i ^ mask) for i in range(count)])


def place():
    position = lax.axis_index("own")
    return lax.axis_index("rep"), lax.shift_right_logical(position, 1), position & 1


def column(index, part):
    return pl.ds(pl.multiple_of(index * part, 128), part)


def tiles(rows, columns):
    return [
        (i, min(8, rows - i), j, min(128, columns - j))
        for i in range(0, rows, 8)
        for j in range(0, columns, 128)
    ]


def two_parts(x):
    high = x.astype(jnp.bfloat16)
    return high, (x - high.astype(f32)).astype(jnp.bfloat16)


def dot(a, b, contract):
    return lax.dot_general(a, b, (contract, ((), ())), preferred_element_type=f32)


def name_places(slots, owners, row_of, block_of, owned):
    blocks, owner_count = row_of.shape[0], owned.shape[0]

    def clear(i, carry):
        block_of[i] = 0
        return carry

    def clear_count(i, carry):
        owned[i] = 0
        return carry

    def name(u, carry):
        owner = owners[u]
        slot = owned[owner]
        row = owner * slots + slot
        row_of[u] = row
        block_of[row] = u
        owned[owner] = slot + 1
        return carry

    short = blocks <= 16
    lax.fori_loop(0, block_of.shape[0], clear, 0, unroll=short)
    lax.fori_loop(0, owner_count, clear_count, 0, unroll=short)
    lax.fori_loop(0, blocks, name, 0, unroll=short)


def start_body(groups, part, owners, anchor, inner, momentum, *refs):
    outs, (quarter, same, other), named, scratch = (
        refs[:groups],
        refs[groups : groups + 3],
        refs[groups + 3 : groups + 6],
        refs[groups + 6 :],
    )
    own, far, near, sem, piece_sem = scratch
    rep, chip, core = place()
    blocks = quarter.shape[0]
    chips = same.shape[0]
    listed = pltpu.make_async_copy(owners, own, sem.at[2])
    listed.start()
    dense_moves = [
        pltpu.make_async_copy(anchor, far, sem.at[0]),
        pltpu.make_async_copy(inner.at[0], near, sem.at[1]),
    ]
    for move in dense_moves:
        move.start()
    pieces = [
        pltpu.make_async_copy(
            momentum.at[:, column((2 * to + (core ^ o)) * groups + rep, part)],
            out.at[to],
            piece_sem.at[2 * to + o],
        )
        for to in range(chips)
        for o, out in enumerate((same, other))
    ]
    for piece in pieces:
        piece.start()
    listed.wait()
    name_places(same.shape[1], own, *named)
    dense_tiles = tiles(blocks, part)
    for move in dense_moves:
        move.wait()
    for k in range(groups):
        for t, (i, height, j, width) in enumerate(dense_tiles):
            columns = pl.ds(pl.multiple_of((rep ^ k) * part + j, 128), width)
            rows = slice(i, i + height)
            outs[k][8 * t : 8 * t + height, :width] = far[rows, columns] - near[rows, columns]
            if k == 0:
                quarter[rows, j : j + width] = far[rows, columns]
    for piece in pieces:
        piece.wait()


def factor_body(anchor, inner, basis_t, out):
    rank = out.shape[0]
    high, low = two_parts(anchor[...] - inner[0])
    basis_high, basis_low = two_parts(basis_t[...])
    both = dot(jnp.concatenate([basis_high, basis_low], axis=0), high, ((1,), (1,)))
    out[...] = both[:rank] + (both[rank:] + dot(basis_high, low, ((1,), (1,))))


def mean_body(groups, direct, block_of, *refs):
    parts, (mean, *outs) = refs[:groups], refs[groups:]
    _, here, core = place()
    dense_tiles = tiles(*mean.shape)
    for t, (i, height, j, width) in enumerate(dense_tiles):
        at = slice(8 * t, 8 * t + height)
        total = parts[0][at, :width]
        for ref in parts[1:]:
            total = total + ref[at, :width]
        mean[i : i + height, j : j + width] = total / groups
    slots = outs[0].shape[-2]

    def fill(k, carry):
        for o in range(2):
            owner = 2 * (here ^ k if direct else k) + (core ^ o)
            for s in range(slots):
                row = mean[pl.ds(block_of[owner * slots + s], 1), :]
                if direct:
                    outs[k][o, pl.ds(s, 1), :] = row
                else:
                    outs[0][k, o, pl.ds(s, 1), :] = row
        return carry

    if direct:
        for k in range(len(outs)):
            fill(k, 0)
    else:
        lax.fori_loop(0, outs[0].shape[0], fill, 0)


def pack_body(direct, same, other, *outs):
    _, chip, _ = place()
    if direct:
        for k, out in enumerate(outs):
            out[0] = same[chip ^ k]
            out[1] = other[chip ^ k]
    else:
        outs[0][:, 0] = same[...]
        outs[0][:, 1] = other[...]


def rows_body(direct, core, *refs):
    *received, out = refs
    chips = len(received) if direct else received[0].shape[0]
    part = received[0].shape[-1]

    def fill(k, carry):
        out[:, column(k, part)] = received[k][core] if direct else received[0][k, core]
        return carry

    if direct:
        for k in range(chips):
            fill(k, 0)
    else:
        lax.fori_loop(0, chips, fill, 0)
    spare = out.shape[1] - chips * part
    out[:, chips * part :] = jnp.zeros((out.shape[0], spare), f32)


def cut_body(ref, out):
    out[...] = ref[: out.shape[0], :]


def fold(tile, out, lane):
    for h in range(0, tile.shape[0], 4):
        out[:, lane + 32 * h : lane + 32 * h + tile.shape[1]] = tile[h : h + 4, :]


def unfold(ref, lane, height, width):
    runs = [ref[:, lane + 32 * h : lane + 32 * h + width] for h in range(0, height, 4)]
    return jnp.concatenate(runs, axis=0)


def again_body(skip, first, second, factor, received1, received2, out1, out2, pair):
    out1[:, :skip] = first[:, :skip]
    out2[:, :skip] = second[:, :skip]
    factor_tiles = tiles(*factor.shape)
    at = received2.shape[0] - 8 * len(factor_tiles)
    count = at // 16
    for t in range(count):
        fold(received1[8 * t : 8 * t + 8, :], out1, skip + 256 * t)
        fold(received2[8 * (count + t) : 8 * (count + t) + 8, :], out2, skip + 256 * t)
    skip += 256 * count
    for t, (i, height, j, width) in enumerate(factor_tiles):
        total = factor[i : i + height, j : j + width] + received2[at : at + height, :width]
        pair[i : i + height, j : j + width] = total
        fold(total, out2, skip + 256 * t)
        at += 8


def copies_body(*refs):
    count = len(refs) // 2
    for ref, out in zip(refs[:count], refs[count:]):
        out[...] = ref[:, : out.shape[1]]


def dense_body(direct, row_of, quarter, mean, factor, *refs):
    *received, plain, with_factor, rows, work = refs
    _, here, core = place()
    slots = received[0].shape[-2]
    blocks = mean.shape[0]
    if direct:
        for k, ref in enumerate(received):
            rows[k] = ref[...]
        table = rows
    else:
        table = received[0]

    def update(block, carry):
        row = row_of[block]
        owner = row // slots
        chip = (owner // 2) ^ here if direct else owner // 2
        momentum = table[chip, (owner % 2) ^ core, pl.ds(row % slots, 1), :]
        mean_row = mean[pl.ds(block, 1), :]
        new_momentum = momentum_decay * momentum + mean_row
        work[pl.ds(block, 1), :] = quarter[pl.ds(block, 1), :] - outer_rate * (
            mean_row + momentum_decay * new_momentum
        )
        return carry

    lax.fori_loop(0, blocks, update, 0, unroll=blocks <= 16)
    dense_tiles = tiles(*work.shape)
    for t, (i, height, j, width) in enumerate(dense_tiles):
        tile = work[i : i + height, j : j + width]
        plain[8 * t : 8 * t + height, :width] = tile
        with_factor[8 * t : 8 * t + height, :width] = tile
    skip = 8 * len(dense_tiles)
    plain[skip:, :] = jnp.zeros((plain.shape[0] - skip, 128), f32)
    for t, (i, height, j, width) in enumerate(tiles(*factor.shape)):
        at = slice(skip + 8 * t, skip + 8 * t + height)
        with_factor[at, :width] = factor[i : i + height, j : j + width]


class Pieces:
    def __init__(self, part, direct, members, owned, momentum, gradient, result, made, sem):
        self.part, self.direct, self.members = part, direct, members
        self.momentum, self.gradient, self.result = momentum, gradient, result
        self.made, self.sem = made, sem
        self.pieces = made.shape[1]
        self.groups = momentum.shape[1] // part // self.pieces
        self.rep, self.here, self.core = place()
        rows = lax.broadcasted_iota(jnp.int32, (momentum.shape[0], part), 0)
        self.live = rows < owned[self.here * 2 + self.core]
        self.short = self.pieces <= 16

    def move(self, n, g, i):
        half = self.pieces // 2
        k, o = i % half, i // half
        piece = 2 * (self.here ^ k if self.direct else k) + (self.core ^ o)
        at = column(piece * self.groups + (self.rep ^ g), self.part)
        target = self.result.at[:, at]
        return at, pltpu.make_async_copy(self.made.at[n, i], target, self.sem.at[n, i])

    def fill(self, h, i, carry):
        half = self.pieces // 2
        for n, g in enumerate(self.members):
            at, copy = self.move(n, g, i + h * half)
            received = self.gradient[2 * n + h][:, column(i, self.part)]
            rows = momentum_decay * self.momentum[:, at] + received
            self.made[n, i + h * half] = jnp.where(self.live, rows, 0.0)
            copy.start()
        return carry

    def wait(self, i, carry):
        for n, g in enumerate(self.members):
            self.move(n, g, i)[1].wait()
        return carry

    def make(self):
        for h in range(2):
            body = functools.partial(self.fill, h)
            lax.fori_loop(0, self.pieces // 2, body, 0, unroll=self.short)

    def finish(self):
        lax.fori_loop(0, self.pieces, self.wait, 0, unroll=self.short)


def finish_body(part, direct, groups, owned, anchor, momentum_t, basis_t, momentum, *refs):
    parts, pair, gradient = refs[: groups - 1], refs[groups - 1], refs[groups : 3 * groups - 2]
    refs = refs[3 * groups - 2 :]
    result0, result1, result2, result3, mean, sem, made, made_sem, *whole = refs
    new_dense, new_emb, new_momentum_t = whole
    copies = [
        pltpu.make_async_copy(ref, result, sem.at[i])
        for i, (ref, result) in enumerate(
            ((new_dense, result0), (new_emb, result1), (new_momentum_t, result2))
        )
    ]
    rep, _, _ = place()
    blocks, (rank, rows) = new_dense.shape[0], mean.shape
    dense_tiles = tiles(blocks, part)
    skip = gradient[3].shape[1] - 256 * len(tiles(rank, rows))
    for t, (i, height, j, width) in enumerate(tiles(rank, rows)):
        here = (slice(i, i + height), slice(j, j + width))
        mean[here] = (pair[here] + unfold(gradient[3], skip + 256 * t, height, width)) / groups
    moved = momentum_decay * momentum_t[...] + mean[...]
    new_momentum_t[...] = moved
    copies[2].start()
    high, low = two_parts(mean[...] + momentum_decay * moved)
    basis_high, basis_low = two_parts(basis_t[...])
    back = dot(
        jnp.concatenate([high, low, high], axis=0),
        jnp.concatenate([basis_high, basis_high, basis_low], axis=0),
        ((0,), (0,)),
    )
    new_emb[...] = anchor[...] - outer_rate * back
    copies[1].start()

    count = len(dense_tiles) // 2
    skip = gradient[4].shape[1] - 256 * count
    for k in range(groups):
        for t, (i, height, j, width) in enumerate(dense_tiles):
            at = pl.multiple_of((rep ^ k) * part + j, 128)
            if k < len(parts):
                tile = parts[k][8 * t : 8 * t + height, :width]
            else:
                ref = gradient[4] if t < count else gradient[3]
                tile = unfold(ref, skip + 256 * (t % count), height, width)
            new_dense[i : i + height, pl.ds(at, width)] = tile
    copies[0].start()

    members = tuple(range(groups - 1))
    pieces = Pieces(part, direct, members, owned, momentum, gradient, result3, made, made_sem)
    pieces.make()
    pieces.finish()
    for copy in copies:
        copy.wait()


def finish_momentum_body(part, direct, members, owned, _, momentum, *refs):
    *gradient, result, made, sem = refs
    pieces = Pieces(part, direct, members, owned, momentum, gradient, result, made, sem)
    pieces.make()
    pieces.finish()


def over_chips(outs, direct, owner_count):
    if direct:
        return [outs[0]] + [swap(outs[k], "own", owner_count, 2 * k) for k in range(1, len(outs))]
    groups = [list(range(core, owner_count, 2)) for core in range(2)]
    return [
        lax.all_to_all(
            outs[0], "own", split_axis=0, concat_axis=0, axis_index_groups=groups, tiled=True
        )
    ]


def per_device(
    owners, inner_dense, anchor_dense, momentum_dense, inner_emb, anchor_emb, momentum_emb, basis
):
    owner_count = lax.axis_size("own")
    groups = lax.axis_size("rep")
    chips = owner_count // 2
    direct = chips <= most_direct_chips
    slot_count = momentum_dense.shape[0]
    blocks, piece_len = anchor_dense.shape
    part = piece_len // groups
    rows, rank = momentum_emb.shape
    basis_t = basis.T
    chunk = (chips, slot_count, part)
    table = (chips, 2, slot_count, part)
    parted = [kept(table[1:])] * chips if direct else [kept(table)]

    *parts, quarter, same, other, row_of, block_of, owned = run(
        functools.partial(start_body, groups, part),
        [kept((8 * len(tiles(blocks, part)), 128))] * groups
        + [kept((blocks, part))]
        + [kept(chunk)] * 2
        + [pltpu.SMEM((n,), jnp.int32) for n in (blocks, owner_count * slot_count, owner_count)],
        [],
        far=[
            owners[:, 0],
            anchor_dense,
            inner_dense,
            momentum_dense,
        ],
        out_specs=[vmem] * (groups + 3) + [smem] * 3,
        scratch=[
            pltpu.SMEM((blocks,), jnp.int32),
            pltpu.VMEM(anchor_dense.shape, f32),
            pltpu.VMEM(anchor_dense.shape, f32),
            pltpu.SemaphoreType.DMA((3,)),
            pltpu.SemaphoreType.DMA((owner_count,)),
        ],
        name="start",
    )
    parts = [parts[0]] + [swap(parts[k], "rep", groups, k) for k in range(1, groups)]

    other = swap(other, "own", owner_count, 1)
    packed = run(functools.partial(pack_body, direct), parted, [same, other], name="pack")
    momentum_rows = over_chips(packed, direct, owner_count)

    (factor,) = run(
        factor_body, [kept((rank, rows))], [anchor_emb, inner_emb, basis_t], name="factor"
    )
    mean, *sent = run(
        functools.partial(mean_body, groups, direct),
        [kept((blocks, part))] + parted,
        parts,
        [block_of],
        after=[factor],
        name="mean",
    )
    gradient_rows = over_chips(sent, direct, owner_count)
    length = chips * part
    (other,) = run(
        functools.partial(rows_body, direct, 1),
        [kept((slot_count, length + 256))],
        gradient_rows,
        after=[gradient_rows[k] for k in (3, 2, 1)] if direct else (),
        name="other",
    )
    (mine,) = run(
        functools.partial(rows_body, direct, 0),
        [kept((slot_count, length + 512))],
        gradient_rows,
        after=[gradient_rows[k] for k in (3, 2, 1)] if direct else (),
        name="mine",
    )
    halves = [mine, swap(other, "own", owner_count, 1)]

    momentum = on_chip(momentum_dense)
    dense_rows = 8 * len(tiles(blocks, part))
    plain, with_factor = run(
        functools.partial(dense_body, direct),
        [kept((dense_rows + 16, 128)), kept((dense_rows + 8 * len(tiles(rank, rows)), 128))],
        [quarter, mean, factor, *momentum_rows],
        [row_of],
        [
            pltpu.VMEM(table if direct else (8, 128), f32),
            pltpu.VMEM((blocks, part), f32),
        ],
        after=[*momentum_rows[:0:-1], momentum],
        name="dense",
    )
    dense = [plain, swap(plain, "rep", groups, 1), swap(with_factor, "rep", groups, 2)]

    passed_on = 16 * dense_rows
    *again, pair = run(
        functools.partial(again_body, length),
        [
            kept((slot_count, length + passed_on)),
            kept((slot_count, length + passed_on + 256 * len(tiles(rank, rows)))),
            kept((rank, rows)),
        ],
        [*halves, factor, dense[1], dense[2]],
        name="again",
    )
    (sign,) = run(
        cut_body, [kept((260, 128))], [plain], after=[dense[k] for k in (2, 1)], name="gathered"
    )
    sign = swap(sign, "own", owner_count, 1)
    near1 = swap(halves[0], "rep", groups, 1)
    near2 = swap(halves[1], "rep", groups, 2)
    passed = run(
        copies_body,
        [kept((slot_count, length))] * 2,
        [near1, near2],
        after=[sign],
        name="pass_on",
    )
    gradient = [
        *halves,
        near1,
        swap(again[1], "rep", groups, 1),
        swap(again[0], "rep", groups, 2),
        near2,
        swap(passed[0], "rep", groups, 2),
        swap(passed[1], "rep", groups, 1),
    ]

    made = [
        pltpu.VMEM((n, owner_count, slot_count, part), f32) for n in (groups - 1, 1)
    ]
    made_sems = [pltpu.SemaphoreType.DMA((n, owner_count)) for n in (groups - 1, 1)]
    shapes = [anchor_dense.shape, anchor_emb.shape, (rank, rows)]
    new_dense, new_emb, new_momentum_t, first_columns = run(
        functools.partial(finish_body, part, direct, groups),
        [stored(shape) for shape in (*shapes, momentum_dense.shape)],
        [
            anchor_emb,
            momentum_emb.T,
            basis_t,
            momentum,
            *dense,
            pair,
            *gradient[: 2 * groups - 2],
        ],
        [owned],
        out_specs=[anywhere] * 4,
        scratch=[
            pltpu.VMEM((rank, rows), f32),
            pltpu.SemaphoreType.DMA((3,)),
            made[0],
            made_sems[0],
        ]
        + [pltpu.VMEM(shape, f32) for shape in shapes],
        name="finish",
    )
    (new_momentum_dense,) = pl.pallas_call(
        functools.partial(finish_momentum_body, part, direct, (groups - 1,)),
        out_shape=[stored(momentum_dense.shape)],
        in_specs=[smem, anywhere] + [vmem] * 3,
        out_specs=[anywhere],
        scratch_shapes=[made[1], made_sems[1]],
        input_output_aliases={1: 0},
        compiler_params=pltpu.CompilerParams(vmem_limit_bytes=vmem_limit),
        name="finish_momentum",
    )(
        in_scalars(owned),
        first_columns,
        on_chip(momentum),
        *[on_chip(x) for x in gradient[2 * groups - 2 :]],
    )
    return (new_dense, new_momentum_dense, new_emb, new_momentum_t.T)


def solution(mesh):
    placed = (
        P(),
        P("rep", None, "own"),
        P(None, "own"),
        P("own", None),
        P("rep", "own", None),
        P("own", None),
        P("own", None),
        P(),
    )
    return jax.shard_map(
        per_device,
        mesh=mesh,
        in_specs=placed,
        out_specs=(P(None, "own"), P("own", None), P("own", None), P("own", None)),
        check_vma=False,
    )
```

time: 39.9 us -> 38.5 us (0.965)
  waiting for transfers between devices: 4.87 us -> 9.01 us
  starting transfers between devices: 26.9 us -> 23.2 us
  Pallas kernels: 6.37 us -> 5.35 us
  local copies, waits for them, and re-layouts: 0.86 us -> 0.02 us
    ppermute x21 -> x20, waiting for transfers between devices: 4.87 us -> 9.01 us  [swap(): return lax.ppermute(x, axis, [(i, i ^ mask) for i in range(count)])]
    ppermute x21 -> x20, starting transfers between devices: 26.9 us -> 23.2 us  [swap(): return lax.ppermute(x, axis, [(i, i ^ mask) for i in range(count)])]
    pallas_call x2 -> x1, Pallas kernels: 1.92 us -> 0.77 us  [per_device(): pl.pallas_call(functools.partial(finish_momentum_body, part, direct, (gro...]
    unnamed x10, local copies, waits for them, and re-layouts: 0.86 us -> 0.02 us
    pallas_call x10 -> x11, Pallas kernels: 4.45 us -> 4.57 us  [run(): pl.pallas_call(whole, out_shape=list(outs), in_specs=[anywhere] * skip +...]
  transfers between devices with their start and end apart: 21 -> 20, of which waited for: 9 -> 8; matrix products, arithmetic and copies ran while one was open for 0% -> 0% of each run, Pallas kernels for 8% -> 8%
where the time goes in v6:
time: 38.5 us; the launch traced here: 38.4 us
  starting transfers between devices  23.2 us (60%)
  waiting for transfers between devices  9.01 us (23%)
  Pallas kernels  5.35 us (14%)
  between operations  0.77 us (2%)
    ppermute x20, starting transfers between devices, swap(): return lax.ppermute(x, axis, [(i, i ^ mask) for i in range(count)])  23.2 us
    ppermute x20, waiting for transfers between devices, swap(): return lax.ppermute(x, axis, [(i, i ^ mask) for i in range(count)])  9.01 us
    pallas_call x11, Pallas kernels, run(): pl.pallas_call(whole, out_shape=list(outs), in_specs=[anywhere] * skip +...  4.57 us
    pallas_call x1, Pallas kernels, per_device(): pl.pallas_call(functools.partial(finish_momentum_body, part, direct, (gro...  0.77 us
  transfers between devices with their start and end apart: 20, of which 8 were waited for; matrix products, arithmetic and copies ran while one was open for 0% of the time, Pallas kernels for 8%

profile of v6, /device:TPU:0, one launch (start us, length us, event | category | flops | bytes accessed | tf_op | source)
XLA Modules:
  0.0 38.4 jit_solution(15841045522965914927)
XLA Ops:
  0.7 1.7 %start.1 = (f32[256,128]{1,0:T(8,128)S(1)}, f32[256,128]{1,0:T(8,128)S(1)}, f32[256,128]{1,0:T(8,128)S(1)}, f32[256,128]{1,0:T(8,128)S(1)}, f32[16,2048]{1,0:T(8...) custom-call(s32[16]{0:T(128)} %bitcast.7, ...), custom_call_target="tpu_custom_call" | custom-call | tf_op jit(solution)/shard_map/start/pallas_call | solution.py:49
  2.4 0.5 %collective-permute-start = (f32[4,4,2048]{2,1,0:T(4,128)S(1)}, f32[4,4,2048]{2,1,0:T(4,128)S(1)}, u32[]{:S(2)}, u32[]{:S(2)}) collective-permute-start(f32[4,4,2048]{2,1,0:T(4,128)S(1)} %get-tuple-element.36), channel_id=1, source_target_pairs={{0,1},{1,0},{2,3},{3,2},{4,5},{5,4},{6,7},{7,6},{8,9},{9,8},{10,11... | collective-permute-start | bytes 393224 | tf_op jit(solution)/shard_map/ppermute | solution.py:69
  2.9 2.6 %collective-permute-start.4 = (f32[256,128]{1,0:T(8,128)S(1)}, f32[256,128]{1,0:T(8,128)S(1)}, u32[]{:S(2)}, u32[]{:S(2)}) collective-permute-start(f32[256,128]{1,0:T(8,128)S(1)} %get-tuple-element.44), channel_id=1, source_target_pairs={{0,8},{8,0},{16,24},{24,16},{1,9},{9,1},{17,25},{25,17},{2,10},{10... | collective-permute-start | bytes 393224 | tf_op jit(solution)/shard_map/ppermute | solution.py:69
  5.4 1.5 %collective-permute-start.5 = (f32[256,128]{1,0:T(8,128)S(1)}, f32[256,128]{1,0:T(8,128)S(1)}, u32[]{:S(2)}, u32[]{:S(2)}) collective-permute-start(f32[256,128]{1,0:T(8,128)S(1)} %get-tuple-element.45), channel_id=1, source_target_pairs={{0,16},{8,24},{16,0},{24,8},{1,17},{9,25},{17,1},{25,9},{2,18},{10... | collective-permute-start | bytes 393224 | tf_op jit(solution)/shard_map/ppermute | solution.py:69
  7.0 4.1 %collective-permute-start.1 = (f32[2,4,2048]{2,1,0:T(4,128)S(1)}, f32[2,4,2048]{2,1,0:T(4,128)S(1)}, u32[]{:S(2)}, u32[]{:S(2)}) collective-permute-start(f32[2,4,2048]{2,1,0:T(4,128)S(1)} %get-tuple-element.37), channel_id=1, source_target_pairs={{0,6},{1,7},{2,4},{3,5},{4,2},{5,3},{6,0},{7,1},{8,14},{9,15},{10,... | collective-permute-start | bytes 196616 | tf_op jit(solution)/shard_map/ppermute | solution.py:69
  11.1 0.6 %collective-permute-start.3 = (f32[2,4,2048]{2,1,0:T(4,128)S(1)}, f32[2,4,2048]{2,1,0:T(4,128)S(1)}, u32[]{:S(2)}, u32[]{:S(2)}) collective-permute-start(f32[2,4,2048]{2,1,0:T(4,128)S(1)} %get-tuple-element.39), channel_id=1, source_target_pairs={{0,2},{1,3},{2,0},{3,1},{4,6},{5,7},{6,4},{7,5},{8,10},{9,11},{10,... | collective-permute-start | bytes 196616 | tf_op jit(solution)/shard_map/ppermute | solution.py:69
  11.8 0.4 %factor.1.refs_0_.refs_7_.refs_2_ = f32[64,200]{1,0:T(8,128)S(1)} custom-call(f32[200,1024]{1,0:T(8,128)S(1)} %copy-done.1, f32[1,200,1024]{2,1,0:T(8,128)S(1)} %copy-done.3, f32[64,1024]{1,0:T(8,128)S(1)} %bitcast.4), custom_call_target="tpu_custom_call" | custom-call | tf_op jit(solution)/shard_map/factor/pallas_call | solution.py:49
  12.2 1.6 %collective-permute-done.5.refs_4_ = f32[256,128]{1,0:T(8,128)S(1)} collective-permute-done((f32[256,128]{1,0:T(8,128)S(1)}, f32[256,128]{1,0:T(8,128)S(1)}, u32[]{:S(2)}, u32[]{:S(2)}) %collective-permute-start.5) | collective-permute-done | bytes 131104 | tf_op jit(solution)/shard_map/ppermute | solution.py:69
  13.8 0.1 mean.1
  13.9 3.7 %collective-permute-start.9 = (f32[2,4,2048]{2,1,0:T(4,128)S(1)}, f32[2,4,2048]{2,1,0:T(4,128)S(1)}, u32[]{:S(2)}, u32[]{:S(2)}) collective-permute-start(f32[2,4,2048]{2,1,0:T(4,128)S(1)} %get-tuple-element.51), channel_id=1, source_target_pairs={{0,6},{1,7},{2,4},{3,5},{4,2},{5,3},{6,0},{7,1},{8,14},{9,15},{10,... | collective-permute-start | bytes 196616 | tf_op jit(solution)/shard_map/ppermute | solution.py:69
  17.6 0.8 %collective-permute-start.11 = (f32[2,4,2048]{2,1,0:T(4,128)S(1)}, f32[2,4,2048]{2,1,0:T(4,128)S(1)}, u32[]{:S(2)}, u32[]{:S(2)}) collective-permute-start(f32[2,4,2048]{2,1,0:T(4,128)S(1)} %get-tuple-element.53), channel_id=1, source_target_pairs={{0,2},{1,3},{2,0},{3,1},{4,6},{5,7},{6,4},{7,5},{8,10},{9,11},{10,... | collective-permute-start | bytes 196616 | tf_op jit(solution)/shard_map/ppermute | solution.py:69
  18.4 0.3 dense.1
  18.7 1.6 %collective-permute-start.8 = (f32[384,128]{1,0:T(8,128)S(1)}, f32[384,128]{1,0:T(8,128)S(1)}, u32[]{:S(2)}, u32[]{:S(2)}) collective-permute-start(f32[384,128]{1,0:T(8,128)S(1)} %get-tuple-element.50), channel_id=1, source_target_pairs={{0,16},{8,24},{16,0},{24,8},{1,17},{9,25},{17,1},{25,9},{2,18},{10... | collective-permute-start | bytes 589832 | tf_op jit(solution)/shard_map/ppermute | solution.py:69
  20.3 0.5 %collective-permute-start.7 = (f32[272,128]{1,0:T(8,128)S(1)}, f32[272,128]{1,0:T(8,128)S(1)}, u32[]{:S(2)}, u32[]{:S(2)}) collective-permute-start(f32[272,128]{1,0:T(8,128)S(1)} %get-tuple-element.49.refs_5_.refs_2_), channel_id=1, source_target_pairs={{0,8},{8,0},{16,24},{24,16},{1,9},{9,1},{17,25},{25,17},{2,10},{10... | collective-permute-start | bytes 417800 | tf_op jit(solution)/shard_map/ppermute | solution.py:69
  20.8 2.1 %collective-permute-done.10.refs_1_.refs_5_ = f32[2,4,2048]{2,1,0:T(4,128)S(1)} collective-permute-done((f32[2,4,2048]{2,1,0:T(4,128)S(1)}, f32[2,4,2048]{2,1,0:T(4,128)S(1)}, u32[]{:S(2)}, u32[]{:S(2)}) %collective-permute-start.10) | collective-permute-done | bytes 65568 | tf_op jit(solution)/shard_map/ppermute | solution.py:69
  22.9 0.1 collective-permute-start.12
  23.0 1.6 %collective-permute-start.13 = (f32[4,8704]{1,0:T(4,128)S(1)}, f32[4,8704]{1,0:T(4,128)S(1)}, u32[]{:S(2)}, u32[]{:S(2)}) collective-permute-start(f32[4,8704]{1,0:T(4,128)S(1)} %mine.1.refs_0_.refs_9_), channel_id=1, source_target_pairs={{0,8},{8,0},{16,24},{24,16},{1,9},{9,1},{17,25},{25,17},{2,10},{10... | collective-permute-start | bytes 417800 | tf_op jit(solution)/shard_map/ppermute | solution.py:69
  24.6 1.3 %collective-permute-start.16 = (f32[4,8448]{1,0:T(4,128)S(1)}, f32[4,8448]{1,0:T(4,128)S(1)}, u32[]{:S(2)}, u32[]{:S(2)}) collective-permute-start(f32[4,8448]{1,0:T(4,128)S(1)} %collective-permute-done.12.refs_1_.refs_10_), channel_id=1, source_target_pairs={{0,16},{8,24},{16,0},{24,8},{1,17},{9,25},{17,1},{25,9},{2,18},{10... | collective-permute-start | bytes 405512 | tf_op jit(solution)/shard_map/ppermute | solution.py:69
  25.9 0.1 collective-permute-start.17
  26.0 0.1 again.1
  26.0 0.8 %collective-permute-start.14 = (f32[4,16384]{1,0:T(4,128)S(1)}, f32[4,16384]{1,0:T(4,128)S(1)}, u32[]{:S(2)}, u32[]{:S(2)}) collective-permute-start(f32[4,16384]{1,0:T(4,128)S(1)} %get-tuple-element.56), channel_id=1, source_target_pairs={{0,8},{8,0},{16,24},{24,16},{1,9},{9,1},{17,25},{25,17},{2,10},{10... | collective-permute-start | bytes 786440 | tf_op jit(solution)/shard_map/ppermute | solution.py:69
  26.9 1.2 %collective-permute-start.15 = (f32[4,12288]{1,0:T(4,128)S(1)}, f32[4,12288]{1,0:T(4,128)S(1)}, u32[]{:S(2)}, u32[]{:S(2)}) collective-permute-start(f32[4,12288]{1,0:T(4,128)S(1)} %get-tuple-element.57), channel_id=1, source_target_pairs={{0,16},{8,24},{16,0},{24,8},{1,17},{9,25},{17,1},{25,9},{2,18},{10... | collective-permute-start | bytes 589832 | tf_op jit(solution)/shard_map/ppermute | solution.py:69
  28.1 1.1 %collective-permute-done.13.refs_11_.refs_1_ = f32[4,8704]{1,0:T(4,128)S(1)} collective-permute-done((f32[4,8704]{1,0:T(4,128)S(1)}, f32[4,8704]{1,0:T(4,128)S(1)}, u32[]{:S(2)}, u32[]{:S(2)}) %collective-permute-start.13) | collective-permute-done | bytes 139296 | tf_op jit(solution)/shard_map/ppermute | solution.py:69
  29.1 1.7 %collective-permute-done.16.refs_14_.refs_2_ = f32[4,8448]{1,0:T(4,128)S(1)} collective-permute-done((f32[4,8448]{1,0:T(4,128)S(1)}, f32[4,8448]{1,0:T(4,128)S(1)}, u32[]{:S(2)}, u32[]{:S(2)}) %collective-permute-start.16) | collective-permute-done | bytes 135200 | tf_op jit(solution)/shard_map/ppermute | solution.py:69
  30.8 1.3 %collective-permute-start.18 = (f32[4,8192]{1,0:T(4,128)S(1)}, f32[4,8192]{1,0:T(4,128)S(1)}, u32[]{:S(2)}, u32[]{:S(2)}) collective-permute-start(f32[4,8192]{1,0:T(4,128)S(1)} %get-tuple-element.60), channel_id=1, source_target_pairs={{0,16},{8,24},{16,0},{24,8},{1,17},{9,25},{17,1},{25,9},{2,18},{10... | collective-permute-start | bytes 393224 | tf_op jit(solution)/shard_map/ppermute | solution.py:69
  32.2 0.9 %collective-permute-start.19 = (f32[4,8192]{1,0:T(4,128)S(1)}, f32[4,8192]{1,0:T(4,128)S(1)}, u32[]{:S(2)}, u32[]{:S(2)}) collective-permute-start(f32[4,8192]{1,0:T(4,128)S(1)} %get-tuple-element.61), channel_id=1, source_target_pairs={{0,8},{8,0},{16,24},{24,16},{1,9},{9,1},{17,25},{25,17},{2,10},{10... | collective-permute-start | bytes 393224 | tf_op jit(solution)/shard_map/ppermute | solution.py:69
  33.1 2.0 %collective-permute-done.15.refs_13_ = f32[4,12288]{1,0:T(4,128)S(1)} collective-permute-done((f32[4,12288]{1,0:T(4,128)S(1)}, f32[4,12288]{1,0:T(4,128)S(1)}, u32[]{:S(2)}, u32[]{:S(2)}) %collective-permute-start.15) | collective-permute-done | bytes 196640 | tf_op jit(solution)/shard_map/ppermute | solution.py:69
  35.0 0.2 collective-permute-done.14.refs_12_
  35.2 2.0 %finish.1 = (f32[16,8192]{1,0:T(8,128)}, f32[200,1024]{1,0:T(8,128)}, f32[64,200]{1,0:T(8,128)}, f32[4,65536]{1,0:T(4,128)}) custom-call(s32[8]{0:T(128)S(4)} %get-tuple-element.34.refs_0_.owned, f32[200,1024]{1,0:T(8,128)S(1)} %copy-done.1, f32[64,200]{1,0:T(8,128)S(1)} %bitcast.6, f32[64,1024]{1,0:T(8,128)S(1)} %bitcast.5, f32[4,65536]{1,0:T(4,128)S(1)} %copy-done, ...), custom_call_target="tpu_custom_call" | custom-call | tf_op jit(solution)/shard_map/finish/pallas_call | solution.py:49
  37.2 0.1 collective-permute-done.18.refs_0_
  37.3 0.3 collective-permute-done.19.refs_1_
  37.6 0.8 %finish_momentum.1 = f32[4,65536]{1,0:T(4,128)} custom-call(s32[8]{0:T(128)S(4)} %get-tuple-element.34.refs_0_.owned, f32[4,65536]{1,0:T(4,128)} %get-tuple-element.59._, f32[4,65536]{1,0:T(4,128)S(1)} %copy-done, f32[4,8192]{1,0:T(4,128)S(1)} %collective-permute-done.18.refs_0_, ...), custom_call_target="tpu_custom_call", output_to_operand_aliasing={{}: (1, {})} | custom-call | tf_op jit(solution)/shard_map/finish_momentum/pallas_call | solution.py:577
  (30 shorter events, 0.1 us)
Async XLA Ops:
  0.6 11.2 %copy-start.1 = (f32[200,1024]{1,0:T(8,128)S(1)}, f32[200,1024]{1,0:T(8,128)}, u32[]{:S(2)}) copy-start(f32[200,1024]{1,0:T(8,128)} %refs_1_.5) | copy-start | bytes 2457604
  0.6 11.1 %copy-start.3 = (f32[1,200,1024]{2,1,0:T(8,128)S(1)}, f32[1,200,1024]{2,1,0:T(8,128)}, u32[]{:S(2)}) copy-start(f32[1,200,1024]{2,1,0:T(8,128)} %refs_1_.4) | copy-start | bytes 2457604
  2.4 9.4 %copy-start.2 = (f32[1024,64]{0,1:T(8,128)S(1)}, f32[1024,64]{0,1:T(8,128)}, u32[]{:S(2)}) copy-start(f32[1024,64]{0,1:T(8,128)} %param.15) | copy-start | bytes 786436
  2.4 4.6 %collective-permute-start = (f32[4,4,2048]{2,1,0:T(4,128)S(1)}, f32[4,4,2048]{2,1,0:T(4,128)S(1)}, u32[]{:S(2)}, u32[]{:S(2)}) collective-permute-start(f32[4,4,2048]{2,1,0:T(4,128)S(1)} %get-tuple-element.36), channel_id=1, source_target_pairs={{0,1},{1,0},{2,3},{3,2},{4,5},{5,4},{6,7},{7,6},{8,9},{9,8},{10,11... | collective-permute-start | bytes 393224 | tf_op jit(solution)/shard_map/ppermute | solution.py:69
  2.9 8.3 %collective-permute-start.4 = (f32[256,128]{1,0:T(8,128)S(1)}, f32[256,128]{1,0:T(8,128)S(1)}, u32[]{:S(2)}, u32[]{:S(2)}) collective-permute-start(f32[256,128]{1,0:T(8,128)S(1)} %get-tuple-element.44), channel_id=1, source_target_pairs={{0,8},{8,0},{16,24},{24,16},{1,9},{9,1},{17,25},{25,17},{2,10},{10... | collective-permute-start | bytes 393224 | tf_op jit(solution)/shard_map/ppermute | solution.py:69
  5.4 8.4 %collective-permute-start.5 = (f32[256,128]{1,0:T(8,128)S(1)}, f32[256,128]{1,0:T(8,128)S(1)}, u32[]{:S(2)}, u32[]{:S(2)}) collective-permute-start(f32[256,128]{1,0:T(8,128)S(1)} %get-tuple-element.45), channel_id=1, source_target_pairs={{0,16},{8,24},{16,0},{24,8},{1,17},{9,25},{17,1},{25,9},{2,18},{10... | collective-permute-start | bytes 393224 | tf_op jit(solution)/shard_map/ppermute | solution.py:69
  7.0 6.9 %collective-permute-start.6 = (f32[256,128]{1,0:T(8,128)S(1)}, f32[256,128]{1,0:T(8,128)S(1)}, u32[]{:S(2)}, u32[]{:S(2)}) collective-permute-start(f32[256,128]{1,0:T(8,128)S(1)} %get-tuple-element.46), channel_id=1, source_target_pairs={{0,24},{8,16},{16,8},{24,0},{1,25},{9,17},{17,9},{25,1},{2,26},{10... | collective-permute-start | bytes 393224 | tf_op jit(solution)/shard_map/ppermute | solution.py:69
  7.0 10.6 %collective-permute-start.1 = (f32[2,4,2048]{2,1,0:T(4,128)S(1)}, f32[2,4,2048]{2,1,0:T(4,128)S(1)}, u32[]{:S(2)}, u32[]{:S(2)}) collective-permute-start(f32[2,4,2048]{2,1,0:T(4,128)S(1)} %get-tuple-element.37), channel_id=1, source_target_pairs={{0,6},{1,7},{2,4},{3,5},{4,2},{5,3},{6,0},{7,1},{8,14},{9,15},{10,... | collective-permute-start | bytes 196616 | tf_op jit(solution)/shard_map/ppermute | solution.py:69
  11.1 7.3 %collective-permute-start.2 = (f32[2,4,2048]{2,1,0:T(4,128)S(1)}, f32[2,4,2048]{2,1,0:T(4,128)S(1)}, u32[]{:S(2)}, u32[]{:S(2)}) collective-permute-start(f32[2,4,2048]{2,1,0:T(4,128)S(1)} %get-tuple-element.38), channel_id=1, source_target_pairs={{0,4},{1,5},{2,6},{3,7},{4,0},{5,1},{6,2},{7,3},{8,12},{9,13},{10,... | collective-permute-start | bytes 196616 | tf_op jit(solution)/shard_map/ppermute | solution.py:69
  11.1 7.3 %collective-permute-start.3 = (f32[2,4,2048]{2,1,0:T(4,128)S(1)}, f32[2,4,2048]{2,1,0:T(4,128)S(1)}, u32[]{:S(2)}, u32[]{:S(2)}) collective-permute-start(f32[2,4,2048]{2,1,0:T(4,128)S(1)} %get-tuple-element.39), channel_id=1, source_target_pairs={{0,2},{1,3},{2,0},{3,1},{4,6},{5,7},{6,4},{7,5},{8,10},{9,11},{10,... | collective-permute-start | bytes 196616 | tf_op jit(solution)/shard_map/ppermute | solution.py:69
  11.8 6.6 %copy-start = (f32[4,65536]{1,0:T(4,128)S(1)}, f32[4,65536]{1,0:T(4,128)}, u32[]{:S(2)}) copy-start(f32[4,65536]{1,0:T(4,128)} %momentum.1) | copy-start | bytes 3145732
  13.9 6.9 %collective-permute-start.9 = (f32[2,4,2048]{2,1,0:T(4,128)S(1)}, f32[2,4,2048]{2,1,0:T(4,128)S(1)}, u32[]{:S(2)}, u32[]{:S(2)}) collective-permute-start(f32[2,4,2048]{2,1,0:T(4,128)S(1)} %get-tuple-element.51), channel_id=1, source_target_pairs={{0,6},{1,7},{2,4},{3,5},{4,2},{5,3},{6,0},{7,1},{8,14},{9,15},{10,... | collective-permute-start | bytes 196616 | tf_op jit(solution)/shard_map/ppermute | solution.py:69
  17.6 5.3 %collective-permute-start.10 = (f32[2,4,2048]{2,1,0:T(4,128)S(1)}, f32[2,4,2048]{2,1,0:T(4,128)S(1)}, u32[]{:S(2)}, u32[]{:S(2)}) collective-permute-start(f32[2,4,2048]{2,1,0:T(4,128)S(1)} %get-tuple-element.52), channel_id=1, source_target_pairs={{0,4},{1,5},{2,6},{3,7},{4,0},{5,1},{6,2},{7,3},{8,12},{9,13},{10,... | collective-permute-start | bytes 196616 | tf_op jit(solution)/shard_map/ppermute | solution.py:69
  17.6 5.3 %collective-permute-start.11 = (f32[2,4,2048]{2,1,0:T(4,128)S(1)}, f32[2,4,2048]{2,1,0:T(4,128)S(1)}, u32[]{:S(2)}, u32[]{:S(2)}) collective-permute-start(f32[2,4,2048]{2,1,0:T(4,128)S(1)} %get-tuple-element.53), channel_id=1, source_target_pairs={{0,2},{1,3},{2,0},{3,1},{4,6},{5,7},{6,4},{7,5},{8,10},{9,11},{10,... | collective-permute-start | bytes 196616 | tf_op jit(solution)/shard_map/ppermute | solution.py:69
  18.7 7.2 %collective-permute-start.8 = (f32[384,128]{1,0:T(8,128)S(1)}, f32[384,128]{1,0:T(8,128)S(1)}, u32[]{:S(2)}, u32[]{:S(2)}) collective-permute-start(f32[384,128]{1,0:T(8,128)S(1)} %get-tuple-element.50), channel_id=1, source_target_pairs={{0,16},{8,24},{16,0},{24,8},{1,17},{9,25},{17,1},{25,9},{2,18},{10... | collective-permute-start | bytes 589832 | tf_op jit(solution)/shard_map/ppermute | solution.py:69
  20.3 5.6 %collective-permute-start.7 = (f32[272,128]{1,0:T(8,128)S(1)}, f32[272,128]{1,0:T(8,128)S(1)}, u32[]{:S(2)}, u32[]{:S(2)}) collective-permute-start(f32[272,128]{1,0:T(8,128)S(1)} %get-tuple-element.49.refs_5_.refs_2_), channel_id=1, source_target_pairs={{0,8},{8,0},{16,24},{24,16},{1,9},{9,1},{17,25},{25,17},{2,10},{10... | collective-permute-start | bytes 417800 | tf_op jit(solution)/shard_map/ppermute | solution.py:69
  22.9 1.7 %collective-permute-start.12 = (f32[4,8448]{1,0:T(4,128)S(1)}, f32[4,8448]{1,0:T(4,128)S(1)}, u32[]{:S(2)}, u32[]{:S(2)}) collective-permute-start(f32[4,8448]{1,0:T(4,128)S(1)} %other.1), channel_id=1, source_target_pairs={{0,1},{1,0},{2,3},{3,2},{4,5},{5,4},{6,7},{7,6},{8,9},{9,8},{10,11... | collective-permute-start | bytes 405512 | tf_op jit(solution)/shard_map/ppermute | solution.py:69
  23.0 6.1 %collective-permute-start.13 = (f32[4,8704]{1,0:T(4,128)S(1)}, f32[4,8704]{1,0:T(4,128)S(1)}, u32[]{:S(2)}, u32[]{:S(2)}) collective-permute-start(f32[4,8704]{1,0:T(4,128)S(1)} %mine.1.refs_0_.refs_9_), channel_id=1, source_target_pairs={{0,8},{8,0},{16,24},{24,16},{1,9},{9,1},{17,25},{25,17},{2,10},{10... | collective-permute-start | bytes 417800 | tf_op jit(solution)/shard_map/ppermute | solution.py:69
  24.6 6.2 %collective-permute-start.16 = (f32[4,8448]{1,0:T(4,128)S(1)}, f32[4,8448]{1,0:T(4,128)S(1)}, u32[]{:S(2)}, u32[]{:S(2)}) collective-permute-start(f32[4,8448]{1,0:T(4,128)S(1)} %collective-permute-done.12.refs_1_.refs_10_), channel_id=1, source_target_pairs={{0,16},{8,24},{16,0},{24,8},{1,17},{9,25},{17,1},{25,9},{2,18},{10... | collective-permute-start | bytes 405512 | tf_op jit(solution)/shard_map/ppermute | solution.py:69
  25.9 4.9 %collective-permute-start.17 = (f32[260,128]{1,0:T(8,128)S(1)}, f32[260,128]{1,0:T(8,128)S(1)}, u32[]{:S(2)}, u32[]{:S(2)}) collective-permute-start(f32[260,128]{1,0:T(8,128)S(1)} %gathered.1), channel_id=1, source_target_pairs={{0,1},{1,0},{2,3},{3,2},{4,5},{5,4},{6,7},{7,6},{8,9},{9,8},{10,11... | collective-permute-start | bytes 399368 | tf_op jit(solution)/shard_map/ppermute | solution.py:69
  26.0 9.2 %collective-permute-start.14 = (f32[4,16384]{1,0:T(4,128)S(1)}, f32[4,16384]{1,0:T(4,128)S(1)}, u32[]{:S(2)}, u32[]{:S(2)}) collective-permute-start(f32[4,16384]{1,0:T(4,128)S(1)} %get-tuple-element.56), channel_id=1, source_target_pairs={{0,8},{8,0},{16,24},{24,16},{1,9},{9,1},{17,25},{25,17},{2,10},{10... | collective-permute-start | bytes 786440 | tf_op jit(solution)/shard_map/ppermute | solution.py:69
  26.9 8.3 %copy-start.4 = (f32[200,64]{0,1:T(8,128)S(1)}, f32[200,64]{0,1:T(8,128)}, u32[]{:S(2)}) copy-start(f32[200,64]{0,1:T(8,128)} %param.14) | copy-start | bytes 153604
  26.9 8.2 %collective-permute-start.15 = (f32[4,12288]{1,0:T(4,128)S(1)}, f32[4,12288]{1,0:T(4,128)S(1)}, u32[]{:S(2)}, u32[]{:S(2)}) collective-permute-start(f32[4,12288]{1,0:T(4,128)S(1)} %get-tuple-element.57), channel_id=1, source_target_pairs={{0,16},{8,24},{16,0},{24,8},{1,17},{9,25},{17,1},{25,9},{2,18},{10... | collective-permute-start | bytes 589832 | tf_op jit(solution)/shard_map/ppermute | solution.py:69
  30.8 6.5 %collective-permute-start.18 = (f32[4,8192]{1,0:T(4,128)S(1)}, f32[4,8192]{1,0:T(4,128)S(1)}, u32[]{:S(2)}, u32[]{:S(2)}) collective-permute-start(f32[4,8192]{1,0:T(4,128)S(1)} %get-tuple-element.60), channel_id=1, source_target_pairs={{0,16},{8,24},{16,0},{24,8},{1,17},{9,25},{17,1},{25,9},{2,18},{10... | collective-permute-start | bytes 393224 | tf_op jit(solution)/shard_map/ppermute | solution.py:69
  32.2 5.4 %collective-permute-start.19 = (f32[4,8192]{1,0:T(4,128)S(1)}, f32[4,8192]{1,0:T(4,128)S(1)}, u32[]{:S(2)}, u32[]{:S(2)}) collective-permute-start(f32[4,8192]{1,0:T(4,128)S(1)} %get-tuple-element.61), channel_id=1, source_target_pairs={{0,8},{8,0},{16,24},{24,16},{1,9},{9,1},{17,25},{25,17},{2,10},{10... | collective-permute-start | bytes 393224 | tf_op jit(solution)/shard_map/ppermute | solution.py:69

commit v7 on v6

--- a/solution.py
+++ b/solution.py
@@ -67,6 +67,24 @@
 
 def swap(x, axis, count, mask):
     return lax.ppermute(x, axis, [(i, i ^ mask) for i in range(count)])
+
+
+def turn(step, core):
+    return 1 + ((step + core) & 1)
+
+
+def swap_in_turn(x, step):
+    groups, owner_count = lax.axis_size("rep"), lax.axis_size("own")
+    pairs = [
+        (rep * owner_count + own, (rep ^ turn(step, own & 1)) * owner_count + own)
+        for rep in range(groups)
+        for own in range(owner_count)
+    ]
+    return lax.ppermute(x, ("rep", "own"), pairs)
+
+
+def member(rep, core, k):
+    return rep ^ (k if k in (0, 3) else turn(k - 1, core))
 
 
 def place():
@@ -309,67 +327,81 @@
 
 
 class Pieces:
-    def __init__(self, part, direct, members, owned, momentum, gradient, result, made, sem):
-        self.part, self.direct, self.members = part, direct, members
+    def __init__(self, part, direct, halves, owned, momentum, gradient, result, made, sem):
+        self.part, self.direct, self.halves = part, direct, halves
         self.momentum, self.gradient, self.result = momentum, gradient, result
         self.made, self.sem = made, sem
-        self.pieces = made.shape[1]
-        self.groups = momentum.shape[1] // part // self.pieces
+        self.chips = made.shape[1]
+        self.groups = momentum.shape[1] // part // (2 * self.chips)
         self.rep, self.here, self.core = place()
         rows = lax.broadcasted_iota(jnp.int32, (momentum.shape[0], part), 0)
         self.live = rows < owned[self.here * 2 + self.core]
-        self.short = self.pieces <= 16
-
-    def move(self, n, g, i):
-        half = self.pieces // 2
-        k, o = i % half, i // half
+        self.short = self.chips <= 8
+
+    def move(self, n, k):
+        g, o = self.halves[n]
         piece = 2 * (self.here ^ k if self.direct else k) + (self.core ^ o)
-        at = column(piece * self.groups + (self.rep ^ g), self.part)
+        at = column(piece * self.groups + member(self.rep, self.core, g), self.part)
         target = self.result.at[:, at]
-        return at, pltpu.make_async_copy(self.made.at[n, i], target, self.sem.at[n, i])
-
-    def fill(self, h, i, carry):
-        half = self.pieces // 2
-        for n, g in enumerate(self.members):
-            at, copy = self.move(n, g, i + h * half)
-            received = self.gradient[2 * n + h][:, column(i, self.part)]
-            rows = momentum_decay * self.momentum[:, at] + received
-            self.made[n, i + h * half] = jnp.where(self.live, rows, 0.0)
+        return at, pltpu.make_async_copy(self.made.at[n, k], target, self.sem.at[n, k])
+
+    def fill(self, k, carry):
+        for n, received in enumerate(self.gradient):
+            at, copy = self.move(n, k)
+            rows = momentum_decay * self.momentum[:, at] + received[:, column(k, self.part)]
+            self.made[n, k] = jnp.where(self.live, rows, 0.0)
             copy.start()
         return carry
 
-    def wait(self, i, carry):
-        for n, g in enumerate(self.members):
-            self.move(n, g, i)[1].wait()
+    def wait(self, k, carry):
+        for n in range(len(self.halves)):
+            self.move(n, k)[1].wait()
         return carry
 
     def make(self):
-        for h in range(2):
-            body = functools.partial(self.fill, h)
-            lax.fori_loop(0, self.pieces // 2, body, 0, unroll=self.short)
+        lax.fori_loop(0, self.chips, self.fill, 0, unroll=self.short)
 
     def finish(self):
-        lax.fori_loop(0, self.pieces, self.wait, 0, unroll=self.short)
-
-
-def finish_body(part, direct, groups, owned, anchor, momentum_t, basis_t, momentum, *refs):
-    parts, pair, gradient = refs[: groups - 1], refs[groups - 1], refs[groups : 3 * groups - 2]
-    refs = refs[3 * groups - 2 :]
+        lax.fori_loop(0, self.chips, self.wait, 0, unroll=self.short)
+
+
+def early_body(part, direct, halves, owned, momentum, *refs):
+    *refs, result0, result1, made, made_sem, new_dense, sem = refs
+    parts, gradient = refs[: -len(halves)], refs[-len(halves) :]
+    rep, _, core = place()
+    blocks = new_dense.shape[1]
+    copies = []
+    for k, ref in enumerate(parts):
+        for t, (i, height, j, width) in enumerate(tiles(blocks, part)):
+            new_dense[k, i : i + height, j : j + width] = ref[8 * t : 8 * t + height, :width]
+        target = result0.at[:, column(member(rep, core, k), part)]
+        copies.append(pltpu.make_async_copy(new_dense.at[k], target, sem.at[k]))
+        copies[-1].start()
+    pieces = Pieces(part, direct, halves, owned, momentum, gradient, result1, made, made_sem)
+    pieces.make()
+    pieces.finish()
+    for copy in copies:
+        copy.wait()
+
+
+def late_body(part, direct, halves, owned, _, __, anchor, momentum_t, basis_t, momentum, *refs):
+    pair, first, second, *refs = refs
     result0, result1, result2, result3, mean, sem, made, made_sem, *whole = refs
     new_dense, new_emb, new_momentum_t = whole
+    rep, _, core = place()
+    groups = momentum.shape[1] // part // (2 * made.shape[1])
+    target = result0.at[:, column(member(rep, core, groups - 1), part)]
     copies = [
         pltpu.make_async_copy(ref, result, sem.at[i])
         for i, (ref, result) in enumerate(
-            ((new_dense, result0), (new_emb, result1), (new_momentum_t, result2))
+            ((new_dense, target), (new_emb, result1), (new_momentum_t, result2))
         )
     ]
-    rep, _, _ = place()
-    blocks, (rank, rows) = new_dense.shape[0], mean.shape
-    dense_tiles = tiles(blocks, part)
-    skip = gradient[3].shape[1] - 256 * len(tiles(rank, rows))
+    rank, rows = mean.shape
+    skip = second.shape[1] - 256 * len(tiles(rank, rows))
     for t, (i, height, j, width) in enumerate(tiles(rank, rows)):
         here = (slice(i, i + height), slice(j, j + width))
-        mean[here] = (pair[here] + unfold(gradient[3], skip + 256 * t, height, width)) / groups
+        mean[here] = (pair[here] + unfold(second, skip + 256 * t, height, width)) / groups
     moved = momentum_decay * momentum_t[...] + mean[...]
     new_momentum_t[...] = moved
     copies[2].start()
@@ -383,30 +415,25 @@
     new_emb[...] = anchor[...] - outer_rate * back
     copies[1].start()
 
+    dense_tiles = tiles(*new_dense.shape)
     count = len(dense_tiles) // 2
-    skip = gradient[4].shape[1] - 256 * count
-    for k in range(groups):
-        for t, (i, height, j, width) in enumerate(dense_tiles):
-            at = pl.multiple_of((rep ^ k) * part + j, 128)
-            if k < len(parts):
-                tile = parts[k][8 * t : 8 * t + height, :width]
-            else:
-                ref = gradient[4] if t < count else gradient[3]
-                tile = unfold(ref, skip + 256 * (t % count), height, width)
-            new_dense[i : i + height, pl.ds(at, width)] = tile
+    skip = first.shape[1] - 256 * count
+    for t, (i, height, j, width) in enumerate(dense_tiles):
+        ref = first if t < count else second
+        tile = unfold(ref, skip + 256 * (t % count), height, width)
+        new_dense[i : i + height, j : j + width] = tile
     copies[0].start()
-
-    members = tuple(range(groups - 1))
-    pieces = Pieces(part, direct, members, owned, momentum, gradient, result3, made, made_sem)
+    gradient = (second, first)
+    pieces = Pieces(part, direct, halves, owned, momentum, gradient, result3, made, made_sem)
     pieces.make()
     pieces.finish()
     for copy in copies:
         copy.wait()
 
 
-def finish_momentum_body(part, direct, members, owned, _, momentum, *refs):
+def last_body(part, direct, halves, owned, _, momentum, *refs):
     *gradient, result, made, sem = refs
-    pieces = Pieces(part, direct, members, owned, momentum, gradient, result, made, sem)
+    pieces = Pieces(part, direct, halves, owned, momentum, gradient, result, made, sem)
     pieces.make()
     pieces.finish()
 
@@ -510,7 +537,7 @@
         after=[*momentum_rows[:0:-1], momentum],
         name="dense",
     )
-    dense = [plain, swap(plain, "rep", groups, 1), swap(with_factor, "rep", groups, 2)]
+    dense = [plain, swap_in_turn(plain, 0), swap_in_turn(with_factor, 1)]
 
     passed_on = 16 * dense_rows
     *again, pair = run(
@@ -527,8 +554,8 @@
         cut_body, [kept((260, 128))], [plain], after=[dense[k] for k in (2, 1)], name="gathered"
     )
     sign = swap(sign, "own", owner_count, 1)
-    near1 = swap(halves[0], "rep", groups, 1)
-    near2 = swap(halves[1], "rep", groups, 2)
+    near1 = swap_in_turn(halves[0], 0)
+    near2 = swap_in_turn(halves[1], 1)
     passed = run(
         copies_body,
         [kept((slot_count, length))] * 2,
@@ -539,55 +566,73 @@
     gradient = [
         *halves,
         near1,
-        swap(again[1], "rep", groups, 1),
-        swap(again[0], "rep", groups, 2),
+        swap_in_turn(again[1], 0),
+        swap_in_turn(again[0], 1),
         near2,
-        swap(passed[0], "rep", groups, 2),
-        swap(passed[1], "rep", groups, 1),
+        swap_in_turn(passed[0], 1),
+        swap_in_turn(passed[1], 0),
     ]
 
-    made = [
-        pltpu.VMEM((n, owner_count, slot_count, part), f32) for n in (groups - 1, 1)
-    ]
-    made_sems = [pltpu.SemaphoreType.DMA((n, owner_count)) for n in (groups - 1, 1)]
-    shapes = [anchor_dense.shape, anchor_emb.shape, (rank, rows)]
-    new_dense, new_emb, new_momentum_t, first_columns = run(
-        functools.partial(finish_body, part, direct, groups),
-        [stored(shape) for shape in (*shapes, momentum_dense.shape)],
-        [
-            anchor_emb,
-            momentum_emb.T,
-            basis_t,
-            momentum,
-            *dense,
-            pair,
-            *gradient[: 2 * groups - 2],
+    own_rows, own_crossed, near1, late2, late1, near2, last1, last2 = gradient
+
+    def finishing(body, halves, outs, operands, aliased=(), scratch=(), name=None):
+        made = (len(halves), chips, slot_count, part)
+        return pl.pallas_call(
+            functools.partial(body, part, direct, halves),
+            out_shape=[stored(shape) for shape in outs],
+            in_specs=[smem] + [anywhere] * len(aliased) + [vmem] * len(operands),
+            out_specs=[anywhere] * len(outs),
+            scratch_shapes=[
+                *scratch[:2],
+                pltpu.VMEM(made, f32),
+                pltpu.SemaphoreType.DMA(made[:2]),
+                *scratch[2:],
+            ],
+            input_output_aliases={1 + i: out for i, (_, out) in enumerate(aliased)},
+            compiler_params=pltpu.CompilerParams(vmem_limit_bytes=vmem_limit),
+            name=name,
+        )(in_scalars(owned), *[x for x, _ in aliased], *[on_chip(x) for x in operands])
+
+    held = momentum_dense.shape
+    new_dense, new_momentum_dense = pl.pallas_call(
+        functools.partial(early_body, part, direct, ((0, 0), (0, 1), (1, 0), (2, 1))),
+        out_shape=[stored(anchor_dense.shape), stored(held)],
+        in_specs=[smem] + [vmem] * (5 + len(dense)),
+        out_specs=[anywhere] * 2,
+        scratch_shapes=[
+            pltpu.VMEM((4, chips, slot_count, part), f32),
+            pltpu.SemaphoreType.DMA((4, chips)),
+            pltpu.VMEM((groups - 1, blocks, part), f32),
+            pltpu.SemaphoreType.DMA((groups - 1,)),
         ],
-        [owned],
-        out_specs=[anywhere] * 4,
+        compiler_params=pltpu.CompilerParams(vmem_limit_bytes=vmem_limit),
+        name="early",
+    )(
+        in_scalars(owned),
+        *[on_chip(x) for x in (momentum, *dense, own_rows, own_crossed, near1, near2)],
+    )
+    new_dense, new_emb, new_momentum_t, new_momentum_dense = finishing(
+        late_body,
+        ((1, 1), (2, 0)),
+        [anchor_dense.shape, anchor_emb.shape, (rank, rows), held],
+        [anchor_emb, momentum_emb.T, basis_t, momentum, pair, late1, late2],
+        aliased=[(new_dense, 0), (new_momentum_dense, 3)],
         scratch=[
             pltpu.VMEM((rank, rows), f32),
             pltpu.SemaphoreType.DMA((3,)),
-            made[0],
-            made_sems[0],
-        ]
-        + [pltpu.VMEM(shape, f32) for shape in shapes],
-        name="finish",
-    )
-    (new_momentum_dense,) = pl.pallas_call(
-        functools.partial(finish_momentum_body, part, direct, (groups - 1,)),
-        out_shape=[stored(momentum_dense.shape)],
-        in_specs=[smem, anywhere] + [vmem] * 3,
-        out_specs=[anywhere],
-        scratch_shapes=[made[1], made_sems[1]],
-        input_output_aliases={1: 0},
-        compiler_params=pltpu.CompilerParams(vmem_limit_bytes=vmem_limit),
-        name="finish_momentum",
-    )(
-        in_scalars(owned),
-        first_columns,
-        on_chip(momentum),
-        *[on_chip(x) for x in gradient[2 * groups - 2 :]],
+            pltpu.VMEM((blocks, part), f32),
+            pltpu.VMEM(anchor_emb.shape, f32),
+            pltpu.VMEM((rank, rows), f32),
+        ],
+        name="late",
+    )
+    (new_momentum_dense,) = finishing(
+        last_body,
+        ((3, 0), (3, 1)),
+        [held],
+        [momentum, last1, last2],
+        aliased=[(new_momentum_dense, 0)],
+        name="last",
     )
     return (new_dense, new_momentum_dense, new_emb, new_momentum_t.T)
 

time: 38.5 us -> 38.3 us (level)
  waiting for transfers between devices: 9.01 us -> 8.2 us
  Pallas kernels: 5.35 us -> 5.88 us
    ppermute x0 -> x8, starting transfers between devices: none -> 9.28 us  [swap_in_turn(): return lax.ppermute(x, ('rep', 'own'), pairs)]
    ppermute x20 -> x12, starting transfers between devices: 23.2 us -> 14 us  [swap(): return lax.ppermute(x, axis, [(i, i ^ mask) for i in range(count)])]
    ppermute x20 -> x12, waiting for transfers between devices: 9.01 us -> 3.74 us  [swap(): return lax.ppermute(x, axis, [(i, i ^ mask) for i in range(count)])]
    ppermute x0 -> x8, waiting for transfers between devices: none -> 4.46 us  [swap_in_turn(): return lax.ppermute(x, ('rep', 'own'), pairs)]
    pallas_call x1 -> x3, Pallas kernels: 0.77 us -> 3.3 us  [the longest x2 2.18 us: finishing(): pl.pallas_call(functools.partial(body, part, direct, halves), out_shape=[...]
    pallas_call x11 -> x10, Pallas kernels: 4.57 us -> 2.58 us  [run(): pl.pallas_call(whole, out_shape=list(outs), in_specs=[anywhere] * skip +...]
  transfers between devices with their start and end apart: 20 -> 20, of which waited for: 8 -> 7; matrix products, arithmetic and copies ran while one was open for 0% -> 0% of each run, Pallas kernels for 8% -> 9%
where the time goes in v7:
time: 38.3 us; the launch traced here: 38.1 us
  starting transfers between devices  23.3 us (61%)
  waiting for transfers between devices  8.2 us (21%)
  Pallas kernels  5.88 us (15%)
  between operations  0.78 us (2%)
    ppermute x12, starting transfers between devices, swap(): return lax.ppermute(x, axis, [(i, i ^ mask) for i in range(count)])  14 us
    ppermute x8, starting transfers between devices, swap_in_turn(): return lax.ppermute(x, ('rep', 'own'), pairs)  9.28 us
    ppermute x8, waiting for transfers between devices, swap_in_turn(): return lax.ppermute(x, ('rep', 'own'), pairs)  4.46 us
    ppermute x12, waiting for transfers between devices, swap(): return lax.ppermute(x, axis, [(i, i ^ mask) for i in range(count)])  3.74 us
    pallas_call x10, Pallas kernels, run(): pl.pallas_call(whole, out_shape=list(outs), in_specs=[anywhere] * skip +...  2.58 us
    pallas_call x2, Pallas kernels, finishing(): pl.pallas_call(functools.partial(body, part, direct, halves), out_shape=[...  2.18 us
    pallas_call x1, Pallas kernels, per_device(): pl.pallas_call(functools.partial(early_body, part, direct, ((0, 0), (0, 1...  1.12 us
  transfers between devices with their start and end apart: 20, of which 7 were waited for; matrix products, arithmetic and copies ran while one was open for 0% of the time, Pallas kernels for 9%

profile of v7, /device:TPU:0, one launch (start us, length us, event | category | flops | bytes accessed | tf_op | source)
XLA Modules:
  0.0 38.1 jit_solution(8079287343017772916)
XLA Ops:
  0.7 1.7 %start.1 = (f32[256,128]{1,0:T(8,128)S(1)}, f32[256,128]{1,0:T(8,128)S(1)}, f32[256,128]{1,0:T(8,128)S(1)}, f32[256,128]{1,0:T(8,128)S(1)}, f32[16,2048]{1,0:T(8...) custom-call(s32[16]{0:T(128)} %bitcast.7, ...), custom_call_target="tpu_custom_call" | custom-call | tf_op jit(solution)/shard_map/start/pallas_call | solution.py:49
  2.4 0.5 %collective-permute-start = (f32[4,4,2048]{2,1,0:T(4,128)S(1)}, f32[4,4,2048]{2,1,0:T(4,128)S(1)}, u32[]{:S(2)}, u32[]{:S(2)}) collective-permute-start(f32[4,4,2048]{2,1,0:T(4,128)S(1)} %get-tuple-element.38), channel_id=1, source_target_pairs={{0,1},{1,0},{2,3},{3,2},{4,5},{5,4},{6,7},{7,6},{8,9},{9,8},{10,11... | collective-permute-start | bytes 393224 | tf_op jit(solution)/shard_map/ppermute | solution.py:69
  2.9 2.6 %collective-permute-start.4 = (f32[256,128]{1,0:T(8,128)S(1)}, f32[256,128]{1,0:T(8,128)S(1)}, u32[]{:S(2)}, u32[]{:S(2)}) collective-permute-start(f32[256,128]{1,0:T(8,128)S(1)} %get-tuple-element.46), channel_id=1, source_target_pairs={{0,8},{8,0},{16,24},{24,16},{1,9},{9,1},{17,25},{25,17},{2,10},{10... | collective-permute-start | bytes 393224 | tf_op jit(solution)/shard_map/ppermute | solution.py:69
  5.4 1.5 %collective-permute-start.5 = (f32[256,128]{1,0:T(8,128)S(1)}, f32[256,128]{1,0:T(8,128)S(1)}, u32[]{:S(2)}, u32[]{:S(2)}) collective-permute-start(f32[256,128]{1,0:T(8,128)S(1)} %get-tuple-element.47), channel_id=1, source_target_pairs={{0,16},{8,24},{16,0},{24,8},{1,17},{9,25},{17,1},{25,9},{2,18},{10... | collective-permute-start | bytes 393224 | tf_op jit(solution)/shard_map/ppermute | solution.py:69
  7.0 4.1 %collective-permute-start.1 = (f32[2,4,2048]{2,1,0:T(4,128)S(1)}, f32[2,4,2048]{2,1,0:T(4,128)S(1)}, u32[]{:S(2)}, u32[]{:S(2)}) collective-permute-start(f32[2,4,2048]{2,1,0:T(4,128)S(1)} %get-tuple-element.39), channel_id=1, source_target_pairs={{0,6},{1,7},{2,4},{3,5},{4,2},{5,3},{6,0},{7,1},{8,14},{9,15},{10,... | collective-permute-start | bytes 196616 | tf_op jit(solution)/shard_map/ppermute | solution.py:69
  11.1 0.6 %collective-permute-start.3 = (f32[2,4,2048]{2,1,0:T(4,128)S(1)}, f32[2,4,2048]{2,1,0:T(4,128)S(1)}, u32[]{:S(2)}, u32[]{:S(2)}) collective-permute-start(f32[2,4,2048]{2,1,0:T(4,128)S(1)} %get-tuple-element.41), channel_id=1, source_target_pairs={{0,2},{1,3},{2,0},{3,1},{4,6},{5,7},{6,4},{7,5},{8,10},{9,11},{10,... | collective-permute-start | bytes 196616 | tf_op jit(solution)/shard_map/ppermute | solution.py:69
  11.8 0.4 %factor.1.refs_0_.refs_7_.refs_2_ = f32[64,200]{1,0:T(8,128)S(1)} custom-call(f32[200,1024]{1,0:T(8,128)S(1)} %copy-done.1, f32[1,200,1024]{2,1,0:T(8,128)S(1)} %copy-done.3, f32[64,1024]{1,0:T(8,128)S(1)} %bitcast.4), custom_call_target="tpu_custom_call" | custom-call | tf_op jit(solution)/shard_map/factor/pallas_call | solution.py:49
  12.2 1.6 %collective-permute-done.5.refs_4_ = f32[256,128]{1,0:T(8,128)S(1)} collective-permute-done((f32[256,128]{1,0:T(8,128)S(1)}, f32[256,128]{1,0:T(8,128)S(1)}, u32[]{:S(2)}, u32[]{:S(2)}) %collective-permute-start.5) | collective-permute-done | bytes 131104 | tf_op jit(solution)/shard_map/ppermute | solution.py:69
  13.8 0.1 mean.1
  13.9 3.7 %collective-permute-start.9 = (f32[2,4,2048]{2,1,0:T(4,128)S(1)}, f32[2,4,2048]{2,1,0:T(4,128)S(1)}, u32[]{:S(2)}, u32[]{:S(2)}) collective-permute-start(f32[2,4,2048]{2,1,0:T(4,128)S(1)} %get-tuple-element.53), channel_id=1, source_target_pairs={{0,6},{1,7},{2,4},{3,5},{4,2},{5,3},{6,0},{7,1},{8,14},{9,15},{10,... | collective-permute-start | bytes 196616 | tf_op jit(solution)/shard_map/ppermute | solution.py:69
  17.6 0.8 %collective-permute-start.11 = (f32[2,4,2048]{2,1,0:T(4,128)S(1)}, f32[2,4,2048]{2,1,0:T(4,128)S(1)}, u32[]{:S(2)}, u32[]{:S(2)}) collective-permute-start(f32[2,4,2048]{2,1,0:T(4,128)S(1)} %get-tuple-element.55), channel_id=1, source_target_pairs={{0,2},{1,3},{2,0},{3,1},{4,6},{5,7},{6,4},{7,5},{8,10},{9,11},{10,... | collective-permute-start | bytes 196616 | tf_op jit(solution)/shard_map/ppermute | solution.py:69
  18.4 0.3 dense.1
  18.7 1.6 %collective-permute-start.8 = (f32[384,128]{1,0:T(8,128)S(1)}, f32[384,128]{1,0:T(8,128)S(1)}, u32[]{:S(2)}, u32[]{:S(2)}) collective-permute-start(f32[384,128]{1,0:T(8,128)S(1)} %get-tuple-element.52), channel_id=1, source_target_pairs={{0,16},{1,9},{2,18},{3,11},{4,20},{5,13},{6,22},{7,15},{8,24},{9,1... | collective-permute-start | bytes 589832 | tf_op jit(solution)/shard_map/ppermute | solution.py:83
  20.3 0.5 %collective-permute-start.7 = (f32[272,128]{1,0:T(8,128)S(1)}, f32[272,128]{1,0:T(8,128)S(1)}, u32[]{:S(2)}, u32[]{:S(2)}) collective-permute-start(f32[272,128]{1,0:T(8,128)S(1)} %get-tuple-element.51.refs_0_.refs_2_), channel_id=1, source_target_pairs={{0,8},{1,17},{2,10},{3,19},{4,12},{5,21},{6,14},{7,23},{8,0},{9,25... | collective-permute-start | bytes 417800 | tf_op jit(solution)/shard_map/ppermute | solution.py:83
  20.8 2.1 %collective-permute-done.10.refs_1_.refs_5_ = f32[2,4,2048]{2,1,0:T(4,128)S(1)} collective-permute-done((f32[2,4,2048]{2,1,0:T(4,128)S(1)}, f32[2,4,2048]{2,1,0:T(4,128)S(1)}, u32[]{:S(2)}, u32[]{:S(2)}) %collective-permute-start.10) | collective-permute-done | bytes 65568 | tf_op jit(solution)/shard_map/ppermute | solution.py:69
  22.9 0.1 collective-permute-start.12
  23.0 1.6 %collective-permute-start.13 = (f32[4,8704]{1,0:T(4,128)S(1)}, f32[4,8704]{1,0:T(4,128)S(1)}, u32[]{:S(2)}, u32[]{:S(2)}) collective-permute-start(f32[4,8704]{1,0:T(4,128)S(1)} %mine.1.refs_3_.refs_0_), channel_id=1, source_target_pairs={{0,8},{1,17},{2,10},{3,19},{4,12},{5,21},{6,14},{7,23},{8,0},{9,25... | collective-permute-start | bytes 417800 | tf_op jit(solution)/shard_map/ppermute | solution.py:83
  24.6 1.3 %collective-permute-start.14 = (f32[4,8448]{1,0:T(4,128)S(1)}, f32[4,8448]{1,0:T(4,128)S(1)}, u32[]{:S(2)}, u32[]{:S(2)}) collective-permute-start(f32[4,8448]{1,0:T(4,128)S(1)} %collective-permute-done.12.refs_4_.refs_1_), channel_id=1, source_target_pairs={{0,16},{1,9},{2,18},{3,11},{4,20},{5,13},{6,22},{7,15},{8,24},{9,1... | collective-permute-start | bytes 405512 | tf_op jit(solution)/shard_map/ppermute | solution.py:83
  25.9 0.1 collective-permute-start.17
  26.0 0.1 again.1
  26.0 0.8 %collective-permute-start.16 = (f32[4,16384]{1,0:T(4,128)S(1)}, f32[4,16384]{1,0:T(4,128)S(1)}, u32[]{:S(2)}, u32[]{:S(2)}) collective-permute-start(f32[4,16384]{1,0:T(4,128)S(1)} %get-tuple-element.61), channel_id=1, source_target_pairs={{0,8},{1,17},{2,10},{3,19},{4,12},{5,21},{6,14},{7,23},{8,0},{9,25... | collective-permute-start | bytes 786440 | tf_op jit(solution)/shard_map/ppermute | solution.py:83
  26.9 1.2 %collective-permute-start.15 = (f32[4,12288]{1,0:T(4,128)S(1)}, f32[4,12288]{1,0:T(4,128)S(1)}, u32[]{:S(2)}, u32[]{:S(2)}) collective-permute-start(f32[4,12288]{1,0:T(4,128)S(1)} %get-tuple-element.60), channel_id=1, source_target_pairs={{0,16},{1,9},{2,18},{3,11},{4,20},{5,13},{6,22},{7,15},{8,24},{9,1... | collective-permute-start | bytes 589832 | tf_op jit(solution)/shard_map/ppermute | solution.py:83
  28.1 0.8 %collective-permute-done.13.refs_5_.refs_1_ = f32[4,8704]{1,0:T(4,128)S(1)} collective-permute-done((f32[4,8704]{1,0:T(4,128)S(1)}, f32[4,8704]{1,0:T(4,128)S(1)}, u32[]{:S(2)}, u32[]{:S(2)}) %collective-permute-start.13) | collective-permute-done | bytes 139296 | tf_op jit(solution)/shard_map/ppermute | solution.py:83
  28.9 1.1 %collective-permute-done.14.refs_6_.refs_2_ = f32[4,8448]{1,0:T(4,128)S(1)} collective-permute-done((f32[4,8448]{1,0:T(4,128)S(1)}, f32[4,8448]{1,0:T(4,128)S(1)}, u32[]{:S(2)}, u32[]{:S(2)}) %collective-permute-start.14) | collective-permute-done | bytes 135200 | tf_op jit(solution)/shard_map/ppermute | solution.py:83
  30.0 2.0 %collective-permute-start.18 = (f32[4,8192]{1,0:T(4,128)S(1)}, f32[4,8192]{1,0:T(4,128)S(1)}, u32[]{:S(2)}, u32[]{:S(2)}) collective-permute-start(f32[4,8192]{1,0:T(4,128)S(1)} %get-tuple-element.64), channel_id=1, source_target_pairs={{0,16},{1,9},{2,18},{3,11},{4,20},{5,13},{6,22},{7,15},{8,24},{9,1... | collective-permute-start | bytes 393224 | tf_op jit(solution)/shard_map/ppermute | solution.py:83
  32.0 0.2 collective-permute-start.19
  32.3 1.1 %early.1 = (f32[16,8192]{1,0:T(8,128)}, f32[4,65536]{1,0:T(4,128)}) custom-call(s32[8]{0:T(128)S(4)} %get-tuple-element.36.owned, f32[4,65536]{1,0:T(4,128)S(1)} %copy-done, f32[272,128]{1,0:T(8,128)S(1)} %get-tuple-element.51.refs_0_.refs_2_, f32[272,128]{1,0:T(8,128)S(1)} %collective-permute-done.7.refs_1_.refs_3_, ...), custom_call_target="tpu_custom_call" | custom-call | tf_op jit(solution)/shard_map/early/pallas_call | solution.py:597
  33.4 1.3 %collective-permute-done.15.refs_1_ = f32[4,12288]{1,0:T(4,128)S(1)} collective-permute-done((f32[4,12288]{1,0:T(4,128)S(1)}, f32[4,12288]{1,0:T(4,128)S(1)}, u32[]{:S(2)}, u32[]{:S(2)}) %collective-permute-start.15) | collective-permute-done | bytes 196640 | tf_op jit(solution)/shard_map/ppermute | solution.py:83
  34.7 0.6 %collective-permute-done.16.refs_2_ = f32[4,16384]{1,0:T(4,128)S(1)} collective-permute-done((f32[4,16384]{1,0:T(4,128)S(1)}, f32[4,16384]{1,0:T(4,128)S(1)}, u32[]{:S(2)}, u32[]{:S(2)}) %collective-permute-start.16) | collective-permute-done | bytes 262176 | tf_op jit(solution)/shard_map/ppermute | solution.py:83
  35.3 1.4 %late.1 = (f32[16,8192]{1,0:T(8,128)}, f32[200,1024]{1,0:T(8,128)}, f32[64,200]{1,0:T(8,128)}, f32[4,65536]{1,0:T(4,128)}) custom-call(s32[8]{0:T(128)S(4)} %get-tuple-element.36.owned, f32[16,8192]{1,0:T(8,128)} %get-tuple-element.57._, f32[4,65536]{1,0:T(4,128)} %get-tuple-element.58.__, ...), custom_call_target="tpu_custom_call", output_to_operand_aliasing={{0}: (1, {}), {3}: (2, {})} | custom-call | tf_op jit(solution)/shard_map/late/pallas_call | solution.py:580
  36.7 0.6 %collective-permute-done.18.refs_0_ = f32[4,8192]{1,0:T(4,128)S(1)} collective-permute-done((f32[4,8192]{1,0:T(4,128)S(1)}, f32[4,8192]{1,0:T(4,128)S(1)}, u32[]{:S(2)}, u32[]{:S(2)}) %collective-permute-start.18) | collective-permute-done | bytes 131104 | tf_op jit(solution)/shard_map/ppermute | solution.py:83
  37.4 0.8 %last.1 = f32[4,65536]{1,0:T(4,128)} custom-call(s32[8]{0:T(128)S(4)} %get-tuple-element.36.owned, f32[4,65536]{1,0:T(4,128)} %get-tuple-element.63._, f32[4,65536]{1,0:T(4,128)S(1)} %copy-done, f32[4,8192]{1,0:T(4,128)S(1)} %collective-permute-done.18.refs_0_, f32[4,8192]{1,0:T(4,128)S(1)} %collective-permute-done.19.refs_1_), custom_call_target="tpu_custom_call", output_to_operand_aliasing={{}: (1, {})} | custom-call | tf_op jit(solution)/shard_map/last/pallas_call | solution.py:580
  (31 shorter events, 0.2 us)
Async XLA Ops:
  0.6 11.2 %copy-start.1 = (f32[200,1024]{1,0:T(8,128)S(1)}, f32[200,1024]{1,0:T(8,128)}, u32[]{:S(2)}) copy-start(f32[200,1024]{1,0:T(8,128)} %anchor.1) | copy-start | bytes 2457604
  0.6 11.1 %copy-start.3 = (f32[1,200,1024]{2,1,0:T(8,128)S(1)}, f32[1,200,1024]{2,1,0:T(8,128)}, u32[]{:S(2)}) copy-start(f32[1,200,1024]{2,1,0:T(8,128)} %refs_1_.3) | copy-start | bytes 2457604
  2.4 9.4 %copy-start.2 = (f32[1024,64]{0,1:T(8,128)S(1)}, f32[1024,64]{0,1:T(8,128)}, u32[]{:S(2)}) copy-start(f32[1024,64]{0,1:T(8,128)} %param.15) | copy-start | bytes 786436
  2.4 4.6 %collective-permute-start = (f32[4,4,2048]{2,1,0:T(4,128)S(1)}, f32[4,4,2048]{2,1,0:T(4,128)S(1)}, u32[]{:S(2)}, u32[]{:S(2)}) collective-permute-start(f32[4,4,2048]{2,1,0:T(4,128)S(1)} %get-tuple-element.38), channel_id=1, source_target_pairs={{0,1},{1,0},{2,3},{3,2},{4,5},{5,4},{6,7},{7,6},{8,9},{9,8},{10,11... | collective-permute-start | bytes 393224 | tf_op jit(solution)/shard_map/ppermute | solution.py:69
  2.9 8.3 %collective-permute-start.4 = (f32[256,128]{1,0:T(8,128)S(1)}, f32[256,128]{1,0:T(8,128)S(1)}, u32[]{:S(2)}, u32[]{:S(2)}) collective-permute-start(f32[256,128]{1,0:T(8,128)S(1)} %get-tuple-element.46), channel_id=1, source_target_pairs={{0,8},{8,0},{16,24},{24,16},{1,9},{9,1},{17,25},{25,17},{2,10},{10... | collective-permute-start | bytes 393224 | tf_op jit(solution)/shard_map/ppermute | solution.py:69
  5.4 8.4 %collective-permute-start.5 = (f32[256,128]{1,0:T(8,128)S(1)}, f32[256,128]{1,0:T(8,128)S(1)}, u32[]{:S(2)}, u32[]{:S(2)}) collective-permute-start(f32[256,128]{1,0:T(8,128)S(1)} %get-tuple-element.47), channel_id=1, source_target_pairs={{0,16},{8,24},{16,0},{24,8},{1,17},{9,25},{17,1},{25,9},{2,18},{10... | collective-permute-start | bytes 393224 | tf_op jit(solution)/shard_map/ppermute | solution.py:69
  7.0 6.9 %collective-permute-start.6 = (f32[256,128]{1,0:T(8,128)S(1)}, f32[256,128]{1,0:T(8,128)S(1)}, u32[]{:S(2)}, u32[]{:S(2)}) collective-permute-start(f32[256,128]{1,0:T(8,128)S(1)} %get-tuple-element.48), channel_id=1, source_target_pairs={{0,24},{8,16},{16,8},{24,0},{1,25},{9,17},{17,9},{25,1},{2,26},{10... | collective-permute-start | bytes 393224 | tf_op jit(solution)/shard_map/ppermute | solution.py:69
  7.0 10.6 %collective-permute-start.1 = (f32[2,4,2048]{2,1,0:T(4,128)S(1)}, f32[2,4,2048]{2,1,0:T(4,128)S(1)}, u32[]{:S(2)}, u32[]{:S(2)}) collective-permute-start(f32[2,4,2048]{2,1,0:T(4,128)S(1)} %get-tuple-element.39), channel_id=1, source_target_pairs={{0,6},{1,7},{2,4},{3,5},{4,2},{5,3},{6,0},{7,1},{8,14},{9,15},{10,... | collective-permute-start | bytes 196616 | tf_op jit(solution)/shard_map/ppermute | solution.py:69
  11.1 7.3 %collective-permute-start.2 = (f32[2,4,2048]{2,1,0:T(4,128)S(1)}, f32[2,4,2048]{2,1,0:T(4,128)S(1)}, u32[]{:S(2)}, u32[]{:S(2)}) collective-permute-start(f32[2,4,2048]{2,1,0:T(4,128)S(1)} %get-tuple-element.40), channel_id=1, source_target_pairs={{0,4},{1,5},{2,6},{3,7},{4,0},{5,1},{6,2},{7,3},{8,12},{9,13},{10,... | collective-permute-start | bytes 196616 | tf_op jit(solution)/shard_map/ppermute | solution.py:69
  11.1 7.3 %collective-permute-start.3 = (f32[2,4,2048]{2,1,0:T(4,128)S(1)}, f32[2,4,2048]{2,1,0:T(4,128)S(1)}, u32[]{:S(2)}, u32[]{:S(2)}) collective-permute-start(f32[2,4,2048]{2,1,0:T(4,128)S(1)} %get-tuple-element.41), channel_id=1, source_target_pairs={{0,2},{1,3},{2,0},{3,1},{4,6},{5,7},{6,4},{7,5},{8,10},{9,11},{10,... | collective-permute-start | bytes 196616 | tf_op jit(solution)/shard_map/ppermute | solution.py:69
  11.8 6.6 %copy-start = (f32[4,65536]{1,0:T(4,128)S(1)}, f32[4,65536]{1,0:T(4,128)}, u32[]{:S(2)}) copy-start(f32[4,65536]{1,0:T(4,128)} %momentum.5) | copy-start | bytes 3145732
  13.9 6.9 %collective-permute-start.9 = (f32[2,4,2048]{2,1,0:T(4,128)S(1)}, f32[2,4,2048]{2,1,0:T(4,128)S(1)}, u32[]{:S(2)}, u32[]{:S(2)}) collective-permute-start(f32[2,4,2048]{2,1,0:T(4,128)S(1)} %get-tuple-element.53), channel_id=1, source_target_pairs={{0,6},{1,7},{2,4},{3,5},{4,2},{5,3},{6,0},{7,1},{8,14},{9,15},{10,... | collective-permute-start | bytes 196616 | tf_op jit(solution)/shard_map/ppermute | solution.py:69
  17.6 5.3 %collective-permute-start.10 = (f32[2,4,2048]{2,1,0:T(4,128)S(1)}, f32[2,4,2048]{2,1,0:T(4,128)S(1)}, u32[]{:S(2)}, u32[]{:S(2)}) collective-permute-start(f32[2,4,2048]{2,1,0:T(4,128)S(1)} %get-tuple-element.54), channel_id=1, source_target_pairs={{0,4},{1,5},{2,6},{3,7},{4,0},{5,1},{6,2},{7,3},{8,12},{9,13},{10,... | collective-permute-start | bytes 196616 | tf_op jit(solution)/shard_map/ppermute | solution.py:69
  17.6 5.3 %collective-permute-start.11 = (f32[2,4,2048]{2,1,0:T(4,128)S(1)}, f32[2,4,2048]{2,1,0:T(4,128)S(1)}, u32[]{:S(2)}, u32[]{:S(2)}) collective-permute-start(f32[2,4,2048]{2,1,0:T(4,128)S(1)} %get-tuple-element.55), channel_id=1, source_target_pairs={{0,2},{1,3},{2,0},{3,1},{4,6},{5,7},{6,4},{7,5},{8,10},{9,11},{10,... | collective-permute-start | bytes 196616 | tf_op jit(solution)/shard_map/ppermute | solution.py:69
  18.7 7.2 %collective-permute-start.8 = (f32[384,128]{1,0:T(8,128)S(1)}, f32[384,128]{1,0:T(8,128)S(1)}, u32[]{:S(2)}, u32[]{:S(2)}) collective-permute-start(f32[384,128]{1,0:T(8,128)S(1)} %get-tuple-element.52), channel_id=1, source_target_pairs={{0,16},{1,9},{2,18},{3,11},{4,20},{5,13},{6,22},{7,15},{8,24},{9,1... | collective-permute-start | bytes 589832 | tf_op jit(solution)/shard_map/ppermute | solution.py:83
  20.3 5.6 %collective-permute-start.7 = (f32[272,128]{1,0:T(8,128)S(1)}, f32[272,128]{1,0:T(8,128)S(1)}, u32[]{:S(2)}, u32[]{:S(2)}) collective-permute-start(f32[272,128]{1,0:T(8,128)S(1)} %get-tuple-element.51.refs_0_.refs_2_), channel_id=1, source_target_pairs={{0,8},{1,17},{2,10},{3,19},{4,12},{5,21},{6,14},{7,23},{8,0},{9,25... | collective-permute-start | bytes 417800 | tf_op jit(solution)/shard_map/ppermute | solution.py:83
  22.9 1.7 %collective-permute-start.12 = (f32[4,8448]{1,0:T(4,128)S(1)}, f32[4,8448]{1,0:T(4,128)S(1)}, u32[]{:S(2)}, u32[]{:S(2)}) collective-permute-start(f32[4,8448]{1,0:T(4,128)S(1)} %other.1), channel_id=1, source_target_pairs={{0,1},{1,0},{2,3},{3,2},{4,5},{5,4},{6,7},{7,6},{8,9},{9,8},{10,11... | collective-permute-start | bytes 405512 | tf_op jit(solution)/shard_map/ppermute | solution.py:69
  23.0 5.9 %collective-permute-start.13 = (f32[4,8704]{1,0:T(4,128)S(1)}, f32[4,8704]{1,0:T(4,128)S(1)}, u32[]{:S(2)}, u32[]{:S(2)}) collective-permute-start(f32[4,8704]{1,0:T(4,128)S(1)} %mine.1.refs_3_.refs_0_), channel_id=1, source_target_pairs={{0,8},{1,17},{2,10},{3,19},{4,12},{5,21},{6,14},{7,23},{8,0},{9,25... | collective-permute-start | bytes 417800 | tf_op jit(solution)/shard_map/ppermute | solution.py:83
  24.6 5.4 %collective-permute-start.14 = (f32[4,8448]{1,0:T(4,128)S(1)}, f32[4,8448]{1,0:T(4,128)S(1)}, u32[]{:S(2)}, u32[]{:S(2)}) collective-permute-start(f32[4,8448]{1,0:T(4,128)S(1)} %collective-permute-done.12.refs_4_.refs_1_), channel_id=1, source_target_pairs={{0,16},{1,9},{2,18},{3,11},{4,20},{5,13},{6,22},{7,15},{8,24},{9,1... | collective-permute-start | bytes 405512 | tf_op jit(solution)/shard_map/ppermute | solution.py:83
  25.9 4.1 %collective-permute-start.17 = (f32[260,128]{1,0:T(8,128)S(1)}, f32[260,128]{1,0:T(8,128)S(1)}, u32[]{:S(2)}, u32[]{:S(2)}) collective-permute-start(f32[260,128]{1,0:T(8,128)S(1)} %gathered.1), channel_id=1, source_target_pairs={{0,1},{1,0},{2,3},{3,2},{4,5},{5,4},{6,7},{7,6},{8,9},{9,8},{10,11... | collective-permute-start | bytes 399368 | tf_op jit(solution)/shard_map/ppermute | solution.py:69
  26.0 9.2 %collective-permute-start.16 = (f32[4,16384]{1,0:T(4,128)S(1)}, f32[4,16384]{1,0:T(4,128)S(1)}, u32[]{:S(2)}, u32[]{:S(2)}) collective-permute-start(f32[4,16384]{1,0:T(4,128)S(1)} %get-tuple-element.61), channel_id=1, source_target_pairs={{0,8},{1,17},{2,10},{3,19},{4,12},{5,21},{6,14},{7,23},{8,0},{9,25... | collective-permute-start | bytes 786440 | tf_op jit(solution)/shard_map/ppermute | solution.py:83
  26.9 7.8 %collective-permute-start.15 = (f32[4,12288]{1,0:T(4,128)S(1)}, f32[4,12288]{1,0:T(4,128)S(1)}, u32[]{:S(2)}, u32[]{:S(2)}) collective-permute-start(f32[4,12288]{1,0:T(4,128)S(1)} %get-tuple-element.60), channel_id=1, source_target_pairs={{0,16},{1,9},{2,18},{3,11},{4,20},{5,13},{6,22},{7,15},{8,24},{9,1... | collective-permute-start | bytes 589832 | tf_op jit(solution)/shard_map/ppermute | solution.py:83
  30.0 7.3 %collective-permute-start.18 = (f32[4,8192]{1,0:T(4,128)S(1)}, f32[4,8192]{1,0:T(4,128)S(1)}, u32[]{:S(2)}, u32[]{:S(2)}) collective-permute-start(f32[4,8192]{1,0:T(4,128)S(1)} %get-tuple-element.64), channel_id=1, source_target_pairs={{0,16},{1,9},{2,18},{3,11},{4,20},{5,13},{6,22},{7,15},{8,24},{9,1... | collective-permute-start | bytes 393224 | tf_op jit(solution)/shard_map/ppermute | solution.py:83
  32.0 5.3 %collective-permute-start.19 = (f32[4,8192]{1,0:T(4,128)S(1)}, f32[4,8192]{1,0:T(4,128)S(1)}, u32[]{:S(2)}, u32[]{:S(2)}) collective-permute-start(f32[4,8192]{1,0:T(4,128)S(1)} %get-tuple-element.65), channel_id=1, source_target_pairs={{0,8},{1,17},{2,10},{3,19},{4,12},{5,21},{6,14},{7,23},{8,0},{9,25... | collective-permute-start | bytes 393224 | tf_op jit(solution)/shard_map/ppermute | solution.py:83
  32.3 3.0 %copy-start.4 = (f32[200,64]{0,1:T(8,128)S(1)}, f32[200,64]{0,1:T(8,128)}, u32[]{:S(2)}) copy-start(f32[200,64]{0,1:T(8,128)} %param.14) | copy-start | bytes 153604

commit v8 on v7

--- a/solution.py
+++ b/solution.py
@@ -551,7 +551,7 @@
         name="again",
     )
     (sign,) = run(
-        cut_body, [kept((260, 128))], [plain], after=[dense[k] for k in (2, 1)], name="gathered"
+        cut_body, [kept((dense_rows + 4, 128))], [plain], after=dense[1:], name="gathered"
     )
     sign = swap(sign, "own", owner_count, 1)
     near1 = swap_in_turn(halves[0], 0)
@@ -563,19 +563,10 @@
         after=[sign],
         name="pass_on",
     )
-    gradient = [
-        *halves,
-        near1,
-        swap_in_turn(again[1], 0),
-        swap_in_turn(again[0], 1),
-        near2,
-        swap_in_turn(passed[0], 1),
-        swap_in_turn(passed[1], 0),
-    ]
-
-    own_rows, own_crossed, near1, late2, late1, near2, last1, last2 = gradient
-
-    def finishing(body, halves, outs, operands, aliased=(), scratch=(), name=None):
+    late2, late1 = swap_in_turn(again[1], 0), swap_in_turn(again[0], 1)
+    last1, last2 = swap_in_turn(passed[0], 1), swap_in_turn(passed[1], 0)
+
+    def finishing(body, halves, outs, operands, aliased=(), before=(), after=(), name=None):
         made = (len(halves), chips, slot_count, part)
         return pl.pallas_call(
             functools.partial(body, part, direct, halves),
@@ -583,10 +574,10 @@
             in_specs=[smem] + [anywhere] * len(aliased) + [vmem] * len(operands),
             out_specs=[anywhere] * len(outs),
             scratch_shapes=[
-                *scratch[:2],
+                *before,
                 pltpu.VMEM(made, f32),
                 pltpu.SemaphoreType.DMA(made[:2]),
-                *scratch[2:],
+                *after,
             ],
             input_output_aliases={1 + i: out for i, (_, out) in enumerate(aliased)},
             compiler_params=pltpu.CompilerParams(vmem_limit_bytes=vmem_limit),
@@ -594,22 +585,16 @@
         )(in_scalars(owned), *[x for x, _ in aliased], *[on_chip(x) for x in operands])
 
     held = momentum_dense.shape
-    new_dense, new_momentum_dense = pl.pallas_call(
-        functools.partial(early_body, part, direct, ((0, 0), (0, 1), (1, 0), (2, 1))),
-        out_shape=[stored(anchor_dense.shape), stored(held)],
-        in_specs=[smem] + [vmem] * (5 + len(dense)),
-        out_specs=[anywhere] * 2,
-        scratch_shapes=[
-            pltpu.VMEM((4, chips, slot_count, part), f32),
-            pltpu.SemaphoreType.DMA((4, chips)),
+    new_dense, new_momentum_dense = finishing(
+        early_body,
+        ((0, 0), (0, 1), (1, 0), (2, 1)),
+        [anchor_dense.shape, held],
+        [momentum, *dense, *halves, near1, near2],
+        after=[
             pltpu.VMEM((groups - 1, blocks, part), f32),
             pltpu.SemaphoreType.DMA((groups - 1,)),
         ],
-        compiler_params=pltpu.CompilerParams(vmem_limit_bytes=vmem_limit),
         name="early",
-    )(
-        in_scalars(owned),
-        *[on_chip(x) for x in (momentum, *dense, own_rows, own_crossed, near1, near2)],
     )
     new_dense, new_emb, new_momentum_t, new_momentum_dense = finishing(
         late_body,
@@ -617,9 +602,8 @@
         [anchor_dense.shape, anchor_emb.shape, (rank, rows), held],
         [anchor_emb, momentum_emb.T, basis_t, momentum, pair, late1, late2],
         aliased=[(new_dense, 0), (new_momentum_dense, 3)],
-        scratch=[
-            pltpu.VMEM((rank, rows), f32),
-            pltpu.SemaphoreType.DMA((3,)),
+        before=[pltpu.VMEM((rank, rows), f32), pltpu.SemaphoreType.DMA((3,))],
+        after=[
             pltpu.VMEM((blocks, part), f32),
             pltpu.VMEM(anchor_emb.shape, f32),
             pltpu.VMEM((rank, rows), f32),

time: 38.3 us -> 38.3 us (level)
    pallas_call x2 -> x3, Pallas kernels: 2.18 us -> 3.3 us  [finishing(): pl.pallas_call(functools.partial(body, part, direct, halves), out_shape=[...]
    pallas_call x1 -> x0, Pallas kernels: 1.12 us -> none  [per_device(): pl.pallas_call(functools.partial(early_body, part, direct, ((0, 0), (0, 1...]
where the time goes in v8:
time: 38.3 us; the launch traced here: 38.1 us
  starting transfers between devices  23.3 us (61%)
  waiting for transfers between devices  8.2 us (21%)
  Pallas kernels  5.88 us (15%)
  between operations  0.78 us (2%)
    ppermute x12, starting transfers between devices, swap(): return lax.ppermute(x, axis, [(i, i ^ mask) for i in range(count)])  14 us
    ppermute x8, starting transfers between devices, swap_in_turn(): return lax.ppermute(x, ('rep', 'own'), pairs)  9.27 us
    ppermute x8, waiting for transfers between devices, swap_in_turn(): return lax.ppermute(x, ('rep', 'own'), pairs)  4.46 us
    ppermute x12, waiting for transfers between devices, swap(): return lax.ppermute(x, axis, [(i, i ^ mask) for i in range(count)])  3.74 us
    pallas_call x3, Pallas kernels, finishing(): pl.pallas_call(functools.partial(body, part, direct, halves), out_shape=[...  3.3 us
    pallas_call x10, Pallas kernels, run(): pl.pallas_call(whole, out_shape=list(outs), in_specs=[anywhere] * skip +...  2.58 us
  transfers between devices with their start and end apart: 20, of which 7 were waited for; matrix products, arithmetic and copies ran while one was open for 0% of the time, Pallas kernels for 9%

profile of v8, /device:TPU:0, one launch (start us, length us, event | category | flops | bytes accessed | tf_op | source)
XLA Modules:
  0.0 38.1 jit_solution(43299741835730072)
XLA Ops:
  0.7 1.7 %start.1 = (f32[256,128]{1,0:T(8,128)S(1)}, f32[256,128]{1,0:T(8,128)S(1)}, f32[256,128]{1,0:T(8,128)S(1)}, f32[256,128]{1,0:T(8,128)S(1)}, f32[16,2048]{1,0:T(8...) custom-call(s32[16]{0:T(128)} %bitcast.7, ...), custom_call_target="tpu_custom_call" | custom-call | tf_op jit(solution)/shard_map/start/pallas_call | solution.py:49
  2.4 0.5 %collective-permute-start = (f32[4,4,2048]{2,1,0:T(4,128)S(1)}, f32[4,4,2048]{2,1,0:T(4,128)S(1)}, u32[]{:S(2)}, u32[]{:S(2)}) collective-permute-start(f32[4,4,2048]{2,1,0:T(4,128)S(1)} %get-tuple-element.38), channel_id=1, source_target_pairs={{0,1},{1,0},{2,3},{3,2},{4,5},{5,4},{6,7},{7,6},{8,9},{9,8},{10,11... | collective-permute-start | bytes 393224 | tf_op jit(solution)/shard_map/ppermute | solution.py:69
  2.9 2.6 %collective-permute-start.4 = (f32[256,128]{1,0:T(8,128)S(1)}, f32[256,128]{1,0:T(8,128)S(1)}, u32[]{:S(2)}, u32[]{:S(2)}) collective-permute-start(f32[256,128]{1,0:T(8,128)S(1)} %get-tuple-element.46), channel_id=1, source_target_pairs={{0,8},{8,0},{16,24},{24,16},{1,9},{9,1},{17,25},{25,17},{2,10},{10... | collective-permute-start | bytes 393224 | tf_op jit(solution)/shard_map/ppermute | solution.py:69
  5.4 1.5 %collective-permute-start.5 = (f32[256,128]{1,0:T(8,128)S(1)}, f32[256,128]{1,0:T(8,128)S(1)}, u32[]{:S(2)}, u32[]{:S(2)}) collective-permute-start(f32[256,128]{1,0:T(8,128)S(1)} %get-tuple-element.47), channel_id=1, source_target_pairs={{0,16},{8,24},{16,0},{24,8},{1,17},{9,25},{17,1},{25,9},{2,18},{10... | collective-permute-start | bytes 393224 | tf_op jit(solution)/shard_map/ppermute | solution.py:69
  7.0 4.1 %collective-permute-start.1 = (f32[2,4,2048]{2,1,0:T(4,128)S(1)}, f32[2,4,2048]{2,1,0:T(4,128)S(1)}, u32[]{:S(2)}, u32[]{:S(2)}) collective-permute-start(f32[2,4,2048]{2,1,0:T(4,128)S(1)} %get-tuple-element.39), channel_id=1, source_target_pairs={{0,6},{1,7},{2,4},{3,5},{4,2},{5,3},{6,0},{7,1},{8,14},{9,15},{10,... | collective-permute-start | bytes 196616 | tf_op jit(solution)/shard_map/ppermute | solution.py:69
  11.1 0.6 %collective-permute-start.3 = (f32[2,4,2048]{2,1,0:T(4,128)S(1)}, f32[2,4,2048]{2,1,0:T(4,128)S(1)}, u32[]{:S(2)}, u32[]{:S(2)}) collective-permute-start(f32[2,4,2048]{2,1,0:T(4,128)S(1)} %get-tuple-element.41), channel_id=1, source_target_pairs={{0,2},{1,3},{2,0},{3,1},{4,6},{5,7},{6,4},{7,5},{8,10},{9,11},{10,... | collective-permute-start | bytes 196616 | tf_op jit(solution)/shard_map/ppermute | solution.py:69
  11.8 0.4 %factor.1.refs_0_.refs_7_.refs_2_ = f32[64,200]{1,0:T(8,128)S(1)} custom-call(f32[200,1024]{1,0:T(8,128)S(1)} %copy-done.1, f32[1,200,1024]{2,1,0:T(8,128)S(1)} %copy-done.3, f32[64,1024]{1,0:T(8,128)S(1)} %bitcast.4), custom_call_target="tpu_custom_call" | custom-call | tf_op jit(solution)/shard_map/factor/pallas_call | solution.py:49
  12.2 1.6 %collective-permute-done.5.refs_4_ = f32[256,128]{1,0:T(8,128)S(1)} collective-permute-done((f32[256,128]{1,0:T(8,128)S(1)}, f32[256,128]{1,0:T(8,128)S(1)}, u32[]{:S(2)}, u32[]{:S(2)}) %collective-permute-start.5) | collective-permute-done | bytes 131104 | tf_op jit(solution)/shard_map/ppermute | solution.py:69
  13.8 0.1 mean.1
  13.9 3.7 %collective-permute-start.9 = (f32[2,4,2048]{2,1,0:T(4,128)S(1)}, f32[2,4,2048]{2,1,0:T(4,128)S(1)}, u32[]{:S(2)}, u32[]{:S(2)}) collective-permute-start(f32[2,4,2048]{2,1,0:T(4,128)S(1)} %get-tuple-element.53), channel_id=1, source_target_pairs={{0,6},{1,7},{2,4},{3,5},{4,2},{5,3},{6,0},{7,1},{8,14},{9,15},{10,... | collective-permute-start | bytes 196616 | tf_op jit(solution)/shard_map/ppermute | solution.py:69
  17.6 0.8 %collective-permute-start.11 = (f32[2,4,2048]{2,1,0:T(4,128)S(1)}, f32[2,4,2048]{2,1,0:T(4,128)S(1)}, u32[]{:S(2)}, u32[]{:S(2)}) collective-permute-start(f32[2,4,2048]{2,1,0:T(4,128)S(1)} %get-tuple-element.55), channel_id=1, source_target_pairs={{0,2},{1,3},{2,0},{3,1},{4,6},{5,7},{6,4},{7,5},{8,10},{9,11},{10,... | collective-permute-start | bytes 196616 | tf_op jit(solution)/shard_map/ppermute | solution.py:69
  18.4 0.3 dense.1
  18.7 1.6 %collective-permute-start.8 = (f32[384,128]{1,0:T(8,128)S(1)}, f32[384,128]{1,0:T(8,128)S(1)}, u32[]{:S(2)}, u32[]{:S(2)}) collective-permute-start(f32[384,128]{1,0:T(8,128)S(1)} %get-tuple-element.52), channel_id=1, source_target_pairs={{0,16},{1,9},{2,18},{3,11},{4,20},{5,13},{6,22},{7,15},{8,24},{9,1... | collective-permute-start | bytes 589832 | tf_op jit(solution)/shard_map/ppermute | solution.py:83
  20.3 0.5 %collective-permute-start.7 = (f32[272,128]{1,0:T(8,128)S(1)}, f32[272,128]{1,0:T(8,128)S(1)}, u32[]{:S(2)}, u32[]{:S(2)}) collective-permute-start(f32[272,128]{1,0:T(8,128)S(1)} %get-tuple-element.51.refs_0_.refs_2_), channel_id=1, source_target_pairs={{0,8},{1,17},{2,10},{3,19},{4,12},{5,21},{6,14},{7,23},{8,0},{9,25... | collective-permute-start | bytes 417800 | tf_op jit(solution)/shard_map/ppermute | solution.py:83
  20.8 2.1 %collective-permute-done.10.refs_1_.refs_5_ = f32[2,4,2048]{2,1,0:T(4,128)S(1)} collective-permute-done((f32[2,4,2048]{2,1,0:T(4,128)S(1)}, f32[2,4,2048]{2,1,0:T(4,128)S(1)}, u32[]{:S(2)}, u32[]{:S(2)}) %collective-permute-start.10) | collective-permute-done | bytes 65568 | tf_op jit(solution)/shard_map/ppermute | solution.py:69
  22.9 0.1 collective-permute-start.12
  23.0 1.6 %collective-permute-start.13 = (f32[4,8704]{1,0:T(4,128)S(1)}, f32[4,8704]{1,0:T(4,128)S(1)}, u32[]{:S(2)}, u32[]{:S(2)}) collective-permute-start(f32[4,8704]{1,0:T(4,128)S(1)} %mine.1.refs_3_.refs_0_), channel_id=1, source_target_pairs={{0,8},{1,17},{2,10},{3,19},{4,12},{5,21},{6,14},{7,23},{8,0},{9,25... | collective-permute-start | bytes 417800 | tf_op jit(solution)/shard_map/ppermute | solution.py:83
  24.6 1.3 %collective-permute-start.14 = (f32[4,8448]{1,0:T(4,128)S(1)}, f32[4,8448]{1,0:T(4,128)S(1)}, u32[]{:S(2)}, u32[]{:S(2)}) collective-permute-start(f32[4,8448]{1,0:T(4,128)S(1)} %collective-permute-done.12.refs_4_.refs_1_), channel_id=1, source_target_pairs={{0,16},{1,9},{2,18},{3,11},{4,20},{5,13},{6,22},{7,15},{8,24},{9,1... | collective-permute-start | bytes 405512 | tf_op jit(solution)/shard_map/ppermute | solution.py:83
  25.9 0.1 collective-permute-start.17
  26.0 0.1 again.1
  26.0 0.8 %collective-permute-start.16 = (f32[4,16384]{1,0:T(4,128)S(1)}, f32[4,16384]{1,0:T(4,128)S(1)}, u32[]{:S(2)}, u32[]{:S(2)}) collective-permute-start(f32[4,16384]{1,0:T(4,128)S(1)} %get-tuple-element.61), channel_id=1, source_target_pairs={{0,8},{1,17},{2,10},{3,19},{4,12},{5,21},{6,14},{7,23},{8,0},{9,25... | collective-permute-start | bytes 786440 | tf_op jit(solution)/shard_map/ppermute | solution.py:83
  26.9 1.2 %collective-permute-start.15 = (f32[4,12288]{1,0:T(4,128)S(1)}, f32[4,12288]{1,0:T(4,128)S(1)}, u32[]{:S(2)}, u32[]{:S(2)}) collective-permute-start(f32[4,12288]{1,0:T(4,128)S(1)} %get-tuple-element.60), channel_id=1, source_target_pairs={{0,16},{1,9},{2,18},{3,11},{4,20},{5,13},{6,22},{7,15},{8,24},{9,1... | collective-permute-start | bytes 589832 | tf_op jit(solution)/shard_map/ppermute | solution.py:83
  28.1 0.8 %collective-permute-done.13.refs_5_.refs_1_ = f32[4,8704]{1,0:T(4,128)S(1)} collective-permute-done((f32[4,8704]{1,0:T(4,128)S(1)}, f32[4,8704]{1,0:T(4,128)S(1)}, u32[]{:S(2)}, u32[]{:S(2)}) %collective-permute-start.13) | collective-permute-done | bytes 139296 | tf_op jit(solution)/shard_map/ppermute | solution.py:83
  28.9 1.1 %collective-permute-done.14.refs_6_.refs_2_ = f32[4,8448]{1,0:T(4,128)S(1)} collective-permute-done((f32[4,8448]{1,0:T(4,128)S(1)}, f32[4,8448]{1,0:T(4,128)S(1)}, u32[]{:S(2)}, u32[]{:S(2)}) %collective-permute-start.14) | collective-permute-done | bytes 135200 | tf_op jit(solution)/shard_map/ppermute | solution.py:83
  30.0 2.0 %collective-permute-start.18 = (f32[4,8192]{1,0:T(4,128)S(1)}, f32[4,8192]{1,0:T(4,128)S(1)}, u32[]{:S(2)}, u32[]{:S(2)}) collective-permute-start(f32[4,8192]{1,0:T(4,128)S(1)} %get-tuple-element.64), channel_id=1, source_target_pairs={{0,16},{1,9},{2,18},{3,11},{4,20},{5,13},{6,22},{7,15},{8,24},{9,1... | collective-permute-start | bytes 393224 | tf_op jit(solution)/shard_map/ppermute | solution.py:83
  32.0 0.2 collective-permute-start.19
  32.3 1.1 %early.1 = (f32[16,8192]{1,0:T(8,128)}, f32[4,65536]{1,0:T(4,128)}) custom-call(s32[8]{0:T(128)S(4)} %get-tuple-element.36.owned, f32[4,65536]{1,0:T(4,128)S(1)} %copy-done, f32[272,128]{1,0:T(8,128)S(1)} %get-tuple-element.51.refs_0_.refs_2_, f32[272,128]{1,0:T(8,128)S(1)} %collective-permute-done.7.refs_1_.refs_3_.refs_0_, ...), custom_call_target="tpu_custom_call" | custom-call | tf_op jit(solution)/shard_map/early/pallas_call | solution.py:571
  33.4 1.3 %collective-permute-done.15.refs_1_ = f32[4,12288]{1,0:T(4,128)S(1)} collective-permute-done((f32[4,12288]{1,0:T(4,128)S(1)}, f32[4,12288]{1,0:T(4,128)S(1)}, u32[]{:S(2)}, u32[]{:S(2)}) %collective-permute-start.15) | collective-permute-done | bytes 196640 | tf_op jit(solution)/shard_map/ppermute | solution.py:83
  34.7 0.6 %collective-permute-done.16.refs_2_ = f32[4,16384]{1,0:T(4,128)S(1)} collective-permute-done((f32[4,16384]{1,0:T(4,128)S(1)}, f32[4,16384]{1,0:T(4,128)S(1)}, u32[]{:S(2)}, u32[]{:S(2)}) %collective-permute-start.16) | collective-permute-done | bytes 262176 | tf_op jit(solution)/shard_map/ppermute | solution.py:83
  35.3 1.4 %late.1 = (f32[16,8192]{1,0:T(8,128)}, f32[200,1024]{1,0:T(8,128)}, f32[64,200]{1,0:T(8,128)}, f32[4,65536]{1,0:T(4,128)}) custom-call(s32[8]{0:T(128)S(4)} %get-tuple-element.36.owned, f32[16,8192]{1,0:T(8,128)} %get-tuple-element.57._, f32[4,65536]{1,0:T(4,128)} %get-tuple-element.58.__, ...), custom_call_target="tpu_custom_call", output_to_operand_aliasing={{0}: (1, {}), {3}: (2, {})} | custom-call | tf_op jit(solution)/shard_map/late/pallas_call | solution.py:571
  36.7 0.6 %collective-permute-done.18.refs_0_ = f32[4,8192]{1,0:T(4,128)S(1)} collective-permute-done((f32[4,8192]{1,0:T(4,128)S(1)}, f32[4,8192]{1,0:T(4,128)S(1)}, u32[]{:S(2)}, u32[]{:S(2)}) %collective-permute-start.18) | collective-permute-done | bytes 131104 | tf_op jit(solution)/shard_map/ppermute | solution.py:83
  37.4 0.8 %last.1 = f32[4,65536]{1,0:T(4,128)} custom-call(s32[8]{0:T(128)S(4)} %get-tuple-element.36.owned, f32[4,65536]{1,0:T(4,128)} %get-tuple-element.63._, f32[4,65536]{1,0:T(4,128)S(1)} %copy-done, f32[4,8192]{1,0:T(4,128)S(1)} %collective-permute-done.18.refs_0_, f32[4,8192]{1,0:T(4,128)S(1)} %collective-permute-done.19.refs_1_), custom_call_target="tpu_custom_call", output_to_operand_aliasing={{}: (1, {})} | custom-call | tf_op jit(solution)/shard_map/last/pallas_call | solution.py:571
  (31 shorter events, 0.2 us)
Async XLA Ops:
  0.6 11.2 %copy-start.1 = (f32[200,1024]{1,0:T(8,128)S(1)}, f32[200,1024]{1,0:T(8,128)}, u32[]{:S(2)}) copy-start(f32[200,1024]{1,0:T(8,128)} %anchor.1) | copy-start | bytes 2457604
  0.6 11.1 %copy-start.3 = (f32[1,200,1024]{2,1,0:T(8,128)S(1)}, f32[1,200,1024]{2,1,0:T(8,128)}, u32[]{:S(2)}) copy-start(f32[1,200,1024]{2,1,0:T(8,128)} %refs_1_.3) | copy-start | bytes 2457604
  2.4 9.4 %copy-start.2 = (f32[1024,64]{0,1:T(8,128)S(1)}, f32[1024,64]{0,1:T(8,128)}, u32[]{:S(2)}) copy-start(f32[1024,64]{0,1:T(8,128)} %param.15) | copy-start | bytes 786436
  2.4 4.6 %collective-permute-start = (f32[4,4,2048]{2,1,0:T(4,128)S(1)}, f32[4,4,2048]{2,1,0:T(4,128)S(1)}, u32[]{:S(2)}, u32[]{:S(2)}) collective-permute-start(f32[4,4,2048]{2,1,0:T(4,128)S(1)} %get-tuple-element.38), channel_id=1, source_target_pairs={{0,1},{1,0},{2,3},{3,2},{4,5},{5,4},{6,7},{7,6},{8,9},{9,8},{10,11... | collective-permute-start | bytes 393224 | tf_op jit(solution)/shard_map/ppermute | solution.py:69
  2.9 8.3 %collective-permute-start.4 = (f32[256,128]{1,0:T(8,128)S(1)}, f32[256,128]{1,0:T(8,128)S(1)}, u32[]{:S(2)}, u32[]{:S(2)}) collective-permute-start(f32[256,128]{1,0:T(8,128)S(1)} %get-tuple-element.46), channel_id=1, source_target_pairs={{0,8},{8,0},{16,24},{24,16},{1,9},{9,1},{17,25},{25,17},{2,10},{10... | collective-permute-start | bytes 393224 | tf_op jit(solution)/shard_map/ppermute | solution.py:69
  5.4 8.4 %collective-permute-start.5 = (f32[256,128]{1,0:T(8,128)S(1)}, f32[256,128]{1,0:T(8,128)S(1)}, u32[]{:S(2)}, u32[]{:S(2)}) collective-permute-start(f32[256,128]{1,0:T(8,128)S(1)} %get-tuple-element.47), channel_id=1, source_target_pairs={{0,16},{8,24},{16,0},{24,8},{1,17},{9,25},{17,1},{25,9},{2,18},{10... | collective-permute-start | bytes 393224 | tf_op jit(solution)/shard_map/ppermute | solution.py:69
  7.0 6.9 %collective-permute-start.6 = (f32[256,128]{1,0:T(8,128)S(1)}, f32[256,128]{1,0:T(8,128)S(1)}, u32[]{:S(2)}, u32[]{:S(2)}) collective-permute-start(f32[256,128]{1,0:T(8,128)S(1)} %get-tuple-element.48), channel_id=1, source_target_pairs={{0,24},{8,16},{16,8},{24,0},{1,25},{9,17},{17,9},{25,1},{2,26},{10... | collective-permute-start | bytes 393224 | tf_op jit(solution)/shard_map/ppermute | solution.py:69
  7.0 10.6 %collective-permute-start.1 = (f32[2,4,2048]{2,1,0:T(4,128)S(1)}, f32[2,4,2048]{2,1,0:T(4,128)S(1)}, u32[]{:S(2)}, u32[]{:S(2)}) collective-permute-start(f32[2,4,2048]{2,1,0:T(4,128)S(1)} %get-tuple-element.39), channel_id=1, source_target_pairs={{0,6},{1,7},{2,4},{3,5},{4,2},{5,3},{6,0},{7,1},{8,14},{9,15},{10,... | collective-permute-start | bytes 196616 | tf_op jit(solution)/shard_map/ppermute | solution.py:69
  11.1 7.3 %collective-permute-start.2 = (f32[2,4,2048]{2,1,0:T(4,128)S(1)}, f32[2,4,2048]{2,1,0:T(4,128)S(1)}, u32[]{:S(2)}, u32[]{:S(2)}) collective-permute-start(f32[2,4,2048]{2,1,0:T(4,128)S(1)} %get-tuple-element.40), channel_id=1, source_target_pairs={{0,4},{1,5},{2,6},{3,7},{4,0},{5,1},{6,2},{7,3},{8,12},{9,13},{10,... | collective-permute-start | bytes 196616 | tf_op jit(solution)/shard_map/ppermute | solution.py:69
  11.1 7.3 %collective-permute-start.3 = (f32[2,4,2048]{2,1,0:T(4,128)S(1)}, f32[2,4,2048]{2,1,0:T(4,128)S(1)}, u32[]{:S(2)}, u32[]{:S(2)}) collective-permute-start(f32[2,4,2048]{2,1,0:T(4,128)S(1)} %get-tuple-element.41), channel_id=1, source_target_pairs={{0,2},{1,3},{2,0},{3,1},{4,6},{5,7},{6,4},{7,5},{8,10},{9,11},{10,... | collective-permute-start | bytes 196616 | tf_op jit(solution)/shard_map/ppermute | solution.py:69
  11.8 6.6 %copy-start = (f32[4,65536]{1,0:T(4,128)S(1)}, f32[4,65536]{1,0:T(4,128)}, u32[]{:S(2)}) copy-start(f32[4,65536]{1,0:T(4,128)} %momentum.5) | copy-start | bytes 3145732
  13.9 6.9 %collective-permute-start.9 = (f32[2,4,2048]{2,1,0:T(4,128)S(1)}, f32[2,4,2048]{2,1,0:T(4,128)S(1)}, u32[]{:S(2)}, u32[]{:S(2)}) collective-permute-start(f32[2,4,2048]{2,1,0:T(4,128)S(1)} %get-tuple-element.53), channel_id=1, source_target_pairs={{0,6},{1,7},{2,4},{3,5},{4,2},{5,3},{6,0},{7,1},{8,14},{9,15},{10,... | collective-permute-start | bytes 196616 | tf_op jit(solution)/shard_map/ppermute | solution.py:69
  17.6 5.3 %collective-permute-start.10 = (f32[2,4,2048]{2,1,0:T(4,128)S(1)}, f32[2,4,2048]{2,1,0:T(4,128)S(1)}, u32[]{:S(2)}, u32[]{:S(2)}) collective-permute-start(f32[2,4,2048]{2,1,0:T(4,128)S(1)} %get-tuple-element.54), channel_id=1, source_target_pairs={{0,4},{1,5},{2,6},{3,7},{4,0},{5,1},{6,2},{7,3},{8,12},{9,13},{10,... | collective-permute-start | bytes 196616 | tf_op jit(solution)/shard_map/ppermute | solution.py:69
  17.6 5.3 %collective-permute-start.11 = (f32[2,4,2048]{2,1,0:T(4,128)S(1)}, f32[2,4,2048]{2,1,0:T(4,128)S(1)}, u32[]{:S(2)}, u32[]{:S(2)}) collective-permute-start(f32[2,4,2048]{2,1,0:T(4,128)S(1)} %get-tuple-element.55), channel_id=1, source_target_pairs={{0,2},{1,3},{2,0},{3,1},{4,6},{5,7},{6,4},{7,5},{8,10},{9,11},{10,... | collective-permute-start | bytes 196616 | tf_op jit(solution)/shard_map/ppermute | solution.py:69
  18.7 7.2 %collective-permute-start.8 = (f32[384,128]{1,0:T(8,128)S(1)}, f32[384,128]{1,0:T(8,128)S(1)}, u32[]{:S(2)}, u32[]{:S(2)}) collective-permute-start(f32[384,128]{1,0:T(8,128)S(1)} %get-tuple-element.52), channel_id=1, source_target_pairs={{0,16},{1,9},{2,18},{3,11},{4,20},{5,13},{6,22},{7,15},{8,24},{9,1... | collective-permute-start | bytes 589832 | tf_op jit(solution)/shard_map/ppermute | solution.py:83
  20.3 5.6 %collective-permute-start.7 = (f32[272,128]{1,0:T(8,128)S(1)}, f32[272,128]{1,0:T(8,128)S(1)}, u32[]{:S(2)}, u32[]{:S(2)}) collective-permute-start(f32[272,128]{1,0:T(8,128)S(1)} %get-tuple-element.51.refs_0_.refs_2_), channel_id=1, source_target_pairs={{0,8},{1,17},{2,10},{3,19},{4,12},{5,21},{6,14},{7,23},{8,0},{9,25... | collective-permute-start | bytes 417800 | tf_op jit(solution)/shard_map/ppermute | solution.py:83
  22.9 1.7 %collective-permute-start.12 = (f32[4,8448]{1,0:T(4,128)S(1)}, f32[4,8448]{1,0:T(4,128)S(1)}, u32[]{:S(2)}, u32[]{:S(2)}) collective-permute-start(f32[4,8448]{1,0:T(4,128)S(1)} %other.1), channel_id=1, source_target_pairs={{0,1},{1,0},{2,3},{3,2},{4,5},{5,4},{6,7},{7,6},{8,9},{9,8},{10,11... | collective-permute-start | bytes 405512 | tf_op jit(solution)/shard_map/ppermute | solution.py:69
  23.0 5.9 %collective-permute-start.13 = (f32[4,8704]{1,0:T(4,128)S(1)}, f32[4,8704]{1,0:T(4,128)S(1)}, u32[]{:S(2)}, u32[]{:S(2)}) collective-permute-start(f32[4,8704]{1,0:T(4,128)S(1)} %mine.1.refs_3_.refs_0_), channel_id=1, source_target_pairs={{0,8},{1,17},{2,10},{3,19},{4,12},{5,21},{6,14},{7,23},{8,0},{9,25... | collective-permute-start | bytes 417800 | tf_op jit(solution)/shard_map/ppermute | solution.py:83
  24.6 5.4 %collective-permute-start.14 = (f32[4,8448]{1,0:T(4,128)S(1)}, f32[4,8448]{1,0:T(4,128)S(1)}, u32[]{:S(2)}, u32[]{:S(2)}) collective-permute-start(f32[4,8448]{1,0:T(4,128)S(1)} %collective-permute-done.12.refs_4_.refs_1_), channel_id=1, source_target_pairs={{0,16},{1,9},{2,18},{3,11},{4,20},{5,13},{6,22},{7,15},{8,24},{9,1... | collective-permute-start | bytes 405512 | tf_op jit(solution)/shard_map/ppermute | solution.py:83
  25.9 4.1 %collective-permute-start.17 = (f32[260,128]{1,0:T(8,128)S(1)}, f32[260,128]{1,0:T(8,128)S(1)}, u32[]{:S(2)}, u32[]{:S(2)}) collective-permute-start(f32[260,128]{1,0:T(8,128)S(1)} %gathered.1), channel_id=1, source_target_pairs={{0,1},{1,0},{2,3},{3,2},{4,5},{5,4},{6,7},{7,6},{8,9},{9,8},{10,11... | collective-permute-start | bytes 399368 | tf_op jit(solution)/shard_map/ppermute | solution.py:69
  26.0 9.2 %collective-permute-start.16 = (f32[4,16384]{1,0:T(4,128)S(1)}, f32[4,16384]{1,0:T(4,128)S(1)}, u32[]{:S(2)}, u32[]{:S(2)}) collective-permute-start(f32[4,16384]{1,0:T(4,128)S(1)} %get-tuple-element.61), channel_id=1, source_target_pairs={{0,8},{1,17},{2,10},{3,19},{4,12},{5,21},{6,14},{7,23},{8,0},{9,25... | collective-permute-start | bytes 786440 | tf_op jit(solution)/shard_map/ppermute | solution.py:83
  26.9 7.8 %collective-permute-start.15 = (f32[4,12288]{1,0:T(4,128)S(1)}, f32[4,12288]{1,0:T(4,128)S(1)}, u32[]{:S(2)}, u32[]{:S(2)}) collective-permute-start(f32[4,12288]{1,0:T(4,128)S(1)} %get-tuple-element.60), channel_id=1, source_target_pairs={{0,16},{1,9},{2,18},{3,11},{4,20},{5,13},{6,22},{7,15},{8,24},{9,1... | collective-permute-start | bytes 589832 | tf_op jit(solution)/shard_map/ppermute | solution.py:83
  30.0 7.3 %collective-permute-start.18 = (f32[4,8192]{1,0:T(4,128)S(1)}, f32[4,8192]{1,0:T(4,128)S(1)}, u32[]{:S(2)}, u32[]{:S(2)}) collective-permute-start(f32[4,8192]{1,0:T(4,128)S(1)} %get-tuple-element.64), channel_id=1, source_target_pairs={{0,16},{1,9},{2,18},{3,11},{4,20},{5,13},{6,22},{7,15},{8,24},{9,1... | collective-permute-start | bytes 393224 | tf_op jit(solution)/shard_map/ppermute | solution.py:83
  32.0 5.3 %collective-permute-start.19 = (f32[4,8192]{1,0:T(4,128)S(1)}, f32[4,8192]{1,0:T(4,128)S(1)}, u32[]{:S(2)}, u32[]{:S(2)}) collective-permute-start(f32[4,8192]{1,0:T(4,128)S(1)} %get-tuple-element.65), channel_id=1, source_target_pairs={{0,8},{1,17},{2,10},{3,19},{4,12},{5,21},{6,14},{7,23},{8,0},{9,25... | collective-permute-start | bytes 393224 | tf_op jit(solution)/shard_map/ppermute | solution.py:83
  32.3 3.0 %copy-start.4 = (f32[200,64]{0,1:T(8,128)S(1)}, f32[200,64]{0,1:T(8,128)}, u32[]{:S(2)}) copy-start(f32[200,64]{0,1:T(8,128)} %param.14) | copy-start | bytes 153604

commit v9 on v8

--- a/solution.py
+++ b/solution.py
@@ -234,13 +234,13 @@
         outs[0][:, 1] = other[...]
 
 
-def rows_body(direct, core, *refs):
+def rows_body(direct, *refs):
     *received, out = refs
     chips = len(received) if direct else received[0].shape[0]
     part = received[0].shape[-1]
 
     def fill(k, carry):
-        out[:, column(k, part)] = received[k][core] if direct else received[0][k, core]
+        out[:, column(k, part)] = received[k][1] if direct else received[0][k, 1]
         return carry
 
     if direct:
@@ -250,6 +250,33 @@
         lax.fori_loop(0, chips, fill, 0)
     spare = out.shape[1] - chips * part
     out[:, chips * part :] = jnp.zeros((out.shape[0], spare), f32)
+
+
+def new_momentum_body(direct, o, owned, momentum, *refs):
+    *received, out = refs
+    rep, here, core = place()
+    slots, groups = momentum.shape[0], lax.axis_size("rep")
+    chips = lax.axis_size("own") // 2
+    part = momentum.shape[1] // (2 * chips * groups)
+    live = lax.broadcasted_iota(jnp.int32, (slots, part), 0) < owned[here * 2 + core]
+
+    def fill(k, carry):
+        piece = 2 * (here ^ k if direct else k) + (core ^ o)
+        if o == 1:
+            rows = received[0][:, column(k, part)]
+        else:
+            rows = received[k][0] if direct else received[0][k, 0]
+        rows = momentum_decay * momentum[:, column(piece * groups + rep, part)] + rows
+        out[:, column(k, part)] = jnp.where(live, rows, 0.0)
+        return carry
+
+    if direct:
+        for k in range(chips):
+            fill(k, 0)
+    else:
+        lax.fori_loop(0, chips, fill, 0)
+    spare = out.shape[1] - chips * part
+    out[:, chips * part :] = jnp.zeros((slots, spare), f32)
 
 
 def cut_body(ref, out):
@@ -327,47 +354,36 @@
 
 
 class Pieces:
-    def __init__(self, part, direct, halves, owned, momentum, gradient, result, made, sem):
+    def __init__(self, part, direct, halves, gradient, result, sem):
         self.part, self.direct, self.halves = part, direct, halves
-        self.momentum, self.gradient, self.result = momentum, gradient, result
-        self.made, self.sem = made, sem
-        self.chips = made.shape[1]
-        self.groups = momentum.shape[1] // part // (2 * self.chips)
+        self.gradient, self.result, self.sem = gradient, result, sem
+        self.chips = sem.shape[1]
+        self.groups = result.shape[1] // part // (2 * self.chips)
         self.rep, self.here, self.core = place()
-        rows = lax.broadcasted_iota(jnp.int32, (momentum.shape[0], part), 0)
-        self.live = rows < owned[self.here * 2 + self.core]
-        self.short = self.chips <= 8
-
-    def move(self, n, k):
-        g, o = self.halves[n]
-        piece = 2 * (self.here ^ k if self.direct else k) + (self.core ^ o)
-        at = column(piece * self.groups + member(self.rep, self.core, g), self.part)
-        target = self.result.at[:, at]
-        return at, pltpu.make_async_copy(self.made.at[n, k], target, self.sem.at[n, k])
-
-    def fill(self, k, carry):
-        for n, received in enumerate(self.gradient):
-            at, copy = self.move(n, k)
-            rows = momentum_decay * self.momentum[:, at] + received[:, column(k, self.part)]
-            self.made[n, k] = jnp.where(self.live, rows, 0.0)
-            copy.start()
-        return carry
-
-    def wait(self, k, carry):
-        for n in range(len(self.halves)):
-            self.move(n, k)[1].wait()
-        return carry
-
-    def make(self):
-        lax.fori_loop(0, self.chips, self.fill, 0, unroll=self.short)
+
+    def each(self, act):
+        def body(k, carry):
+            for n, (g, o) in enumerate(self.halves):
+                piece = 2 * (self.here ^ k if self.direct else k) + (self.core ^ o)
+                at = column(piece * self.groups + member(self.rep, self.core, g), self.part)
+                source = self.gradient[n].at[:, column(k, self.part)]
+                act(pltpu.make_async_copy(source, self.result.at[:, at], self.sem.at[n, k]))
+            return carry
+
+        lax.fori_loop(0, self.chips, body, 0, unroll=self.chips <= 8)
+
+    def start(self):
+        self.each(lambda copy: copy.start())
 
     def finish(self):
-        lax.fori_loop(0, self.chips, self.wait, 0, unroll=self.short)
-
-
-def early_body(part, direct, halves, owned, momentum, *refs):
-    *refs, result0, result1, made, made_sem, new_dense, sem = refs
+        self.each(lambda copy: copy.wait())
+
+
+def early_body(part, direct, halves, *refs):
+    *refs, result0, result1, piece_sem, new_dense, sem = refs
     parts, gradient = refs[: -len(halves)], refs[-len(halves) :]
+    pieces = Pieces(part, direct, halves, gradient, result1, piece_sem)
+    pieces.start()
     rep, _, core = place()
     blocks = new_dense.shape[1]
     copies = []
@@ -377,19 +393,19 @@
         target = result0.at[:, column(member(rep, core, k), part)]
         copies.append(pltpu.make_async_copy(new_dense.at[k], target, sem.at[k]))
         copies[-1].start()
-    pieces = Pieces(part, direct, halves, owned, momentum, gradient, result1, made, made_sem)
-    pieces.make()
     pieces.finish()
     for copy in copies:
         copy.wait()
 
 
-def late_body(part, direct, halves, owned, _, __, anchor, momentum_t, basis_t, momentum, *refs):
+def late_body(part, direct, halves, _, __, anchor, momentum_t, basis_t, *refs):
     pair, first, second, *refs = refs
-    result0, result1, result2, result3, mean, sem, made, made_sem, *whole = refs
+    result0, result1, result2, result3, mean, sem, piece_sem, *whole = refs
     new_dense, new_emb, new_momentum_t = whole
+    pieces = Pieces(part, direct, halves, (second, first), result3, piece_sem)
+    pieces.start()
     rep, _, core = place()
-    groups = momentum.shape[1] // part // (2 * made.shape[1])
+    groups = pieces.groups
     target = result0.at[:, column(member(rep, core, groups - 1), part)]
     copies = [
         pltpu.make_async_copy(ref, result, sem.at[i])
@@ -423,18 +439,15 @@
         tile = unfold(ref, skip + 256 * (t % count), height, width)
         new_dense[i : i + height, j : j + width] = tile
     copies[0].start()
-    gradient = (second, first)
-    pieces = Pieces(part, direct, halves, owned, momentum, gradient, result3, made, made_sem)
-    pieces.make()
     pieces.finish()
     for copy in copies:
         copy.wait()
 
 
-def last_body(part, direct, halves, owned, _, momentum, *refs):
-    *gradient, result, made, sem = refs
-    pieces = Pieces(part, direct, halves, owned, momentum, gradient, result, made, sem)
-    pieces.make()
+def last_body(part, direct, halves, _, *refs):
+    *gradient, result, sem = refs
+    pieces = Pieces(part, direct, halves, gradient, result, sem)
+    pieces.start()
     pieces.finish()
 
 
@@ -508,22 +521,30 @@
     gradient_rows = over_chips(sent, direct, owner_count)
     length = chips * part
     (other,) = run(
-        functools.partial(rows_body, direct, 1),
+        functools.partial(rows_body, direct),
         [kept((slot_count, length + 256))],
         gradient_rows,
         after=[gradient_rows[k] for k in (3, 2, 1)] if direct else (),
         name="other",
     )
+    momentum = on_chip(momentum_dense)
     (mine,) = run(
-        functools.partial(rows_body, direct, 0),
+        functools.partial(new_momentum_body, direct, 0),
         [kept((slot_count, length + 512))],
-        gradient_rows,
+        [momentum, *gradient_rows],
+        [owned],
         after=[gradient_rows[k] for k in (3, 2, 1)] if direct else (),
         name="mine",
     )
-    halves = [mine, swap(other, "own", owner_count, 1)]
-
-    momentum = on_chip(momentum_dense)
+    (crossed,) = run(
+        functools.partial(new_momentum_body, direct, 1),
+        [kept((slot_count, length + 256))],
+        [momentum, swap(other, "own", owner_count, 1)],
+        [owned],
+        name="crossed",
+    )
+    halves = [mine, crossed]
+
     dense_rows = 8 * len(tiles(blocks, part))
     plain, with_factor = run(
         functools.partial(dense_body, direct),
@@ -567,29 +588,27 @@
     last1, last2 = swap_in_turn(passed[0], 1), swap_in_turn(passed[1], 0)
 
     def finishing(body, halves, outs, operands, aliased=(), before=(), after=(), name=None):
-        made = (len(halves), chips, slot_count, part)
         return pl.pallas_call(
             functools.partial(body, part, direct, halves),
             out_shape=[stored(shape) for shape in outs],
-            in_specs=[smem] + [anywhere] * len(aliased) + [vmem] * len(operands),
+            in_specs=[anywhere] * len(aliased) + [vmem] * len(operands),
             out_specs=[anywhere] * len(outs),
             scratch_shapes=[
                 *before,
-                pltpu.VMEM(made, f32),
-                pltpu.SemaphoreType.DMA(made[:2]),
+                pltpu.SemaphoreType.DMA((len(halves), chips)),
                 *after,
             ],
-            input_output_aliases={1 + i: out for i, (_, out) in enumerate(aliased)},
+            input_output_aliases={i: out for i, (_, out) in enumerate(aliased)},
             compiler_params=pltpu.CompilerParams(vmem_limit_bytes=vmem_limit),
             name=name,
-        )(in_scalars(owned), *[x for x, _ in aliased], *[on_chip(x) for x in operands])
+        )(*[x for x, _ in aliased], *[on_chip(x) for x in operands])
 
     held = momentum_dense.shape
     new_dense, new_momentum_dense = finishing(
         early_body,
         ((0, 0), (0, 1), (1, 0), (2, 1)),
         [anchor_dense.shape, held],
-        [momentum, *dense, *halves, near1, near2],
+        [*dense, *halves, near1, near2],
         after=[
             pltpu.VMEM((groups - 1, blocks, part), f32),
             pltpu.SemaphoreType.DMA((groups - 1,)),
@@ -600,7 +619,7 @@
         late_body,
         ((1, 1), (2, 0)),
         [anchor_dense.shape, anchor_emb.shape, (rank, rows), held],
-        [anchor_emb, momentum_emb.T, basis_t, momentum, pair, late1, late2],
+        [anchor_emb, momentum_emb.T, basis_t, pair, late1, late2],
         aliased=[(new_dense, 0), (new_momentum_dense, 3)],
         before=[pltpu.VMEM((rank, rows), f32), pltpu.SemaphoreType.DMA((3,))],
         after=[
@@ -614,7 +633,7 @@
         last_body,
         ((3, 0), (3, 1)),
         [held],
-        [momentum, last1, last2],
+        [last1, last2],
         aliased=[(new_momentum_dense, 0)],
         name="last",
     )

time: 38.3 us -> 38.4 us (level)
    pallas_call x10 -> x11, Pallas kernels: 2.58 us -> 2.67 us  [run(): pl.pallas_call(whole, out_shape=list(outs), in_specs=[anywhere] * skip +...]
where the time goes in v9:
time: 38.4 us; the launch traced here: 38.2 us
  starting transfers between devices  23.3 us (61%)
  waiting for transfers between devices  8.32 us (22%)
  Pallas kernels  5.85 us (15%)
  between operations  0.78 us (2%)
    ppermute x12, starting transfers between devices, swap(): return lax.ppermute(x, axis, [(i, i ^ mask) for i in range(count)])  14 us
    ppermute x8, starting transfers between devices, swap_in_turn(): return lax.ppermute(x, ('rep', 'own'), pairs)  9.3 us
    ppermute x8, waiting for transfers between devices, swap_in_turn(): return lax.ppermute(x, ('rep', 'own'), pairs)  4.6 us
    ppermute x12, waiting for transfers between devices, swap(): return lax.ppermute(x, axis, [(i, i ^ mask) for i in range(count)])  3.72 us
    pallas_call x3, Pallas kernels, finishing(): pl.pallas_call(functools.partial(body, part, direct, halves), out_shape=[...  3.18 us
    pallas_call x11, Pallas kernels, run(): pl.pallas_call(whole, out_shape=list(outs), in_specs=[anywhere] * skip +...  2.67 us
  transfers between devices with their start and end apart: 20, of which 7 were waited for; matrix products, arithmetic and copies ran while one was open for 0% of the time, Pallas kernels for 9%

profile of v9, /device:TPU:0, one launch (start us, length us, event | category | flops | bytes accessed | tf_op | source)
XLA Modules:
  0.0 38.2 jit_solution(11838555169681799852)
XLA Ops:
  0.7 1.7 %start.1 = (f32[256,128]{1,0:T(8,128)S(1)}, f32[256,128]{1,0:T(8,128)S(1)}, f32[256,128]{1,0:T(8,128)S(1)}, f32[256,128]{1,0:T(8,128)S(1)}, f32[16,2048]{1,0:T(8...) custom-call(s32[16]{0:T(128)} %bitcast.7, ...), custom_call_target="tpu_custom_call" | custom-call | tf_op jit(solution)/shard_map/start/pallas_call | solution.py:49
  2.4 0.5 %collective-permute-start = (f32[4,4,2048]{2,1,0:T(4,128)S(1)}, f32[4,4,2048]{2,1,0:T(4,128)S(1)}, u32[]{:S(2)}, u32[]{:S(2)}) collective-permute-start(f32[4,4,2048]{2,1,0:T(4,128)S(1)} %get-tuple-element.37), channel_id=1, source_target_pairs={{0,1},{1,0},{2,3},{3,2},{4,5},{5,4},{6,7},{7,6},{8,9},{9,8},{10,11... | collective-permute-start | bytes 393224 | tf_op jit(solution)/shard_map/ppermute | solution.py:69
  2.9 2.6 %collective-permute-start.4 = (f32[256,128]{1,0:T(8,128)S(1)}, f32[256,128]{1,0:T(8,128)S(1)}, u32[]{:S(2)}, u32[]{:S(2)}) collective-permute-start(f32[256,128]{1,0:T(8,128)S(1)} %get-tuple-element.45), channel_id=1, source_target_pairs={{0,8},{8,0},{16,24},{24,16},{1,9},{9,1},{17,25},{25,17},{2,10},{10... | collective-permute-start | bytes 393224 | tf_op jit(solution)/shard_map/ppermute | solution.py:69
  5.4 1.5 %collective-permute-start.5 = (f32[256,128]{1,0:T(8,128)S(1)}, f32[256,128]{1,0:T(8,128)S(1)}, u32[]{:S(2)}, u32[]{:S(2)}) collective-permute-start(f32[256,128]{1,0:T(8,128)S(1)} %get-tuple-element.46), channel_id=1, source_target_pairs={{0,16},{8,24},{16,0},{24,8},{1,17},{9,25},{17,1},{25,9},{2,18},{10... | collective-permute-start | bytes 393224 | tf_op jit(solution)/shard_map/ppermute | solution.py:69
  7.0 4.1 %collective-permute-start.1 = (f32[2,4,2048]{2,1,0:T(4,128)S(1)}, f32[2,4,2048]{2,1,0:T(4,128)S(1)}, u32[]{:S(2)}, u32[]{:S(2)}) collective-permute-start(f32[2,4,2048]{2,1,0:T(4,128)S(1)} %get-tuple-element.38), channel_id=1, source_target_pairs={{0,6},{1,7},{2,4},{3,5},{4,2},{5,3},{6,0},{7,1},{8,14},{9,15},{10,... | collective-permute-start | bytes 196616 | tf_op jit(solution)/shard_map/ppermute | solution.py:69
  11.1 0.6 %collective-permute-start.3 = (f32[2,4,2048]{2,1,0:T(4,128)S(1)}, f32[2,4,2048]{2,1,0:T(4,128)S(1)}, u32[]{:S(2)}, u32[]{:S(2)}) collective-permute-start(f32[2,4,2048]{2,1,0:T(4,128)S(1)} %get-tuple-element.40), channel_id=1, source_target_pairs={{0,2},{1,3},{2,0},{3,1},{4,6},{5,7},{6,4},{7,5},{8,10},{9,11},{10,... | collective-permute-start | bytes 196616 | tf_op jit(solution)/shard_map/ppermute | solution.py:69
  11.8 0.4 %factor.1.refs_0_.refs_7_.refs_2_ = f32[64,200]{1,0:T(8,128)S(1)} custom-call(f32[200,1024]{1,0:T(8,128)S(1)} %copy-done.1, f32[1,200,1024]{2,1,0:T(8,128)S(1)} %copy-done.3, f32[64,1024]{1,0:T(8,128)S(1)} %bitcast.4), custom_call_target="tpu_custom_call" | custom-call | tf_op jit(solution)/shard_map/factor/pallas_call | solution.py:49
  12.2 1.6 %collective-permute-done.5.refs_4_ = f32[256,128]{1,0:T(8,128)S(1)} collective-permute-done((f32[256,128]{1,0:T(8,128)S(1)}, f32[256,128]{1,0:T(8,128)S(1)}, u32[]{:S(2)}, u32[]{:S(2)}) %collective-permute-start.5) | collective-permute-done | bytes 131104 | tf_op jit(solution)/shard_map/ppermute | solution.py:69
  13.8 0.1 mean.1
  13.9 3.7 %collective-permute-start.9 = (f32[2,4,2048]{2,1,0:T(4,128)S(1)}, f32[2,4,2048]{2,1,0:T(4,128)S(1)}, u32[]{:S(2)}, u32[]{:S(2)}) collective-permute-start(f32[2,4,2048]{2,1,0:T(4,128)S(1)} %get-tuple-element.52), channel_id=1, source_target_pairs={{0,6},{1,7},{2,4},{3,5},{4,2},{5,3},{6,0},{7,1},{8,14},{9,15},{10,... | collective-permute-start | bytes 196616 | tf_op jit(solution)/shard_map/ppermute | solution.py:69
  17.6 0.8 %collective-permute-start.11 = (f32[2,4,2048]{2,1,0:T(4,128)S(1)}, f32[2,4,2048]{2,1,0:T(4,128)S(1)}, u32[]{:S(2)}, u32[]{:S(2)}) collective-permute-start(f32[2,4,2048]{2,1,0:T(4,128)S(1)} %get-tuple-element.54), channel_id=1, source_target_pairs={{0,2},{1,3},{2,0},{3,1},{4,6},{5,7},{6,4},{7,5},{8,10},{9,11},{10,... | collective-permute-start | bytes 196616 | tf_op jit(solution)/shard_map/ppermute | solution.py:69
  18.4 0.3 dense.1
  18.7 1.6 %collective-permute-start.8 = (f32[384,128]{1,0:T(8,128)S(1)}, f32[384,128]{1,0:T(8,128)S(1)}, u32[]{:S(2)}, u32[]{:S(2)}) collective-permute-start(f32[384,128]{1,0:T(8,128)S(1)} %get-tuple-element.51), channel_id=1, source_target_pairs={{0,16},{1,9},{2,18},{3,11},{4,20},{5,13},{6,22},{7,15},{8,24},{9,1... | collective-permute-start | bytes 589832 | tf_op jit(solution)/shard_map/ppermute | solution.py:83
  20.3 0.5 %collective-permute-start.7 = (f32[272,128]{1,0:T(8,128)S(1)}, f32[272,128]{1,0:T(8,128)S(1)}, u32[]{:S(2)}, u32[]{:S(2)}) collective-permute-start(f32[272,128]{1,0:T(8,128)S(1)} %get-tuple-element.50.refs_0_.refs_2_), channel_id=1, source_target_pairs={{0,8},{1,17},{2,10},{3,19},{4,12},{5,21},{6,14},{7,23},{8,0},{9,25... | collective-permute-start | bytes 417800 | tf_op jit(solution)/shard_map/ppermute | solution.py:83
  20.8 2.1 %collective-permute-done.10.refs_1_.refs_7_.refs_5_ = f32[2,4,2048]{2,1,0:T(4,128)S(1)} collective-permute-done((f32[2,4,2048]{2,1,0:T(4,128)S(1)}, f32[2,4,2048]{2,1,0:T(4,128)S(1)}, u32[]{:S(2)}, u32[]{:S(2)}) %collective-permute-start.10) | collective-permute-done | bytes 65568 | tf_op jit(solution)/shard_map/ppermute | solution.py:69
  22.9 0.1 collective-permute-start.12
  23.0 1.6 %collective-permute-start.13 = (f32[4,8704]{1,0:T(4,128)S(1)}, f32[4,8704]{1,0:T(4,128)S(1)}, u32[]{:S(2)}, u32[]{:S(2)}) collective-permute-start(f32[4,8704]{1,0:T(4,128)S(1)} %mine.1.refs_3_.refs_0_), channel_id=1, source_target_pairs={{0,8},{1,17},{2,10},{3,19},{4,12},{5,21},{6,14},{7,23},{8,0},{9,25... | collective-permute-start | bytes 417800 | tf_op jit(solution)/shard_map/ppermute | solution.py:83
  24.6 1.3 %collective-permute-start.14 = (f32[4,8448]{1,0:T(4,128)S(1)}, f32[4,8448]{1,0:T(4,128)S(1)}, u32[]{:S(2)}, u32[]{:S(2)}) collective-permute-start(f32[4,8448]{1,0:T(4,128)S(1)} %crossed.1.refs_4_.refs_1_), channel_id=1, source_target_pairs={{0,16},{1,9},{2,18},{3,11},{4,20},{5,13},{6,22},{7,15},{8,24},{9,1... | collective-permute-start | bytes 405512 | tf_op jit(solution)/shard_map/ppermute | solution.py:83
  26.0 0.1 collective-permute-start.17
  26.1 0.1 again.1
  26.1 0.9 %collective-permute-start.16 = (f32[4,16384]{1,0:T(4,128)S(1)}, f32[4,16384]{1,0:T(4,128)S(1)}, u32[]{:S(2)}, u32[]{:S(2)}) collective-permute-start(f32[4,16384]{1,0:T(4,128)S(1)} %get-tuple-element.61), channel_id=1, source_target_pairs={{0,8},{1,17},{2,10},{3,19},{4,12},{5,21},{6,14},{7,23},{8,0},{9,25... | collective-permute-start | bytes 786440 | tf_op jit(solution)/shard_map/ppermute | solution.py:83
  27.0 1.2 %collective-permute-start.15 = (f32[4,12288]{1,0:T(4,128)S(1)}, f32[4,12288]{1,0:T(4,128)S(1)}, u32[]{:S(2)}, u32[]{:S(2)}) collective-permute-start(f32[4,12288]{1,0:T(4,128)S(1)} %get-tuple-element.60), channel_id=1, source_target_pairs={{0,16},{1,9},{2,18},{3,11},{4,20},{5,13},{6,22},{7,15},{8,24},{9,1... | collective-permute-start | bytes 589832 | tf_op jit(solution)/shard_map/ppermute | solution.py:83
  28.2 0.6 %collective-permute-done.13.refs_5_.refs_1_ = f32[4,8704]{1,0:T(4,128)S(1)} collective-permute-done((f32[4,8704]{1,0:T(4,128)S(1)}, f32[4,8704]{1,0:T(4,128)S(1)}, u32[]{:S(2)}, u32[]{:S(2)}) %collective-permute-start.13) | collective-permute-done | bytes 139296 | tf_op jit(solution)/shard_map/ppermute | solution.py:83
  28.8 1.4 %collective-permute-done.14.refs_6_.refs_2_ = f32[4,8448]{1,0:T(4,128)S(1)} collective-permute-done((f32[4,8448]{1,0:T(4,128)S(1)}, f32[4,8448]{1,0:T(4,128)S(1)}, u32[]{:S(2)}, u32[]{:S(2)}) %collective-permute-start.14) | collective-permute-done | bytes 135200 | tf_op jit(solution)/shard_map/ppermute | solution.py:83
  30.2 1.9 %collective-permute-start.18 = (f32[4,8192]{1,0:T(4,128)S(1)}, f32[4,8192]{1,0:T(4,128)S(1)}, u32[]{:S(2)}, u32[]{:S(2)}) collective-permute-start(f32[4,8192]{1,0:T(4,128)S(1)} %get-tuple-element.64), channel_id=1, source_target_pairs={{0,16},{1,9},{2,18},{3,11},{4,20},{5,13},{6,22},{7,15},{8,24},{9,1... | collective-permute-start | bytes 393224 | tf_op jit(solution)/shard_map/ppermute | solution.py:83
  32.1 0.3 collective-permute-start.19
  32.4 1.1 %early.1 = (f32[16,8192]{1,0:T(8,128)}, f32[4,65536]{1,0:T(4,128)}) custom-call(f32[272,128]{1,0:T(8,128)S(1)} %get-tuple-element.50.refs_0_.refs_2_, f32[272,128]{1,0:T(8,128)S(1)} %collective-permute-done.7.refs_1_.refs_3_.refs_0_, f32[384,128]{1,0:T(8,128)S(1)} %collective-permute-done.8.refs_2_.refs_4_.refs_1_, f32[4,8704]{1,0:T(4,128)S(1)} %mine.1.refs_3_.refs_0_, ...), custom_call_target="tpu_custom_call" | custom-call | tf_op jit(solution)/shard_map/early/pallas_call | solution.py:591
  33.5 1.3 %collective-permute-done.15.refs_1_ = f32[4,12288]{1,0:T(4,128)S(1)} collective-permute-done((f32[4,12288]{1,0:T(4,128)S(1)}, f32[4,12288]{1,0:T(4,128)S(1)}, u32[]{:S(2)}, u32[]{:S(2)}) %collective-permute-start.15) | collective-permute-done | bytes 196640 | tf_op jit(solution)/shard_map/ppermute | solution.py:83
  34.8 0.6 %collective-permute-done.16.refs_2_ = f32[4,16384]{1,0:T(4,128)S(1)} collective-permute-done((f32[4,16384]{1,0:T(4,128)S(1)}, f32[4,16384]{1,0:T(4,128)S(1)}, u32[]{:S(2)}, u32[]{:S(2)}) %collective-permute-start.16) | collective-permute-done | bytes 262176 | tf_op jit(solution)/shard_map/ppermute | solution.py:83
  35.4 1.3 %late.1 = (f32[16,8192]{1,0:T(8,128)}, f32[200,1024]{1,0:T(8,128)}, f32[64,200]{1,0:T(8,128)}, f32[4,65536]{1,0:T(4,128)}) custom-call(f32[16,8192]{1,0:T(8,128)} %get-tuple-element.57._, f32[4,65536]{1,0:T(4,128)} %get-tuple-element.58.__, f32[200,1024]{1,0:T(8,128)S(1)} %copy-done.1, ...), custom_call_target="tpu_custom_call", output_to_operand_aliasing={{0}: (0, {}), {3}: (1, {})} | custom-call | tf_op jit(solution)/shard_map/late/pallas_call | solution.py:591
  36.7 0.7 %collective-permute-done.18.refs_0_ = f32[4,8192]{1,0:T(4,128)S(1)} collective-permute-done((f32[4,8192]{1,0:T(4,128)S(1)}, f32[4,8192]{1,0:T(4,128)S(1)}, u32[]{:S(2)}, u32[]{:S(2)}) %collective-permute-start.18) | collective-permute-done | bytes 131104 | tf_op jit(solution)/shard_map/ppermute | solution.py:83
  37.5 0.8 %last.1 = f32[4,65536]{1,0:T(4,128)} custom-call(f32[4,65536]{1,0:T(4,128)} %get-tuple-element.63._, f32[4,8192]{1,0:T(4,128)S(1)} %collective-permute-done.18.refs_0_, f32[4,8192]{1,0:T(4,128)S(1)} %collective-permute-done.19.refs_1_), custom_call_target="tpu_custom_call", output_to_operand_aliasing={{}: (0, {})} | custom-call | tf_op jit(solution)/shard_map/last/pallas_call | solution.py:591
  (32 shorter events, 0.3 us)
Async XLA Ops:
  0.6 11.2 %copy-start.1 = (f32[200,1024]{1,0:T(8,128)S(1)}, f32[200,1024]{1,0:T(8,128)}, u32[]{:S(2)}) copy-start(f32[200,1024]{1,0:T(8,128)} %anchor.1) | copy-start | bytes 2457604
  0.6 11.1 %copy-start.3 = (f32[1,200,1024]{2,1,0:T(8,128)S(1)}, f32[1,200,1024]{2,1,0:T(8,128)}, u32[]{:S(2)}) copy-start(f32[1,200,1024]{2,1,0:T(8,128)} %refs_1_.4) | copy-start | bytes 2457604
  2.4 9.4 %copy-start.2 = (f32[1024,64]{0,1:T(8,128)S(1)}, f32[1024,64]{0,1:T(8,128)}, u32[]{:S(2)}) copy-start(f32[1024,64]{0,1:T(8,128)} %param.15) | copy-start | bytes 786436
  2.4 4.6 %collective-permute-start = (f32[4,4,2048]{2,1,0:T(4,128)S(1)}, f32[4,4,2048]{2,1,0:T(4,128)S(1)}, u32[]{:S(2)}, u32[]{:S(2)}) collective-permute-start(f32[4,4,2048]{2,1,0:T(4,128)S(1)} %get-tuple-element.37), channel_id=1, source_target_pairs={{0,1},{1,0},{2,3},{3,2},{4,5},{5,4},{6,7},{7,6},{8,9},{9,8},{10,11... | collective-permute-start | bytes 393224 | tf_op jit(solution)/shard_map/ppermute | solution.py:69
  2.9 8.3 %collective-permute-start.4 = (f32[256,128]{1,0:T(8,128)S(1)}, f32[256,128]{1,0:T(8,128)S(1)}, u32[]{:S(2)}, u32[]{:S(2)}) collective-permute-start(f32[256,128]{1,0:T(8,128)S(1)} %get-tuple-element.45), channel_id=1, source_target_pairs={{0,8},{8,0},{16,24},{24,16},{1,9},{9,1},{17,25},{25,17},{2,10},{10... | collective-permute-start | bytes 393224 | tf_op jit(solution)/shard_map/ppermute | solution.py:69
  5.4 8.4 %collective-permute-start.5 = (f32[256,128]{1,0:T(8,128)S(1)}, f32[256,128]{1,0:T(8,128)S(1)}, u32[]{:S(2)}, u32[]{:S(2)}) collective-permute-start(f32[256,128]{1,0:T(8,128)S(1)} %get-tuple-element.46), channel_id=1, source_target_pairs={{0,16},{8,24},{16,0},{24,8},{1,17},{9,25},{17,1},{25,9},{2,18},{10... | collective-permute-start | bytes 393224 | tf_op jit(solution)/shard_map/ppermute | solution.py:69
  7.0 6.9 %collective-permute-start.6 = (f32[256,128]{1,0:T(8,128)S(1)}, f32[256,128]{1,0:T(8,128)S(1)}, u32[]{:S(2)}, u32[]{:S(2)}) collective-permute-start(f32[256,128]{1,0:T(8,128)S(1)} %get-tuple-element.47), channel_id=1, source_target_pairs={{0,24},{8,16},{16,8},{24,0},{1,25},{9,17},{17,9},{25,1},{2,26},{10... | collective-permute-start | bytes 393224 | tf_op jit(solution)/shard_map/ppermute | solution.py:69
  7.0 10.6 %collective-permute-start.1 = (f32[2,4,2048]{2,1,0:T(4,128)S(1)}, f32[2,4,2048]{2,1,0:T(4,128)S(1)}, u32[]{:S(2)}, u32[]{:S(2)}) collective-permute-start(f32[2,4,2048]{2,1,0:T(4,128)S(1)} %get-tuple-element.38), channel_id=1, source_target_pairs={{0,6},{1,7},{2,4},{3,5},{4,2},{5,3},{6,0},{7,1},{8,14},{9,15},{10,... | collective-permute-start | bytes 196616 | tf_op jit(solution)/shard_map/ppermute | solution.py:69
  11.1 7.3 %collective-permute-start.2 = (f32[2,4,2048]{2,1,0:T(4,128)S(1)}, f32[2,4,2048]{2,1,0:T(4,128)S(1)}, u32[]{:S(2)}, u32[]{:S(2)}) collective-permute-start(f32[2,4,2048]{2,1,0:T(4,128)S(1)} %get-tuple-element.39), channel_id=1, source_target_pairs={{0,4},{1,5},{2,6},{3,7},{4,0},{5,1},{6,2},{7,3},{8,12},{9,13},{10,... | collective-permute-start | bytes 196616 | tf_op jit(solution)/shard_map/ppermute | solution.py:69
  11.1 7.3 %collective-permute-start.3 = (f32[2,4,2048]{2,1,0:T(4,128)S(1)}, f32[2,4,2048]{2,1,0:T(4,128)S(1)}, u32[]{:S(2)}, u32[]{:S(2)}) collective-permute-start(f32[2,4,2048]{2,1,0:T(4,128)S(1)} %get-tuple-element.40), channel_id=1, source_target_pairs={{0,2},{1,3},{2,0},{3,1},{4,6},{5,7},{6,4},{7,5},{8,10},{9,11},{10,... | collective-permute-start | bytes 196616 | tf_op jit(solution)/shard_map/ppermute | solution.py:69
  11.8 6.6 %copy-start = (f32[4,65536]{1,0:T(4,128)S(1)}, f32[4,65536]{1,0:T(4,128)}, u32[]{:S(2)}) copy-start(f32[4,65536]{1,0:T(4,128)} %refs_1_.5) | copy-start | bytes 3145732
  13.9 6.9 %collective-permute-start.9 = (f32[2,4,2048]{2,1,0:T(4,128)S(1)}, f32[2,4,2048]{2,1,0:T(4,128)S(1)}, u32[]{:S(2)}, u32[]{:S(2)}) collective-permute-start(f32[2,4,2048]{2,1,0:T(4,128)S(1)} %get-tuple-element.52), channel_id=1, source_target_pairs={{0,6},{1,7},{2,4},{3,5},{4,2},{5,3},{6,0},{7,1},{8,14},{9,15},{10,... | collective-permute-start | bytes 196616 | tf_op jit(solution)/shard_map/ppermute | solution.py:69
  17.6 5.3 %collective-permute-start.10 = (f32[2,4,2048]{2,1,0:T(4,128)S(1)}, f32[2,4,2048]{2,1,0:T(4,128)S(1)}, u32[]{:S(2)}, u32[]{:S(2)}) collective-permute-start(f32[2,4,2048]{2,1,0:T(4,128)S(1)} %get-tuple-element.53), channel_id=1, source_target_pairs={{0,4},{1,5},{2,6},{3,7},{4,0},{5,1},{6,2},{7,3},{8,12},{9,13},{10,... | collective-permute-start | bytes 196616 | tf_op jit(solution)/shard_map/ppermute | solution.py:69
  17.6 5.3 %collective-permute-start.11 = (f32[2,4,2048]{2,1,0:T(4,128)S(1)}, f32[2,4,2048]{2,1,0:T(4,128)S(1)}, u32[]{:S(2)}, u32[]{:S(2)}) collective-permute-start(f32[2,4,2048]{2,1,0:T(4,128)S(1)} %get-tuple-element.54), channel_id=1, source_target_pairs={{0,2},{1,3},{2,0},{3,1},{4,6},{5,7},{6,4},{7,5},{8,10},{9,11},{10,... | collective-permute-start | bytes 196616 | tf_op jit(solution)/shard_map/ppermute | solution.py:69
  18.7 7.3 %collective-permute-start.8 = (f32[384,128]{1,0:T(8,128)S(1)}, f32[384,128]{1,0:T(8,128)S(1)}, u32[]{:S(2)}, u32[]{:S(2)}) collective-permute-start(f32[384,128]{1,0:T(8,128)S(1)} %get-tuple-element.51), channel_id=1, source_target_pairs={{0,16},{1,9},{2,18},{3,11},{4,20},{5,13},{6,22},{7,15},{8,24},{9,1... | collective-permute-start | bytes 589832 | tf_op jit(solution)/shard_map/ppermute | solution.py:83
  20.3 5.7 %collective-permute-start.7 = (f32[272,128]{1,0:T(8,128)S(1)}, f32[272,128]{1,0:T(8,128)S(1)}, u32[]{:S(2)}, u32[]{:S(2)}) collective-permute-start(f32[272,128]{1,0:T(8,128)S(1)} %get-tuple-element.50.refs_0_.refs_2_), channel_id=1, source_target_pairs={{0,8},{1,17},{2,10},{3,19},{4,12},{5,21},{6,14},{7,23},{8,0},{9,25... | collective-permute-start | bytes 417800 | tf_op jit(solution)/shard_map/ppermute | solution.py:83
  22.9 1.7 %collective-permute-start.12 = (f32[4,8448]{1,0:T(4,128)S(1)}, f32[4,8448]{1,0:T(4,128)S(1)}, u32[]{:S(2)}, u32[]{:S(2)}) collective-permute-start(f32[4,8448]{1,0:T(4,128)S(1)} %other.1), channel_id=1, source_target_pairs={{0,1},{1,0},{2,3},{3,2},{4,5},{5,4},{6,7},{7,6},{8,9},{9,8},{10,11... | collective-permute-start | bytes 405512 | tf_op jit(solution)/shard_map/ppermute | solution.py:69
  23.0 5.8 %collective-permute-start.13 = (f32[4,8704]{1,0:T(4,128)S(1)}, f32[4,8704]{1,0:T(4,128)S(1)}, u32[]{:S(2)}, u32[]{:S(2)}) collective-permute-start(f32[4,8704]{1,0:T(4,128)S(1)} %mine.1.refs_3_.refs_0_), channel_id=1, source_target_pairs={{0,8},{1,17},{2,10},{3,19},{4,12},{5,21},{6,14},{7,23},{8,0},{9,25... | collective-permute-start | bytes 417800 | tf_op jit(solution)/shard_map/ppermute | solution.py:83
  24.6 5.5 %collective-permute-start.14 = (f32[4,8448]{1,0:T(4,128)S(1)}, f32[4,8448]{1,0:T(4,128)S(1)}, u32[]{:S(2)}, u32[]{:S(2)}) collective-permute-start(f32[4,8448]{1,0:T(4,128)S(1)} %crossed.1.refs_4_.refs_1_), channel_id=1, source_target_pairs={{0,16},{1,9},{2,18},{3,11},{4,20},{5,13},{6,22},{7,15},{8,24},{9,1... | collective-permute-start | bytes 405512 | tf_op jit(solution)/shard_map/ppermute | solution.py:83
  26.0 4.2 %collective-permute-start.17 = (f32[260,128]{1,0:T(8,128)S(1)}, f32[260,128]{1,0:T(8,128)S(1)}, u32[]{:S(2)}, u32[]{:S(2)}) collective-permute-start(f32[260,128]{1,0:T(8,128)S(1)} %gathered.1), channel_id=1, source_target_pairs={{0,1},{1,0},{2,3},{3,2},{4,5},{5,4},{6,7},{7,6},{8,9},{9,8},{10,11... | collective-permute-start | bytes 399368 | tf_op jit(solution)/shard_map/ppermute | solution.py:69
  26.1 9.2 %collective-permute-start.16 = (f32[4,16384]{1,0:T(4,128)S(1)}, f32[4,16384]{1,0:T(4,128)S(1)}, u32[]{:S(2)}, u32[]{:S(2)}) collective-permute-start(f32[4,16384]{1,0:T(4,128)S(1)} %get-tuple-element.61), channel_id=1, source_target_pairs={{0,8},{1,17},{2,10},{3,19},{4,12},{5,21},{6,14},{7,23},{8,0},{9,25... | collective-permute-start | bytes 786440 | tf_op jit(solution)/shard_map/ppermute | solution.py:83
  27.0 7.8 %collective-permute-start.15 = (f32[4,12288]{1,0:T(4,128)S(1)}, f32[4,12288]{1,0:T(4,128)S(1)}, u32[]{:S(2)}, u32[]{:S(2)}) collective-permute-start(f32[4,12288]{1,0:T(4,128)S(1)} %get-tuple-element.60), channel_id=1, source_target_pairs={{0,16},{1,9},{2,18},{3,11},{4,20},{5,13},{6,22},{7,15},{8,24},{9,1... | collective-permute-start | bytes 589832 | tf_op jit(solution)/shard_map/ppermute | solution.py:83
  30.2 7.3 %collective-permute-start.18 = (f32[4,8192]{1,0:T(4,128)S(1)}, f32[4,8192]{1,0:T(4,128)S(1)}, u32[]{:S(2)}, u32[]{:S(2)}) collective-permute-start(f32[4,8192]{1,0:T(4,128)S(1)} %get-tuple-element.64), channel_id=1, source_target_pairs={{0,16},{1,9},{2,18},{3,11},{4,20},{5,13},{6,22},{7,15},{8,24},{9,1... | collective-permute-start | bytes 393224 | tf_op jit(solution)/shard_map/ppermute | solution.py:83
  32.1 3.3 %copy-start.4 = (f32[200,64]{0,1:T(8,128)S(1)}, f32[200,64]{0,1:T(8,128)}, u32[]{:S(2)}) copy-start(f32[200,64]{0,1:T(8,128)} %param.14) | copy-start | bytes 153604
  32.1 5.4 %collective-permute-start.19 = (f32[4,8192]{1,0:T(4,128)S(1)}, f32[4,8192]{1,0:T(4,128)S(1)}, u32[]{:S(2)}, u32[]{:S(2)}) collective-permute-start(f32[4,8192]{1,0:T(4,128)S(1)} %get-tuple-element.65), channel_id=1, source_target_pairs={{0,8},{1,17},{2,10},{3,19},{4,12},{5,21},{6,14},{7,23},{8,0},{9,25... | collective-permute-start | bytes 393224 | tf_op jit(solution)/shard_map/ppermute | solution.py:83

commit v10 on v9

--- a/solution.py
+++ b/solution.py
@@ -248,8 +248,6 @@
             fill(k, 0)
     else:
         lax.fori_loop(0, chips, fill, 0)
-    spare = out.shape[1] - chips * part
-    out[:, chips * part :] = jnp.zeros((out.shape[0], spare), f32)
 
 
 def new_momentum_body(direct, o, owned, momentum, *refs):
@@ -522,7 +520,7 @@
     length = chips * part
     (other,) = run(
         functools.partial(rows_body, direct),
-        [kept((slot_count, length + 256))],
+        [kept((slot_count, length))],
         gradient_rows,
         after=[gradient_rows[k] for k in (3, 2, 1)] if direct else (),
         name="other",
@@ -530,7 +528,7 @@
     momentum = on_chip(momentum_dense)
     (mine,) = run(
         functools.partial(new_momentum_body, direct, 0),
-        [kept((slot_count, length + 512))],
+        [kept((slot_count, length + 256))],
         [momentum, *gradient_rows],
         [owned],
         after=[gradient_rows[k] for k in (3, 2, 1)] if direct else (),
@@ -538,7 +536,7 @@
     )
     (crossed,) = run(
         functools.partial(new_momentum_body, direct, 1),
-        [kept((slot_count, length + 256))],
+        [kept((slot_count, length + 128))],
         [momentum, swap(other, "own", owner_count, 1)],
         [owned],
         name="crossed",
@@ -548,7 +546,7 @@
     dense_rows = 8 * len(tiles(blocks, part))
     plain, with_factor = run(
         functools.partial(dense_body, direct),
-        [kept((dense_rows + 16, 128)), kept((dense_rows + 8 * len(tiles(rank, rows)), 128))],
+        [kept((dense_rows + 8, 128)), kept((dense_rows + 8 * len(tiles(rank, rows)), 128))],
         [quarter, mean, factor, *momentum_rows],
         [row_of],
         [
@@ -572,18 +570,21 @@
         name="again",
     )
     (sign,) = run(
-        cut_body, [kept((dense_rows + 4, 128))], [plain], after=dense[1:], name="gathered"
+        cut_body, [kept((dense_rows + 2, 128))], [plain], after=dense[1:], name="gathered"
     )
     sign = swap(sign, "own", owner_count, 1)
     near1 = swap_in_turn(halves[0], 0)
     near2 = swap_in_turn(halves[1], 1)
-    passed = run(
-        copies_body,
-        [kept((slot_count, length))] * 2,
-        [near1, near2],
-        after=[sign],
-        name="pass_on",
-    )
+    passed = [
+        run(copies_body, [kept((slot_count, length + 128))], [near1], name="pass_first")[0],
+        run(
+            copies_body,
+            [kept((slot_count, length))],
+            [near2],
+            after=[sign],
+            name="pass_second",
+        )[0],
+    ]
     late2, late1 = swap_in_turn(again[1], 0), swap_in_turn(again[0], 1)
     last1, last2 = swap_in_turn(passed[0], 1), swap_in_turn(passed[1], 0)
 

time: 38.4 us -> 38.4 us (level)
  waiting for transfers between devices: 8.32 us -> 7.42 us
  starting transfers between devices: 23.3 us -> 24.2 us
    ppermute x8, waiting for transfers between devices: 4.6 us -> 3.7 us  [swap_in_turn(): return lax.ppermute(x, ('rep', 'own'), pairs)]
    ppermute x8, starting transfers between devices: 9.3 us -> 10.2 us  [swap_in_turn(): return lax.ppermute(x, ('rep', 'own'), pairs)]
    pallas_call x11 -> x12, Pallas kernels: 2.67 us -> 2.66 us  [run(): pl.pallas_call(whole, out_shape=list(outs), in_specs=[anywhere] * skip +...]
where the time goes in v10:
time: 38.4 us; the launch traced here: 38.3 us
  starting transfers between devices  24.2 us (63%)
  waiting for transfers between devices  7.42 us (19%)
  Pallas kernels  5.85 us (15%)
  between operations  0.79 us (2%)
    ppermute x12, starting transfers between devices, swap(): return lax.ppermute(x, axis, [(i, i ^ mask) for i in range(count)])  14 us
    ppermute x8, starting transfers between devices, swap_in_turn(): return lax.ppermute(x, ('rep', 'own'), pairs)  10.2 us
    ppermute x12, waiting for transfers between devices, swap(): return lax.ppermute(x, axis, [(i, i ^ mask) for i in range(count)])  3.72 us
    ppermute x8, waiting for transfers between devices, swap_in_turn(): return lax.ppermute(x, ('rep', 'own'), pairs)  3.7 us
    pallas_call x3, Pallas kernels, finishing(): pl.pallas_call(functools.partial(body, part, direct, halves), out_shape=[...  3.18 us
    pallas_call x12, Pallas kernels, run(): pl.pallas_call(whole, out_shape=list(outs), in_specs=[anywhere] * skip +...  2.66 us
  transfers between devices with their start and end apart: 20, of which 7 were waited for; matrix products, arithmetic and copies ran while one was open for 0% of the time, Pallas kernels for 9%

profile of v10, /device:TPU:0, one launch (start us, length us, event | category | flops | bytes accessed | tf_op | source)
XLA Modules:
  0.0 38.3 jit_solution(15727458024001543474)
XLA Ops:
  0.7 1.7 %start.1 = (f32[256,128]{1,0:T(8,128)S(1)}, f32[256,128]{1,0:T(8,128)S(1)}, f32[256,128]{1,0:T(8,128)S(1)}, f32[256,128]{1,0:T(8,128)S(1)}, f32[16,2048]{1,0:T(8...) custom-call(s32[16]{0:T(128)} %bitcast.7, ...), custom_call_target="tpu_custom_call" | custom-call | tf_op jit(solution)/shard_map/start/pallas_call | solution.py:49
  2.4 0.5 %collective-permute-start = (f32[4,4,2048]{2,1,0:T(4,128)S(1)}, f32[4,4,2048]{2,1,0:T(4,128)S(1)}, u32[]{:S(2)}, u32[]{:S(2)}) collective-permute-start(f32[4,4,2048]{2,1,0:T(4,128)S(1)} %get-tuple-element.35), channel_id=1, source_target_pairs={{0,1},{1,0},{2,3},{3,2},{4,5},{5,4},{6,7},{7,6},{8,9},{9,8},{10,11... | collective-permute-start | bytes 393224 | tf_op jit(solution)/shard_map/ppermute | solution.py:69
  2.9 2.6 %collective-permute-start.4 = (f32[256,128]{1,0:T(8,128)S(1)}, f32[256,128]{1,0:T(8,128)S(1)}, u32[]{:S(2)}, u32[]{:S(2)}) collective-permute-start(f32[256,128]{1,0:T(8,128)S(1)} %get-tuple-element.43), channel_id=1, source_target_pairs={{0,8},{8,0},{16,24},{24,16},{1,9},{9,1},{17,25},{25,17},{2,10},{10... | collective-permute-start | bytes 393224 | tf_op jit(solution)/shard_map/ppermute | solution.py:69
  5.4 1.5 %collective-permute-start.5 = (f32[256,128]{1,0:T(8,128)S(1)}, f32[256,128]{1,0:T(8,128)S(1)}, u32[]{:S(2)}, u32[]{:S(2)}) collective-permute-start(f32[256,128]{1,0:T(8,128)S(1)} %get-tuple-element.44), channel_id=1, source_target_pairs={{0,16},{8,24},{16,0},{24,8},{1,17},{9,25},{17,1},{25,9},{2,18},{10... | collective-permute-start | bytes 393224 | tf_op jit(solution)/shard_map/ppermute | solution.py:69
  7.0 4.1 %collective-permute-start.1 = (f32[2,4,2048]{2,1,0:T(4,128)S(1)}, f32[2,4,2048]{2,1,0:T(4,128)S(1)}, u32[]{:S(2)}, u32[]{:S(2)}) collective-permute-start(f32[2,4,2048]{2,1,0:T(4,128)S(1)} %get-tuple-element.36), channel_id=1, source_target_pairs={{0,6},{1,7},{2,4},{3,5},{4,2},{5,3},{6,0},{7,1},{8,14},{9,15},{10,... | collective-permute-start | bytes 196616 | tf_op jit(solution)/shard_map/ppermute | solution.py:69
  11.1 0.6 %collective-permute-start.3 = (f32[2,4,2048]{2,1,0:T(4,128)S(1)}, f32[2,4,2048]{2,1,0:T(4,128)S(1)}, u32[]{:S(2)}, u32[]{:S(2)}) collective-permute-start(f32[2,4,2048]{2,1,0:T(4,128)S(1)} %get-tuple-element.38), channel_id=1, source_target_pairs={{0,2},{1,3},{2,0},{3,1},{4,6},{5,7},{6,4},{7,5},{8,10},{9,11},{10,... | collective-permute-start | bytes 196616 | tf_op jit(solution)/shard_map/ppermute | solution.py:69
  11.8 0.4 %factor.1.refs_0_.refs_7_.refs_2_ = f32[64,200]{1,0:T(8,128)S(1)} custom-call(f32[200,1024]{1,0:T(8,128)S(1)} %copy-done.1, f32[1,200,1024]{2,1,0:T(8,128)S(1)} %copy-done.3, f32[64,1024]{1,0:T(8,128)S(1)} %bitcast.4), custom_call_target="tpu_custom_call" | custom-call | tf_op jit(solution)/shard_map/factor/pallas_call | solution.py:49
  12.2 1.6 %collective-permute-done.5.refs_4_ = f32[256,128]{1,0:T(8,128)S(1)} collective-permute-done((f32[256,128]{1,0:T(8,128)S(1)}, f32[256,128]{1,0:T(8,128)S(1)}, u32[]{:S(2)}, u32[]{:S(2)}) %collective-permute-start.5) | collective-permute-done | bytes 131104 | tf_op jit(solution)/shard_map/ppermute | solution.py:69
  13.8 0.1 mean.1
  13.9 3.7 %collective-permute-start.9 = (f32[2,4,2048]{2,1,0:T(4,128)S(1)}, f32[2,4,2048]{2,1,0:T(4,128)S(1)}, u32[]{:S(2)}, u32[]{:S(2)}) collective-permute-start(f32[2,4,2048]{2,1,0:T(4,128)S(1)} %get-tuple-element.50), channel_id=1, source_target_pairs={{0,6},{1,7},{2,4},{3,5},{4,2},{5,3},{6,0},{7,1},{8,14},{9,15},{10,... | collective-permute-start | bytes 196616 | tf_op jit(solution)/shard_map/ppermute | solution.py:69
  17.6 0.8 %collective-permute-start.11 = (f32[2,4,2048]{2,1,0:T(4,128)S(1)}, f32[2,4,2048]{2,1,0:T(4,128)S(1)}, u32[]{:S(2)}, u32[]{:S(2)}) collective-permute-start(f32[2,4,2048]{2,1,0:T(4,128)S(1)} %get-tuple-element.52), channel_id=1, source_target_pairs={{0,2},{1,3},{2,0},{3,1},{4,6},{5,7},{6,4},{7,5},{8,10},{9,11},{10,... | collective-permute-start | bytes 196616 | tf_op jit(solution)/shard_map/ppermute | solution.py:69
  18.4 0.3 dense.1
  18.7 1.6 %collective-permute-start.8 = (f32[384,128]{1,0:T(8,128)S(1)}, f32[384,128]{1,0:T(8,128)S(1)}, u32[]{:S(2)}, u32[]{:S(2)}) collective-permute-start(f32[384,128]{1,0:T(8,128)S(1)} %get-tuple-element.49), channel_id=1, source_target_pairs={{0,16},{1,9},{2,18},{3,11},{4,20},{5,13},{6,22},{7,15},{8,24},{9,1... | collective-permute-start | bytes 589832 | tf_op jit(solution)/shard_map/ppermute | solution.py:83
  20.3 0.5 %collective-permute-start.7 = (f32[264,128]{1,0:T(8,128)S(1)}, f32[264,128]{1,0:T(8,128)S(1)}, u32[]{:S(2)}, u32[]{:S(2)}) collective-permute-start(f32[264,128]{1,0:T(8,128)S(1)} %get-tuple-element.48.refs_0_.refs_2_), channel_id=1, source_target_pairs={{0,8},{1,17},{2,10},{3,19},{4,12},{5,21},{6,14},{7,23},{8,0},{9,25... | collective-permute-start | bytes 405512 | tf_op jit(solution)/shard_map/ppermute | solution.py:83
  20.8 2.1 %collective-permute-done.10.refs_1_.refs_7_.refs_5_ = f32[2,4,2048]{2,1,0:T(4,128)S(1)} collective-permute-done((f32[2,4,2048]{2,1,0:T(4,128)S(1)}, f32[2,4,2048]{2,1,0:T(4,128)S(1)}, u32[]{:S(2)}, u32[]{:S(2)}) %collective-permute-start.10) | collective-permute-done | bytes 65568 | tf_op jit(solution)/shard_map/ppermute | solution.py:69
  22.9 0.1 collective-permute-start.12
  23.0 1.6 %collective-permute-start.13 = (f32[4,8448]{1,0:T(4,128)S(1)}, f32[4,8448]{1,0:T(4,128)S(1)}, u32[]{:S(2)}, u32[]{:S(2)}) collective-permute-start(f32[4,8448]{1,0:T(4,128)S(1)} %mine.1.refs_3_.refs_0_), channel_id=1, source_target_pairs={{0,8},{1,17},{2,10},{3,19},{4,12},{5,21},{6,14},{7,23},{8,0},{9,25... | collective-permute-start | bytes 405512 | tf_op jit(solution)/shard_map/ppermute | solution.py:83
  24.6 1.3 %collective-permute-start.14 = (f32[4,8320]{1,0:T(4,128)S(1)}, f32[4,8320]{1,0:T(4,128)S(1)}, u32[]{:S(2)}, u32[]{:S(2)}) collective-permute-start(f32[4,8320]{1,0:T(4,128)S(1)} %crossed.1.refs_4_.refs_1_), channel_id=1, source_target_pairs={{0,16},{1,9},{2,18},{3,11},{4,20},{5,13},{6,22},{7,15},{8,24},{9,1... | collective-permute-start | bytes 399368 | tf_op jit(solution)/shard_map/ppermute | solution.py:83
  26.0 0.1 collective-permute-start.18
  26.1 0.1 again.1
  26.1 0.9 %collective-permute-start.16 = (f32[4,16384]{1,0:T(4,128)S(1)}, f32[4,16384]{1,0:T(4,128)S(1)}, u32[]{:S(2)}, u32[]{:S(2)}) collective-permute-start(f32[4,16384]{1,0:T(4,128)S(1)} %get-tuple-element.59), channel_id=1, source_target_pairs={{0,8},{1,17},{2,10},{3,19},{4,12},{5,21},{6,14},{7,23},{8,0},{9,25... | collective-permute-start | bytes 786440 | tf_op jit(solution)/shard_map/ppermute | solution.py:83
  27.0 1.2 %collective-permute-start.15 = (f32[4,12288]{1,0:T(4,128)S(1)}, f32[4,12288]{1,0:T(4,128)S(1)}, u32[]{:S(2)}, u32[]{:S(2)}) collective-permute-start(f32[4,12288]{1,0:T(4,128)S(1)} %get-tuple-element.58), channel_id=1, source_target_pairs={{0,16},{1,9},{2,18},{3,11},{4,20},{5,13},{6,22},{7,15},{8,24},{9,1... | collective-permute-start | bytes 589832 | tf_op jit(solution)/shard_map/ppermute | solution.py:83
  28.2 0.5 %collective-permute-done.13.refs_5_.refs_0_ = f32[4,8448]{1,0:T(4,128)S(1)} collective-permute-done((f32[4,8448]{1,0:T(4,128)S(1)}, f32[4,8448]{1,0:T(4,128)S(1)}, u32[]{:S(2)}, u32[]{:S(2)}) %collective-permute-start.13) | collective-permute-done | bytes 135200 | tf_op jit(solution)/shard_map/ppermute | solution.py:83
  28.7 2.0 %collective-permute-start.17 = (f32[4,8320]{1,0:T(4,128)S(1)}, f32[4,8320]{1,0:T(4,128)S(1)}, u32[]{:S(2)}, u32[]{:S(2)}) collective-permute-start(f32[4,8320]{1,0:T(4,128)S(1)} %pass_first.1), channel_id=1, source_target_pairs={{0,16},{1,9},{2,18},{3,11},{4,20},{5,13},{6,22},{7,15},{8,24},{9,1... | collective-permute-start | bytes 399368 | tf_op jit(solution)/shard_map/ppermute | solution.py:83
  30.8 1.1 %collective-permute-start.19 = (f32[4,8192]{1,0:T(4,128)S(1)}, f32[4,8192]{1,0:T(4,128)S(1)}, u32[]{:S(2)}, u32[]{:S(2)}) collective-permute-start(f32[4,8192]{1,0:T(4,128)S(1)} %pass_second.1), channel_id=1, source_target_pairs={{0,8},{1,17},{2,10},{3,19},{4,12},{5,21},{6,14},{7,23},{8,0},{9,25... | collective-permute-start | bytes 393224 | tf_op jit(solution)/shard_map/ppermute | solution.py:83
  31.9 1.1 %early.1 = (f32[16,8192]{1,0:T(8,128)}, f32[4,65536]{1,0:T(4,128)}) custom-call(f32[264,128]{1,0:T(8,128)S(1)} %get-tuple-element.48.refs_0_.refs_2_, f32[264,128]{1,0:T(8,128)S(1)} %collective-permute-done.7.refs_1_.refs_3_.refs_0_, f32[384,128]{1,0:T(8,128)S(1)} %collective-permute-done.8.refs_2_.refs_4_.refs_1_, f32[4,8448]{1,0:T(4,128)S(1)} %mine.1.refs_3_.refs_0_, ...), custom_call_target="tpu_custom_call" | custom-call | tf_op jit(solution)/shard_map/early/pallas_call | solution.py:592
  33.0 1.8 %collective-permute-done.15.refs_1_ = f32[4,12288]{1,0:T(4,128)S(1)} collective-permute-done((f32[4,12288]{1,0:T(4,128)S(1)}, f32[4,12288]{1,0:T(4,128)S(1)}, u32[]{:S(2)}, u32[]{:S(2)}) %collective-permute-start.15) | collective-permute-done | bytes 196640 | tf_op jit(solution)/shard_map/ppermute | solution.py:83
  34.8 0.5 %collective-permute-done.16.refs_2_ = f32[4,16384]{1,0:T(4,128)S(1)} collective-permute-done((f32[4,16384]{1,0:T(4,128)S(1)}, f32[4,16384]{1,0:T(4,128)S(1)}, u32[]{:S(2)}, u32[]{:S(2)}) %collective-permute-start.16) | collective-permute-done | bytes 262176 | tf_op jit(solution)/shard_map/ppermute | solution.py:83
  35.4 1.3 %late.1 = (f32[16,8192]{1,0:T(8,128)}, f32[200,1024]{1,0:T(8,128)}, f32[64,200]{1,0:T(8,128)}, f32[4,65536]{1,0:T(4,128)}) custom-call(f32[16,8192]{1,0:T(8,128)} %get-tuple-element.55._, f32[4,65536]{1,0:T(4,128)} %get-tuple-element.56.__, f32[200,1024]{1,0:T(8,128)S(1)} %copy-done.1, ...), custom_call_target="tpu_custom_call", output_to_operand_aliasing={{0}: (0, {}), {3}: (1, {})} | custom-call | tf_op jit(solution)/shard_map/late/pallas_call | solution.py:592
  36.7 0.7 %collective-permute-done.17.refs_0_ = f32[4,8320]{1,0:T(4,128)S(1)} collective-permute-done((f32[4,8320]{1,0:T(4,128)S(1)}, f32[4,8320]{1,0:T(4,128)S(1)}, u32[]{:S(2)}, u32[]{:S(2)}) %collective-permute-start.17) | collective-permute-done | bytes 133152 | tf_op jit(solution)/shard_map/ppermute | solution.py:83
  37.4 0.1 collective-permute-done.19.refs_1_
  37.5 0.8 %last.1 = f32[4,65536]{1,0:T(4,128)} custom-call(f32[4,65536]{1,0:T(4,128)} %get-tuple-element.61._, f32[4,8320]{1,0:T(4,128)S(1)} %collective-permute-done.17.refs_0_, f32[4,8192]{1,0:T(4,128)S(1)} %collective-permute-done.19.refs_1_), custom_call_target="tpu_custom_call", output_to_operand_aliasing={{}: (0, {})} | custom-call | tf_op jit(solution)/shard_map/last/pallas_call | solution.py:592
  (33 shorter events, 0.2 us)
Async XLA Ops:
  0.6 11.2 %copy-start.1 = (f32[200,1024]{1,0:T(8,128)S(1)}, f32[200,1024]{1,0:T(8,128)}, u32[]{:S(2)}) copy-start(f32[200,1024]{1,0:T(8,128)} %anchor.1) | copy-start | bytes 2457604
  0.6 11.1 %copy-start.3 = (f32[1,200,1024]{2,1,0:T(8,128)S(1)}, f32[1,200,1024]{2,1,0:T(8,128)}, u32[]{:S(2)}) copy-start(f32[1,200,1024]{2,1,0:T(8,128)} %refs_1_.4) | copy-start | bytes 2457604
  2.4 9.4 %copy-start.2 = (f32[1024,64]{0,1:T(8,128)S(1)}, f32[1024,64]{0,1:T(8,128)}, u32[]{:S(2)}) copy-start(f32[1024,64]{0,1:T(8,128)} %param.15) | copy-start | bytes 786436
  2.4 4.6 %collective-permute-start = (f32[4,4,2048]{2,1,0:T(4,128)S(1)}, f32[4,4,2048]{2,1,0:T(4,128)S(1)}, u32[]{:S(2)}, u32[]{:S(2)}) collective-permute-start(f32[4,4,2048]{2,1,0:T(4,128)S(1)} %get-tuple-element.35), channel_id=1, source_target_pairs={{0,1},{1,0},{2,3},{3,2},{4,5},{5,4},{6,7},{7,6},{8,9},{9,8},{10,11... | collective-permute-start | bytes 393224 | tf_op jit(solution)/shard_map/ppermute | solution.py:69
  2.9 8.3 %collective-permute-start.4 = (f32[256,128]{1,0:T(8,128)S(1)}, f32[256,128]{1,0:T(8,128)S(1)}, u32[]{:S(2)}, u32[]{:S(2)}) collective-permute-start(f32[256,128]{1,0:T(8,128)S(1)} %get-tuple-element.43), channel_id=1, source_target_pairs={{0,8},{8,0},{16,24},{24,16},{1,9},{9,1},{17,25},{25,17},{2,10},{10... | collective-permute-start | bytes 393224 | tf_op jit(solution)/shard_map/ppermute | solution.py:69
  5.4 8.4 %collective-permute-start.5 = (f32[256,128]{1,0:T(8,128)S(1)}, f32[256,128]{1,0:T(8,128)S(1)}, u32[]{:S(2)}, u32[]{:S(2)}) collective-permute-start(f32[256,128]{1,0:T(8,128)S(1)} %get-tuple-element.44), channel_id=1, source_target_pairs={{0,16},{8,24},{16,0},{24,8},{1,17},{9,25},{17,1},{25,9},{2,18},{10... | collective-permute-start | bytes 393224 | tf_op jit(solution)/shard_map/ppermute | solution.py:69
  7.0 6.9 %collective-permute-start.6 = (f32[256,128]{1,0:T(8,128)S(1)}, f32[256,128]{1,0:T(8,128)S(1)}, u32[]{:S(2)}, u32[]{:S(2)}) collective-permute-start(f32[256,128]{1,0:T(8,128)S(1)} %get-tuple-element.45), channel_id=1, source_target_pairs={{0,24},{8,16},{16,8},{24,0},{1,25},{9,17},{17,9},{25,1},{2,26},{10... | collective-permute-start | bytes 393224 | tf_op jit(solution)/shard_map/ppermute | solution.py:69
  7.0 10.6 %collective-permute-start.1 = (f32[2,4,2048]{2,1,0:T(4,128)S(1)}, f32[2,4,2048]{2,1,0:T(4,128)S(1)}, u32[]{:S(2)}, u32[]{:S(2)}) collective-permute-start(f32[2,4,2048]{2,1,0:T(4,128)S(1)} %get-tuple-element.36), channel_id=1, source_target_pairs={{0,6},{1,7},{2,4},{3,5},{4,2},{5,3},{6,0},{7,1},{8,14},{9,15},{10,... | collective-permute-start | bytes 196616 | tf_op jit(solution)/shard_map/ppermute | solution.py:69
  11.1 7.3 %collective-permute-start.2 = (f32[2,4,2048]{2,1,0:T(4,128)S(1)}, f32[2,4,2048]{2,1,0:T(4,128)S(1)}, u32[]{:S(2)}, u32[]{:S(2)}) collective-permute-start(f32[2,4,2048]{2,1,0:T(4,128)S(1)} %get-tuple-element.37), channel_id=1, source_target_pairs={{0,4},{1,5},{2,6},{3,7},{4,0},{5,1},{6,2},{7,3},{8,12},{9,13},{10,... | collective-permute-start | bytes 196616 | tf_op jit(solution)/shard_map/ppermute | solution.py:69
  11.1 7.3 %collective-permute-start.3 = (f32[2,4,2048]{2,1,0:T(4,128)S(1)}, f32[2,4,2048]{2,1,0:T(4,128)S(1)}, u32[]{:S(2)}, u32[]{:S(2)}) collective-permute-start(f32[2,4,2048]{2,1,0:T(4,128)S(1)} %get-tuple-element.38), channel_id=1, source_target_pairs={{0,2},{1,3},{2,0},{3,1},{4,6},{5,7},{6,4},{7,5},{8,10},{9,11},{10,... | collective-permute-start | bytes 196616 | tf_op jit(solution)/shard_map/ppermute | solution.py:69
  11.8 6.6 %copy-start = (f32[4,65536]{1,0:T(4,128)S(1)}, f32[4,65536]{1,0:T(4,128)}, u32[]{:S(2)}) copy-start(f32[4,65536]{1,0:T(4,128)} %refs_1_.5) | copy-start | bytes 3145732
  13.9 6.9 %collective-permute-start.9 = (f32[2,4,2048]{2,1,0:T(4,128)S(1)}, f32[2,4,2048]{2,1,0:T(4,128)S(1)}, u32[]{:S(2)}, u32[]{:S(2)}) collective-permute-start(f32[2,4,2048]{2,1,0:T(4,128)S(1)} %get-tuple-element.50), channel_id=1, source_target_pairs={{0,6},{1,7},{2,4},{3,5},{4,2},{5,3},{6,0},{7,1},{8,14},{9,15},{10,... | collective-permute-start | bytes 196616 | tf_op jit(solution)/shard_map/ppermute | solution.py:69
  17.6 5.3 %collective-permute-start.10 = (f32[2,4,2048]{2,1,0:T(4,128)S(1)}, f32[2,4,2048]{2,1,0:T(4,128)S(1)}, u32[]{:S(2)}, u32[]{:S(2)}) collective-permute-start(f32[2,4,2048]{2,1,0:T(4,128)S(1)} %get-tuple-element.51), channel_id=1, source_target_pairs={{0,4},{1,5},{2,6},{3,7},{4,0},{5,1},{6,2},{7,3},{8,12},{9,13},{10,... | collective-permute-start | bytes 196616 | tf_op jit(solution)/shard_map/ppermute | solution.py:69
  17.6 5.3 %collective-permute-start.11 = (f32[2,4,2048]{2,1,0:T(4,128)S(1)}, f32[2,4,2048]{2,1,0:T(4,128)S(1)}, u32[]{:S(2)}, u32[]{:S(2)}) collective-permute-start(f32[2,4,2048]{2,1,0:T(4,128)S(1)} %get-tuple-element.52), channel_id=1, source_target_pairs={{0,2},{1,3},{2,0},{3,1},{4,6},{5,7},{6,4},{7,5},{8,10},{9,11},{10,... | collective-permute-start | bytes 196616 | tf_op jit(solution)/shard_map/ppermute | solution.py:69
  18.7 7.3 %collective-permute-start.8 = (f32[384,128]{1,0:T(8,128)S(1)}, f32[384,128]{1,0:T(8,128)S(1)}, u32[]{:S(2)}, u32[]{:S(2)}) collective-permute-start(f32[384,128]{1,0:T(8,128)S(1)} %get-tuple-element.49), channel_id=1, source_target_pairs={{0,16},{1,9},{2,18},{3,11},{4,20},{5,13},{6,22},{7,15},{8,24},{9,1... | collective-permute-start | bytes 589832 | tf_op jit(solution)/shard_map/ppermute | solution.py:83
  20.3 5.7 %collective-permute-start.7 = (f32[264,128]{1,0:T(8,128)S(1)}, f32[264,128]{1,0:T(8,128)S(1)}, u32[]{:S(2)}, u32[]{:S(2)}) collective-permute-start(f32[264,128]{1,0:T(8,128)S(1)} %get-tuple-element.48.refs_0_.refs_2_), channel_id=1, source_target_pairs={{0,8},{1,17},{2,10},{3,19},{4,12},{5,21},{6,14},{7,23},{8,0},{9,25... | collective-permute-start | bytes 405512 | tf_op jit(solution)/shard_map/ppermute | solution.py:83
  22.9 1.7 %collective-permute-start.12 = (f32[4,8192]{1,0:T(4,128)S(1)}, f32[4,8192]{1,0:T(4,128)S(1)}, u32[]{:S(2)}, u32[]{:S(2)}) collective-permute-start(f32[4,8192]{1,0:T(4,128)S(1)} %other.1), channel_id=1, source_target_pairs={{0,1},{1,0},{2,3},{3,2},{4,5},{5,4},{6,7},{7,6},{8,9},{9,8},{10,11... | collective-permute-start | bytes 393224 | tf_op jit(solution)/shard_map/ppermute | solution.py:69
  23.0 5.7 %collective-permute-start.13 = (f32[4,8448]{1,0:T(4,128)S(1)}, f32[4,8448]{1,0:T(4,128)S(1)}, u32[]{:S(2)}, u32[]{:S(2)}) collective-permute-start(f32[4,8448]{1,0:T(4,128)S(1)} %mine.1.refs_3_.refs_0_), channel_id=1, source_target_pairs={{0,8},{1,17},{2,10},{3,19},{4,12},{5,21},{6,14},{7,23},{8,0},{9,25... | collective-permute-start | bytes 405512 | tf_op jit(solution)/shard_map/ppermute | solution.py:83
  24.6 6.1 %collective-permute-start.14 = (f32[4,8320]{1,0:T(4,128)S(1)}, f32[4,8320]{1,0:T(4,128)S(1)}, u32[]{:S(2)}, u32[]{:S(2)}) collective-permute-start(f32[4,8320]{1,0:T(4,128)S(1)} %crossed.1.refs_4_.refs_1_), channel_id=1, source_target_pairs={{0,16},{1,9},{2,18},{3,11},{4,20},{5,13},{6,22},{7,15},{8,24},{9,1... | collective-permute-start | bytes 399368 | tf_op jit(solution)/shard_map/ppermute | solution.py:83
  26.0 4.8 %collective-permute-start.18 = (f32[258,128]{1,0:T(8,128)S(1)}, f32[258,128]{1,0:T(8,128)S(1)}, u32[]{:S(2)}, u32[]{:S(2)}) collective-permute-start(f32[258,128]{1,0:T(8,128)S(1)} %gathered.1), channel_id=1, source_target_pairs={{0,1},{1,0},{2,3},{3,2},{4,5},{5,4},{6,7},{7,6},{8,9},{9,8},{10,11... | collective-permute-start | bytes 396296 | tf_op jit(solution)/shard_map/ppermute | solution.py:69
  26.1 9.2 %collective-permute-start.16 = (f32[4,16384]{1,0:T(4,128)S(1)}, f32[4,16384]{1,0:T(4,128)S(1)}, u32[]{:S(2)}, u32[]{:S(2)}) collective-permute-start(f32[4,16384]{1,0:T(4,128)S(1)} %get-tuple-element.59), channel_id=1, source_target_pairs={{0,8},{1,17},{2,10},{3,19},{4,12},{5,21},{6,14},{7,23},{8,0},{9,25... | collective-permute-start | bytes 786440 | tf_op jit(solution)/shard_map/ppermute | solution.py:83
  27.0 7.8 %collective-permute-start.15 = (f32[4,12288]{1,0:T(4,128)S(1)}, f32[4,12288]{1,0:T(4,128)S(1)}, u32[]{:S(2)}, u32[]{:S(2)}) collective-permute-start(f32[4,12288]{1,0:T(4,128)S(1)} %get-tuple-element.58), channel_id=1, source_target_pairs={{0,16},{1,9},{2,18},{3,11},{4,20},{5,13},{6,22},{7,15},{8,24},{9,1... | collective-permute-start | bytes 589832 | tf_op jit(solution)/shard_map/ppermute | solution.py:83
  28.7 8.7 %collective-permute-start.17 = (f32[4,8320]{1,0:T(4,128)S(1)}, f32[4,8320]{1,0:T(4,128)S(1)}, u32[]{:S(2)}, u32[]{:S(2)}) collective-permute-start(f32[4,8320]{1,0:T(4,128)S(1)} %pass_first.1), channel_id=1, source_target_pairs={{0,16},{1,9},{2,18},{3,11},{4,20},{5,13},{6,22},{7,15},{8,24},{9,1... | collective-permute-start | bytes 399368 | tf_op jit(solution)/shard_map/ppermute | solution.py:83
  30.8 4.6 %copy-start.4 = (f32[200,64]{0,1:T(8,128)S(1)}, f32[200,64]{0,1:T(8,128)}, u32[]{:S(2)}) copy-start(f32[200,64]{0,1:T(8,128)} %param.14) | copy-start | bytes 153604
  30.8 6.7 %collective-permute-start.19 = (f32[4,8192]{1,0:T(4,128)S(1)}, f32[4,8192]{1,0:T(4,128)S(1)}, u32[]{:S(2)}, u32[]{:S(2)}) collective-permute-start(f32[4,8192]{1,0:T(4,128)S(1)} %pass_second.1), channel_id=1, source_target_pairs={{0,8},{1,17},{2,10},{3,19},{4,12},{5,21},{6,14},{7,23},{8,0},{9,25... | collective-permute-start | bytes 393224 | tf_op jit(solution)/shard_map/ppermute | solution.py:83

commit v11 on v9

--- a/solution.py
+++ b/solution.py
@@ -555,7 +555,7 @@
             pltpu.VMEM(table if direct else (8, 128), f32),
             pltpu.VMEM((blocks, part), f32),
         ],
-        after=[*momentum_rows[:0:-1], momentum],
+        after=[*([momentum_rows[k] for k in (2, 3, 1)] if direct else []), momentum],
         name="dense",
     )
     dense = [plain, swap_in_turn(plain, 0), swap_in_turn(with_factor, 1)]

time: 38.4 us -> 38.4 us (level)
  no operation moved by 1% of the time
where the time goes in v11:
time: 38.4 us; the launch traced here: 38.2 us
  starting transfers between devices  23.2 us (60%)
  waiting for transfers between devices  8.38 us (22%)
  Pallas kernels  5.84 us (15%)
  between operations  0.78 us (2%)
    ppermute x12, starting transfers between devices, swap(): return lax.ppermute(x, axis, [(i, i ^ mask) for i in range(count)])  13.9 us
    ppermute x8, starting transfers between devices, swap_in_turn(): return lax.ppermute(x, ('rep', 'own'), pairs)  9.3 us
    ppermute x8, waiting for transfers between devices, swap_in_turn(): return lax.ppermute(x, ('rep', 'own'), pairs)  4.6 us
    ppermute x12, waiting for transfers between devices, swap(): return lax.ppermute(x, axis, [(i, i ^ mask) for i in range(count)])  3.78 us
    pallas_call x3, Pallas kernels, finishing(): pl.pallas_call(functools.partial(body, part, direct, halves), out_shape=[...  3.18 us
    pallas_call x11, Pallas kernels, run(): pl.pallas_call(whole, out_shape=list(outs), in_specs=[anywhere] * skip +...  2.66 us
  transfers between devices with their start and end apart: 20, of which 7 were waited for; matrix products, arithmetic and copies ran while one was open for 0% of the time, Pallas kernels for 9%

profile of v11, /device:TPU:0, one launch (start us, length us, event | category | flops | bytes accessed | tf_op | source)
XLA Modules:
  0.0 38.2 jit_solution(2225301981660015052)
XLA Ops:
  0.7 1.7 %start.1 = (f32[256,128]{1,0:T(8,128)S(1)}, f32[256,128]{1,0:T(8,128)S(1)}, f32[256,128]{1,0:T(8,128)S(1)}, f32[256,128]{1,0:T(8,128)S(1)}, f32[16,2048]{1,0:T(8...) custom-call(s32[16]{0:T(128)} %bitcast.7, ...), custom_call_target="tpu_custom_call" | custom-call | tf_op jit(solution)/shard_map/start/pallas_call | solution.py:49
  2.4 0.5 %collective-permute-start = (f32[4,4,2048]{2,1,0:T(4,128)S(1)}, f32[4,4,2048]{2,1,0:T(4,128)S(1)}, u32[]{:S(2)}, u32[]{:S(2)}) collective-permute-start(f32[4,4,2048]{2,1,0:T(4,128)S(1)} %get-tuple-element.37), channel_id=1, source_target_pairs={{0,1},{1,0},{2,3},{3,2},{4,5},{5,4},{6,7},{7,6},{8,9},{9,8},{10,11... | collective-permute-start | bytes 393224 | tf_op jit(solution)/shard_map/ppermute | solution.py:69
  2.9 2.6 %collective-permute-start.4 = (f32[256,128]{1,0:T(8,128)S(1)}, f32[256,128]{1,0:T(8,128)S(1)}, u32[]{:S(2)}, u32[]{:S(2)}) collective-permute-start(f32[256,128]{1,0:T(8,128)S(1)} %get-tuple-element.45), channel_id=1, source_target_pairs={{0,8},{8,0},{16,24},{24,16},{1,9},{9,1},{17,25},{25,17},{2,10},{10... | collective-permute-start | bytes 393224 | tf_op jit(solution)/shard_map/ppermute | solution.py:69
  5.4 1.5 %collective-permute-start.5 = (f32[256,128]{1,0:T(8,128)S(1)}, f32[256,128]{1,0:T(8,128)S(1)}, u32[]{:S(2)}, u32[]{:S(2)}) collective-permute-start(f32[256,128]{1,0:T(8,128)S(1)} %get-tuple-element.46), channel_id=1, source_target_pairs={{0,16},{8,24},{16,0},{24,8},{1,17},{9,25},{17,1},{25,9},{2,18},{10... | collective-permute-start | bytes 393224 | tf_op jit(solution)/shard_map/ppermute | solution.py:69
  7.0 3.1 %collective-permute-start.1 = (f32[2,4,2048]{2,1,0:T(4,128)S(1)}, f32[2,4,2048]{2,1,0:T(4,128)S(1)}, u32[]{:S(2)}, u32[]{:S(2)}) collective-permute-start(f32[2,4,2048]{2,1,0:T(4,128)S(1)} %get-tuple-element.38), channel_id=1, source_target_pairs={{0,4},{1,5},{2,6},{3,7},{4,0},{5,1},{6,2},{7,3},{8,12},{9,13},{10,... | collective-permute-start | bytes 196616 | tf_op jit(solution)/shard_map/ppermute | solution.py:69
  10.1 1.3 %collective-permute-start.2 = (f32[2,4,2048]{2,1,0:T(4,128)S(1)}, f32[2,4,2048]{2,1,0:T(4,128)S(1)}, u32[]{:S(2)}, u32[]{:S(2)}) collective-permute-start(f32[2,4,2048]{2,1,0:T(4,128)S(1)} %get-tuple-element.39), channel_id=1, source_target_pairs={{0,6},{1,7},{2,4},{3,5},{4,2},{5,3},{6,0},{7,1},{8,14},{9,15},{10,... | collective-permute-start | bytes 196616 | tf_op jit(solution)/shard_map/ppermute | solution.py:69
  11.5 0.2 collective-permute-start.3
  11.7 0.4 %factor.1.refs_0_.refs_7_.refs_2_ = f32[64,200]{1,0:T(8,128)S(1)} custom-call(f32[200,1024]{1,0:T(8,128)S(1)} %copy-done.1, f32[1,200,1024]{2,1,0:T(8,128)S(1)} %copy-done.3, f32[64,1024]{1,0:T(8,128)S(1)} %bitcast.4), custom_call_target="tpu_custom_call" | custom-call | tf_op jit(solution)/shard_map/factor/pallas_call | solution.py:49
  12.2 1.7 %collective-permute-done.5.refs_4_ = f32[256,128]{1,0:T(8,128)S(1)} collective-permute-done((f32[256,128]{1,0:T(8,128)S(1)}, f32[256,128]{1,0:T(8,128)S(1)}, u32[]{:S(2)}, u32[]{:S(2)}) %collective-permute-start.5) | collective-permute-done | bytes 131104 | tf_op jit(solution)/shard_map/ppermute | solution.py:69
  13.8 0.1 mean.1
  13.9 3.7 %collective-permute-start.9 = (f32[2,4,2048]{2,1,0:T(4,128)S(1)}, f32[2,4,2048]{2,1,0:T(4,128)S(1)}, u32[]{:S(2)}, u32[]{:S(2)}) collective-permute-start(f32[2,4,2048]{2,1,0:T(4,128)S(1)} %get-tuple-element.52), channel_id=1, source_target_pairs={{0,6},{1,7},{2,4},{3,5},{4,2},{5,3},{6,0},{7,1},{8,14},{9,15},{10,... | collective-permute-start | bytes 196616 | tf_op jit(solution)/shard_map/ppermute | solution.py:69
  17.6 0.8 %collective-permute-start.11 = (f32[2,4,2048]{2,1,0:T(4,128)S(1)}, f32[2,4,2048]{2,1,0:T(4,128)S(1)}, u32[]{:S(2)}, u32[]{:S(2)}) collective-permute-start(f32[2,4,2048]{2,1,0:T(4,128)S(1)} %get-tuple-element.54), channel_id=1, source_target_pairs={{0,2},{1,3},{2,0},{3,1},{4,6},{5,7},{6,4},{7,5},{8,10},{9,11},{10,... | collective-permute-start | bytes 196616 | tf_op jit(solution)/shard_map/ppermute | solution.py:69
  18.4 0.3 dense.1
  18.7 1.6 %collective-permute-start.8 = (f32[384,128]{1,0:T(8,128)S(1)}, f32[384,128]{1,0:T(8,128)S(1)}, u32[]{:S(2)}, u32[]{:S(2)}) collective-permute-start(f32[384,128]{1,0:T(8,128)S(1)} %get-tuple-element.51), channel_id=1, source_target_pairs={{0,16},{1,9},{2,18},{3,11},{4,20},{5,13},{6,22},{7,15},{8,24},{9,1... | collective-permute-start | bytes 589832 | tf_op jit(solution)/shard_map/ppermute | solution.py:83
  20.3 0.5 %collective-permute-start.7 = (f32[272,128]{1,0:T(8,128)S(1)}, f32[272,128]{1,0:T(8,128)S(1)}, u32[]{:S(2)}, u32[]{:S(2)}) collective-permute-start(f32[272,128]{1,0:T(8,128)S(1)} %get-tuple-element.50.refs_0_.refs_2_), channel_id=1, source_target_pairs={{0,8},{1,17},{2,10},{3,19},{4,12},{5,21},{6,14},{7,23},{8,0},{9,25... | collective-permute-start | bytes 417800 | tf_op jit(solution)/shard_map/ppermute | solution.py:83
  20.8 2.1 %collective-permute-done.10.refs_1_.refs_7_.refs_5_ = f32[2,4,2048]{2,1,0:T(4,128)S(1)} collective-permute-done((f32[2,4,2048]{2,1,0:T(4,128)S(1)}, f32[2,4,2048]{2,1,0:T(4,128)S(1)}, u32[]{:S(2)}, u32[]{:S(2)}) %collective-permute-start.10) | collective-permute-done | bytes 65568 | tf_op jit(solution)/shard_map/ppermute | solution.py:69
  22.9 0.1 collective-permute-start.12
  23.0 1.6 %collective-permute-start.13 = (f32[4,8704]{1,0:T(4,128)S(1)}, f32[4,8704]{1,0:T(4,128)S(1)}, u32[]{:S(2)}, u32[]{:S(2)}) collective-permute-start(f32[4,8704]{1,0:T(4,128)S(1)} %mine.1.refs_3_.refs_0_), channel_id=1, source_target_pairs={{0,8},{1,17},{2,10},{3,19},{4,12},{5,21},{6,14},{7,23},{8,0},{9,25... | collective-permute-start | bytes 417800 | tf_op jit(solution)/shard_map/ppermute | solution.py:83
  24.6 1.3 %collective-permute-start.14 = (f32[4,8448]{1,0:T(4,128)S(1)}, f32[4,8448]{1,0:T(4,128)S(1)}, u32[]{:S(2)}, u32[]{:S(2)}) collective-permute-start(f32[4,8448]{1,0:T(4,128)S(1)} %crossed.1.refs_4_.refs_1_), channel_id=1, source_target_pairs={{0,16},{1,9},{2,18},{3,11},{4,20},{5,13},{6,22},{7,15},{8,24},{9,1... | collective-permute-start | bytes 405512 | tf_op jit(solution)/shard_map/ppermute | solution.py:83
  26.0 0.1 collective-permute-start.17
  26.1 0.9 %collective-permute-start.16 = (f32[4,16384]{1,0:T(4,128)S(1)}, f32[4,16384]{1,0:T(4,128)S(1)}, u32[]{:S(2)}, u32[]{:S(2)}) collective-permute-start(f32[4,16384]{1,0:T(4,128)S(1)} %get-tuple-element.61), channel_id=1, source_target_pairs={{0,8},{1,17},{2,10},{3,19},{4,12},{5,21},{6,14},{7,23},{8,0},{9,25... | collective-permute-start | bytes 786440 | tf_op jit(solution)/shard_map/ppermute | solution.py:83
  27.0 1.2 %collective-permute-start.15 = (f32[4,12288]{1,0:T(4,128)S(1)}, f32[4,12288]{1,0:T(4,128)S(1)}, u32[]{:S(2)}, u32[]{:S(2)}) collective-permute-start(f32[4,12288]{1,0:T(4,128)S(1)} %get-tuple-element.60), channel_id=1, source_target_pairs={{0,16},{1,9},{2,18},{3,11},{4,20},{5,13},{6,22},{7,15},{8,24},{9,1... | collective-permute-start | bytes 589832 | tf_op jit(solution)/shard_map/ppermute | solution.py:83
  28.2 0.6 %collective-permute-done.13.refs_5_.refs_1_ = f32[4,8704]{1,0:T(4,128)S(1)} collective-permute-done((f32[4,8704]{1,0:T(4,128)S(1)}, f32[4,8704]{1,0:T(4,128)S(1)}, u32[]{:S(2)}, u32[]{:S(2)}) %collective-permute-start.13) | collective-permute-done | bytes 139296 | tf_op jit(solution)/shard_map/ppermute | solution.py:83
  28.8 1.4 %collective-permute-done.14.refs_6_.refs_2_ = f32[4,8448]{1,0:T(4,128)S(1)} collective-permute-done((f32[4,8448]{1,0:T(4,128)S(1)}, f32[4,8448]{1,0:T(4,128)S(1)}, u32[]{:S(2)}, u32[]{:S(2)}) %collective-permute-start.14) | collective-permute-done | bytes 135200 | tf_op jit(solution)/shard_map/ppermute | solution.py:83
  30.2 1.9 %collective-permute-start.18 = (f32[4,8192]{1,0:T(4,128)S(1)}, f32[4,8192]{1,0:T(4,128)S(1)}, u32[]{:S(2)}, u32[]{:S(2)}) collective-permute-start(f32[4,8192]{1,0:T(4,128)S(1)} %get-tuple-element.64), channel_id=1, source_target_pairs={{0,16},{1,9},{2,18},{3,11},{4,20},{5,13},{6,22},{7,15},{8,24},{9,1... | collective-permute-start | bytes 393224 | tf_op jit(solution)/shard_map/ppermute | solution.py:83
  32.1 0.3 collective-permute-start.19
  32.4 1.1 %early.1 = (f32[16,8192]{1,0:T(8,128)}, f32[4,65536]{1,0:T(4,128)}) custom-call(f32[272,128]{1,0:T(8,128)S(1)} %get-tuple-element.50.refs_0_.refs_2_, f32[272,128]{1,0:T(8,128)S(1)} %collective-permute-done.7.refs_1_.refs_3_.refs_0_, f32[384,128]{1,0:T(8,128)S(1)} %collective-permute-done.8.refs_2_.refs_4_.refs_1_, f32[4,8704]{1,0:T(4,128)S(1)} %mine.1.refs_3_.refs_0_, ...), custom_call_target="tpu_custom_call" | custom-call | tf_op jit(solution)/shard_map/early/pallas_call | solution.py:591
  33.5 1.3 %collective-permute-done.15.refs_1_ = f32[4,12288]{1,0:T(4,128)S(1)} collective-permute-done((f32[4,12288]{1,0:T(4,128)S(1)}, f32[4,12288]{1,0:T(4,128)S(1)}, u32[]{:S(2)}, u32[]{:S(2)}) %collective-permute-start.15) | collective-permute-done | bytes 196640 | tf_op jit(solution)/shard_map/ppermute | solution.py:83
  34.8 0.6 %collective-permute-done.16.refs_2_ = f32[4,16384]{1,0:T(4,128)S(1)} collective-permute-done((f32[4,16384]{1,0:T(4,128)S(1)}, f32[4,16384]{1,0:T(4,128)S(1)}, u32[]{:S(2)}, u32[]{:S(2)}) %collective-permute-start.16) | collective-permute-done | bytes 262176 | tf_op jit(solution)/shard_map/ppermute | solution.py:83
  35.4 1.3 %late.1 = (f32[16,8192]{1,0:T(8,128)}, f32[200,1024]{1,0:T(8,128)}, f32[64,200]{1,0:T(8,128)}, f32[4,65536]{1,0:T(4,128)}) custom-call(f32[16,8192]{1,0:T(8,128)} %get-tuple-element.57._, f32[4,65536]{1,0:T(4,128)} %get-tuple-element.58.__, f32[200,1024]{1,0:T(8,128)S(1)} %copy-done.1, ...), custom_call_target="tpu_custom_call", output_to_operand_aliasing={{0}: (0, {}), {3}: (1, {})} | custom-call | tf_op jit(solution)/shard_map/late/pallas_call | solution.py:591
  36.7 0.7 %collective-permute-done.18.refs_0_ = f32[4,8192]{1,0:T(4,128)S(1)} collective-permute-done((f32[4,8192]{1,0:T(4,128)S(1)}, f32[4,8192]{1,0:T(4,128)S(1)}, u32[]{:S(2)}, u32[]{:S(2)}) %collective-permute-start.18) | collective-permute-done | bytes 131104 | tf_op jit(solution)/shard_map/ppermute | solution.py:83
  37.5 0.8 %last.1 = f32[4,65536]{1,0:T(4,128)} custom-call(f32[4,65536]{1,0:T(4,128)} %get-tuple-element.63._, f32[4,8192]{1,0:T(4,128)S(1)} %collective-permute-done.18.refs_0_, f32[4,8192]{1,0:T(4,128)S(1)} %collective-permute-done.19.refs_1_), custom_call_target="tpu_custom_call", output_to_operand_aliasing={{}: (0, {})} | custom-call | tf_op jit(solution)/shard_map/last/pallas_call | solution.py:591
  (32 shorter events, 0.3 us)
Async XLA Ops:
  0.6 11.1 %copy-start.1 = (f32[200,1024]{1,0:T(8,128)S(1)}, f32[200,1024]{1,0:T(8,128)}, u32[]{:S(2)}) copy-start(f32[200,1024]{1,0:T(8,128)} %anchor.1) | copy-start | bytes 2457604
  0.6 11.1 %copy-start.3 = (f32[1,200,1024]{2,1,0:T(8,128)S(1)}, f32[1,200,1024]{2,1,0:T(8,128)}, u32[]{:S(2)}) copy-start(f32[1,200,1024]{2,1,0:T(8,128)} %refs_1_.4) | copy-start | bytes 2457604
  2.4 9.4 %copy-start.2 = (f32[1024,64]{0,1:T(8,128)S(1)}, f32[1024,64]{0,1:T(8,128)}, u32[]{:S(2)}) copy-start(f32[1024,64]{0,1:T(8,128)} %param.15) | copy-start | bytes 786436
  2.4 4.6 %collective-permute-start = (f32[4,4,2048]{2,1,0:T(4,128)S(1)}, f32[4,4,2048]{2,1,0:T(4,128)S(1)}, u32[]{:S(2)}, u32[]{:S(2)}) collective-permute-start(f32[4,4,2048]{2,1,0:T(4,128)S(1)} %get-tuple-element.37), channel_id=1, source_target_pairs={{0,1},{1,0},{2,3},{3,2},{4,5},{5,4},{6,7},{7,6},{8,9},{9,8},{10,11... | collective-permute-start | bytes 393224 | tf_op jit(solution)/shard_map/ppermute | solution.py:69
  2.9 8.6 %collective-permute-start.4 = (f32[256,128]{1,0:T(8,128)S(1)}, f32[256,128]{1,0:T(8,128)S(1)}, u32[]{:S(2)}, u32[]{:S(2)}) collective-permute-start(f32[256,128]{1,0:T(8,128)S(1)} %get-tuple-element.45), channel_id=1, source_target_pairs={{0,8},{8,0},{16,24},{24,16},{1,9},{9,1},{17,25},{25,17},{2,10},{10... | collective-permute-start | bytes 393224 | tf_op jit(solution)/shard_map/ppermute | solution.py:69
  5.4 8.4 %collective-permute-start.5 = (f32[256,128]{1,0:T(8,128)S(1)}, f32[256,128]{1,0:T(8,128)S(1)}, u32[]{:S(2)}, u32[]{:S(2)}) collective-permute-start(f32[256,128]{1,0:T(8,128)S(1)} %get-tuple-element.46), channel_id=1, source_target_pairs={{0,16},{8,24},{16,0},{24,8},{1,17},{9,25},{17,1},{25,9},{2,18},{10... | collective-permute-start | bytes 393224 | tf_op jit(solution)/shard_map/ppermute | solution.py:69
  7.0 6.9 %collective-permute-start.6 = (f32[256,128]{1,0:T(8,128)S(1)}, f32[256,128]{1,0:T(8,128)S(1)}, u32[]{:S(2)}, u32[]{:S(2)}) collective-permute-start(f32[256,128]{1,0:T(8,128)S(1)} %get-tuple-element.47), channel_id=1, source_target_pairs={{0,24},{8,16},{16,8},{24,0},{1,25},{9,17},{17,9},{25,1},{2,26},{10... | collective-permute-start | bytes 393224 | tf_op jit(solution)/shard_map/ppermute | solution.py:69
  7.0 10.6 %collective-permute-start.1 = (f32[2,4,2048]{2,1,0:T(4,128)S(1)}, f32[2,4,2048]{2,1,0:T(4,128)S(1)}, u32[]{:S(2)}, u32[]{:S(2)}) collective-permute-start(f32[2,4,2048]{2,1,0:T(4,128)S(1)} %get-tuple-element.38), channel_id=1, source_target_pairs={{0,4},{1,5},{2,6},{3,7},{4,0},{5,1},{6,2},{7,3},{8,12},{9,13},{10,... | collective-permute-start | bytes 196616 | tf_op jit(solution)/shard_map/ppermute | solution.py:69
  10.1 8.3 %collective-permute-start.2 = (f32[2,4,2048]{2,1,0:T(4,128)S(1)}, f32[2,4,2048]{2,1,0:T(4,128)S(1)}, u32[]{:S(2)}, u32[]{:S(2)}) collective-permute-start(f32[2,4,2048]{2,1,0:T(4,128)S(1)} %get-tuple-element.39), channel_id=1, source_target_pairs={{0,6},{1,7},{2,4},{3,5},{4,2},{5,3},{6,0},{7,1},{8,14},{9,15},{10,... | collective-permute-start | bytes 196616 | tf_op jit(solution)/shard_map/ppermute | solution.py:69
  11.5 6.9 %collective-permute-start.3 = (f32[2,4,2048]{2,1,0:T(4,128)S(1)}, f32[2,4,2048]{2,1,0:T(4,128)S(1)}, u32[]{:S(2)}, u32[]{:S(2)}) collective-permute-start(f32[2,4,2048]{2,1,0:T(4,128)S(1)} %get-tuple-element.40), channel_id=1, source_target_pairs={{0,2},{1,3},{2,0},{3,1},{4,6},{5,7},{6,4},{7,5},{8,10},{9,11},{10,... | collective-permute-start | bytes 196616 | tf_op jit(solution)/shard_map/ppermute | solution.py:69
  11.7 6.7 %copy-start = (f32[4,65536]{1,0:T(4,128)S(1)}, f32[4,65536]{1,0:T(4,128)}, u32[]{:S(2)}) copy-start(f32[4,65536]{1,0:T(4,128)} %refs_1_.5) | copy-start | bytes 3145732
  13.9 6.9 %collective-permute-start.9 = (f32[2,4,2048]{2,1,0:T(4,128)S(1)}, f32[2,4,2048]{2,1,0:T(4,128)S(1)}, u32[]{:S(2)}, u32[]{:S(2)}) collective-permute-start(f32[2,4,2048]{2,1,0:T(4,128)S(1)} %get-tuple-element.52), channel_id=1, source_target_pairs={{0,6},{1,7},{2,4},{3,5},{4,2},{5,3},{6,0},{7,1},{8,14},{9,15},{10,... | collective-permute-start | bytes 196616 | tf_op jit(solution)/shard_map/ppermute | solution.py:69
  17.6 5.3 %collective-permute-start.10 = (f32[2,4,2048]{2,1,0:T(4,128)S(1)}, f32[2,4,2048]{2,1,0:T(4,128)S(1)}, u32[]{:S(2)}, u32[]{:S(2)}) collective-permute-start(f32[2,4,2048]{2,1,0:T(4,128)S(1)} %get-tuple-element.53), channel_id=1, source_target_pairs={{0,4},{1,5},{2,6},{3,7},{4,0},{5,1},{6,2},{7,3},{8,12},{9,13},{10,... | collective-permute-start | bytes 196616 | tf_op jit(solution)/shard_map/ppermute | solution.py:69
  17.6 5.3 %collective-permute-start.11 = (f32[2,4,2048]{2,1,0:T(4,128)S(1)}, f32[2,4,2048]{2,1,0:T(4,128)S(1)}, u32[]{:S(2)}, u32[]{:S(2)}) collective-permute-start(f32[2,4,2048]{2,1,0:T(4,128)S(1)} %get-tuple-element.54), channel_id=1, source_target_pairs={{0,2},{1,3},{2,0},{3,1},{4,6},{5,7},{6,4},{7,5},{8,10},{9,11},{10,... | collective-permute-start | bytes 196616 | tf_op jit(solution)/shard_map/ppermute | solution.py:69
  18.7 7.3 %collective-permute-start.8 = (f32[384,128]{1,0:T(8,128)S(1)}, f32[384,128]{1,0:T(8,128)S(1)}, u32[]{:S(2)}, u32[]{:S(2)}) collective-permute-start(f32[384,128]{1,0:T(8,128)S(1)} %get-tuple-element.51), channel_id=1, source_target_pairs={{0,16},{1,9},{2,18},{3,11},{4,20},{5,13},{6,22},{7,15},{8,24},{9,1... | collective-permute-start | bytes 589832 | tf_op jit(solution)/shard_map/ppermute | solution.py:83
  20.3 5.7 %collective-permute-start.7 = (f32[272,128]{1,0:T(8,128)S(1)}, f32[272,128]{1,0:T(8,128)S(1)}, u32[]{:S(2)}, u32[]{:S(2)}) collective-permute-start(f32[272,128]{1,0:T(8,128)S(1)} %get-tuple-element.50.refs_0_.refs_2_), channel_id=1, source_target_pairs={{0,8},{1,17},{2,10},{3,19},{4,12},{5,21},{6,14},{7,23},{8,0},{9,25... | collective-permute-start | bytes 417800 | tf_op jit(solution)/shard_map/ppermute | solution.py:83
  22.9 1.7 %collective-permute-start.12 = (f32[4,8448]{1,0:T(4,128)S(1)}, f32[4,8448]{1,0:T(4,128)S(1)}, u32[]{:S(2)}, u32[]{:S(2)}) collective-permute-start(f32[4,8448]{1,0:T(4,128)S(1)} %other.1), channel_id=1, source_target_pairs={{0,1},{1,0},{2,3},{3,2},{4,5},{5,4},{6,7},{7,6},{8,9},{9,8},{10,11... | collective-permute-start | bytes 405512 | tf_op jit(solution)/shard_map/ppermute | solution.py:69
  23.0 5.8 %collective-permute-start.13 = (f32[4,8704]{1,0:T(4,128)S(1)}, f32[4,8704]{1,0:T(4,128)S(1)}, u32[]{:S(2)}, u32[]{:S(2)}) collective-permute-start(f32[4,8704]{1,0:T(4,128)S(1)} %mine.1.refs_3_.refs_0_), channel_id=1, source_target_pairs={{0,8},{1,17},{2,10},{3,19},{4,12},{5,21},{6,14},{7,23},{8,0},{9,25... | collective-permute-start | bytes 417800 | tf_op jit(solution)/shard_map/ppermute | solution.py:83
  24.6 5.5 %collective-permute-start.14 = (f32[4,8448]{1,0:T(4,128)S(1)}, f32[4,8448]{1,0:T(4,128)S(1)}, u32[]{:S(2)}, u32[]{:S(2)}) collective-permute-start(f32[4,8448]{1,0:T(4,128)S(1)} %crossed.1.refs_4_.refs_1_), channel_id=1, source_target_pairs={{0,16},{1,9},{2,18},{3,11},{4,20},{5,13},{6,22},{7,15},{8,24},{9,1... | collective-permute-start | bytes 405512 | tf_op jit(solution)/shard_map/ppermute | solution.py:83
  26.0 4.2 %collective-permute-start.17 = (f32[260,128]{1,0:T(8,128)S(1)}, f32[260,128]{1,0:T(8,128)S(1)}, u32[]{:S(2)}, u32[]{:S(2)}) collective-permute-start(f32[260,128]{1,0:T(8,128)S(1)} %gathered.1), channel_id=1, source_target_pairs={{0,1},{1,0},{2,3},{3,2},{4,5},{5,4},{6,7},{7,6},{8,9},{9,8},{10,11... | collective-permute-start | bytes 399368 | tf_op jit(solution)/shard_map/ppermute | solution.py:69
  26.1 9.2 %collective-permute-start.16 = (f32[4,16384]{1,0:T(4,128)S(1)}, f32[4,16384]{1,0:T(4,128)S(1)}, u32[]{:S(2)}, u32[]{:S(2)}) collective-permute-start(f32[4,16384]{1,0:T(4,128)S(1)} %get-tuple-element.61), channel_id=1, source_target_pairs={{0,8},{1,17},{2,10},{3,19},{4,12},{5,21},{6,14},{7,23},{8,0},{9,25... | collective-permute-start | bytes 786440 | tf_op jit(solution)/shard_map/ppermute | solution.py:83
  27.0 7.8 %collective-permute-start.15 = (f32[4,12288]{1,0:T(4,128)S(1)}, f32[4,12288]{1,0:T(4,128)S(1)}, u32[]{:S(2)}, u32[]{:S(2)}) collective-permute-start(f32[4,12288]{1,0:T(4,128)S(1)} %get-tuple-element.60), channel_id=1, source_target_pairs={{0,16},{1,9},{2,18},{3,11},{4,20},{5,13},{6,22},{7,15},{8,24},{9,1... | collective-permute-start | bytes 589832 | tf_op jit(solution)/shard_map/ppermute | solution.py:83
  30.2 7.3 %collective-permute-start.18 = (f32[4,8192]{1,0:T(4,128)S(1)}, f32[4,8192]{1,0:T(4,128)S(1)}, u32[]{:S(2)}, u32[]{:S(2)}) collective-permute-start(f32[4,8192]{1,0:T(4,128)S(1)} %get-tuple-element.64), channel_id=1, source_target_pairs={{0,16},{1,9},{2,18},{3,11},{4,20},{5,13},{6,22},{7,15},{8,24},{9,1... | collective-permute-start | bytes 393224 | tf_op jit(solution)/shard_map/ppermute | solution.py:83
  32.1 3.3 %copy-start.4 = (f32[200,64]{0,1:T(8,128)S(1)}, f32[200,64]{0,1:T(8,128)}, u32[]{:S(2)}) copy-start(f32[200,64]{0,1:T(8,128)} %param.14) | copy-start | bytes 153604
  32.1 5.4 %collective-permute-start.19 = (f32[4,8192]{1,0:T(4,128)S(1)}, f32[4,8192]{1,0:T(4,128)S(1)}, u32[]{:S(2)}, u32[]{:S(2)}) collective-permute-start(f32[4,8192]{1,0:T(4,128)S(1)} %get-tuple-element.65), channel_id=1, source_target_pairs={{0,8},{1,17},{2,10},{3,19},{4,12},{5,21},{6,14},{7,23},{8,0},{9,25... | collective-permute-start | bytes 393224 | tf_op jit(solution)/shard_map/ppermute | solution.py:83
